TPU v7x, 32 devices: a whole 2x2x4 slice. The times are simulated.
32 devices in a mesh: grp: 4 (over y, x), tok: 8 (over z, core).
Axes of the slice: x: 2, y: 2, z: 4, core: 2. Of those that a mesh axis runs over, the one named last changes fastest.
Arguments:
- patches: bfloat16 [32768, 1152], P(('grp', 'tok')), may hold values from -6 to 6
- labels: int32 [32768], P(('grp', 'tok')), may hold values from 0 to 149
- valid_mask: int32 [32768], P(('grp', 'tok')), may hold values from 0 to 1
- crop_counts: int32 [4, 2], P('grp'), may hold values from 31 to 53, as said below
- owners: int32 [13], replicated, may hold values from 0 to 7, as said below
- slot_weight: float32 [16, 409600], P('tok', 'grp')
- slot_moment: float32 [16, 409600], P('tok', 'grp'), may hold values from -0.00048828125 to 0.00048828125
- slot_second: float32 [16, 409600], P('tok', 'grp'), may hold values from 6.1035155e-10 to 2.4414062e-09
- norm_params: float32 [22, 320], replicated
- norm_moment: float32 [22, 320], replicated, may hold values from -0.00048828125 to 0.00048828125
- norm_second: float32 [22, 320], replicated
- head_weight: float32 [320, 150], replicated, may hold values from -0.625 to 0.625
- head_moment: float32 [320, 150], replicated, may hold values from -0.00048828125 to 0.00048828125
- head_second: float32 [320, 150], replicated
Outputs:
- loss_sum: float32 [], replicated
- pixel_total: float32 [], replicated
- new_slot_moment: float32 [16, 409600], P('tok', 'grp')
- new_slot_second: float32 [16, 409600], P('tok', 'grp')
- new_slot_weight: float32 [16, 409600], P('tok', 'grp')
- new_norm_moment: float32 [22, 320], replicated
- new_norm_second: float32 [22, 320], replicated
- new_norm_params: float32 [22, 320], replicated
- new_head_moment: float32 [320, 150], replicated
- new_head_second: float32 [320, 150], replicated
- new_head_weight: float32 [320, 150], replicated
Inputs may be any that keep to these rules, and one draw needn't show every extreme that they name: `owners`: each owner holds at most 2 units, and some owner holds exactly 2. `crop_counts`: A group's large crops number 32 to 36; its small crops fill the rest, leaving fewer than 6^2 padding tokens.
All inputs are finite; a program needn't handle non-finite values.
Results may differ from a plain program's by a relative error of at most 0.02.
The roundings to bfloat16 on the way count: a program that leaves them out, or rounds other values in their place, can miss the bound.
Values may be sent and summed in bfloat16 or wider, within the bound.
A program may use at most 960 MiB of HBM per device.

v0:
```python
import jax
import jax.numpy as jnp
from jax import lax
from jax.sharding import PartitionSpec as P

C = 320
HEADS = 5
HD = 64
FF = 1280
PIN = 1152
BLOCKS = 3
BIG_SIDE = 14
SMALL_SIDE = 6
STEP = 10
KVH = 49


EPS_NORM = 1e-06
BETA_ONE = 0.9
BETA_TWO = 0.999
ADAM_EPS = 1e-08
RATE_MATRIX = 0.05
RATE_VECTOR = 0.3
DECAY_RATE = 0.05
NEG_FILL = -1e30
PREC_HIGH = lax.Precision.HIGHEST


def extended(block, sides, width):
    for axis, dim in sides:
        count = lax.axis_size(axis)
        forward = [(i, i + 1) for i in range(count - 1)]
        backward = [(target, source) for source, target in forward]
        low = lax.ppermute(
            lax.slice_in_dim(block, block.shape[dim] - width, None, axis=dim), axis, forward
        )
        high = lax.ppermute(lax.slice_in_dim(block, 0, width, axis=dim), axis, backward)
        block = jnp.concatenate([low, block, high], axis=dim)
    return block


def layer_norm(values, gain_vec, shift_vec):
    center = values - jnp.mean(values, -1, keepdims=True)
    inverse = lax.rsqrt(jnp.mean(center * center, -1, keepdims=True) + EPS_NORM)
    return center * inverse * gain_vec + shift_vec


def gelu_exact(values):
    return jax.nn.gelu(values, approximate=False)


def image_layout(positions, counts):
    big_tok = BIG_SIDE * BIG_SIDE
    small_tok = SMALL_SIDE * SMALL_SIDE
    big_end = counts[0] * big_tok
    small_end = big_end + counts[1] * small_tok
    is_big = positions < big_end
    is_small = jnp.logical_and(positions >= big_end, positions < small_end)
    side_len = jnp.where(is_big, BIG_SIDE, jnp.where(is_small, SMALL_SIDE, 0))
    begin_at = jnp.where(
        is_big,
        positions // big_tok * big_tok,
        jnp.where(is_small, big_end + (positions - big_end) // small_tok * small_tok, small_end),
    )
    image_id = jnp.where(
        is_big,
        positions // big_tok,
        jnp.where(is_small, counts[0] + (positions - big_end) // small_tok, counts[0] + counts[1]),
    )
    half_side = jnp.maximum(side_len // 2, 1)
    within = positions - begin_at
    tile_idx = within // 4
    sub_idx = within % 4
    row_pos = tile_idx // half_side * 2 + sub_idx // 2
    col_pos = tile_idx % half_side * 2 + sub_idx % 2
    neighbours = []
    for shift_y in (-1, 0, 1):
        for shift_x in (-1, 0, 1):
            row_at = row_pos + shift_y
            col_at = col_pos + shift_x
            inside = (row_at >= 0) & (row_at < side_len) & (col_at >= 0) & (col_at < side_len)
            if shift_y == 0 and shift_x == 0:
                inside = jnp.ones_like(inside)
            target = (
                begin_at + (row_at // 2 * half_side + col_at // 2) * 4 + row_at % 2 * 2 + col_at % 2
            )
            neighbours.append(jnp.where(inside, target, -1))
    return (image_id, jnp.stack(neighbours, 1), positions < small_end)


def depthwise(values, neighbours, kernel):
    result = jnp.zeros((neighbours.shape[0], values.shape[1]), jnp.float32)
    for offset in range(9):
        column = neighbours[:, offset]
        picked = jnp.take(values, jnp.maximum(column, 0), axis=0).astype(jnp.float32)
        result = result + jnp.where((column >= 0)[:, None], picked, 0.0) * kernel[offset].astype(
            jnp.float32
        )
    return result


def kernel_grad(gradient, values, neighbours):
    tap_rows = []
    for offset in range(9):
        column = neighbours[:, offset]
        picked = jnp.take(values, jnp.maximum(column, 0), axis=0).astype(jnp.float32)
        tap_rows.append(jnp.sum(jnp.where((column >= 0)[:, None], picked, 0.0) * gradient, 0))
    return jnp.stack(tap_rows)


def unpack(unit_rows):
    embedding = unit_rows[0, : PIN * C].reshape(PIN, C)
    kernels = unit_rows[0, PIN * C : PIN * C + BLOCKS * 9 * FF].reshape(BLOCKS, 9, FF)
    layers = []
    for layer_at in range(BLOCKS):
        anchor = 1 + 4 * layer_at
        layers.append(
            (
                unit_rows[anchor, : C * C].reshape(C, C),
                unit_rows[anchor, C * C : 2 * C * C].reshape(C, C),
                unit_rows[anchor, 2 * C * C :].reshape(C, 2 * C),
                unit_rows[anchor + 1].reshape(4 * C, C),
                unit_rows[anchor + 2].reshape(C, FF),
                unit_rows[anchor + 3].reshape(FF, C),
            )
        )
    return (embedding, kernels, layers)


def adamw_step(weight, moment, second, gradient, rate_now, decay_now):
    moment = BETA_ONE * moment + (1.0 - BETA_ONE) * gradient
    second = BETA_TWO * second + (1.0 - BETA_TWO) * gradient * gradient
    m_hat = moment / (1.0 - BETA_ONE**STEP)
    v_hat = second / (1.0 - BETA_TWO**STEP)
    weight = weight - rate_now * (m_hat / (jnp.sqrt(v_hat) + ADAM_EPS) + decay_now * weight)
    return (moment, second, weight)


def product(left, right):
    return jnp.dot(left, right, preferred_element_type=jnp.float32)


def outer_sum(left, right):
    return lax.dot_general(
        left, right, (((0,), (0,)), ((), ())), preferred_element_type=jnp.float32
    )


def back_product(gradient, weight):
    return lax.dot_general(
        gradient, weight, (((1,), (1,)), ((), ())), preferred_element_type=jnp.float32
    )


def norm_back(values, gain_vec, shift_vec, gradient):
    _, pull_back = jax.vjp(layer_norm, values, gain_vec, shift_vec)
    return pull_back(gradient)


def block_views(queries, keyval, image_id, kv_id, block_index, block_rows):
    quarter = block_rows // 4
    span_rows = quarter + 2 * KVH
    q_block = lax.dynamic_slice_in_dim(queries, block_index * block_rows, block_rows, 0).reshape(
        block_rows, HEADS, HD
    )
    kv_block = lax.dynamic_slice_in_dim(keyval, block_index * quarter, span_rows, 0)
    keys_blk = kv_block[:, :C].reshape(span_rows, HEADS, HD)
    vals_blk = kv_block[:, C:].reshape(span_rows, HEADS, HD)
    allowed = (
        lax.dynamic_slice_in_dim(image_id, block_index * block_rows, block_rows, 0)[:, None]
        == lax.dynamic_slice_in_dim(kv_id, block_index * quarter, span_rows, 0)[None, :]
    )
    scores = jnp.einsum(
        "qhd,khd->hqk", q_block, keys_blk, preferred_element_type=jnp.float32
    ) * HD ** (-0.5)
    return (q_block, keys_blk, vals_blk, scores + jnp.where(allowed, 0.0, NEG_FILL))


def attend_forward(queries, keyval, image_id, kv_id, block_rows):

    def one_block(block_index):
        q_block, keys_blk, vals_blk, scores = block_views(
            queries, keyval, image_id, kv_id, block_index, block_rows
        )
        row_peak = jnp.max(scores, -1, keepdims=True)
        weights = jnp.exp(scores - row_peak)
        denom_sum = jnp.sum(weights, -1, keepdims=True)
        probs_low = (weights / denom_sum).astype(jnp.bfloat16)
        output = jnp.einsum("hqk,khd->qhd", probs_low, vals_blk, preferred_element_type=jnp.float32)
        return (
            output.reshape(block_rows, C).astype(jnp.bfloat16),
            (row_peak + jnp.log(denom_sum))[..., 0],
        )

    outputs, log_sums = lax.map(one_block, jnp.arange(queries.shape[0] // block_rows))
    return (outputs.reshape(queries.shape[0], C), log_sums)


def attend_backward(grad_out, queries, keyval, log_sums, image_id, kv_id, block_rows):
    quarter = block_rows // 4
    span_rows = quarter + 2 * KVH

    def one_step(block_index, carry):
        grad_query, grad_keyval = carry
        q_block, keys_blk, vals_blk, scores = block_views(
            queries, keyval, image_id, kv_id, block_index, block_rows
        )
        probs = jnp.exp(scores - log_sums[block_index][..., None])
        g_block = lax.dynamic_slice_in_dim(
            grad_out, block_index * block_rows, block_rows, 0
        ).reshape(block_rows, HEADS, HD)
        grad_probs = jnp.einsum(
            "qhd,khd->hqk", g_block, vals_blk, preferred_element_type=jnp.float32
        )
        inner = jnp.sum(probs * grad_probs, -1, keepdims=True)
        grad_scores = (probs * (grad_probs - inner) * HD ** (-0.5)).astype(jnp.bfloat16)
        grad_q_blk = jnp.einsum(
            "hqk,khd->qhd", grad_scores, keys_blk, preferred_element_type=jnp.float32
        )
        grad_keys = jnp.einsum(
            "hqk,qhd->khd", grad_scores, q_block, preferred_element_type=jnp.float32
        )
        grad_vals = jnp.einsum(
            "hqk,qhd->khd", probs.astype(jnp.bfloat16), g_block, preferred_element_type=jnp.float32
        )
        grad_query = lax.dynamic_update_slice_in_dim(
            grad_query, grad_q_blk.reshape(block_rows, C), block_index * block_rows, 0
        )
        piece = jnp.concatenate(
            [grad_keys.reshape(span_rows, C), grad_vals.reshape(span_rows, C)], 1
        )
        current = lax.dynamic_slice_in_dim(grad_keyval, block_index * quarter, span_rows, 0)
        grad_keyval = lax.dynamic_update_slice_in_dim(
            grad_keyval, current + piece, block_index * quarter, 0
        )
        return (grad_query, grad_keyval)

    start_vals = (jnp.zeros(queries.shape, jnp.float32), jnp.zeros(keyval.shape, jnp.float32))
    return lax.fori_loop(0, queries.shape[0] // block_rows, one_step, start_vals)


def layer_forward(resid, weights, kernel, gain_rows, context):
    w_query, w_out, w_keyval, w_reduce, w_up, w_down = weights
    image_id, kv_id, conv_taps, block_rows, tok_index = context
    normed_in = layer_norm(resid, gain_rows[0], gain_rows[1]).astype(jnp.bfloat16)
    queries = product(normed_in, w_query).astype(jnp.bfloat16)
    grouped = normed_in.reshape(normed_in.shape[0] // 4, 4 * C)
    reduced = product(grouped, w_reduce)
    normed_kv = layer_norm(reduced, gain_rows[2], gain_rows[3]).astype(jnp.bfloat16)
    keyval = product(normed_kv, w_keyval).astype(jnp.bfloat16)
    keyval_ext = extended(keyval, (("tok", 0),), KVH)
    attended, log_sums = attend_forward(queries, keyval_ext, image_id, kv_id, block_rows)
    middle = resid + product(attended, w_out)
    normed_mlp = layer_norm(middle, gain_rows[4], gain_rows[5]).astype(jnp.bfloat16)
    hidden = product(normed_mlp, w_up).astype(jnp.bfloat16)
    spread = lax.all_to_all(hidden, "tok", split_axis=1, concat_axis=0, tiled=True)
    channel_part = spread.shape[1]
    kernel_part = lax.dynamic_slice_in_dim(kernel, tok_index * channel_part, channel_part, 1)
    mixed_hid = depthwise(spread, conv_taps, kernel_part)
    active = lax.all_to_all(
        gelu_exact(mixed_hid).astype(jnp.bfloat16), "tok", split_axis=0, concat_axis=1, tiled=True
    )
    output = middle + product(active, w_down)
    kept_state = (
        resid,
        normed_in,
        queries,
        grouped,
        reduced,
        normed_kv,
        keyval_ext,
        attended,
        log_sums,
        middle,
        normed_mlp,
        spread,
        mixed_hid,
        active,
    )
    return (output, kept_state)


def layer_backward(grad_res, kept_state, weights, kernel, gain_rows, context):
    w_query, w_out, w_keyval, w_reduce, w_up, w_down = weights
    image_id, kv_id, conv_taps, block_rows, tok_index = context
    (
        resid,
        normed_in,
        queries,
        grouped,
        reduced,
        normed_kv,
        keyval_ext,
        attended,
        log_sums,
        middle,
        normed_mlp,
        spread,
        mixed_hid,
        active,
    ) = kept_state
    grad_low = grad_res.astype(jnp.bfloat16)
    d_down = outer_sum(active, grad_low)
    d_active = back_product(grad_low, w_down).astype(jnp.bfloat16)
    d_spread = lax.all_to_all(d_active, "tok", split_axis=1, concat_axis=0, tiled=True)
    d_mixed = jax.vjp(gelu_exact, mixed_hid)[1](d_spread.astype(jnp.float32))[0]
    channel_part = d_spread.shape[1]
    kernel_part = lax.dynamic_slice_in_dim(kernel, tok_index * channel_part, channel_part, 1)
    d_hidden = depthwise(d_mixed, conv_taps, kernel_part[::-1]).astype(jnp.bfloat16)
    d_kernel = lax.dynamic_update_slice_in_dim(
        jnp.zeros(kernel.shape, jnp.float32),
        kernel_grad(d_mixed, spread, conv_taps),
        tok_index * channel_part,
        1,
    )
    d_hidden = lax.all_to_all(d_hidden, "tok", split_axis=0, concat_axis=1, tiled=True)
    d_up = outer_sum(normed_mlp, d_hidden)
    d_middle, gain_four, gain_five = norm_back(
        middle, gain_rows[4], gain_rows[5], back_product(d_hidden, w_up)
    )
    grad_res = grad_res + d_middle
    grad_low = grad_res.astype(jnp.bfloat16)
    d_out = outer_sum(attended, grad_low)
    d_attended = back_product(grad_low, w_out).astype(jnp.bfloat16)
    d_query, d_kv_ext = attend_backward(
        d_attended, queries, keyval_ext, log_sums, image_id, kv_id, block_rows
    )
    edges = jnp.concatenate([d_kv_ext[:KVH], d_kv_ext[-KVH:]], 0)
    returned = extended(edges.astype(jnp.bfloat16), (("tok", 0),), KVH).astype(edges.dtype)
    own_rows = d_kv_ext[KVH:-KVH]
    own_rows = own_rows.at[:KVH].add(returned[:KVH]).at[-KVH:].add(returned[3 * KVH :])
    d_keyval = own_rows.astype(jnp.bfloat16)
    d_wkv = outer_sum(normed_kv, d_keyval)
    d_reduced, gain_two, gain_three = norm_back(
        reduced, gain_rows[2], gain_rows[3], back_product(d_keyval, w_keyval)
    )
    d_reduced = d_reduced.astype(jnp.bfloat16)
    d_reduce = outer_sum(grouped, d_reduced)
    d_grouped = back_product(d_reduced, w_reduce).reshape(normed_in.shape)
    d_query = d_query.astype(jnp.bfloat16)
    d_wq = outer_sum(normed_in, d_query)
    d_first = back_product(d_query, w_query) + d_grouped
    d_resid, gain_zero, gain_one = norm_back(resid, gain_rows[0], gain_rows[1], d_first)
    gain_grads = jnp.stack([gain_zero, gain_one, gain_two, gain_three, gain_four, gain_five])
    return (grad_res + d_resid, (d_wq, d_out, d_wkv, d_reduce, d_up, d_down), d_kernel, gain_grads)


def body(
    patches,
    labels,
    valid_mask,
    crop_counts,
    owners,
    slot_weight,
    slot_moment,
    slot_second,
    norm_params,
    norm_moment,
    norm_second,
    head_weight,
    head_moment,
    head_second,
):
    tok_dev = patches.shape[0]
    tok_index = lax.axis_index("tok")
    group_tok = tok_dev * lax.axis_size("tok")
    counts = crop_counts[0]
    n_unit = owners.shape[0]
    slot_rows = slot_weight.shape[0]
    unit_order = jnp.arange(n_unit, dtype=jnp.int32)
    same_owner = owners[:, None] == owners[None, :]
    rank_of = jnp.sum(same_owner & (unit_order[None, :] < unit_order[:, None]), 1)
    slot_of = owners * slot_rows + rank_of
    local_cols = lax.all_gather(slot_weight.astype(jnp.bfloat16), "grp", axis=1, tiled=True)
    all_slots = lax.all_gather(local_cols, "tok", axis=0, tiled=True)
    unit_rows = jnp.take(all_slots, slot_of, axis=0)
    embedding, kernels, layers = unpack(unit_rows)
    first_tok = tok_index * tok_dev
    positions = first_tok + jnp.arange(tok_dev, dtype=jnp.int32)
    image_id, neighbours, is_real = image_layout(positions, counts)
    keep_mask = valid_mask.astype(jnp.float32) * is_real.astype(jnp.float32)
    pixel_total = lax.psum(jnp.sum(keep_mask), ("grp", "tok"))
    kv_rows = first_tok // 4 - KVH + jnp.arange(tok_dev // 4 + 2 * KVH, dtype=jnp.int32)
    kv_inside = (kv_rows >= 0) & (kv_rows < group_tok // 4)
    kv_id = jnp.where(
        kv_inside, image_layout(jnp.clip(kv_rows, 0, group_tok // 4 - 1) * 4, counts)[0], -7
    )
    conv_taps = image_layout(jnp.arange(group_tok, dtype=jnp.int32), counts)[1]
    context = (image_id, kv_id, conv_taps, min(512, tok_dev), tok_index)
    tail = 6 * BLOCKS
    embed_pre = product(patches, embedding)
    resid = layer_norm(embed_pre, norm_params[tail], norm_params[tail + 1])
    kept_all = []
    for layer_at in range(BLOCKS):
        resid, kept_state = layer_forward(
            resid,
            layers[layer_at],
            kernels[layer_at],
            norm_params[6 * layer_at : 6 * layer_at + 6],
            context,
        )
        kept_all.append(kept_state)
    final = layer_norm(resid, norm_params[tail + 2], norm_params[tail + 3]).astype(jnp.bfloat16)
    head_low = head_weight.astype(jnp.bfloat16)
    logits = product(final, head_low)
    row_peak = jnp.max(logits, -1, keepdims=True)
    log_norm = row_peak[:, 0] + jnp.log(jnp.sum(jnp.exp(logits - row_peak), -1))
    onehot = (labels[:, None] == jnp.arange(head_weight.shape[1], dtype=jnp.int32)[None, :]).astype(
        jnp.float32
    )
    picked = jnp.sum(logits * onehot, 1)
    loss_local = jnp.sum((log_norm - picked) * keep_mask)
    probs = jnp.exp(logits - log_norm[:, None])
    d_logits = ((probs - onehot) * (keep_mask / pixel_total)[:, None]).astype(jnp.bfloat16)
    d_head = outer_sum(final, d_logits)
    grad_res, gain_final, shift_final = norm_back(
        resid, norm_params[tail + 2], norm_params[tail + 3], back_product(d_logits, head_low)
    )
    matrix_grads = [None] * BLOCKS
    kernel_grads = [None] * BLOCKS
    gain_grads = [None] * BLOCKS
    for layer_at in reversed(range(BLOCKS)):
        grad_res, matrix_grads[layer_at], kernel_grads[layer_at], gain_grads[layer_at] = (
            layer_backward(
                grad_res,
                kept_all[layer_at],
                layers[layer_at],
                kernels[layer_at],
                norm_params[6 * layer_at : 6 * layer_at + 6],
                context,
            )
        )
    d_embed_pre, gain_embed, shift_embed = norm_back(
        embed_pre, norm_params[tail], norm_params[tail + 1], grad_res
    )
    d_embedding = outer_sum(patches, d_embed_pre.astype(jnp.bfloat16))
    unit_size = unit_rows.shape[1]
    used = PIN * C + BLOCKS * 9 * FF
    unit_list = [
        jnp.concatenate(
            [
                d_embedding.reshape(-1),
                jnp.stack(kernel_grads).reshape(-1),
                jnp.zeros((unit_size - used,), jnp.float32),
            ]
        )
    ]
    for layer_at in range(BLOCKS):
        d_wq, d_out, d_wkv, d_reduce, d_up, d_down = matrix_grads[layer_at]
        unit_list.append(jnp.concatenate([d_wq.reshape(-1), d_out.reshape(-1), d_wkv.reshape(-1)]))
        unit_list.append(d_reduce.reshape(-1))
        unit_list.append(d_up.reshape(-1))
        unit_list.append(d_down.reshape(-1))
    stacked = jnp.stack(unit_list)
    norm_grads = jnp.concatenate(
        gain_grads + [jnp.stack([gain_embed, shift_embed, gain_final, shift_final])], 0
    )
    group_cols = lax.psum_scatter(
        stacked.astype(jnp.bfloat16), "grp", scatter_dimension=1, tiled=True
    ).astype(jnp.float32)
    row_ids = jnp.arange(slot_rows * lax.axis_size("tok"), dtype=jnp.int32)
    select = (slot_of[None, :] == row_ids[:, None]).astype(jnp.float32)
    owned = lax.psum_scatter(
        jnp.dot(select, group_cols, precision=PREC_HIGH).astype(jnp.bfloat16),
        "tok",
        scatter_dimension=0,
        tiled=True,
    ).astype(jnp.float32)
    norm_total, head_total, loss_sum = lax.psum((norm_grads, d_head, loss_local), ("grp", "tok"))
    slot_m, slot_v, slot_w = adamw_step(
        slot_weight, slot_moment, slot_second, owned, RATE_MATRIX, DECAY_RATE
    )
    norm_m, norm_v, norm_w = adamw_step(
        norm_params, norm_moment, norm_second, norm_total, RATE_VECTOR, 0.0
    )
    head_m, head_v, head_w = adamw_step(
        head_weight, head_moment, head_second, head_total, RATE_MATRIX, DECAY_RATE
    )
    return (
        loss_sum,
        pixel_total,
        slot_m,
        slot_v,
        slot_w,
        norm_m,
        norm_v,
        norm_w,
        head_m,
        head_v,
        head_w,
    )


def solution(mesh):
    in_specs = (
        P(("grp", "tok"), None),
        P(("grp", "tok")),
        P(("grp", "tok")),
        P("grp", None),
        P(),
        P("tok", "grp"),
        P("tok", "grp"),
        P("tok", "grp"),
        P(),
        P(),
        P(),
        P(),
        P(),
        P(),
    )
    out_specs = (
        P(),
        P(),
        P("tok", "grp"),
        P("tok", "grp"),
        P("tok", "grp"),
        P(),
        P(),
        P(),
        P(),
        P(),
        P(),
    )
    return jax.shard_map(body, mesh=mesh, in_specs=in_specs, out_specs=out_specs, check_vma=False)
```

profile of v0, /device:TPU:1, one launch (start us, length us, event | category | flops | bytes accessed | tf_op | source)
XLA Modules:
  0.0 4377.4 jit_solution(2410071625080233391)
XLA Ops:
  9.6 34.4 all-gather.4.cloned.1.call-done
  55.3 111.8 %all-gather.6.cloned.1.call-done = bf16[8,2,409600]{2,1,0:T(2,128)(2,1)} async-done(((bf16[1,2,409600]{2,1,0:T(2,128)(2,1)}), bf16[8,2,409600]{2,1,0:T(2,128)(2,1)}) %all-gather.6.cloned.1.call-update) | async-done | bytes 13107216 | tf_op jit(solution)/shard_map/all_gather | solution.py:375
  272.8 60.8 %slice_reduce_fusion = (bf16[409600]{0:T(1024)(128)(2,1)}, bf16[409600]{0:T(1024)(128)(2,1)}, bf16[409600]{0:T(1024)(128)(2,1)}, bf16[409600]{0:T(1024)(128)(2,1...) fusion(bf16[13,409600]{1,0:T(8,128)(2,1)} %maximum_select_fusion), kind=kLoop, calls=%fused_computation.430 | loop fusion | bytes 14745600 | tf_op jit(solution)/shard_map/slice | solution.py:124
  432.4 42.8 all-to-all-done
  481.2 33.8 gather_fusion.5
  582.6 33.8 gather_fusion.8
  717.8 33.9 gather_fusion.12
  751.7 33.8 gather_fusion.4
  785.8 45.6 %multiply_convert_fusion.5 = (bf16[8192,160]{1,0:T(8,128)(2,1)}, f32[8192,160]{1,0:T(8,128)}, f32[8192,160]{1,0:T(8,128)}) fusion(f32[160]{0:T(256)S(1)} %bitcast.662, bf16[8192,160]{1,0:T(8,128)(2,1)} %gather_fusion.12, pred[8192]{0:T(1024)(128)(4,1)S(1)} %get-tuple-element.1255, pred[8192]{0:T(1024)(128)(4,1)S(1)} %get-tuple-element.1280, ...), kind=kLoop, calls=%fused_computation.346 | loop fusion | flops 142868480 | bytes 36853376 | tf_op jit(solution)/shard_map/convert_element_type | solution.py:261
  855.7 46.8 %all-to-all-done.1 = bf16[8,1024,160]{1,2,0:T(8,128)(2,1)} async-done(((bf16[8,1024,160]{1,2,0:T(8,128)(2,1)}), bf16[8,1024,160]{1,2,0:T(8,128)(2,1)}, u32[]{:S(2)}, u32[]{:S(2)}) %all-to-all-start.1) | async-done | bytes 2621472 | tf_op jit(solution)/shard_map/all_to_all | solution.py:260
  958.5 58.3 %all-to-all-done.2 = bf16[1024,8,160]{0,2,1:T(8,128)(2,1)} async-done(((bf16[1024,8,160]{0,2,1:T(8,128)(2,1)}), bf16[1024,8,160]{0,2,1:T(8,128)(2,1)}, u32[]{:S(2)}, u32[]{:S(2)}) %all-to-all-start.2) | async-done | bytes 2621472 | tf_op jit(solution)/shard_map/all_to_all | solution.py:256
  1022.7 33.9 gather_fusion.14
  1157.9 33.9 gather_fusion.18
  1259.3 33.9 gather_fusion.13
  1293.4 33.9 gather_fusion.21
  1327.5 45.6 %multiply_convert_fusion.4 = (bf16[8192,160]{1,0:T(8,128)(2,1)}, f32[8192,160]{1,0:T(8,128)}, f32[8192,160]{1,0:T(8,128)}) fusion(f32[160]{0:T(256)S(1)} %bitcast.664, bf16[8192,160]{1,0:T(8,128)(2,1)} %gather_fusion.21, pred[8192]{0:T(1024)(128)(4,1)S(1)} %get-tuple-element.1255, pred[8192]{0:T(1024)(128)(4,1)S(1)} %copy-done.204, f32[160]{0:T(256)S(1)} %bitcast.678, ...), kind=kLoop, calls=%fused_computation.323 | loop fusion | flops 142868480 | bytes 36853376 | tf_op jit(solution)/shard_map/convert_element_type | solution.py:261
  1397.3 46.8 %all-to-all-done.3 = bf16[8,1024,160]{1,2,0:T(8,128)(2,1)} async-done(((bf16[8,1024,160]{1,2,0:T(8,128)(2,1)}), bf16[8,1024,160]{1,2,0:T(8,128)(2,1)}, u32[]{:S(2)}, u32[]{:S(2)}) %all-to-all-start.3) | async-done | bytes 2621472 | tf_op jit(solution)/shard_map/all_to_all | solution.py:260
  1494.5 63.6 %all_to_all.210 = bf16[1024,8,160]{0,2,1:T(8,128)(2,1)} all-to-all(bf16[1024,8,160]{0,2,1:T(8,128)(2,1)} %bitcast.618), channel_id=1, replica_groups=mesh['grp'=4,'tok'=8] {'tok'}, dimensions={1} | all-to-all | bytes 5242880 | tf_op jit(solution)/shard_map/all_to_all | solution.py:256
  1564.1 33.9 gather_fusion.23
  1631.8 33.8 gather_fusion.25
  1699.5 33.8 gather_fusion.27
  1733.3 33.9 gather_fusion.28
  1835.0 33.9 gather_fusion.30
  1869.1 45.6 %multiply_convert_fusion.3 = (bf16[8192,160]{1,0:T(8,128)(2,1)}, f32[8192,160]{1,0:T(8,128)}, f32[8192,160]{1,0:T(8,128)}) fusion(f32[160]{0:T(256)S(1)} %bitcast.698, bf16[8192,160]{1,0:T(8,128)(2,1)} %gather_fusion.30, pred[8192]{0:T(1024)(128)(4,1)S(1)} %get-tuple-element.1255, pred[8192]{0:T(1024)(128)(4,1)S(1)} %copy-done.205, f32[160]{0:T(256)S(1)} %bitcast.684, ...), kind=kLoop, calls=%fused_computation.300 | loop fusion | flops 142868480 | bytes 36853376 | tf_op jit(solution)/shard_map/convert_element_type | solution.py:261
  1928.6 57.6 %all-to-all-done.5 = bf16[8,1024,160]{1,2,0:T(8,128)(2,1)} async-done(((bf16[8,1024,160]{1,2,0:T(8,128)(2,1)}), bf16[8,1024,160]{1,2,0:T(8,128)(2,1)}, u32[]{:S(2)}, u32[]{:S(2)}) %all-to-all-start.5) | async-done | bytes 2621472 | tf_op jit(solution)/shard_map/all_to_all | solution.py:260
  1993.0 37.5 psum.29
  2043.0 65.0 %all_to_all.211 = bf16[1024,8,160]{0,2,1:T(8,128)(2,1)S(1)} all-to-all(bf16[1024,8,160]{0,2,1:T(8,128)(2,1)} %bitcast.620), channel_id=1, replica_groups=mesh['grp'=4,'tok'=8] {'tok'}, dimensions={1} | all-to-all | bytes 5242880 | tf_op jit(solution)/shard_map/all_to_all | solution.py:305
  2145.9 34.8 gather_fusion.32
  2180.8 34.9 gather_fusion.33
  2215.6 34.9 gather_fusion.34
  2250.5 34.9 gather_fusion.35
  2285.4 34.8 gather_fusion.36
  2320.2 35.0 gather_fusion.37
  2355.2 34.9 gather_fusion.38
  2390.1 34.8 gather_fusion.31
  2425.2 34.9 gather_fusion.39
  2499.0 59.6 %all-to-all-done.7 = bf16[8,1024,160]{1,2,0:T(8,128)(2,1)} async-done(((bf16[8,1024,160]{1,2,0:T(8,128)(2,1)}), bf16[8,1024,160]{1,2,0:T(8,128)(2,1)}, u32[]{:S(2)}, u32[]{:S(2)}) %all-to-all-start.7) | async-done | bytes 2621472 | tf_op jit(solution)/shard_map/all_to_all | solution.py:316
  2568.7 52.1 %while.90 = (s32[]{:T(128)}, bf16[1024,320]{0,1:T(8,128)(2,1)}, f32[354,640]{0,1:T(8,128)}, bf16[354,640]{0,1:T(8,128)(2,1)}, bf16[1024,320]{0,1:T(8,128)(2,1)},...) while((s32[]{:T(128)}, bf16[1024,320]{0,1:T(8,128)(2,1)}, ...), condition=%wide.region_48.51_spmd, body=%wide.region_46.50_spmd.sunk | while | flops 378904512 | bytes 26410736 | solution.py:239
  2772.5 34.9 gather_fusion.46
  2807.3 34.9 gather_fusion.47
  2842.3 34.9 gather_fusion.41
  2877.1 34.9 gather_fusion.42
  2912.0 34.9 gather_fusion.43
  2946.9 34.8 gather_fusion.44
  2981.7 35.0 gather_fusion.45
  3016.7 35.0 gather_fusion.40
  3052.0 34.9 gather_fusion.48
  3135.2 49.5 %all-to-all-done.9 = bf16[8,1024,160]{1,2,0:T(8,128)(2,1)} async-done(((bf16[8,1024,160]{1,2,0:T(8,128)(2,1)}), bf16[8,1024,160]{1,2,0:T(8,128)(2,1)}, u32[]{:S(2)}, u32[]{:S(2)}) %all-to-all-start.9) | async-done | bytes 2621472 | tf_op jit(solution)/shard_map/all_to_all | solution.py:316
  3199.1 53.3 %while.91 = (s32[]{:T(128)}, bf16[1024,320]{0,1:T(8,128)(2,1)}, f32[354,640]{0,1:T(8,128)}, bf16[354,640]{0,1:T(8,128)(2,1)}, bf16[1024,320]{0,1:T(8,128)(2,1)},...) while((s32[]{:T(128)}, bf16[1024,320]{0,1:T(8,128)(2,1)}, ...), condition=%wide.region_57.60_spmd, body=%wide.region_55.59_spmd.sunk | while | flops 378904512 | bytes 26410736 | solution.py:239
  3329.6 49.2 %all-to-all-done.10 = bf16[1024,8,160]{0,2,1:T(8,128)(2,1)} async-done(((bf16[1024,8,160]{0,2,1:T(8,128)(2,1)}), bf16[1024,8,160]{0,2,1:T(8,128)(2,1)}, u32[]{:S(2)}, u32[]{:S(2)}) %all-to-all-start.10) | async-done | bytes 2621472 | tf_op jit(solution)/shard_map/all_to_all | solution.py:305
  3418.3 35.0 gather_fusion.50
  3453.3 34.9 gather_fusion.51
  3488.2 34.9 gather_fusion.52
  3523.2 34.9 gather_fusion.53
  3558.0 35.0 gather_fusion.54
  3593.0 34.8 gather_fusion.55
  3627.8 34.9 gather_fusion.56
  3662.7 34.9 gather_fusion.49
  3697.9 34.9 gather_fusion.57
  3845.1 50.7 %while.92 = (s32[]{:T(128)}, bf16[1024,320]{0,1:T(8,128)(2,1)}, f32[354,640]{0,1:T(8,128)}, bf16[354,640]{0,1:T(8,128)(2,1)}, bf16[1024,320]{0,1:T(8,128)(2,1)},...) while((s32[]{:T(128)}, bf16[1024,320]{0,1:T(8,128)(2,1)}, ...), condition=%wide.region_66.69_spmd, body=%wide.region_64.68_spmd.sunk | while | flops 378904512 | bytes 26410736 | solution.py:239
  3964.3 63.8 %stack.186 = bf16[13,409600]{1,0:T(8,128)(2,1)} concatenate(bf16[1,409600]{1,0:T(2,128)(2,1)} %stack.182, bf16[1,409600]{1,0:T(2,128)(2,1)} %stack.183, bf16[1,409600]{1,0:T(2,128)(2,1)} %stack_reshape.36, bf16[1,409600]{1,0:T(2,128)(2,1)} %bitcast.632, bf16[1,409600]{1,0:T(2,128)(2,1)} %stack_reshape.38, bf16[1,409600]{1,0:T(2,128)(2,1)} %stack.184, ...), dimensions={0} | concatenate | bytes 21299200 | tf_op jit(solution)/shard_map/stack | solution.py:454
  4031.6 121.6 %reduce-scatter.2.cloned.1.call-done = bf16[13,102400]{1,0:T(8,128)(2,1)} async-done(((bf16[13,409600]{1,0:T(8,128)(2,1)}), bf16[13,102400]{1,0:T(8,128)(2,1)}) %reduce-scatter.2.cloned.1.call-update) | async-done | bytes 2662416 | tf_op jit(solution)/shard_map/reduce_scatter | solution.py:458
  4162.3 121.0 %all-reduce.5.cloned.1.call-done = f32[320,150]{0,1:T(8,128)} async-done(((f32[320,150]{0,1:T(8,128)}), f32[320,150]{0,1:T(8,128)}) %all-reduce.5.cloned.1.call-update) | async-done | bytes 192016 | tf_op jit(solution)/shard_map/psum | solution.py:469
  4294.5 41.4 all-reduce.1
  (1527 shorter events, 1735.5 us)
Async XLA Ops:
  7.2 36.9 all-gather.4.cloned.1.call-start
  9.6 157.6 %all-gather.6.cloned.1.call-start = ((), (), s32[]{:S(2)}) async-start(), calls=%async_computation.16 | async-start | bytes 14745600 | tf_op jit(solution)/shard_map/all_gather | solution.py:375
  369.7 11.7 collective-permute-start
  371.7 9.8 collective-permute-start.1
  412.0 63.2 %all-to-all-start = ((bf16[1024,8,160]{0,2,1:T(8,128)(2,1)}), bf16[1024,8,160]{0,2,1:T(8,128)(2,1)}, u32[]{:S(2)}, u32[]{:S(2)}) async-start(bf16[1024,8,160]{0,2,1:T(8,128)(2,1)} %bitcast.614), calls=%async_computation | async-start | bytes 5242880 | tf_op jit(solution)/shard_map/all_to_all | solution.py:256
  417.3 368.2 %copy-start.134 = (pred[8192]{0:T(1024)(128)(4,1)}, pred[8192]{0:T(1024)(128)(4,1)S(1)}, u32[]{:S(2)}) copy-start(pred[8192]{0:T(1024)(128)(4,1)S(1)} %get-tuple-element.1256) | copy-start | bytes 24580
  417.3 1701.7 %copy-start.130 = (pred[8192]{0:T(1024)(128)(4,1)}, pred[8192]{0:T(1024)(128)(4,1)S(1)}, u32[]{:S(2)}) copy-start(pred[8192]{0:T(1024)(128)(4,1)S(1)} %get-tuple-element.1255) | copy-start | bytes 24580
  418.3 367.2 %copy-start.140 = (pred[8192]{0:T(1024)(128)(4,1)}, pred[8192]{0:T(1024)(128)(4,1)S(1)}, u32[]{:S(2)}) copy-start(pred[8192]{0:T(1024)(128)(4,1)S(1)} %get-tuple-element.1259) | copy-start | bytes 24580
  418.3 367.2 %copy-start.146 = (pred[8192]{0:T(1024)(128)(4,1)}, pred[8192]{0:T(1024)(128)(4,1)S(1)}, u32[]{:S(2)}) copy-start(pred[8192]{0:T(1024)(128)(4,1)S(1)} %get-tuple-element.1260) | copy-start | bytes 24580
  419.2 366.3 %copy-start.152 = (pred[8192]{0:T(1024)(128)(4,1)}, pred[8192]{0:T(1024)(128)(4,1)S(1)}, u32[]{:S(2)}) copy-start(pred[8192]{0:T(1024)(128)(4,1)S(1)} %get-tuple-element.1263) | copy-start | bytes 24580
  419.2 366.3 %copy-start.158 = (pred[8192]{0:T(1024)(128)(4,1)}, pred[8192]{0:T(1024)(128)(4,1)S(1)}, u32[]{:S(2)}) copy-start(pred[8192]{0:T(1024)(128)(4,1)S(1)} %get-tuple-element.1264) | copy-start | bytes 24580
  420.2 365.4 %copy-start.164 = (pred[8192]{0:T(1024)(128)(4,1)}, pred[8192]{0:T(1024)(128)(4,1)S(1)}, u32[]{:S(2)}) copy-start(pred[8192]{0:T(1024)(128)(4,1)S(1)} %get-tuple-element.1272) | copy-start | bytes 24580
  420.2 365.4 %copy-start.226 = (pred[8192]{0:T(1024)(128)(4,1)}, pred[8192]{0:T(1024)(128)(4,1)S(1)}, u32[]{:S(2)}) copy-start(pred[8192]{0:T(1024)(128)(4,1)S(1)} %get-tuple-element.1271) | copy-start | bytes 24580
  421.2 364.4 %copy-start.170 = (pred[8192]{0:T(1024)(128)(4,1)}, pred[8192]{0:T(1024)(128)(4,1)S(1)}, u32[]{:S(2)}) copy-start(pred[8192]{0:T(1024)(128)(4,1)S(1)} %get-tuple-element.1273) | copy-start | bytes 24580
  421.2 364.4 %copy-start.177 = (pred[8192]{0:T(1024)(128)(4,1)}, pred[8192]{0:T(1024)(128)(4,1)S(1)}, u32[]{:S(2)}) copy-start(pred[8192]{0:T(1024)(128)(4,1)S(1)} %get-tuple-element.1274) | copy-start | bytes 24580
  422.1 363.5 %copy-start.185 = (pred[8192]{0:T(1024)(128)(4,1)}, pred[8192]{0:T(1024)(128)(4,1)S(1)}, u32[]{:S(2)}) copy-start(pred[8192]{0:T(1024)(128)(4,1)S(1)} %get-tuple-element.1275) | copy-start | bytes 24580
  422.1 363.5 %copy-start.194 = (pred[8192]{0:T(1024)(128)(4,1)}, pred[8192]{0:T(1024)(128)(4,1)S(1)}, u32[]{:S(2)}) copy-start(pred[8192]{0:T(1024)(128)(4,1)S(1)} %get-tuple-element.1276) | copy-start | bytes 24580
  423.1 362.5 %copy-start.203 = (pred[8192]{0:T(1024)(128)(4,1)}, pred[8192]{0:T(1024)(128)(4,1)S(1)}, u32[]{:S(2)}) copy-start(pred[8192]{0:T(1024)(128)(4,1)S(1)} %get-tuple-element.1280) | copy-start | bytes 24580
  423.1 362.5 %copy-start.232 = (pred[8192]{0:T(1024)(128)(4,1)}, pred[8192]{0:T(1024)(128)(4,1)S(1)}, u32[]{:S(2)}) copy-start(pred[8192]{0:T(1024)(128)(4,1)S(1)} %get-tuple-element.1279) | copy-start | bytes 24580
  424.0 361.6 %copy-start.238 = (pred[8192]{0:T(1024)(128)(4,1)}, pred[8192]{0:T(1024)(128)(4,1)S(1)}, u32[]{:S(2)}) copy-start(pred[8192]{0:T(1024)(128)(4,1)S(1)} %get-tuple-element.1267) | copy-start | bytes 24580
  424.0 361.6 %copy-start.244 = (pred[8192]{0:T(1024)(128)(4,1)}, pred[8192]{0:T(1024)(128)(4,1)S(1)}, u32[]{:S(2)}) copy-start(pred[8192]{0:T(1024)(128)(4,1)S(1)} %get-tuple-element.1268) | copy-start | bytes 24580
  425.0 360.7 %copy-start.250 = (pred[8192]{0:T(1024)(128)(4,1)}, pred[8192]{0:T(1024)(128)(4,1)S(1)}, u32[]{:S(2)}) copy-start(pred[8192]{0:T(1024)(128)(4,1)S(1)} %get-tuple-element.1277) | copy-start | bytes 24580
  425.0 360.7 %copy-start.256 = (pred[8192]{0:T(1024)(128)(4,1)}, pred[8192]{0:T(1024)(128)(4,1)S(1)}, u32[]{:S(2)}) copy-start(pred[8192]{0:T(1024)(128)(4,1)S(1)} %get-tuple-element.1278) | copy-start | bytes 24580
  425.9 1375.1 %copy-start.82 = (s32[8192]{0:T(1024)}, s32[8192]{0:T(1024)S(1)}, u32[]{:S(2)}) copy-start(s32[8192]{0:T(1024)S(1)} %maximum_clamp_fusion.8) | copy-start | bytes 98308
  426.8 629.7 %copy-start.107 = (s32[8192]{0:T(1024)}, s32[8192]{0:T(1024)S(1)}, u32[]{:S(2)}) copy-start(s32[8192]{0:T(1024)S(1)} %get-tuple-element.1269) | copy-start | bytes 98308
  427.8 1237.9 %copy-start.99 = (s32[8192]{0:T(1024)}, s32[8192]{0:T(1024)S(1)}, u32[]{:S(2)}) copy-start(s32[8192]{0:T(1024)S(1)} %get-tuple-element.1265) | copy-start | bytes 98308
  429.1 1270.3 %copy-start.103 = (s32[8192]{0:T(1024)}, s32[8192]{0:T(1024)S(1)}, u32[]{:S(2)}) copy-start(s32[8192]{0:T(1024)S(1)} %get-tuple-element.1262) | copy-start | bytes 98308
  429.2 1304.1 %copy-start.91 = (s32[8192]{0:T(1024)}, s32[8192]{0:T(1024)S(1)}, u32[]{:S(2)}) copy-start(s32[8192]{0:T(1024)S(1)} %get-tuple-element.1261) | copy-start | bytes 98308
  430.1 1337.0 %copy-start.95 = (s32[8192]{0:T(1024)}, s32[8192]{0:T(1024)S(1)}, u32[]{:S(2)}) copy-start(s32[8192]{0:T(1024)S(1)} %get-tuple-element.1258) | copy-start | bytes 98308
  432.4 353.3 %copy-start.367 = (f32[1,160]{1,0:T(1,128)}, f32[1,160]{1,0:T(1,128)S(1)}, u32[]{:S(2)}) copy-start(f32[1,160]{1,0:T(1,128)S(1)} %get-tuple-element.1214) | copy-start | bytes 1924
  432.4 353.3 %copy-start.369 = (f32[1,160]{1,0:T(1,128)}, f32[1,160]{1,0:T(1,128)S(1)}, u32[]{:S(2)}) copy-start(f32[1,160]{1,0:T(1,128)S(1)} %get-tuple-element.1215) | copy-start | bytes 1924
  432.4 353.3 %copy-start.371 = (f32[1,160]{1,0:T(1,128)}, f32[1,160]{1,0:T(1,128)S(1)}, u32[]{:S(2)}) copy-start(f32[1,160]{1,0:T(1,128)S(1)} %get-tuple-element.1216) | copy-start | bytes 1924
  432.4 353.3 %copy-start.373 = (f32[1,160]{1,0:T(1,128)}, f32[1,160]{1,0:T(1,128)S(1)}, u32[]{:S(2)}) copy-start(f32[1,160]{1,0:T(1,128)S(1)} %get-tuple-element.1217) | copy-start | bytes 1924
  837.6 64.8 %all-to-all-start.1 = ((bf16[8,1024,160]{1,2,0:T(8,128)(2,1)}), bf16[8,1024,160]{1,2,0:T(8,128)(2,1)}, u32[]{:S(2)}, u32[]{:S(2)}) async-start(bf16[8,1024,160]{1,2,0:T(8,128)(2,1)} %copy.122), calls=%async_computation.1 | async-start | bytes 5242880 | tf_op jit(solution)/shard_map/all_to_all | solution.py:260
  916.7 6.9 collective-permute-start.2
  918.6 5.7 collective-permute-start.3
  952.7 64.0 %all-to-all-start.2 = ((bf16[1024,8,160]{0,2,1:T(8,128)(2,1)}), bf16[1024,8,160]{0,2,1:T(8,128)(2,1)}, u32[]{:S(2)}, u32[]{:S(2)}) async-start(bf16[1024,8,160]{0,2,1:T(8,128)(2,1)} %bitcast.616), calls=%async_computation.2 | async-start | bytes 5242880 | tf_op jit(solution)/shard_map/all_to_all | solution.py:256
  958.4 368.9 %copy-start.381 = (f32[1,160]{1,0:T(1,128)}, f32[1,160]{1,0:T(1,128)S(1)}, u32[]{:S(2)}) copy-start(f32[1,160]{1,0:T(1,128)S(1)} %get-tuple-element.1281) | copy-start | bytes 1924
  958.4 368.9 %copy-start.383 = (f32[1,160]{1,0:T(1,128)}, f32[1,160]{1,0:T(1,128)S(1)}, u32[]{:S(2)}) copy-start(f32[1,160]{1,0:T(1,128)S(1)} %get-tuple-element.1282) | copy-start | bytes 1924
  958.4 368.9 %copy-start.385 = (f32[1,160]{1,0:T(1,128)}, f32[1,160]{1,0:T(1,128)S(1)}, u32[]{:S(2)}) copy-start(f32[1,160]{1,0:T(1,128)S(1)} %get-tuple-element.1283) | copy-start | bytes 1924
  958.4 368.9 %copy-start.387 = (f32[1,160]{1,0:T(1,128)}, f32[1,160]{1,0:T(1,128)S(1)}, u32[]{:S(2)}) copy-start(f32[1,160]{1,0:T(1,128)S(1)} %get-tuple-element.1284) | copy-start | bytes 1924
  958.4 368.9 %copy-start.389 = (f32[1,160]{1,0:T(1,128)}, f32[1,160]{1,0:T(1,128)S(1)}, u32[]{:S(2)}) copy-start(f32[1,160]{1,0:T(1,128)S(1)} %get-tuple-element.1285) | copy-start | bytes 1924
  958.4 368.9 %copy-start.391 = (f32[1,160]{1,0:T(1,128)}, f32[1,160]{1,0:T(1,128)S(1)}, u32[]{:S(2)}) copy-start(f32[1,160]{1,0:T(1,128)S(1)} %get-tuple-element.1286) | copy-start | bytes 1924
  958.4 368.9 %copy-start.393 = (f32[1,160]{1,0:T(1,128)}, f32[1,160]{1,0:T(1,128)S(1)}, u32[]{:S(2)}) copy-start(f32[1,160]{1,0:T(1,128)S(1)} %get-tuple-element.1287) | copy-start | bytes 1924
  958.4 368.9 %copy-start.395 = (f32[1,160]{1,0:T(1,128)}, f32[1,160]{1,0:T(1,128)S(1)}, u32[]{:S(2)}) copy-start(f32[1,160]{1,0:T(1,128)S(1)} %get-tuple-element.1288) | copy-start | bytes 1924
  958.4 368.9 %copy-start.397 = (f32[1,160]{1,0:T(1,128)}, f32[1,160]{1,0:T(1,128)S(1)}, u32[]{:S(2)}) copy-start(f32[1,160]{1,0:T(1,128)S(1)} %get-tuple-element.1289) | copy-start | bytes 1924
  1379.2 65.0 %all-to-all-start.3 = ((bf16[8,1024,160]{1,2,0:T(8,128)(2,1)}), bf16[8,1024,160]{1,2,0:T(8,128)(2,1)}, u32[]{:S(2)}, u32[]{:S(2)}) async-start(bf16[8,1024,160]{1,2,0:T(8,128)(2,1)} %copy.128), calls=%async_computation.3 | async-start | bytes 5242880 | tf_op jit(solution)/shard_map/all_to_all | solution.py:260
  1458.5 6.9 collective-permute-start.4
  1460.4 5.7 collective-permute-start.5
  1920.8 65.4 %all-to-all-start.5 = ((bf16[8,1024,160]{1,2,0:T(8,128)(2,1)}), bf16[8,1024,160]{1,2,0:T(8,128)(2,1)}, u32[]{:S(2)}, u32[]{:S(2)}) async-start(bf16[8,1024,160]{1,2,0:T(8,128)(2,1)} %copy.134), calls=%async_computation.5 | async-start | bytes 5242880 | tf_op jit(solution)/shard_map/all_to_all | solution.py:260
  2493.5 65.0 %all-to-all-start.7 = ((bf16[8,1024,160]{1,2,0:T(8,128)(2,1)}), bf16[8,1024,160]{1,2,0:T(8,128)(2,1)}, u32[]{:S(2)}, u32[]{:S(2)}) async-start(bf16[8,1024,160]{1,2,0:T(8,128)(2,1)} %copy.137), calls=%async_computation.7 | async-start | bytes 5242880 | tf_op jit(solution)/shard_map/all_to_all | solution.py:316
  2622.2 6.0 collective-permute-start.6
  2624.1 6.6 collective-permute-start.7
  2668.5 64.2 %all-to-all-start.8 = ((bf16[1024,8,160]{0,2,1:T(8,128)(2,1)}), bf16[1024,8,160]{0,2,1:T(8,128)(2,1)}, u32[]{:S(2)}, u32[]{:S(2)}) async-start(bf16[1024,8,160]{0,2,1:T(8,128)(2,1)} %bitcast.615), calls=%async_computation.8 | async-start | bytes 5242880 | tf_op jit(solution)/shard_map/all_to_all | solution.py:305
  3120.2 64.6 %all-to-all-start.9 = ((bf16[8,1024,160]{1,2,0:T(8,128)(2,1)}), bf16[8,1024,160]{1,2,0:T(8,128)(2,1)}, u32[]{:S(2)}, u32[]{:S(2)}) async-start(bf16[8,1024,160]{1,2,0:T(8,128)(2,1)} %copy.142), calls=%async_computation.9 | async-start | bytes 5242880 | tf_op jit(solution)/shard_map/all_to_all | solution.py:316
  3254.6 15.1 collective-permute-start.8
  3256.5 13.2 collective-permute-start.9
  3314.8 63.9 %all-to-all-start.10 = ((bf16[1024,8,160]{0,2,1:T(8,128)(2,1)}), bf16[1024,8,160]{0,2,1:T(8,128)(2,1)}, u32[]{:S(2)}, u32[]{:S(2)}) async-start(bf16[1024,8,160]{0,2,1:T(8,128)(2,1)} %bitcast.617), calls=%async_computation.10 | async-start | bytes 5242880 | tf_op jit(solution)/shard_map/all_to_all | solution.py:305
  3766.0 64.7 %all-to-all-start.11 = ((bf16[8,1024,160]{1,2,0:T(8,128)(2,1)}), bf16[8,1024,160]{1,2,0:T(8,128)(2,1)}, u32[]{:S(2)}, u32[]{:S(2)}) async-start(bf16[8,1024,160]{1,2,0:T(8,128)(2,1)} %copy.147), calls=%async_computation.11 | async-start | bytes 5242880 | tf_op jit(solution)/shard_map/all_to_all | solution.py:316
  3771.4 381.7 %reduce-scatter.2.cloned.1.call-start = ((), (), s32[]{:S(2)}) async-start(), calls=%async_computation.14 | async-start | bytes 16384000 | tf_op jit(solution)/shard_map/reduce_scatter | solution.py:458
  3897.9 14.2 collective-permute-start.10
  3899.9 12.3 collective-permute-start.11
  4028.2 255.1 %all-reduce.5.cloned.1.call-start = ((), (), s32[]{:S(2)}) async-start(), calls=%async_computation.15 | async-start | bytes 466944 | tf_op jit(solution)/shard_map/psum | solution.py:469
  4031.5 333.9 %all-reduce.7.cloned.1.call-start = ((), (), s32[]{:S(2)}) async-start(), calls=%async_computation.17 | async-start | bytes 6553600
  (438 other events, 15438.3 us)
Sparse Core Ops, SparseCore 0:
  10.4 33.5 all-gather.3
  45.7 121.4 all-gather.5
  4028.4 124.7 reduce-scatter.1
  4159.1 124.2 all-reduce.4
  4285.6 79.7 all-reduce.6
where the time goes:
time: 4400 us; the launch traced here: 4380 us
  local copies, waits for them, and re-layouts  2480 us (56%)
  waiting for transfers between devices  890 us (20%)
  other arithmetic  435 us (10%)
  matrix products  254 us (6%)
  blocking collectives  207 us (5%)
  starting transfers between devices  79.2 us (2%)
    gather x54, local copies, waits for them, and re-layouts, depthwise(): jnp.take(values, jnp.maximum(column, 0), axis=0).astype(jnp.float32)  1860 us
    all_to_all x3, waiting for transfers between devices, layer_forward(): lax.all_to_all(gelu_exact(mixed_hid).astype(jnp.bfloat16), 'tok', split_a...  151 us
    all_to_all x3, waiting for transfers between devices, layer_backward(): lax.all_to_all(d_hidden, 'tok', split_axis=0, concat_axis=1, tiled=True)  142 us
    convert_element_type x3, other arithmetic, layer_forward(): gelu_exact(mixed_hid).astype(jnp.bfloat16)  137 us
    reduce_scatter x1, waiting for transfers between devices, body(): lax.psum_scatter(stacked.astype(jnp.bfloat16), 'grp', scatter_dimension=1...  122 us
    psum x1, waiting for transfers between devices, body(): lax.psum((norm_grads, d_head, loss_local), ('grp', 'tok'))  121 us
    all_gather x1, waiting for transfers between devices, body(): all_slots = lax.all_gather(local_cols, 'tok', axis=0, tiled=True)  112 us
    reduce_sum x4, other arithmetic, kernel_grad(): jnp.sum(jnp.where((column >= 0)[:, None], picked, 0.0) * gradient, 0)  105 us
  transfers between devices with their start and end apart: 27, of which 18 were waited for; matrix products, arithmetic and copies ran while one was open for 4% of the time, Pallas kernels for 0%

commit v1 on v0

v1 whole, which is shorter than its diff:
```python
import jax
import jax.numpy as jnp
from jax import lax
from jax.sharding import PartitionSpec as P

C = 320
HEADS = 5
HD = 64
FF = 1280
PIN = 1152
BLOCKS = 3
BIG_SIDE = 14
SMALL_SIDE = 6
STEP = 10
KVH = 49


EPS_NORM = 1e-06
BETA_ONE = 0.9
BETA_TWO = 0.999
ADAM_EPS = 1e-08
RATE_MATRIX = 0.05
RATE_VECTOR = 0.3
DECAY_RATE = 0.05
NEG_FILL = -1e30
PREC_HIGH = lax.Precision.HIGHEST


def layer_norm(values, gain_vec, shift_vec):
    center = values - jnp.mean(values, -1, keepdims=True)
    inverse = lax.rsqrt(jnp.mean(center * center, -1, keepdims=True) + EPS_NORM)
    return center * inverse * gain_vec + shift_vec


def gelu_exact(values):
    return jax.nn.gelu(values, approximate=False)


def adamw_step(weight, moment, second, gradient, rate_now, decay_now):
    moment = BETA_ONE * moment + (1.0 - BETA_ONE) * gradient
    second = BETA_TWO * second + (1.0 - BETA_TWO) * gradient * gradient
    m_hat = moment / (1.0 - BETA_ONE**STEP)
    v_hat = second / (1.0 - BETA_TWO**STEP)
    weight = weight - rate_now * (m_hat / (jnp.sqrt(v_hat) + ADAM_EPS) + decay_now * weight)
    return (moment, second, weight)


def product(left, right):
    return jnp.dot(left, right, preferred_element_type=jnp.float32)


def outer_sum(left, right):
    return lax.dot_general(
        left, right, (((0,), (0,)), ((), ())), preferred_element_type=jnp.float32
    )


def back_product(gradient, weight):
    return lax.dot_general(
        gradient, weight, (((1,), (1,)), ((), ())), preferred_element_type=jnp.float32
    )


def norm_back(values, gain_vec, shift_vec, gradient):
    _, pull_back = jax.vjp(layer_norm, values, gain_vec, shift_vec)
    return pull_back(gradient)


OVER = 4 * KVH - 4


def image_layout(positions, counts):
    big_tok = BIG_SIDE * BIG_SIDE
    small_tok = SMALL_SIDE * SMALL_SIDE
    big_end = counts[0] * big_tok
    small_end = big_end + counts[1] * small_tok
    is_big = positions < big_end
    is_small = jnp.logical_and(positions >= big_end, positions < small_end)
    half_side = jnp.where(is_big, BIG_SIDE // 2, SMALL_SIDE // 2)
    begin_at = jnp.where(
        is_big,
        positions // big_tok * big_tok,
        jnp.where(is_small, big_end + (positions - big_end) // small_tok * small_tok, small_end),
    )
    tile_idx = (positions - begin_at) // 4
    return (begin_at, half_side, tile_idx // half_side, tile_idx % half_side, positions < small_end)


def shift_matrices(begin_at, half_side, tile_y, tile_x, is_real):
    count = begin_at.shape[0]
    own = jnp.arange(count, dtype=jnp.int32)
    offset = own[None, :] - own[:, None]
    inside = {
        (0, -1): tile_x > 0,
        (0, 1): tile_x < half_side - 1,
        (-1, 0): tile_y > 0,
        (1, 0): tile_y < half_side - 1,
    }
    result = {}
    for step_y in (-1, 0, 1):
        for step_x in (-1, 0, 1):
            if step_y == 0 and step_x == 0:
                continue
            allowed = is_real
            if step_y:
                allowed = allowed & inside[step_y, 0]
            if step_x:
                allowed = allowed & inside[0, step_x]
            hit = (offset == (step_y * half_side + step_x)[:, None]) & allowed[:, None]
            result[step_y, step_x] = hit.astype(jnp.bfloat16)
    return result


def tap_source(sub, tap):
    y_at = sub // 2 + tap // 3 - 1
    x_at = sub % 2 + tap % 3 - 1
    return (y_at % 2 * 2 + x_at % 2, y_at // 2, x_at // 2)


def shifted_planes(planes, shifts):
    moved = {}
    for sub in range(4):
        step_y = 1 - 2 * (sub // 2)
        step_x = 1 - 2 * (sub % 2)
        moved[sub, 0, 0] = planes[sub]
        for key in ((0, step_x), (step_y, 0), (step_y, step_x)):
            moved[(sub,) + key] = product(shifts[key], planes[sub]).astype(jnp.bfloat16)
    return moved


def depthwise(moved, kernel, is_real):
    rows = []
    for sub in range(4):
        center = moved[sub, 0, 0].astype(jnp.float32) * kernel[4]
        total = center
        for tap in range(9):
            if tap != 4:
                total = total + moved[tap_source(sub, tap)].astype(jnp.float32) * kernel[tap]
        rows.append(jnp.where(is_real[:, None], total, center))
    return jnp.stack(rows)


def kernel_grad(moved, hidden):
    taps = []
    for tap in range(9):
        total = 0.0
        for sub in range(4):
            total = total + hidden[sub].astype(jnp.float32) * moved[tap_source(sub, tap)].astype(jnp.float32)
        taps.append(jnp.sum(total, 0))
    return jnp.stack(taps[::-1])


def split_heads(values):
    return values.reshape(values.shape[0], HEADS, HD)


def attend_scores(queries, keyval, allowed):
    scores = jnp.einsum(
        "qhd,khd->hqk", split_heads(queries), split_heads(keyval[:, :C]), preferred_element_type=jnp.float32
    ) * HD ** (-0.5)
    scores = scores + jnp.where(allowed, 0.0, NEG_FILL)
    weights = jnp.exp(scores - jnp.max(scores, -1, keepdims=True))
    return weights / jnp.sum(weights, -1, keepdims=True)


def attend_forward(queries, keyval, allowed):
    probs = attend_scores(queries, keyval, allowed).astype(jnp.bfloat16)
    output = jnp.einsum("hqk,khd->qhd", probs, split_heads(keyval[:, C:]), preferred_element_type=jnp.float32)
    return output.reshape(queries.shape).astype(jnp.bfloat16)


def attend_backward(grad_out, queries, keyval, allowed):
    probs = attend_scores(queries, keyval, allowed)
    g_heads = split_heads(grad_out)
    grad_probs = jnp.einsum(
        "qhd,khd->hqk", g_heads, split_heads(keyval[:, C:]), preferred_element_type=jnp.float32
    )
    inner = jnp.sum(probs * grad_probs, -1, keepdims=True)
    grad_scores = (probs * (grad_probs - inner) * HD ** (-0.5)).astype(jnp.bfloat16)
    grad_q = jnp.einsum(
        "hqk,khd->qhd", grad_scores, split_heads(keyval[:, :C]), preferred_element_type=jnp.float32
    )
    grad_k = jnp.einsum("hqk,qhd->khd", grad_scores, split_heads(queries), preferred_element_type=jnp.float32)
    grad_v = jnp.einsum(
        "hqk,qhd->khd", probs.astype(jnp.bfloat16), g_heads, preferred_element_type=jnp.float32
    )
    rows = keyval.shape[0]
    return (
        grad_q.reshape(queries.shape).astype(jnp.bfloat16),
        jnp.concatenate([grad_k.reshape(rows, C), grad_v.reshape(rows, C)], 1).astype(jnp.bfloat16),
    )


def beside(values):
    tiles = values.shape[0] // 4
    return jnp.concatenate([values[sub * tiles : (sub + 1) * tiles] for sub in range(4)], 1)


def unbeside(values):
    return jnp.concatenate([values[:, sub * C : (sub + 1) * C] for sub in range(4)], 0)


def layer_forward(resid, weights, kernel, gain_rows, context):
    w_query, w_out, w_keyval, w_reduce, w_up, w_down = weights
    allowed, shifts, is_real = context
    normed_in = layer_norm(resid, gain_rows[0], gain_rows[1]).astype(jnp.bfloat16)
    queries = product(normed_in, w_query).astype(jnp.bfloat16)
    grouped = beside(normed_in)
    reduced = product(grouped, w_reduce)
    normed_kv = layer_norm(reduced, gain_rows[2], gain_rows[3]).astype(jnp.bfloat16)
    keyval = product(normed_kv, w_keyval).astype(jnp.bfloat16)
    attended = attend_forward(queries, keyval, allowed)
    middle = resid + product(attended, w_out)
    normed_mlp = layer_norm(middle, gain_rows[4], gain_rows[5]).astype(jnp.bfloat16)
    hidden = product(normed_mlp, w_up).astype(jnp.bfloat16)
    planes = hidden.reshape(4, -1, FF)
    mixed = depthwise(shifted_planes(planes, shifts), kernel, is_real).reshape(hidden.shape)
    active = gelu_exact(mixed).astype(jnp.bfloat16)
    output = middle + product(active, w_down)
    kept = (resid, normed_in, queries, grouped, reduced, normed_kv, keyval, attended, middle, normed_mlp, hidden, mixed, active)
    return (output, kept)


def layer_backward(grad_res, kept, weights, kernel, gain_rows, context):
    w_query, w_out, w_keyval, w_reduce, w_up, w_down = weights
    allowed, shifts, is_real = context
    resid, normed_in, queries, grouped, reduced, normed_kv, keyval, attended, middle, normed_mlp, hidden, mixed, active = kept
    grad_low = grad_res.astype(jnp.bfloat16)
    d_down = outer_sum(active, grad_low)
    d_active = back_product(grad_low, w_down).astype(jnp.bfloat16)
    d_mixed = jax.vjp(gelu_exact, mixed)[1](d_active.astype(jnp.float32))[0]
    moved = shifted_planes(d_mixed.astype(jnp.bfloat16).reshape(4, -1, FF), shifts)
    d_hidden = depthwise(moved, kernel[::-1], is_real).astype(jnp.bfloat16).reshape(hidden.shape)
    d_kernel = kernel_grad(moved, hidden.reshape(4, -1, FF))
    d_up = outer_sum(normed_mlp, d_hidden)
    d_middle, gain_four, gain_five = norm_back(
        middle, gain_rows[4], gain_rows[5], back_product(d_hidden, w_up)
    )
    grad_res = grad_res + d_middle
    grad_low = grad_res.astype(jnp.bfloat16)
    d_out = outer_sum(attended, grad_low)
    d_attended = back_product(grad_low, w_out).astype(jnp.bfloat16)
    d_query, d_keyval = attend_backward(d_attended, queries, keyval, allowed)
    d_wkv = outer_sum(normed_kv, d_keyval)
    d_reduced, gain_two, gain_three = norm_back(
        reduced, gain_rows[2], gain_rows[3], back_product(d_keyval, w_keyval)
    )
    d_reduced = d_reduced.astype(jnp.bfloat16)
    d_reduce = outer_sum(grouped, d_reduced)
    d_grouped = unbeside(back_product(d_reduced, w_reduce))
    d_wq = outer_sum(normed_in, d_query)
    d_first = back_product(d_query, w_query) + d_grouped
    d_resid, gain_zero, gain_one = norm_back(resid, gain_rows[0], gain_rows[1], d_first)
    gain_grads = jnp.stack([gain_zero, gain_one, gain_two, gain_three, gain_four, gain_five])
    low = [part.astype(jnp.bfloat16) for part in (d_wq, d_out, d_wkv, d_reduce, d_up, d_down)]
    units = jnp.stack(
        [
            jnp.concatenate([low[0], low[1], low[2].reshape(-1, C)], 0),
            low[3],
            low[4].reshape(-1, C),
            low[5],
        ]
    )
    return (grad_res + d_resid, units, d_kernel, gain_grads)


BOTH = ("grp", "tok")


def body(
    patches,
    labels,
    valid_mask,
    crop_counts,
    owners,
    slot_weight,
    slot_moment,
    slot_second,
    norm_params,
    norm_moment,
    norm_second,
    head_weight,
    head_moment,
    head_second,
):
    tok_dev = patches.shape[0]
    n_tok = lax.axis_size("tok")
    n_grp = lax.axis_size("grp")
    tok_index = lax.axis_index("tok")
    group_tok = tok_dev * n_tok
    counts = crop_counts[0]
    n_unit = owners.shape[0]
    slot_rows, columns = slot_weight.shape
    unit_order = jnp.arange(n_unit, dtype=jnp.int32)
    same_owner = owners[:, None] == owners[None, :]
    rank_of = jnp.sum(same_owner & (unit_order[None, :] < unit_order[:, None]), 1)
    slot_of = owners * slot_rows + rank_of
    chunk = columns // n_tok // C
    pieces = slot_weight.astype(jnp.bfloat16).reshape(slot_rows, n_tok, chunk, C)
    pieces = lax.all_to_all(pieces, "tok", split_axis=1, concat_axis=0, tiled=True)
    unit_part = jnp.take(pieces.reshape(slot_rows * n_tok, chunk, C), slot_of, axis=0)
    first_unit = lax.all_gather(unit_part[0], BOTH, axis=0, tiled=True)
    embedding = first_unit[:PIN]
    kernels = first_unit[PIN : PIN + BLOCKS * 9 * FF // C].reshape(BLOCKS, 9, FF).astype(jnp.float32)
    layers = []
    for layer_at in range(BLOCKS):
        own = lax.all_gather(unit_part[1 + 4 * layer_at : 5 + 4 * layer_at], BOTH, axis=1, tiled=True)
        layers.append(
            (own[0, :C], own[0, C : 2 * C], own[0, 2 * C :].reshape(C, 2 * C), own[1], own[2].reshape(C, FF), own[3])
        )

    towards = [(i + 1, i) for i in range(n_tok - 1)]
    window = tok_dev + OVER
    tiles = window // 4
    patches = jnp.concatenate([patches, lax.ppermute(patches[:OVER], "tok", towards)], 0)
    marks = jnp.stack([labels, valid_mask])
    marks = jnp.concatenate([marks, lax.ppermute(marks[:, :OVER], "tok", towards)], 1)
    patches = patches.reshape(tiles, 4, PIN).transpose(1, 0, 2).reshape(window, PIN)
    marks = marks.reshape(2, tiles, 4).transpose(0, 2, 1).reshape(2, window)
    labels = marks[0]
    first_tok = tok_index * tok_dev
    positions = first_tok + 4 * jnp.arange(tiles, dtype=jnp.int32)
    begin_at, half_side, tile_y, tile_x, _ = image_layout(positions, counts)
    own_image = (begin_at >= first_tok) & (begin_at < first_tok + tok_dev) & (positions < group_tok)
    is_real = positions < counts[0] * BIG_SIDE**2 + counts[1] * SMALL_SIDE**2
    shifts = shift_matrices(begin_at, half_side, tile_y, tile_x, is_real)
    image_of = jnp.where(positions < group_tok, begin_at, -1)
    allowed = jnp.tile(image_of, 4)[:, None] == image_of[None, :]
    keep_mask = marks[1].astype(jnp.float32) * jnp.tile((own_image & is_real).astype(jnp.float32), 4)
    pixel_total = lax.psum(jnp.sum(keep_mask), BOTH)
    context = (allowed, shifts, is_real)
    tail = 6 * BLOCKS
    embed_pre = product(patches, embedding)
    resid = layer_norm(embed_pre, norm_params[tail], norm_params[tail + 1])
    kept_all = []
    for layer_at in range(BLOCKS):
        resid, kept_state = layer_forward(
            resid,
            layers[layer_at],
            kernels[layer_at],
            norm_params[6 * layer_at : 6 * layer_at + 6],
            context,
        )
        kept_all.append(kept_state)
    final = layer_norm(resid, norm_params[tail + 2], norm_params[tail + 3]).astype(jnp.bfloat16)
    head_low = head_weight.astype(jnp.bfloat16)
    logits = product(final, head_low)
    row_peak = jnp.max(logits, -1, keepdims=True)
    log_norm = row_peak[:, 0] + jnp.log(jnp.sum(jnp.exp(logits - row_peak), -1))
    onehot = (labels[:, None] == jnp.arange(head_weight.shape[1], dtype=jnp.int32)[None, :]).astype(
        jnp.float32
    )
    picked = jnp.sum(logits * onehot, 1)
    loss_local = jnp.sum((log_norm - picked) * keep_mask)
    probs = jnp.exp(logits - log_norm[:, None])
    d_logits = ((probs - onehot) * (keep_mask / pixel_total)[:, None]).astype(jnp.bfloat16)
    d_head = outer_sum(final, d_logits)
    grad_res, gain_final, shift_final = norm_back(
        resid, norm_params[tail + 2], norm_params[tail + 3], back_product(d_logits, head_low)
    )
    unit_grads = [None] * BLOCKS
    kernel_grads = [None] * BLOCKS
    gain_grads = [None] * BLOCKS
    for layer_at in reversed(range(BLOCKS)):
        grad_res, units, kernel_grads[layer_at], gain_grads[layer_at] = (
            layer_backward(
                grad_res,
                kept_all[layer_at],
                layers[layer_at],
                kernels[layer_at],
                norm_params[6 * layer_at : 6 * layer_at + 6],
                context,
            )
        )
        unit_grads[layer_at] = lax.psum_scatter(units, BOTH, scatter_dimension=1, tiled=True)
    d_embed_pre, gain_embed, shift_embed = norm_back(
        embed_pre, norm_params[tail], norm_params[tail + 1], grad_res
    )
    d_embedding = outer_sum(patches, d_embed_pre.astype(jnp.bfloat16))
    first_grad = jnp.concatenate(
        [
            d_embedding.astype(jnp.bfloat16),
            jnp.stack(kernel_grads).reshape(-1, C).astype(jnp.bfloat16),
            jnp.zeros((C * FF // C - PIN - BLOCKS * 9 * FF // C, C), jnp.bfloat16),
        ]
    )
    first_grad = lax.psum_scatter(first_grad, BOTH, scatter_dimension=0, tiled=True)
    stacked = jnp.concatenate([first_grad[None]] + unit_grads, 0)
    norm_grads = jnp.concatenate(
        gain_grads + [jnp.stack([gain_embed, shift_embed, gain_final, shift_final])], 0
    )
    row_ids = jnp.arange(slot_rows * n_tok, dtype=jnp.int32)
    matches = slot_of[None, :] == row_ids[:, None]
    unit_at = jnp.where(jnp.any(matches, 1), jnp.argmax(matches, 1), n_unit)
    padded = jnp.concatenate([stacked, jnp.zeros_like(stacked[:1])], 0)
    placed = jnp.take(padded, unit_at, axis=0)[:, None]
    owned = lax.all_to_all(placed, "tok", split_axis=0, concat_axis=1, tiled=True)
    owned = owned.astype(jnp.float32).reshape(slot_rows, columns)
    norm_total, head_total, loss_sum = lax.psum((norm_grads, d_head, loss_local), BOTH)
    slot_m, slot_v, slot_w = adamw_step(
        slot_weight, slot_moment, slot_second, owned, RATE_MATRIX, DECAY_RATE
    )
    norm_m, norm_v, norm_w = adamw_step(
        norm_params, norm_moment, norm_second, norm_total, RATE_VECTOR, 0.0
    )
    head_m, head_v, head_w = adamw_step(
        head_weight, head_moment, head_second, head_total, RATE_MATRIX, DECAY_RATE
    )
    return (
        loss_sum,
        pixel_total,
        slot_m,
        slot_v,
        slot_w,
        norm_m,
        norm_v,
        norm_w,
        head_m,
        head_v,
        head_w,
    )


def solution(mesh):
    in_specs = (
        P(("grp", "tok"), None),
        P(("grp", "tok")),
        P(("grp", "tok")),
        P("grp", None),
        P(),
        P("tok", "grp"),
        P("tok", "grp"),
        P("tok", "grp"),
        P(),
        P(),
        P(),
        P(),
        P(),
        P(),
    )
    out_specs = (
        P(),
        P(),
        P("tok", "grp"),
        P("tok", "grp"),
        P("tok", "grp"),
        P(),
        P(),
        P(),
        P(),
        P(),
        P(),
    )
    return jax.shard_map(body, mesh=mesh, in_specs=in_specs, out_specs=out_specs, check_vma=False)
```

time: 4400 us -> 1130 us (0.26)
  local copies, waits for them, and re-layouts: 2480 us -> 121 us
  waiting for transfers between devices: 890 us -> 335 us
  other arithmetic: 435 us -> 156 us
  matrix products: 254 us -> 341 us
  blocking collectives: 207 us -> 127 us
  starting transfers between devices: 79.2 us -> 15.7 us
    gather x59 -> x2, local copies, waits for them, and re-layouts: 1900 us -> 1.3 us  [the longest x1 0.66 us: body(): placed = jnp.take(padded, unit_at, axis=0)[:, None]]
    all_to_all x10 -> x2, waiting for transfers between devices: 468 us -> 13.6 us  [the longest x1 13.6 us: body(): lax.all_to_all(pieces, 'tok', split_axis=1, concat_axis=0, tiled=True)]
    unnamed x6, waiting for transfers between devices: 28.9 us -> 231 us
    convert_element_type x13 -> x11, other arithmetic: 236 us -> 48.3 us  [the longest x3 44.9 us: layer_forward(): active = gelu_exact(mixed).astype(jnp.bfloat16)]
    all_gather x2 -> x3, waiting for transfers between devices: 146 us -> 0.02 us  [body(): lax.all_gather(unit_part[1 + 4 * layer_at:5 + 4 * layer_at], BOTH, axis=1...]
    all_to_all x2 -> x0, blocking collectives: 129 us -> none  [the longest x1 65 us: layer_backward(): lax.all_to_all(d_active, 'tok', split_axis=1, concat_axis=0, tiled=True)]
    reduce_scatter x1 -> x0, waiting for transfers between devices: 122 us -> none  [body(): lax.psum_scatter(stacked.astype(jnp.bfloat16), 'grp', scatter_dimension=1...]
    another operation x54 -> x48, local copies, waits for them, and re-layouts: 150 us -> 46.5 us  [the longest x9 26 us: layer_backward(): jnp.stack([jnp.concatenate([low[0], low[1], low[2].reshape(-1, C)], 0), l...]
  transfers between devices with their start and end apart: 27 -> 9, of which waited for: 18 -> 3; matrix products, arithmetic and copies ran while one was open for 4% -> 13% of each run, Pallas kernels for 0% -> 0%
where the time goes in v1:
time: 1130 us; the launch traced here: 1120 us
  matrix products  341 us (30%)
  waiting for transfers between devices  335 us (30%)
  other arithmetic  156 us (14%)
  blocking collectives  127 us (11%)
  local copies, waits for them, and re-layouts  121 us (11%)
  between operations  21.4 us (2%)
  starting transfers between devices  15.7 us (1%)
    unnamed x6, waiting for transfers between devices  231 us
    dot_general x92, matrix products, product(): return jnp.dot(left, right, preferred_element_type=jnp.float32)  122 us
    psum x1, waiting for transfers between devices, body(): lax.psum((norm_grads, d_head, loss_local), BOTH)  90.3 us
    dot_general x19, matrix products, back_product(): lax.dot_general(gradient, weight, (((1,), (1,)), ((), ())), preferred_ele...  50.8 us
    mul x3, other arithmetic, gelu_exact(): return jax.nn.gelu(values, approximate=False)  46.3 us
    all_gather x1, blocking collectives, body(): first_unit = lax.all_gather(unit_part[0], BOTH, axis=0, tiled=True)  45.8 us
    convert_element_type x3, other arithmetic, layer_forward(): active = gelu_exact(mixed).astype(jnp.bfloat16)  44.9 us
    psum x1, blocking collectives, body(): pixel_total = lax.psum(jnp.sum(keep_mask), BOTH)  40.9 us
  transfers between devices with their start and end apart: 9, of which 3 were waited for; matrix products, arithmetic and copies ran while one was open for 13% of the time, Pallas kernels for 0%

profile of v1, /device:TPU:1, one launch (start us, length us, event | category | flops | bytes accessed | tf_op | source)
XLA Modules:
  0.0 1116.6 jit_solution(11645323051923579980)
XLA Ops:
  10.0 6.5 all-to-all-start
  16.8 13.6 %all-to-all-done = bf16[2,8,40,320]{3,2,0,1:T(8,128)(2,1)S(1)} async-done(((bf16[2,8,40,320]{3,2,0,1:T(8,128)(2,1)}), bf16[2,8,40,320]{3,2,0,1:T(8,128)(2,1)S(1)}, u32[]{:S(2)}, u32[]{:S(2)}) %all-to-all-start) | async-done | bytes 409632 | tf_op jit(solution)/shard_map/all_to_all | solution.py:300
  31.9 2.8 collective-permute-start.1
  46.6 40.9 %psum.29 = f32[]{:T(128)} all-reduce(f32[]{:T(128)} %fusion.655), channel_id=1, replica_groups=mesh['grp'=4,'tok'=8] {'grp','tok'}, use_global_device_ids=true, to_apply=%region_35.36 | all-reduce | flops 1 | bytes 8 | tf_op jit(solution)/shard_map/psum | solution.py:330
  93.4 3.7 copy.149
  97.1 45.8 %all-gather = bf16[1,1280,320]{2,1,0:T(8,128)(2,1)S(1)} all-gather(bf16[1,40,320]{2,1,0:T(8,128)(2,1)S(1)} %slice.1122), channel_id=2, replica_groups=mesh['grp'=4,'tok'=8] {'grp','tok'}, dimensions={1}, use_global_device_ids=true | all-gather | bytes 844800 | tf_op jit(solution)/shard_map/all_gather | solution.py:302
  144.6 3.1 fusion.903
  157.4 2.4 fusion.904
  161.6 2.6 convolution_convert_fusion.21
  164.2 7.1 fusion.905
  171.3 4.3 convolution_convert_fusion.20
  198.5 2.5 slice.1162
  201.0 2.7 reshape_squeeze.21
  203.9 4.0 fusion.188
  213.9 15.1 %negate_multiply_fusion.2 = (f32[4,304,1280]{2,1,0:T(8,128)}, bf16[4,304,1280]{2,1,0:T(8,128)(2,1)S(1)}, f32[4,304,1280]{2,1,0:T(8,128)}) fusion(f32[1,304,1280]{2,1,0:T(8,128)S(1)} %fusion.188, f32[1,304,1280]{2,1,0:T(8,128)S(1)} %fusion.181, f32[1,304,1280]{2,1,0:T(8,128)S(1)} %fusion.172, f32[1,304,1280]{2,1,0:T(8,128)S(1)} %fusion.158), kind=kLoop, calls=%fused_computation.279 | loop fusion | flops 105840640 | bytes 21790720 | tf_op jit(solution)/shard_map/mul | solution.py:36
  238.6 7.3 fusion.909
  245.9 4.1 convolution_convert_fusion.18
  261.3 2.7 fusion.230
  264.0 2.8 fusion.214
  266.8 2.8 fusion.200
  269.6 2.9 fusion.223
  276.7 17.3 %negate_multiply_fusion.1 = (f32[4,304,1280]{2,1,0:T(8,128)}, bf16[4,304,1280]{2,1,0:T(8,128)(2,1)S(1)}, f32[4,304,1280]{2,1,0:T(8,128)}) fusion(f32[1,304,1280]{2,1,0:T(8,128)} %fusion.230, f32[1,304,1280]{2,1,0:T(8,128)} %fusion.223, f32[1,304,1280]{2,1,0:T(8,128)} %fusion.214, f32[1,304,1280]{2,1,0:T(8,128)} %fusion.200), kind=kLoop, calls=%fused_computation.214 | loop fusion | flops 105840640 | bytes 21790720 | tf_op jit(solution)/shard_map/mul | solution.py:36
  294.0 2.5 fusion.911
  305.0 7.3 fusion.913
  312.3 4.3 convolution_convert_fusion.16
  332.8 13.8 %negate_multiply_fusion = (f32[4,304,1280]{2,1,0:T(8,128)S(1)}, bf16[4,304,1280]{2,1,0:T(8,128)(2,1)S(1)}, f32[4,304,1280]{2,1,0:T(8,128)S(1)}) fusion(f32[1,304,1280]{2,1,0:T(8,128)S(1)} %fusion.272, f32[1,304,1280]{2,1,0:T(8,128)S(1)} %fusion.265, f32[1,304,1280]{2,1,0:T(8,128)S(1)} %fusion.256, f32[1,304,1280]{2,1,0:T(8,128)S(1)} %fusion.242), kind=kLoop, calls=%fused_computation.149 | loop fusion | flops 105840640 | bytes 21790720 | tf_op jit(solution)/shard_map/mul | solution.py:36
  353.3 14.8 %fusion.56 = (bf16[1216,1280]{1,0:T(8,128)(2,1)}, f32[1216,1280]{1,0:T(8,128)}, f32[1216,1280]{1,0:T(8,128)}) fusion(f32[4,304,1280]{2,1,0:T(8,128)S(1)} %get-tuple-element.196, f32[4,304,1280]{2,1,0:T(8,128)S(1)} %get-tuple-element.194), kind=kLoop, calls=%fused_computation.103 | loop fusion | flops 96501760 | bytes 28016640 | tf_op jit(solution)/shard_map/convert_element_type | solution.py:218
  368.1 7.9 fusion.23
  384.9 3.9 fusion.565
  390.2 3.3 fusion.569
  408.2 4.4 fusion.917
  412.6 13.2 %fusion.585 = bf16[5,64,304]{2,1,0:T(8,128)(2,1)} fusion(bf16[1216,5,64]{0,2,1:T(8,128)(2,1)} %bitcast.528, f32[5,1216,304]{1,2,0:T(8,128)} %fusion.917, f32[5,1216,304]{1,2,0:T(8,128)} %get-tuple-element.275, f32[5,1216]{1,0:T(8,128)} %copy-done.416), kind=kOutput, calls=%fused_computation.1043 | convolution fusion | flops 249626864 | bytes 15783680 | tf_op jit(solution)/shard_map/hqk,qhd->khd/dot_general | solution.py:183
  425.8 13.3 %fusion.144 = bf16[5,64,1216]{2,1,0:T(8,128)(2,1)} fusion(bf16[304,5,64]{0,2,1:T(8,128)(2,1)S(1)} %bitcast.536, f32[5,1216,304]{1,2,0:T(8,128)} %fusion.917, f32[5,1216,304]{1,2,0:T(8,128)} %get-tuple-element.275, f32[5,1216]{1,0:T(8,128)} %copy-done.416), kind=kOutput, calls=%fused_computation.483 | convolution fusion | flops 249918704 | bytes 15783680 | tf_op jit(solution)/shard_map/hqk,khd->qhd/dot_general | solution.py:180
  439.2 2.7 multiply_reduce_fusion.27
  449.7 2.8 concatenate.60
  452.5 3.4 multiply_reduce_fusion.6
  457.5 15.1 %fusion.54 = (bf16[1216,1280]{1,0:T(8,128)(2,1)}, f32[1216,1280]{1,0:T(8,128)S(1)}, f32[1216,1280]{1,0:T(8,128)}) fusion(f32[4,304,1280]{2,1,0:T(8,128)S(1)} %bitcast.479, f32[4,304,1280]{2,1,0:T(8,128)} %get-tuple-element.197), kind=kLoop, calls=%fused_computation.96 | loop fusion | flops 96501760 | bytes 28016640 | tf_op jit(solution)/shard_map/convert_element_type | solution.py:218
  472.6 5.9 fusion.30
  487.9 4.0 fusion.529
  493.3 3.3 fusion.533
  511.2 4.3 fusion.918
  515.5 12.1 %fusion.582 = bf16[5,64,304]{2,1,0:T(8,128)(2,1)} fusion(bf16[1216,5,64]{0,2,1:T(8,128)(2,1)S(1)} %bitcast.526, f32[5,1216,304]{1,2,0:T(8,128)} %fusion.918, f32[5,1216,304]{1,2,0:T(8,128)} %get-tuple-element.267, f32[5,1216]{1,0:T(8,128)S(1)} %copy-done.415), kind=kOutput, calls=%fused_computation.1042 | convolution fusion | flops 249626864 | bytes 15783680 | tf_op jit(solution)/shard_map/hqk,qhd->khd/dot_general | solution.py:183
  527.8 13.3 %fusion.141 = bf16[5,64,1216]{2,1,0:T(8,128)(2,1)} fusion(bf16[304,5,64]{0,2,1:T(8,128)(2,1)S(1)} %bitcast.534, f32[5,1216,304]{1,2,0:T(8,128)} %fusion.918, f32[5,1216,304]{1,2,0:T(8,128)} %get-tuple-element.267, f32[5,1216]{1,0:T(8,128)S(1)} %copy-done.415), kind=kOutput, calls=%fused_computation.482 | convolution fusion | flops 249918704 | bytes 15783680 | tf_op jit(solution)/shard_map/hqk,khd->qhd/dot_general | solution.py:180
  551.4 2.9 concatenate.62
  554.3 3.4 multiply_reduce_fusion.8
  559.3 15.0 %fusion.52 = (bf16[1216,1280]{1,0:T(8,128)(2,1)}, f32[1216,1280]{1,0:T(8,128)S(1)}, f32[1216,1280]{1,0:T(8,128)}) fusion(f32[4,304,1280]{2,1,0:T(8,128)S(1)} %bitcast.476, f32[4,304,1280]{2,1,0:T(8,128)} %get-tuple-element.200), kind=kLoop, calls=%fused_computation.89 | loop fusion | flops 96501760 | bytes 28016640 | tf_op jit(solution)/shard_map/convert_element_type | solution.py:218
  574.3 5.9 fusion.37
  589.6 4.0 fusion.493
  595.0 3.3 fusion.497
  613.5 4.3 fusion.919
  617.8 11.5 %fusion.579 = bf16[5,64,304]{2,1,0:T(8,128)(2,1)S(1)} fusion(bf16[1216,5,64]{0,2,1:T(8,128)(2,1)S(1)} %bitcast.524, f32[5,1216,304]{1,2,0:T(8,128)} %fusion.919, f32[5,1216,304]{1,2,0:T(8,128)} %get-tuple-element.259, f32[5,1216]{1,0:T(8,128)S(1)} %copy-done.413), kind=kOutput, calls=%fused_computation.1041 | convolution fusion | flops 249626864 | bytes 15783680 | tf_op jit(solution)/shard_map/hqk,qhd->khd/dot_general | solution.py:183
  629.4 13.3 %fusion.138 = bf16[5,64,1216]{2,1,0:T(8,128)(2,1)} fusion(bf16[304,5,64]{0,2,1:T(8,128)(2,1)S(1)} %bitcast.532, f32[5,1216,304]{1,2,0:T(8,128)} %fusion.919, f32[5,1216,304]{1,2,0:T(8,128)} %get-tuple-element.259, f32[5,1216]{1,0:T(8,128)S(1)} %copy-done.413), kind=kOutput, calls=%fused_computation.481 | convolution fusion | flops 249918704 | bytes 15783680 | tf_op jit(solution)/shard_map/hqk,khd->qhd/dot_general | solution.py:180
  646.0 4.1 fusion.287
  659.4 6.3 copy.181
  665.8 4.3 fusion.286
  681.7 6.4 copy.178
  688.4 4.3 fusion.285
  699.2 2.6 fusion.288
  705.0 6.3 copy.175
  728.2 231.3 %all-reduce.11.cloned.1.call-done = (bf16[1280,320]{0,1:T(8,128)(2,1)}, bf16[4,1280,320]{2,0,1:T(4,128)(2,1)}, bf16[4,1280,320]{2,0,1:T(4,128)(2,1)}, bf16[4,1280,320]{2,0,1:T(4,128)(2,1)}) async-done(((bf16[1280,320]{0,1:T(8,128)(2,1)}, bf16[4,1280,320]{2,0,1:T(4,128)(2,1)}, bf16[4,1280,320]{2,0,1:T(4,128)(2,1)}, bf16[4,1280,320]{2,0,1:T(4,128)(2,1)}), (bf16[1280,320]{0,1:T(8,128)(2,1)}, ...) | async-done | bytes 10649616
  964.6 4.1 all-to-all-start.1
  970.4 39.9 %all-reduce.4 = (f32[]{:T(128)}, f32[22,320]{1,0:T(8,128)S(1)}) all-reduce(f32[]{:T(128)} %get-tuple-element.162, f32[22,320]{1,0:T(8,128)S(1)} %concatenate.70), channel_id=1, replica_groups=mesh['grp'=4,'tok'=8] {'grp','tok'}, use_global_device_ids=true, to_apply=%region_33.34 | all-reduce | flops 7041 | bytes 56328 | tf_op jit(solution)/shard_map/psum | solution.py:399
  1011.0 90.3 %all-reduce.9.cloned.1.call-done = f32[320,150]{0,1:T(8,128)} async-done(((f32[320,150]{0,1:T(8,128)}), f32[320,150]{0,1:T(8,128)}) %all-reduce.9.cloned.1.call-update) | async-done | bytes 192016 | tf_op jit(solution)/shard_map/psum | solution.py:399
  1104.7 4.8 multiply_subtract_fusion
  (1249 shorter events, 274.3 us)
Async XLA Ops:
  10.0 21.9 %copy-start.315 = (s32[1024]{0:T(1024)S(1)}, s32[1024]{0:T(1024)}, u32[]{:S(2)}) copy-start(s32[1024]{0:T(1024)} %param.16) | copy-start | bytes 12292
  10.0 21.9 %copy-start.316 = (s32[1024]{0:T(1024)S(1)}, s32[1024]{0:T(1024)}, u32[]{:S(2)}) copy-start(s32[1024]{0:T(1024)} %param.15) | copy-start | bytes 12292
  10.0 20.3 %all-to-all-start = ((bf16[2,8,40,320]{3,2,0,1:T(8,128)(2,1)}), bf16[2,8,40,320]{3,2,0,1:T(8,128)(2,1)S(1)}, u32[]{:S(2)}, u32[]{:S(2)}) async-start(bf16[2,8,40,320]{3,2,0,1:T(8,128)(2,1)} %copy.150), calls=%async_computation | async-start | bytes 983040 | tf_op jit(solution)/shard_map/all_to_all | solution.py:300
  16.5 135.0 %all-gather.5.cloned.1.call-start = ((), (), s32[]{:S(2)}) async-start(), calls=%async_computation.2 | async-start | bytes 4055040 | tf_op jit(solution)/shard_map/all_gather | solution.py:307
  16.7 19.1 %copy-start.407 = (s32[13]{0:T(128)}, s32[13]{0:T(128)S(1)}, u32[]{:S(2)}) copy-start(s32[13]{0:T(128)S(1)} %get-tuple-element.178) | copy-start | bytes 160
  31.9 163.4 %all-gather.7.cloned.1.call-start = ((), (), s32[]{:S(2)}) async-start(), calls=%async_computation.3 | async-start | bytes 4055040 | tf_op jit(solution)/shard_map/all_gather | solution.py:307
  31.9 13.0 %collective-permute-start.1 = (s32[2,192]{1,0:T(2,128)S(1)}, s32[2,192]{1,0:T(2,128)S(1)}, u32[]{:S(2)}, u32[]{:S(2)}) collective-permute-start(s32[2,192]{1,0:T(2,128)S(1)} %pad_add_fusion.1), channel_id=1, source_target_pairs={{1,0},{2,1},{3,2},{4,3},{5,4},{6,5},{7,6},{9,8},{10,9},{11,10},{12... | collective-permute-start | bytes 4616 | tf_op jit(solution)/shard_map/ppermute | solution.py:317
  35.8 53.3 %collective-permute-start = (bf16[192,1152]{1,0:T(8,128)(2,1)S(1)}, bf16[192,1152]{1,0:T(8,128)(2,1)}, u32[]{:S(2)}, u32[]{:S(2)}) collective-permute-start(bf16[192,1152]{1,0:T(8,128)(2,1)S(1)} %slice.447), channel_id=1, source_target_pairs={{1,0},{2,1},{3,2},{4,3},{5,4},{6,5},{7,6},{9,8},{10,9},{11,10},{12... | collective-permute-start | bytes 1327112 | tf_op jit(solution)/shard_map/ppermute | solution.py:315
  39.7 232.8 %all-gather.9.cloned.1.call-start = ((), (), s32[]{:S(2)}) async-start(), calls=%async_computation.4 | async-start | bytes 4055040 | tf_op jit(solution)/shard_map/all_gather | solution.py:307
  40.5 108.9 %copy-start.221 = (f32[320]{0:T(512)}, f32[320]{0:T(512)S(1)}, u32[]{:S(2)}) copy-start(f32[320]{0:T(512)S(1)} %get-tuple-element.122) | copy-start | bytes 3844
  40.5 119.6 %copy-start.288 = (f32[320]{0:T(512)}, f32[320]{0:T(512)S(1)}, u32[]{:S(2)}) copy-start(f32[320]{0:T(512)S(1)} %get-tuple-element.120) | copy-start | bytes 3844
  40.5 136.3 %copy-start.311 = (f32[320]{0:T(512)}, f32[320]{0:T(512)S(1)}, u32[]{:S(2)}) copy-start(f32[320]{0:T(512)S(1)} %get-tuple-element.118) | copy-start | bytes 3844
  41.2 148.8 %copy-start.229 = (pred[304]{0:T(512)(128)(4,1)}, pred[304]{0:T(512)(128)(4,1)S(1)}, u32[]{:S(2)}) copy-start(pred[304]{0:T(512)(128)(4,1)S(1)} %get-tuple-element.169) | copy-start | bytes 916
  41.8 140.7 %copy-start.234 = (pred[304]{0:T(512)(128)(4,1)}, pred[304]{0:T(512)(128)(4,1)S(1)}, u32[]{:S(2)}) copy-start(pred[304]{0:T(512)(128)(4,1)S(1)} %get-tuple-element.176) | copy-start | bytes 916
  41.8 144.3 %copy-start.264 = (pred[304]{0:T(512)(128)(4,1)}, pred[304]{0:T(512)(128)(4,1)S(1)}, u32[]{:S(2)}) copy-start(pred[304]{0:T(512)(128)(4,1)S(1)} %get-tuple-element.241) | copy-start | bytes 916
  42.3 151.2 %copy-start.269 = (pred[304]{0:T(512)(128)(4,1)}, pred[304]{0:T(512)(128)(4,1)S(1)}, u32[]{:S(2)}) copy-start(pred[304]{0:T(512)(128)(4,1)S(1)} %get-tuple-element.251) | copy-start | bytes 916
  42.9 139.5 %copy-start.198 = (s32[304]{0:T(512)}, s32[304]{0:T(512)S(1)}, u32[]{:S(2)}) copy-start(s32[304]{0:T(512)S(1)} %get-tuple-element.249) | copy-start | bytes 3652
  42.9 147.1 %copy-start.195 = (s32[304]{0:T(512)}, s32[304]{0:T(512)S(1)}, u32[]{:S(2)}) copy-start(s32[304]{0:T(512)S(1)} %get-tuple-element.247) | copy-start | bytes 3652
  45.0 130.7 %copy-start.177 = (f32[320]{0:T(512)}, f32[320]{0:T(512)S(1)}, u32[]{:S(2)}) copy-start(f32[320]{0:T(512)S(1)} %get-tuple-element.125) | copy-start | bytes 3844
  45.0 130.7 %copy-start.181 = (f32[320]{0:T(512)}, f32[320]{0:T(512)S(1)}, u32[]{:S(2)}) copy-start(f32[320]{0:T(512)S(1)} %get-tuple-element.124) | copy-start | bytes 3844
  144.6 67.5 %copy-start.132 = (f32[1280]{0:T(1024)}, f32[1280]{0:T(1024)S(1)}, u32[]{:S(2)}) copy-start(f32[1280]{0:T(1024)S(1)} %get-tuple-element.95) | copy-start | bytes 15364
  144.6 125.0 %copy-start.134 = (f32[1280]{0:T(1024)}, f32[1280]{0:T(1024)S(1)}, u32[]{:S(2)}) copy-start(f32[1280]{0:T(1024)S(1)} %get-tuple-element.86) | copy-start | bytes 15364
  144.6 125.0 %copy-start.136 = (f32[1280]{0:T(1024)}, f32[1280]{0:T(1024)S(1)}, u32[]{:S(2)}) copy-start(f32[1280]{0:T(1024)S(1)} %get-tuple-element.87) | copy-start | bytes 15364
  144.6 125.0 %copy-start.138 = (f32[1280]{0:T(1024)}, f32[1280]{0:T(1024)S(1)}, u32[]{:S(2)}) copy-start(f32[1280]{0:T(1024)S(1)} %get-tuple-element.88) | copy-start | bytes 15364
  147.7 27.9 %copy-start = (f32[1216,320]{0,1:T(8,128)}, f32[1216,320]{0,1:T(8,128)S(1)}, u32[]{:S(2)}) copy-start(f32[1216,320]{0,1:T(8,128)S(1)} %get-tuple-element.255) | copy-start | bytes 4669444
  147.7 27.9 %copy-start.75 = (f32[1216]{0:T(1024)}, f32[1216]{0:T(1024)S(1)}, u32[]{:S(2)}) copy-start(f32[1216]{0:T(1024)S(1)} %broadcast_multiply_fusion.7) | copy-start | bytes 14596
  147.9 27.7 %copy-start.93 = (f32[1216]{0:T(1024)}, f32[1216]{0:T(1024)S(1)}, u32[]{:S(2)}) copy-start(f32[1216]{0:T(1024)S(1)} %fusion.663) | copy-start | bytes 14596
  149.9 11.7 %copy-start.19 = (bf16[1216,320]{0,1:T(8,128)(2,1)}, bf16[1216,320]{0,1:T(8,128)(2,1)S(1)}, u32[]{:S(2)}) copy-start(bf16[1216,320]{0,1:T(8,128)(2,1)S(1)} %add_convert_fusion.7) | copy-start | bytes 2334724
  151.2 808.3 %all-reduce.11.cloned.1.call-start = ((), (), s32[]{:S(2)}) async-start(), calls=%async_computation.6 | async-start | bytes 25231360
  180.3 31.8 %copy-start.6 = (bf16[1216,1280]{1,0:T(8,128)(2,1)}, bf16[1216,1280]{1,0:T(8,128)(2,1)S(1)}, u32[]{:S(2)}) copy-start(bf16[1216,1280]{1,0:T(8,128)(2,1)S(1)} %convolution_convert_fusion.5) | copy-start | bytes 9338884
  198.5 36.2 %copy-start.56 = (bf16[320,640]{1,0:T(8,128)(2,1)}, bf16[320,640]{1,0:T(8,128)(2,1)S(1)}, u32[]{:S(2)}) copy-start(bf16[320,640]{1,0:T(8,128)(2,1)S(1)} %reshape_squeeze.20) | copy-start | bytes 1228804
  213.9 15.1 %copy-start.11 = (f32[1216,320]{0,1:T(8,128)S(1)}, f32[1216,320]{0,1:T(8,128)}, u32[]{:S(2)}) copy-start(f32[1216,320]{0,1:T(8,128)} %copy-done.10) | copy-start | bytes 4669444
  213.9 15.1 %copy-start.26 = (bf16[4,1280,320]{2,1,0:T(8,128)(2,1)S(1)}, bf16[4,1280,320]{2,1,0:T(8,128)(2,1)}, u32[]{:S(2)}) copy-start(bf16[4,1280,320]{2,1,0:T(8,128)(2,1)} %all-gather.5.cloned.1.call-done) | copy-start | bytes 9830404
  230.4 19.7 %copy-start.2 = (f32[1216,320]{0,1:T(8,128)}, f32[1216,320]{0,1:T(8,128)S(1)}, u32[]{:S(2)}) copy-start(f32[1216,320]{0,1:T(8,128)S(1)} %get-tuple-element.263) | copy-start | bytes 4669444
  252.0 42.0 %copy-start.13 = (f32[1216,320]{0,1:T(8,128)}, f32[1216,320]{0,1:T(8,128)S(1)}, u32[]{:S(2)}) copy-start(f32[1216,320]{0,1:T(8,128)S(1)} %get-tuple-element.269) | copy-start | bytes 4669444
  255.8 13.8 %copy-start.8 = (bf16[1216,1280]{1,0:T(8,128)(2,1)}, bf16[1216,1280]{1,0:T(8,128)(2,1)S(1)}, u32[]{:S(2)}) copy-start(bf16[1216,1280]{1,0:T(8,128)(2,1)S(1)} %convolution_convert_fusion.4) | copy-start | bytes 9338884
  317.7 83.7 %copy-start.204 = (f32[1216]{0:T(1024)}, f32[1216]{0:T(1024)S(1)}, u32[]{:S(2)}) copy-start(f32[1216]{0:T(1024)S(1)} %fusion.669) | copy-start | bytes 14596
  353.2 49.5 %copy-start.17 = (f32[1216,320]{0,1:T(8,128)}, f32[1216,320]{0,1:T(8,128)S(1)}, u32[]{:S(2)}) copy-start(f32[1216,320]{0,1:T(8,128)S(1)} %get-tuple-element.161) | copy-start | bytes 4669444
  353.3 49.4 %copy-start.202 = (f32[1216]{0:T(1024)}, f32[1216]{0:T(1024)S(1)}, u32[]{:S(2)}) copy-start(f32[1216]{0:T(1024)S(1)} %negate_multiply_fusion.10) | copy-start | bytes 14596
  404.1 52.3 %copy-start.4 = (f32[1216,320]{0,1:T(8,128)}, f32[1216,320]{0,1:T(8,128)S(1)}, u32[]{:S(2)}) copy-start(f32[1216,320]{0,1:T(8,128)S(1)} %add_add_fusion.13) | copy-start | bytes 4669444
  412.6 13.2 %copy-start.127 = (bf16[304,320]{0,1:T(8,128)(2,1)S(1)}, bf16[304,320]{0,1:T(8,128)(2,1)}, u32[]{:S(2)}) copy-start(bf16[304,320]{0,1:T(8,128)(2,1)} %copy.156) | copy-start | bytes 583684
  425.8 13.3 %copy-start.245 = (f32[304]{0:T(512)S(1)}, f32[304]{0:T(512)}, u32[]{:S(2)}) copy-start(f32[304]{0:T(512)} %copy-done.244) | copy-start | bytes 3652
  425.8 13.3 %copy-start.294 = (f32[320]{0:T(512)S(1)}, f32[320]{0:T(512)}, u32[]{:S(2)}) copy-start(f32[320]{0:T(512)} %get-tuple-element.108) | copy-start | bytes 3844
  456.7 15.9 %copy-start.48 = (bf16[1216,320]{0,1:T(8,128)(2,1)}, bf16[1216,320]{0,1:T(8,128)(2,1)S(1)}, u32[]{:S(2)}) copy-start(bf16[1216,320]{0,1:T(8,128)(2,1)S(1)} %fusion.603) | copy-start | bytes 2334724
  515.5 12.2 %copy-start.126 = (bf16[304,320]{0,1:T(8,128)(2,1)S(1)}, bf16[304,320]{0,1:T(8,128)(2,1)}, u32[]{:S(2)}) copy-start(bf16[304,320]{0,1:T(8,128)(2,1)} %copy.154) | copy-start | bytes 583684
  527.7 13.3 %copy-start.36 = (f32[304,320]{1,0:T(8,128)S(1)}, f32[304,320]{1,0:T(8,128)}, u32[]{:S(2)}) copy-start(f32[304,320]{1,0:T(8,128)} %copy-done.35) | copy-start | bytes 1167364
  527.7 13.3 %copy-start.57 = (bf16[320,640]{1,0:T(8,128)(2,1)S(1)}, bf16[320,640]{1,0:T(8,128)(2,1)}, u32[]{:S(2)}) copy-start(bf16[320,640]{1,0:T(8,128)(2,1)} %copy-done.56) | copy-start | bytes 1228804
  527.7 13.3 %copy-start.243 = (f32[304]{0:T(512)S(1)}, f32[304]{0:T(512)}, u32[]{:S(2)}) copy-start(f32[304]{0:T(512)} %copy-done.242) | copy-start | bytes 3652
  527.7 13.3 %copy-start.292 = (f32[320]{0:T(512)S(1)}, f32[320]{0:T(512)}, u32[]{:S(2)}) copy-start(f32[320]{0:T(512)} %get-tuple-element.114) | copy-start | bytes 3844
  527.7 13.3 %copy-start.302 = (f32[304]{0:T(512)S(1)}, f32[304]{0:T(512)}, u32[]{:S(2)}) copy-start(f32[304]{0:T(512)} %copy-done.301) | copy-start | bytes 3652
  558.5 15.9 %copy-start.49 = (bf16[1216,320]{0,1:T(8,128)(2,1)}, bf16[1216,320]{0,1:T(8,128)(2,1)S(1)}, u32[]{:S(2)}) copy-start(bf16[1216,320]{0,1:T(8,128)(2,1)S(1)} %fusion.604) | copy-start | bytes 2334724
  629.3 13.3 %copy-start.33 = (f32[304,320]{1,0:T(8,128)S(1)}, f32[304,320]{1,0:T(8,128)}, u32[]{:S(2)}) copy-start(f32[304,320]{1,0:T(8,128)} %copy-done.32) | copy-start | bytes 1167364
  629.3 13.3 %copy-start.55 = (bf16[320,640]{1,0:T(8,128)(2,1)S(1)}, bf16[320,640]{1,0:T(8,128)(2,1)}, u32[]{:S(2)}) copy-start(bf16[320,640]{1,0:T(8,128)(2,1)} %reshape_squeeze.18) | copy-start | bytes 1228804
  629.3 13.3 %copy-start.240 = (f32[304]{0:T(512)S(1)}, f32[304]{0:T(512)}, u32[]{:S(2)}) copy-start(f32[304]{0:T(512)} %copy-done.239) | copy-start | bytes 3652
  629.3 13.3 %copy-start.289 = (f32[320]{0:T(512)S(1)}, f32[320]{0:T(512)}, u32[]{:S(2)}) copy-start(f32[320]{0:T(512)} %copy-done.288) | copy-start | bytes 3844
  629.4 13.3 %copy-start.299 = (f32[304]{0:T(512)S(1)}, f32[304]{0:T(512)}, u32[]{:S(2)}) copy-start(f32[304]{0:T(512)} %copy-done.298) | copy-start | bytes 3652
  964.5 45.8 %copy-start.180 = (f32[22,320]{1,0:T(8,128)S(1)}, f32[22,320]{1,0:T(8,128)}, u32[]{:S(2)}) copy-start(f32[22,320]{1,0:T(8,128)} %param.22) | copy-start | bytes 84484
  964.5 45.8 %copy-start.223 = (f32[22,320]{1,0:T(8,128)S(1)}, f32[22,320]{1,0:T(8,128)}, u32[]{:S(2)}) copy-start(f32[22,320]{1,0:T(8,128)} %param.24) | copy-start | bytes 84484
  964.5 45.8 %copy-start.224 = (f32[22,320]{1,0:T(8,128)S(1)}, f32[22,320]{1,0:T(8,128)}, u32[]{:S(2)}) copy-start(f32[22,320]{1,0:T(8,128)} %param.23) | copy-start | bytes 84484
  964.5 136.8 %copy-start.74 = (f32[320,150]{0,1:T(8,128)S(1)}, f32[320,150]{0,1:T(8,128)}, u32[]{:S(2)}) copy-start(f32[320,150]{0,1:T(8,128)} %param.25) | copy-start | bytes 576004
  964.6 136.8 %copy-start.128 = (f32[320,150]{0,1:T(8,128)S(1)}, f32[320,150]{0,1:T(8,128)}, u32[]{:S(2)}) copy-start(f32[320,150]{0,1:T(8,128)} %param.27) | copy-start | bytes 576004
  964.6 136.8 %copy-start.129 = (f32[320,150]{0,1:T(8,128)S(1)}, f32[320,150]{0,1:T(8,128)}, u32[]{:S(2)}) copy-start(f32[320,150]{0,1:T(8,128)} %param.26) | copy-start | bytes 576004
  964.6 138.7 %all-to-all-start.1 = ((bf16[16,1,40,320]{3,2,1,0:T(8,128)(2,1)}), bf16[16,1,40,320]{3,2,1,0:T(8,128)(2,1)S(1)}, u32[]{:S(2)}, u32[]{:S(2)}) async-start(bf16[16,1,40,320]{3,2,1,0:T(8,128)(2,1)} %bitcast_select_fusion), calls=%async_computation.1 | async-start | bytes 983040 | tf_op jit(solution)/shard_map/all_to_all | solution.py:397
  968.7 132.6 %all-reduce.9.cloned.1.call-start = ((), (), s32[]{:S(2)}) async-start(), calls=%async_computation.5 | async-start | bytes 466944 | tf_op jit(solution)/shard_map/psum | solution.py:399
  (375 other events, 1062.4 us)
Sparse Core Ops, SparseCore 0:
  32.0 61.3 all-gather.4
  97.0 61.0 all-gather.6
  161.6 60.2 all-gather.8
  726.6 232.8 all-reduce.10
  976.3 125.0 all-reduce.8

commit v2 on v1

--- a/solution.py
+++ b/solution.py
@@ -265,6 +265,68 @@
 
 
 BOTH = ("grp", "tok")
+
+
+def axis_bits(axis):
+    count = lax.axis_size(axis)
+    return [1 << place for place in reversed(range(count.bit_length() - 1))]
+
+
+def swap(values, axis, bit):
+    count = lax.axis_size(axis)
+    return lax.ppermute(values, axis, [(i, i ^ bit) for i in range(count)])
+
+
+def my_bit(axis, bit):
+    return lax.axis_index(axis) // bit % 2
+
+
+def bit_order():
+    tok_bits = axis_bits("tok")
+    return [("grp", bit) for bit in axis_bits("grp")] + [("tok", bit) for bit in tok_bits]
+
+
+def sum_all(values):
+    for axis, bit in reversed(bit_order()):
+        values = values + swap(values, axis, bit)
+    return values
+
+
+def scatter_order():
+    bits = bit_order()
+    return [bits[-1]] + bits[:-1][::-1][len(axis_bits("tok")) - 1 :] + bits[:-1][::-1][: len(axis_bits("tok")) - 1]
+
+
+def scatter_units(units):
+    bits = bit_order()
+    count = units.shape[0]
+    chunk = units.shape[1] >> len(bits)
+    left = list(bits)
+    values = units.reshape((count,) + (2,) * len(bits) + (chunk, C))
+    for axis, bit in scatter_order():
+        dim = 1 + left.index((axis, bit))
+        left.remove((axis, bit))
+        mine = my_bit(axis, bit)
+        away = lax.dynamic_index_in_dim(values, 1 - mine, dim, keepdims=False)
+        stay = lax.dynamic_index_in_dim(values, mine, dim, keepdims=False)
+        back = swap(away, axis, bit)
+        values = (stay.astype(jnp.float32) + back.astype(jnp.float32)).astype(jnp.bfloat16)
+    return values
+
+
+def gather_unit(piece):
+    bits = bit_order()
+    held = []
+    values = piece[None]
+    for axis, bit in reversed(scatter_order()):
+        other = swap(values, axis, bit)
+        mine = my_bit(axis, bit) == 0
+        pair = jnp.stack([jnp.where(mine, values, other), jnp.where(mine, other, values)])
+        held.insert(0, (axis, bit))
+        values = pair
+    values = values.reshape((2,) * len(bits) + piece.shape)
+    order = [held.index(name) for name in bits] + [len(bits), len(bits) + 1]
+    return values.transpose(order).reshape(-1, piece.shape[1])
 
 
 def body(
@@ -299,7 +361,7 @@
     pieces = slot_weight.astype(jnp.bfloat16).reshape(slot_rows, n_tok, chunk, C)
     pieces = lax.all_to_all(pieces, "tok", split_axis=1, concat_axis=0, tiled=True)
     unit_part = jnp.take(pieces.reshape(slot_rows * n_tok, chunk, C), slot_of, axis=0)
-    first_unit = lax.all_gather(unit_part[0], BOTH, axis=0, tiled=True)
+    first_unit = gather_unit(unit_part[0])
     embedding = first_unit[:PIN]
     kernels = first_unit[PIN : PIN + BLOCKS * 9 * FF // C].reshape(BLOCKS, 9, FF).astype(jnp.float32)
     layers = []
@@ -327,7 +389,7 @@
     image_of = jnp.where(positions < group_tok, begin_at, -1)
     allowed = jnp.tile(image_of, 4)[:, None] == image_of[None, :]
     keep_mask = marks[1].astype(jnp.float32) * jnp.tile((own_image & is_real).astype(jnp.float32), 4)
-    pixel_total = lax.psum(jnp.sum(keep_mask), BOTH)
+    pixel_total = sum_all(jnp.sum(keep_mask)[None])[0]
     context = (allowed, shifts, is_real)
     tail = 6 * BLOCKS
     embed_pre = product(patches, embedding)
@@ -372,7 +434,7 @@
                 context,
             )
         )
-        unit_grads[layer_at] = lax.psum_scatter(units, BOTH, scatter_dimension=1, tiled=True)
+        unit_grads[layer_at] = scatter_units(units)
     d_embed_pre, gain_embed, shift_embed = norm_back(
         embed_pre, norm_params[tail], norm_params[tail + 1], grad_res
     )
@@ -384,8 +446,8 @@
             jnp.zeros((C * FF // C - PIN - BLOCKS * 9 * FF // C, C), jnp.bfloat16),
         ]
     )
-    first_grad = lax.psum_scatter(first_grad, BOTH, scatter_dimension=0, tiled=True)
-    stacked = jnp.concatenate([first_grad[None]] + unit_grads, 0)
+    first_grad = scatter_units(first_grad[None])
+    stacked = jnp.concatenate([first_grad] + unit_grads, 0)
     norm_grads = jnp.concatenate(
         gain_grads + [jnp.stack([gain_embed, shift_embed, gain_final, shift_final])], 0
     )
@@ -396,7 +458,10 @@
     placed = jnp.take(padded, unit_at, axis=0)[:, None]
     owned = lax.all_to_all(placed, "tok", split_axis=0, concat_axis=1, tiled=True)
     owned = owned.astype(jnp.float32).reshape(slot_rows, columns)
-    norm_total, head_total, loss_sum = lax.psum((norm_grads, d_head, loss_local), BOTH)
+    head_total = sum_all(d_head)
+    small = jnp.concatenate([norm_grads, jnp.full((1, C), loss_local)], 0)
+    small = sum_all(small)
+    norm_total, loss_sum = (small[:-1], small[-1, 0])
     slot_m, slot_v, slot_w = adamw_step(
         slot_weight, slot_moment, slot_second, owned, RATE_MATRIX, DECAY_RATE
     )

time: 1130 us -> 870 us (0.77)
  waiting for transfers between devices: 335 us -> 137 us
  blocking collectives: 127 us -> 0 us
  starting transfers between devices: 15.7 us -> 65.6 us
    unnamed x6 -> x3, waiting for transfers between devices: 231 us -> 0.73 us
    ppermute x0 -> x40, waiting for transfers between devices: none -> 115 us  [swap(): return lax.ppermute(values, axis, [(i, i ^ bit) for i in range(count)])]
    psum x1 -> x0, waiting for transfers between devices: 90.3 us -> none  [body(): lax.psum((norm_grads, d_head, loss_local), BOTH)]
    psum x2 -> x0, blocking collectives: 80.8 us -> none  [the longest x1 40.9 us: body(): pixel_total = lax.psum(jnp.sum(keep_mask), BOTH)]
    ppermute x0 -> x40, starting transfers between devices: none -> 49.7 us  [swap(): return lax.ppermute(values, axis, [(i, i ^ bit) for i in range(count)])]
    all_gather x1 -> x0, blocking collectives: 45.8 us -> none  [body(): first_unit = lax.all_gather(unit_part[0], BOTH, axis=0, tiled=True)]
    mul x3 -> x1, other arithmetic: 46.3 us -> 13.8 us  [gelu_exact(): return jax.nn.gelu(values, approximate=False)]
    convert_element_type x3 -> x5, other arithmetic: 44.9 us -> 77.1 us  [layer_forward(): active = gelu_exact(mixed).astype(jnp.bfloat16)]
  transfers between devices with their start and end apart: 9 -> 47, of which waited for: 3 -> 27; matrix products, arithmetic and copies ran while one was open for 13% -> 27% of each run, Pallas kernels for 0% -> 0%
where the time goes in v2:
time: 870 us; the launch traced here: 857 us
  matrix products  336 us (39%)
  other arithmetic  166 us (19%)
  waiting for transfers between devices  137 us (16%)
  local copies, waits for them, and re-layouts  126 us (14%)
  starting transfers between devices  65.6 us (8%)
  between operations  25.9 us (3%)
    dot_general x92, matrix products, product(): return jnp.dot(left, right, preferred_element_type=jnp.float32)  122 us
    ppermute x40, waiting for transfers between devices, swap(): return lax.ppermute(values, axis, [(i, i ^ bit) for i in range(count)])  115 us
    convert_element_type x5, other arithmetic, layer_forward(): active = gelu_exact(mixed).astype(jnp.bfloat16)  77.1 us
    dot_general x19, matrix products, back_product(): lax.dot_general(gradient, weight, (((1,), (1,)), ((), ())), preferred_ele...  50.8 us
    ppermute x40, starting transfers between devices, swap(): return lax.ppermute(values, axis, [(i, i ^ bit) for i in range(count)])  49.7 us
    dot_general x3, matrix products, attend_backward(): jnp.einsum('hqk,khd->qhd', grad_scores, split_heads(keyval[:, :C]), prefe...  39 us
    dot_general x3, matrix products, attend_backward(): jnp.einsum('hqk,qhd->khd', grad_scores, split_heads(queries), preferred_e...  36.7 us
    dot_general x20, matrix products, outer_sum(): lax.dot_general(left, right, (((0,), (0,)), ((), ())), preferred_element_...  35.2 us
  transfers between devices with their start and end apart: 47, of which 27 were waited for; matrix products, arithmetic and copies ran while one was open for 27% of the time, Pallas kernels for 0%

profile of v2, /device:TPU:1, one launch (start us, length us, event | category | flops | bytes accessed | tf_op | source)
XLA Modules:
  0.0 857.4 jit_solution(15237676246056079150)
XLA Ops:
  10.0 6.5 all-to-all-start
  16.7 13.6 %all-to-all-done = bf16[2,8,40,320]{3,2,0,1:T(8,128)(2,1)S(1)} async-done(((bf16[2,8,40,320]{3,2,0,1:T(8,128)(2,1)}), bf16[2,8,40,320]{3,2,0,1:T(8,128)(2,1)S(1)}, u32[]{:S(2)}, u32[]{:S(2)}) %all-to-all-start) | async-done | bytes 409632 | tf_op jit(solution)/shard_map/all_to_all | solution.py:362
  46.3 3.0 collective-permute-done.1
  60.1 4.7 collective-permute-start.7
  67.1 3.3 collective-permute-start.8
  82.6 4.6 collective-permute-start.5
  91.8 3.7 copy.259
  99.8 3.1 fusion.930
  119.1 7.2 fusion.932
  126.3 4.3 convolution_convert_fusion.20
  150.3 8.1 all-gather.6.cloned.1.call-done
  166.9 4.0 fusion.191
  177.1 15.0 %fusion.41 = (bf16[4,304,1280]{2,1,0:T(8,128)(2,1)S(1)}, f32[4,304,1280]{2,1,0:T(8,128)}, f32[4,304,1280]{2,1,0:T(8,128)}) fusion(f32[1,304,1280]{2,1,0:T(8,128)S(1)} %fusion.191, f32[1,304,1280]{2,1,0:T(8,128)S(1)} %fusion.184, f32[1,304,1280]{2,1,0:T(8,128)S(1)} %fusion.175, f32[1,304,1280]{2,1,0:T(8,128)S(1)} %fusion.161), kind=kLoop, calls=%fused_computation.67 | loop fusion | flops 105840640 | bytes 21790720 | tf_op jit(solution)/shard_map/convert_element_type | solution.py:218
  201.8 7.2 fusion.936
  209.0 4.2 convolution_convert_fusion.18
  230.0 2.8 fusion.203
  239.7 17.2 %fusion.44 = (bf16[4,304,1280]{2,1,0:T(8,128)(2,1)S(1)}, f32[4,304,1280]{2,1,0:T(8,128)}, f32[4,304,1280]{2,1,0:T(8,128)}) fusion(f32[1,304,1280]{2,1,0:T(8,128)} %fusion.233, f32[1,304,1280]{2,1,0:T(8,128)} %fusion.226, f32[1,304,1280]{2,1,0:T(8,128)} %fusion.217, f32[1,304,1280]{2,1,0:T(8,128)} %fusion.203), kind=kLoop, calls=%fused_computation.70 | loop fusion | flops 105840640 | bytes 21790720 | tf_op jit(solution)/shard_map/convert_element_type | solution.py:218
  267.9 7.3 fusion.940
  275.2 4.3 convolution_convert_fusion.16
  295.8 13.8 %negate_multiply_fusion = (f32[4,304,1280]{2,1,0:T(8,128)S(1)}, bf16[4,304,1280]{2,1,0:T(8,128)(2,1)S(1)}, f32[4,304,1280]{2,1,0:T(8,128)S(1)}) fusion(f32[1,304,1280]{2,1,0:T(8,128)S(1)} %fusion.275, f32[1,304,1280]{2,1,0:T(8,128)S(1)} %fusion.268, f32[1,304,1280]{2,1,0:T(8,128)S(1)} %fusion.259, f32[1,304,1280]{2,1,0:T(8,128)S(1)} %fusion.245), kind=kLoop, calls=%fused_computation.149 | loop fusion | flops 105840640 | bytes 21790720 | tf_op jit(solution)/shard_map/mul | solution.py:36
  316.7 14.7 %fusion.56 = (bf16[1216,1280]{1,0:T(8,128)(2,1)}, f32[1216,1280]{1,0:T(8,128)}, f32[1216,1280]{1,0:T(8,128)}) fusion(f32[4,304,1280]{2,1,0:T(8,128)S(1)} %get-tuple-element.189, f32[4,304,1280]{2,1,0:T(8,128)S(1)} %get-tuple-element.187), kind=kLoop, calls=%fused_computation.103 | loop fusion | flops 96501760 | bytes 28016640 | tf_op jit(solution)/shard_map/convert_element_type | solution.py:218
  331.4 7.9 fusion.23
  348.2 3.9 fusion.565
  353.6 3.3 fusion.569
  371.5 4.4 fusion.944
  375.8 13.1 %fusion.585 = bf16[5,64,304]{2,1,0:T(8,128)(2,1)} fusion(bf16[1216,5,64]{0,2,1:T(8,128)(2,1)} %bitcast.708, f32[5,1216,304]{1,2,0:T(8,128)} %fusion.944, f32[5,1216,304]{1,2,0:T(8,128)} %get-tuple-element.274, f32[5,1216]{1,0:T(8,128)} %copy-done.405), kind=kOutput, calls=%fused_computation.1054 | convolution fusion | flops 249626864 | bytes 15783680 | tf_op jit(solution)/shard_map/hqk,qhd->khd/dot_general | solution.py:183
  388.9 13.2 %fusion.147 = bf16[5,64,1216]{2,1,0:T(8,128)(2,1)} fusion(bf16[304,5,64]{0,2,1:T(8,128)(2,1)S(1)} %bitcast.714, f32[5,1216,304]{1,2,0:T(8,128)} %fusion.944, f32[5,1216,304]{1,2,0:T(8,128)} %get-tuple-element.274, f32[5,1216]{1,0:T(8,128)} %copy-done.405), kind=kOutput, calls=%fused_computation.489 | convolution fusion | flops 249918704 | bytes 15783680 | tf_op jit(solution)/shard_map/hqk,khd->qhd/dot_general | solution.py:180
  412.7 2.8 concatenate.63
  415.5 3.4 multiply_reduce_fusion.8
  420.5 15.1 %fusion.54 = (bf16[1216,1280]{1,0:T(8,128)(2,1)}, f32[1216,1280]{1,0:T(8,128)S(1)}, f32[1216,1280]{1,0:T(8,128)}) fusion(f32[4,304,1280]{2,1,0:T(8,128)S(1)} %bitcast.647, f32[4,304,1280]{2,1,0:T(8,128)} %get-tuple-element.191), kind=kLoop, calls=%fused_computation.96 | loop fusion | flops 96501760 | bytes 28016640 | tf_op jit(solution)/shard_map/convert_element_type | solution.py:218
  435.6 5.9 fusion.30
  450.9 4.0 fusion.529
  456.3 3.3 fusion.533
  475.5 4.3 fusion.945
  479.8 12.2 %fusion.582 = bf16[5,64,304]{2,1,0:T(8,128)(2,1)} fusion(bf16[1216,5,64]{0,2,1:T(8,128)(2,1)S(1)} %bitcast.706, f32[5,1216,304]{1,2,0:T(8,128)} %fusion.945, f32[5,1216,304]{1,2,0:T(8,128)} %get-tuple-element.266, f32[5,1216]{1,0:T(8,128)S(1)} %copy-done.404), kind=kOutput, calls=%fused_computation.1053 | convolution fusion | flops 249626864 | bytes 15783680 | tf_op jit(solution)/shard_map/hqk,qhd->khd/dot_general | solution.py:183
  492.1 12.5 %fusion.144 = bf16[5,64,1216]{2,1,0:T(8,128)(2,1)S(1)} fusion(bf16[304,5,64]{0,2,1:T(8,128)(2,1)} %bitcast.712, f32[5,1216,304]{1,2,0:T(8,128)} %fusion.945, f32[5,1216,304]{1,2,0:T(8,128)} %get-tuple-element.266, f32[5,1216]{1,0:T(8,128)S(1)} %copy-done.404), kind=kOutput, calls=%fused_computation.488 | convolution fusion | flops 249918704 | bytes 15783680 | tf_op jit(solution)/shard_map/hqk,khd->qhd/dot_general | solution.py:180
  515.4 2.9 concatenate.65
  518.3 3.4 multiply_reduce_fusion.10
  523.3 15.1 %fusion.52 = (bf16[1216,1280]{1,0:T(8,128)(2,1)}, f32[1216,1280]{1,0:T(8,128)S(1)}, f32[1216,1280]{1,0:T(8,128)}) fusion(f32[4,304,1280]{2,1,0:T(8,128)S(1)} %bitcast.644, f32[4,304,1280]{2,1,0:T(8,128)} %get-tuple-element.194), kind=kLoop, calls=%fused_computation.89 | loop fusion | flops 96501760 | bytes 28016640 | tf_op jit(solution)/shard_map/convert_element_type | solution.py:218
  538.4 5.9 fusion.37
  553.4 4.0 fusion.493
  558.8 3.3 fusion.497
  577.4 4.3 fusion.946
  581.7 11.5 %fusion.579 = bf16[5,64,304]{2,1,0:T(8,128)(2,1)S(1)} fusion(bf16[1216,5,64]{0,2,1:T(8,128)(2,1)S(1)} %bitcast.704, f32[5,1216,304]{1,2,0:T(8,128)} %fusion.946, f32[5,1216,304]{1,2,0:T(8,128)} %get-tuple-element.258, f32[5,1216]{1,0:T(8,128)S(1)} %copy-done.402), kind=kOutput, calls=%fused_computation.1052 | convolution fusion | flops 249626864 | bytes 15783680 | tf_op jit(solution)/shard_map/hqk,qhd->khd/dot_general | solution.py:183
  593.2 13.3 %fusion.141 = bf16[5,64,1216]{2,1,0:T(8,128)(2,1)} fusion(bf16[304,5,64]{0,2,1:T(8,128)(2,1)S(1)} %bitcast.710, f32[5,1216,304]{1,2,0:T(8,128)} %fusion.946, f32[5,1216,304]{1,2,0:T(8,128)} %get-tuple-element.258, f32[5,1216]{1,0:T(8,128)S(1)} %copy-done.402), kind=kOutput, calls=%fused_computation.487 | convolution fusion | flops 249918704 | bytes 15783680 | tf_op jit(solution)/shard_map/hqk,khd->qhd/dot_general | solution.py:180
  610.0 3.1 convolution_convert_fusion.6
  624.4 4.0 convolution_convert_fusion.7
  636.9 2.9 stack.433
  650.8 2.9 constant_dynamic-slice_fusion.1
  682.7 2.8 convolution_convert_fusion.24
  690.8 5.2 collective-permute-done.18
  703.1 5.5 collective-permute-done.38
  722.7 11.8 %collective-permute-done.28 = bf16[4,2,2,2,40,320]{5,4,0,2,3,1:T(8,128)(2,1)S(1)} collective-permute-done((bf16[4,2,2,2,40,320]{5,4,0,2,3,1:T(8,128)(2,1)S(1)}, bf16[4,2,2,2,40,320]{5,4,0,2,3,1:T(8,128)(2,1)S(1)}, u32[]{:S(2)}, u32[]{:S(2)}) %collective-permute-start.28) | collective-permute-done | bytes 819232 | tf_op jit(solution)/shard_map/ppermute | solution.py:277
  735.2 20.4 %collective-permute-done.33 = bf16[4,2,2,2,40,320]{5,4,0,2,3,1:T(8,128)(2,1)S(1)} collective-permute-done((bf16[4,2,2,2,40,320]{5,4,0,2,3,1:T(8,128)(2,1)S(1)}, bf16[4,2,2,2,40,320]{5,4,0,2,3,1:T(8,128)(2,1)S(1)}, u32[]{:S(2)}, u32[]{:S(2)}) %collective-permute-start.33) | collective-permute-done | bytes 819232 | tf_op jit(solution)/shard_map/ppermute | solution.py:277
  756.3 20.4 %collective-permute-done.23 = bf16[4,2,2,2,40,320]{5,4,3,2,1,0:T(8,128)(2,1)S(1)} collective-permute-done((bf16[4,2,2,2,40,320]{5,4,3,2,1,0:T(8,128)(2,1)S(1)}, bf16[4,2,2,2,40,320]{5,4,3,2,1,0:T(8,128)(2,1)S(1)}, u32[]{:S(2)}, u32[]{:S(2)}) %collective-permute-start.23) | collective-permute-done | bytes 819232 | tf_op jit(solution)/shard_map/ppermute | solution.py:277
  779.3 7.5 collective-permute-done.24
  789.6 5.8 collective-permute-done.25
  798.1 7.8 collective-permute-done.26
  806.0 3.8 collective-permute-done.36
  811.7 4.6 all-to-all-start.1
  821.6 3.9 collective-permute-done.13
  825.5 3.8 collective-permute-start.14
  838.8 3.5 collective-permute-done.41
  844.7 4.8 multiply_subtract_fusion
  (1361 shorter events, 381.7 us)
Async XLA Ops:
  10.0 20.3 %all-to-all-start = ((bf16[2,8,40,320]{3,2,0,1:T(8,128)(2,1)}), bf16[2,8,40,320]{3,2,0,1:T(8,128)(2,1)S(1)}, u32[]{:S(2)}, u32[]{:S(2)}) async-start(bf16[2,8,40,320]{3,2,0,1:T(8,128)(2,1)} %copy.260), calls=%async_computation | async-start | bytes 983040 | tf_op jit(solution)/shard_map/all_to_all | solution.py:362
  16.5 89.8 %all-gather.4.cloned.1.call-start = ((), (), s32[]{:S(2)}) async-start(), calls=%async_computation.2 | async-start | bytes 4055040 | tf_op jit(solution)/shard_map/all_gather | solution.py:369
  31.9 126.5 %all-gather.6.cloned.1.call-start = ((), (), s32[]{:S(2)}) async-start(), calls=%async_computation.3 | async-start | bytes 4055040 | tf_op jit(solution)/shard_map/all_gather | solution.py:369
  32.6 203.0 %all-gather.8.cloned.1.call-start = ((), (), s32[]{:S(2)}) async-start(), calls=%async_computation.4 | async-start | bytes 4055040 | tf_op jit(solution)/shard_map/all_gather | solution.py:369
  32.7 21.2 %collective-permute-start.6 = (s32[2,192]{1,0:T(2,128)S(1)}, s32[2,192]{1,0:T(2,128)S(1)}, u32[]{:S(2)}, u32[]{:S(2)}) collective-permute-start(s32[2,192]{1,0:T(2,128)S(1)} %pad_add_fusion.1), channel_id=1, source_target_pairs={{1,0},{2,1},{3,2},{4,3},{5,4},{6,5},{7,6},{9,8},{10,9},{11,10},{12... | collective-permute-start | bytes 4616 | tf_op jit(solution)/shard_map/ppermute | solution.py:379
  36.5 50.7 %collective-permute-start = (bf16[192,1152]{1,0:T(8,128)(2,1)S(1)}, bf16[192,1152]{1,0:T(8,128)(2,1)}, u32[]{:S(2)}, u32[]{:S(2)}) collective-permute-start(bf16[192,1152]{1,0:T(8,128)(2,1)S(1)} %slice.451), channel_id=1, source_target_pairs={{1,0},{2,1},{3,2},{4,3},{5,4},{6,5},{7,6},{9,8},{10,9},{11,10},{12... | collective-permute-start | bytes 1327112 | tf_op jit(solution)/shard_map/ppermute | solution.py:377
  42.5 102.4 %copy-start.236 = (pred[304]{0:T(512)(128)(4,1)}, pred[304]{0:T(512)(128)(4,1)S(1)}, u32[]{:S(2)}) copy-start(pred[304]{0:T(512)(128)(4,1)S(1)} %get-tuple-element.162) | copy-start | bytes 916
  43.0 94.8 %copy-start.240 = (pred[304]{0:T(512)(128)(4,1)}, pred[304]{0:T(512)(128)(4,1)S(1)}, u32[]{:S(2)}) copy-start(pred[304]{0:T(512)(128)(4,1)S(1)} %get-tuple-element.169) | copy-start | bytes 916
  43.0 98.4 %copy-start.264 = (pred[304]{0:T(512)(128)(4,1)}, pred[304]{0:T(512)(128)(4,1)S(1)}, u32[]{:S(2)}) copy-start(pred[304]{0:T(512)(128)(4,1)S(1)} %get-tuple-element.240) | copy-start | bytes 916
  43.6 104.8 %copy-start.268 = (pred[304]{0:T(512)(128)(4,1)}, pred[304]{0:T(512)(128)(4,1)S(1)}, u32[]{:S(2)}) copy-start(pred[304]{0:T(512)(128)(4,1)S(1)} %get-tuple-element.250) | copy-start | bytes 916
  44.2 93.7 %copy-start.205 = (s32[304]{0:T(512)}, s32[304]{0:T(512)S(1)}, u32[]{:S(2)}) copy-start(s32[304]{0:T(512)S(1)} %get-tuple-element.248) | copy-start | bytes 3652
  44.2 100.7 %copy-start.202 = (s32[304]{0:T(512)}, s32[304]{0:T(512)S(1)}, u32[]{:S(2)}) copy-start(s32[304]{0:T(512)S(1)} %get-tuple-element.246) | copy-start | bytes 3652
  45.6 3.8 collective-permute-start.1
  46.3 58.2 %copy-start.228 = (f32[320]{0:T(512)}, f32[320]{0:T(512)S(1)}, u32[]{:S(2)}) copy-start(f32[320]{0:T(512)S(1)} %get-tuple-element.120) | copy-start | bytes 3844
  46.3 68.7 %copy-start.284 = (f32[320]{0:T(512)}, f32[320]{0:T(512)S(1)}, u32[]{:S(2)}) copy-start(f32[320]{0:T(512)S(1)} %get-tuple-element.118) | copy-start | bytes 3844
  46.3 85.5 %copy-start.306 = (f32[320]{0:T(512)}, f32[320]{0:T(512)S(1)}, u32[]{:S(2)}) copy-start(f32[320]{0:T(512)S(1)} %get-tuple-element.116) | copy-start | bytes 3844
  49.4 3.1 collective-permute-start.2
  51.0 79.5 %copy-start.184 = (f32[320]{0:T(512)}, f32[320]{0:T(512)S(1)}, u32[]{:S(2)}) copy-start(f32[320]{0:T(512)S(1)} %get-tuple-element.123) | copy-start | bytes 3844
  51.1 79.5 %copy-start.188 = (f32[320]{0:T(512)}, f32[320]{0:T(512)S(1)}, u32[]{:S(2)}) copy-start(f32[320]{0:T(512)S(1)} %get-tuple-element.122) | copy-start | bytes 3844
  52.6 3.8 collective-permute-start.3
  56.5 25.1 %collective-permute-start.4 = (bf16[2,2,2,1,40,320]{5,4,2,1,0,3:T(8,128)(2,1)S(1)}, bf16[2,2,2,1,40,320]{5,4,2,1,0,3:T(8,128)(2,1)S(1)}, u32[]{:S(2)}, u32[]{:S(2)}) collective-permute-start(bf16[2,2,2,1,40,320]{5,4,2,1,0,3:T(8,128)(2,1)S(1)} %fusion.672), channel_id=1, source_target_pairs={{0,8},{8,0},{16,24},{24,16},{1,9},{9,1},{17,25},{25,17},{2,10},{10... | collective-permute-start | bytes 614408 | tf_op jit(solution)/shard_map/ppermute | solution.py:277
  60.1 5.8 collective-permute-start.7
  67.1 3.5 collective-permute-start.8
  71.2 3.3 collective-permute-start.9
  75.0 2.4 collective-permute-start.10
  78.0 3.1 collective-permute-start.11
  82.6 12.9 %collective-permute-start.5 = (bf16[2,2,2,2,1,40,320]{6,5,3,2,1,0,4:T(8,128)(2,1)}, bf16[2,2,2,2,1,40,320]{6,5,3,2,1,0,4:T(8,128)(2,1)}, u32[]{:S(2)}, u32[]{:S(2)}) collective-permute-start(bf16[2,2,2,2,1,40,320]{6,5,3,2,1,0,4:T(8,128)(2,1)} %fusion.641), channel_id=1, source_target_pairs={{0,1},{1,0},{2,3},{3,2},{4,5},{5,4},{6,7},{7,6},{8,9},{9,8},{10,11... | collective-permute-start | bytes 1228808 | tf_op jit(solution)/shard_map/ppermute | solution.py:277
  99.8 75.4 %copy-start.139 = (f32[1280]{0:T(1024)}, f32[1280]{0:T(1024)S(1)}, u32[]{:S(2)}) copy-start(f32[1280]{0:T(1024)S(1)} %get-tuple-element.93) | copy-start | bytes 15364
  99.8 133.0 %copy-start.141 = (f32[1280]{0:T(1024)}, f32[1280]{0:T(1024)S(1)}, u32[]{:S(2)}) copy-start(f32[1280]{0:T(1024)S(1)} %get-tuple-element.84) | copy-start | bytes 15364
  99.8 133.0 %copy-start.143 = (f32[1280]{0:T(1024)}, f32[1280]{0:T(1024)S(1)}, u32[]{:S(2)}) copy-start(f32[1280]{0:T(1024)S(1)} %get-tuple-element.85) | copy-start | bytes 15364
  99.8 133.0 %copy-start.145 = (f32[1280]{0:T(1024)}, f32[1280]{0:T(1024)S(1)}, u32[]{:S(2)}) copy-start(f32[1280]{0:T(1024)S(1)} %get-tuple-element.86) | copy-start | bytes 15364
  280.6 84.0 %copy-start.211 = (f32[1216]{0:T(1024)}, f32[1216]{0:T(1024)S(1)}, u32[]{:S(2)}) copy-start(f32[1216]{0:T(1024)S(1)} %fusion.697) | copy-start | bytes 14596
  367.4 52.1 %copy-start.4 = (f32[1216,320]{0,1:T(8,128)}, f32[1216,320]{0,1:T(8,128)S(1)}, u32[]{:S(2)}) copy-start(f32[1216,320]{0,1:T(8,128)S(1)} %add_add_fusion.13) | copy-start | bytes 4669444
  609.7 90.5 %collective-permute-start.37 = (f32[320,150]{0,1:T(8,128)}, f32[320,150]{0,1:T(8,128)}, u32[]{:S(2)}, u32[]{:S(2)}) collective-permute-start(f32[320,150]{0,1:T(8,128)} %fusion.769), channel_id=1, source_target_pairs={{0,1},{1,0},{2,3},{3,2},{4,5},{5,4},{6,7},{7,6},{8,9},{9,8},{10,11... | collective-permute-start | bytes 576008 | tf_op jit(solution)/shard_map/ppermute | solution.py:277
  656.8 54.4 %collective-permute-start.27 = (bf16[4,2,2,2,2,40,320]{6,5,0,3,4,1,2:T(8,128)(2,1)}, bf16[4,2,2,2,2,40,320]{6,5,0,3,4,1,2:T(8,128)(2,1)}, u32[]{:S(2)}, u32[]{:S(2)}) collective-permute-start(bf16[4,2,2,2,2,40,320]{6,5,0,3,4,1,2:T(8,128)(2,1)} %bitcast.642), channel_id=1, source_target_pairs={{0,1},{1,0},{2,3},{3,2},{4,5},{5,4},{6,7},{7,6},{8,9},{9,8},{10,11... | collective-permute-start | bytes 4915208 | tf_op jit(solution)/shard_map/ppermute | solution.py:277
  657.0 56.6 %collective-permute-start.32 = (bf16[4,2,2,2,2,40,320]{6,5,0,3,4,1,2:T(8,128)(2,1)}, bf16[4,2,2,2,2,40,320]{6,5,0,3,4,1,2:T(8,128)(2,1)}, u32[]{:S(2)}, u32[]{:S(2)}) collective-permute-start(bf16[4,2,2,2,2,40,320]{6,5,0,3,4,1,2:T(8,128)(2,1)} %bitcast.641), channel_id=1, source_target_pairs={{0,1},{1,0},{2,3},{3,2},{4,5},{5,4},{6,7},{7,6},{8,9},{9,8},{10,11... | collective-permute-start | bytes 4915208 | tf_op jit(solution)/shard_map/ppermute | solution.py:277
  682.4 4.9 collective-permute-start.17
  688.6 7.4 collective-permute-start.18
  696.1 6.3 collective-permute-start.19
  698.9 18.5 %collective-permute-start.22 = (bf16[4,2,2,2,2,40,320]{6,5,4,3,2,1,0:T(8,128)(2,1)}, bf16[4,2,2,2,2,40,320]{6,5,4,3,2,1,0:T(8,128)(2,1)}, u32[]{:S(2)}, u32[]{:S(2)}) collective-permute-start(bf16[4,2,2,2,2,40,320]{6,5,4,3,2,1,0:T(8,128)(2,1)} %dynamic-slice_bitcast_fusion), channel_id=1, source_target_pairs={{0,1},{1,0},{2,3},{3,2},{4,5},{5,4},{6,7},{7,6},{8,9},{9,8},{10,11... | collective-permute-start | bytes 4915208 | tf_op jit(solution)/shard_map/ppermute | solution.py:277
  701.4 7.2 collective-permute-start.38
  702.5 7.4 collective-permute-start.20
  708.6 107.7 %collective-permute-start.39 = (f32[320,150]{0,1:T(8,128)S(1)}, f32[320,150]{0,1:T(8,128)S(1)}, u32[]{:S(2)}, u32[]{:S(2)}) collective-permute-start(f32[320,150]{0,1:T(8,128)S(1)} %add.2099), channel_id=1, source_target_pairs={{0,4},{1,5},{2,6},{3,7},{4,0},{5,1},{6,2},{7,3},{8,12},{9,13},{10,... | collective-permute-start | bytes 576008 | tf_op jit(solution)/shard_map/ppermute | solution.py:277
  709.9 12.8 %collective-permute-start.21 = (bf16[1,40,320]{2,1,0:T(8,128)(2,1)S(1)}, bf16[1,40,320]{2,1,0:T(8,128)(2,1)S(1)}, u32[]{:S(2)}, u32[]{:S(2)}) collective-permute-start(bf16[1,40,320]{2,1,0:T(8,128)(2,1)S(1)} %dynamic-slice_bitcast_fusion.17), channel_id=1, source_target_pairs={{0,4},{1,5},{2,6},{3,7},{4,0},{5,1},{6,2},{7,3},{8,12},{9,13},{10,... | collective-permute-start | bytes 76808 | tf_op jit(solution)/shard_map/ppermute | solution.py:277
  713.3 21.2 %collective-permute-start.28 = (bf16[4,2,2,2,40,320]{5,4,0,2,3,1:T(8,128)(2,1)S(1)}, bf16[4,2,2,2,40,320]{5,4,0,2,3,1:T(8,128)(2,1)S(1)}, u32[]{:S(2)}, u32[]{:S(2)}) collective-permute-start(bf16[4,2,2,2,40,320]{5,4,0,2,3,1:T(8,128)(2,1)S(1)} %dynamic-slice_bitcast_fusion.2), channel_id=1, source_target_pairs={{0,8},{8,0},{16,24},{24,16},{1,9},{9,1},{17,25},{25,17},{2,10},{10... | collective-permute-start | bytes 2457608 | tf_op jit(solution)/shard_map/ppermute | solution.py:277
  717.1 38.5 %collective-permute-start.33 = (bf16[4,2,2,2,40,320]{5,4,0,2,3,1:T(8,128)(2,1)S(1)}, bf16[4,2,2,2,40,320]{5,4,0,2,3,1:T(8,128)(2,1)S(1)}, u32[]{:S(2)}, u32[]{:S(2)}) collective-permute-start(bf16[4,2,2,2,40,320]{5,4,0,2,3,1:T(8,128)(2,1)S(1)} %dynamic-slice_bitcast_fusion.1), channel_id=1, source_target_pairs={{0,8},{8,0},{16,24},{24,16},{1,9},{9,1},{17,25},{25,17},{2,10},{10... | collective-permute-start | bytes 2457608 | tf_op jit(solution)/shard_map/ppermute | solution.py:277
  719.7 57.0 %collective-permute-start.23 = (bf16[4,2,2,2,40,320]{5,4,3,2,1,0:T(8,128)(2,1)S(1)}, bf16[4,2,2,2,40,320]{5,4,3,2,1,0:T(8,128)(2,1)S(1)}, u32[]{:S(2)}, u32[]{:S(2)}) collective-permute-start(bf16[4,2,2,2,40,320]{5,4,3,2,1,0:T(8,128)(2,1)S(1)} %dynamic-slice_bitcast_fusion.3), channel_id=1, source_target_pairs={{0,8},{8,0},{16,24},{24,16},{1,9},{9,1},{17,25},{25,17},{2,10},{10... | collective-permute-start | bytes 2457608 | tf_op jit(solution)/shard_map/ppermute | solution.py:277
  734.9 42.5 %collective-permute-start.29 = (bf16[4,2,2,40,320]{4,3,0,1,2:T(8,128)(2,1)S(1)}, bf16[4,2,2,40,320]{4,3,0,1,2:T(8,128)(2,1)S(1)}, u32[]{:S(2)}, u32[]{:S(2)}) collective-permute-start(bf16[4,2,2,40,320]{4,3,0,1,2:T(8,128)(2,1)S(1)} %dynamic-slice_bitcast_fusion.5), channel_id=1, source_target_pairs={{0,16},{8,24},{16,0},{24,8},{1,17},{9,25},{17,1},{25,9},{2,18},{10... | collective-permute-start | bytes 1228808 | tf_op jit(solution)/shard_map/ppermute | solution.py:277
  756.0 22.7 %collective-permute-start.34 = (bf16[4,2,2,40,320]{4,3,0,1,2:T(8,128)(2,1)S(1)}, bf16[4,2,2,40,320]{4,3,0,1,2:T(8,128)(2,1)S(1)}, u32[]{:S(2)}, u32[]{:S(2)}) collective-permute-start(bf16[4,2,2,40,320]{4,3,0,1,2:T(8,128)(2,1)S(1)} %dynamic-slice_bitcast_fusion.4), channel_id=1, source_target_pairs={{0,16},{8,24},{16,0},{24,8},{1,17},{9,25},{17,1},{25,9},{2,18},{10... | collective-permute-start | bytes 1228808 | tf_op jit(solution)/shard_map/ppermute | solution.py:277
  777.0 9.8 %collective-permute-start.24 = (bf16[4,2,2,40,320]{4,3,2,1,0:T(8,128)(2,1)S(1)}, bf16[4,2,2,40,320]{4,3,2,1,0:T(8,128)(2,1)S(1)}, u32[]{:S(2)}, u32[]{:S(2)}) collective-permute-start(bf16[4,2,2,40,320]{4,3,2,1,0:T(8,128)(2,1)S(1)} %dynamic-slice_bitcast_fusion.6), channel_id=1, source_target_pairs={{0,16},{8,24},{16,0},{24,8},{1,17},{9,25},{17,1},{25,9},{2,18},{10... | collective-permute-start | bytes 1228808 | tf_op jit(solution)/shard_map/ppermute | solution.py:277
  777.6 10.5 %collective-permute-start.30 = (bf16[4,2,40,320]{3,2,0,1:T(8,128)(2,1)S(1)}, bf16[4,2,40,320]{3,2,0,1:T(8,128)(2,1)S(1)}, u32[]{:S(2)}, u32[]{:S(2)}) collective-permute-start(bf16[4,2,40,320]{3,2,0,1:T(8,128)(2,1)S(1)} %dynamic-slice_bitcast_fusion.9), channel_id=1, source_target_pairs={{0,2},{1,3},{2,0},{3,1},{4,6},{5,7},{6,4},{7,5},{8,10},{9,11},{10,... | collective-permute-start | bytes 614408 | tf_op jit(solution)/shard_map/ppermute | solution.py:277
  778.8 16.9 %collective-permute-start.35 = (bf16[4,2,40,320]{3,2,0,1:T(8,128)(2,1)S(1)}, bf16[4,2,40,320]{3,2,0,1:T(8,128)(2,1)S(1)}, u32[]{:S(2)}, u32[]{:S(2)}) collective-permute-start(bf16[4,2,40,320]{3,2,0,1:T(8,128)(2,1)S(1)} %dynamic-slice_bitcast_fusion.8), channel_id=1, source_target_pairs={{0,2},{1,3},{2,0},{3,1},{4,6},{5,7},{6,4},{7,5},{8,10},{9,11},{10,... | collective-permute-start | bytes 614408 | tf_op jit(solution)/shard_map/ppermute | solution.py:277
  787.0 8.5 collective-permute-start.25
  788.2 17.8 %collective-permute-start.31 = (bf16[4,40,320]{2,1,0:T(8,128)(2,1)S(1)}, bf16[4,40,320]{2,1,0:T(8,128)(2,1)S(1)}, u32[]{:S(2)}, u32[]{:S(2)}) collective-permute-start(bf16[4,40,320]{2,1,0:T(8,128)(2,1)S(1)} %dynamic-slice_bitcast_fusion.13), channel_id=1, source_target_pairs={{0,4},{1,5},{2,6},{3,7},{4,0},{5,1},{6,2},{7,3},{8,12},{9,13},{10,... | collective-permute-start | bytes 307208 | tf_op jit(solution)/shard_map/ppermute | solution.py:277
  795.5 10.4 %collective-permute-start.26 = (bf16[4,40,320]{2,1,0:T(8,128)(2,1)S(1)}, bf16[4,40,320]{2,1,0:T(8,128)(2,1)S(1)}, u32[]{:S(2)}, u32[]{:S(2)}) collective-permute-start(bf16[4,40,320]{2,1,0:T(8,128)(2,1)S(1)} %dynamic-slice_bitcast_fusion.14), channel_id=1, source_target_pairs={{0,4},{1,5},{2,6},{3,7},{4,0},{5,1},{6,2},{7,3},{8,12},{9,13},{10,... | collective-permute-start | bytes 307208 | tf_op jit(solution)/shard_map/ppermute | solution.py:277
  795.8 14.0 %collective-permute-start.36 = (bf16[4,40,320]{2,1,0:T(8,128)(2,1)S(1)}, bf16[4,40,320]{2,1,0:T(8,128)(2,1)S(1)}, u32[]{:S(2)}, u32[]{:S(2)}) collective-permute-start(bf16[4,40,320]{2,1,0:T(8,128)(2,1)S(1)} %dynamic-slice_bitcast_fusion.12), channel_id=1, source_target_pairs={{0,4},{1,5},{2,6},{3,7},{4,0},{5,1},{6,2},{7,3},{8,12},{9,13},{10,... | collective-permute-start | bytes 307208 | tf_op jit(solution)/shard_map/ppermute | solution.py:277
  811.7 31.5 %all-to-all-start.1 = ((bf16[16,1,40,320]{3,2,1,0:T(8,128)(2,1)}), bf16[16,1,40,320]{3,2,1,0:T(8,128)(2,1)S(1)}, u32[]{:S(2)}, u32[]{:S(2)}) async-start(bf16[16,1,40,320]{3,2,1,0:T(8,128)(2,1)} %fusion.615), calls=%async_computation.1 | async-start | bytes 983040 | tf_op jit(solution)/shard_map/all_to_all | solution.py:459
  816.4 20.5 %collective-permute-start.40 = (f32[320,150]{0,1:T(8,128)S(1)}, f32[320,150]{0,1:T(8,128)S(1)}, u32[]{:S(2)}, u32[]{:S(2)}) collective-permute-start(f32[320,150]{0,1:T(8,128)S(1)} %add.2100), channel_id=1, source_target_pairs={{0,8},{8,0},{16,24},{24,16},{1,9},{9,1},{17,25},{25,17},{2,10},{10... | collective-permute-start | bytes 576008 | tf_op jit(solution)/shard_map/ppermute | solution.py:277
  818.6 1.3 collective-permute-start.12
  819.9 5.6 collective-permute-start.13
  825.5 5.2 collective-permute-start.14
  830.7 2.8 collective-permute-start.15
  833.5 2.8 collective-permute-start.16
  836.9 5.4 collective-permute-start.41
  (402 other events, 1796.6 us)
Sparse Core Ops, SparseCore 0:
  32.0 62.5 all-gather.3
  98.1 60.2 all-gather.5
  162.0 60.2 all-gather.7

commit v3 on v2

v3 whole, which is shorter than its diff:
```python
import jax
import jax.numpy as jnp
from jax import lax
from jax.experimental import pallas as pl
from jax.experimental.pallas import tpu as pltpu
from jax.sharding import PartitionSpec as P

C = 320
HEADS = 5
HD = 64
FF = 1280
PIN = 1152
BLOCKS = 3
BIG_SIDE = 14
SMALL_SIDE = 6
STEP = 10
KVH = 49


EPS_NORM = 1e-06
BETA_ONE = 0.9
BETA_TWO = 0.999
ADAM_EPS = 1e-08
RATE_MATRIX = 0.05
RATE_VECTOR = 0.3
DECAY_RATE = 0.05
NEG_FILL = -1e30
PREC_HIGH = lax.Precision.HIGHEST


def layer_norm(values, gain_vec, shift_vec):
    center = values - jnp.mean(values, -1, keepdims=True)
    inverse = lax.rsqrt(jnp.mean(center * center, -1, keepdims=True) + EPS_NORM)
    return center * inverse * gain_vec + shift_vec


def adamw_step(weight, moment, second, gradient, rate_now, decay_now):
    moment = BETA_ONE * moment + (1.0 - BETA_ONE) * gradient
    second = BETA_TWO * second + (1.0 - BETA_TWO) * gradient * gradient
    m_hat = moment / (1.0 - BETA_ONE**STEP)
    v_hat = second / (1.0 - BETA_TWO**STEP)
    weight = weight - rate_now * (m_hat / (jnp.sqrt(v_hat) + ADAM_EPS) + decay_now * weight)
    return (moment, second, weight)


def product(left, right):
    return jnp.dot(left, right, preferred_element_type=jnp.float32)


def outer_sum(left, right):
    return lax.dot_general(
        left, right, (((0,), (0,)), ((), ())), preferred_element_type=jnp.float32
    )


def back_product(gradient, weight):
    return lax.dot_general(
        gradient, weight, (((1,), (1,)), ((), ())), preferred_element_type=jnp.float32
    )


def norm_back(values, gain_vec, shift_vec, gradient):
    _, pull_back = jax.vjp(layer_norm, values, gain_vec, shift_vec)
    return pull_back(gradient)


OVER = 4 * KVH - 4


def image_layout(positions, counts):
    big_tok = BIG_SIDE * BIG_SIDE
    small_tok = SMALL_SIDE * SMALL_SIDE
    big_end = counts[0] * big_tok
    small_end = big_end + counts[1] * small_tok
    is_big = positions < big_end
    is_small = jnp.logical_and(positions >= big_end, positions < small_end)
    half_side = jnp.where(is_big, BIG_SIDE // 2, SMALL_SIDE // 2)
    begin_at = jnp.where(
        is_big,
        positions // big_tok * big_tok,
        jnp.where(is_small, big_end + (positions - big_end) // small_tok * small_tok, small_end),
    )
    tile_idx = (positions - begin_at) // 4
    return (begin_at, half_side, tile_idx // half_side, tile_idx % half_side, positions < small_end)


def shift_matrices(begin_at, half_side, tile_y, tile_x, is_real):
    count = begin_at.shape[0]
    own = jnp.arange(count, dtype=jnp.int32)
    offset = own[None, :] - own[:, None]
    inside = {
        (0, -1): tile_x > 0,
        (0, 1): tile_x < half_side - 1,
        (-1, 0): tile_y > 0,
        (1, 0): tile_y < half_side - 1,
    }
    result = {}
    for step_y in (-1, 0, 1):
        for step_x in (-1, 0, 1):
            if step_y == 0 and step_x == 0:
                continue
            allowed = is_real
            if step_y:
                allowed = allowed & inside[step_y, 0]
            if step_x:
                allowed = allowed & inside[0, step_x]
            hit = (offset == (step_y * half_side + step_x)[:, None]) & allowed[:, None]
            result[step_y, step_x] = hit.astype(jnp.bfloat16)
    return result


def tap_source(sub, tap):
    y_at = sub // 2 + tap // 3 - 1
    x_at = sub % 2 + tap % 3 - 1
    return (y_at % 2 * 2 + x_at % 2, y_at // 2, x_at // 2)


SQRT_HALF = 0.7071067811865476
INV_SQRT_TWO_PI = 0.3989422804014327
TAPS_OF = [[tap_source(sub, tap) for tap in range(9)] for sub in range(4)]
VMEM_LIMIT = 56 * 1024 * 1024
SPAN = 256
ROWS = 16
LANES = 128


def row_cut(tiles):
    return (tiles // 2 + 15) // 16 * 16


def shift_stacks(shifts):
    tiles = shifts[0, 1].shape[0]
    cut = row_cut(tiles)
    upper, lower = [], []
    for sub in range(4):
        step_y = 1 - 2 * (sub // 2)
        step_x = 1 - 2 * (sub % 2)
        for key in ((0, step_x), (step_y, 0), (step_y, step_x)):
            upper.append(shifts[key][:cut, :SPAN])
            lower.append(shifts[key][cut:, tiles - SPAN :])
    return (jnp.stack(upper).reshape(4, 3 * cut, SPAN), jnp.stack(lower).reshape(4, 3 * (tiles - cut), SPAN))


def move_planes(planes_ref, upper_ref, lower_ref, moved_ref):
    tiles = planes_ref.shape[0] // 4
    cut = row_cut(tiles)
    for sub in range(4):
        base = sub * tiles
        part = product(upper_ref[sub], planes_ref[base : base + SPAN, :])
        for key in range(3):
            moved_ref[sub, key, :cut, :] = part[key * cut : (key + 1) * cut]
        part = product(lower_ref[sub], planes_ref[base + tiles - SPAN : base + tiles, :])
        for key in range(3):
            moved_ref[sub, key, cut:, :] = part[key * (tiles - cut) : (key + 1) * (tiles - cut)]


def chunk_sources(planes_ref, moved_ref, row, lanes):
    tiles = planes_ref.shape[0] // 4
    found = {}
    for sub in range(4):
        found[sub, 0, 0] = planes_ref[pl.ds(pl.multiple_of(sub * tiles + row, ROWS), ROWS), lanes].astype(jnp.float32)
        step_y = 1 - 2 * (sub // 2)
        step_x = 1 - 2 * (sub % 2)
        for key, step in enumerate(((0, step_x), (step_y, 0), (step_y, step_x))):
            found[(sub,) + step] = moved_ref[sub, key, pl.ds(row, ROWS), lanes]
    return found


def norm_rows(values, gain, shift):
    center = values - jnp.mean(values, -1, keepdims=True)
    inverse = lax.rsqrt(jnp.mean(center * center, -1, keepdims=True) + EPS_NORM)
    unit = center * inverse
    return (unit, inverse, unit * gain + shift)


def norm_rows_back(unit, inverse, gain, grad):
    scaled = grad * gain
    return inverse * (
        scaled - jnp.mean(scaled, -1, keepdims=True) - unit * jnp.mean(scaled * unit, -1, keepdims=True)
    )


def mlp_forward_kernel(
    middle_ref, gains_ref, up_ref, down_ref, kern_ref, upper_ref, lower_ref, real_ref,
    out_ref, hidden_ref, active_ref, slope_ref,
    normed_ref, moved_ref,
):
    rows = middle_ref.shape[0]
    tiles = rows // 4

    @pl.when(pl.program_id(0) == 0)
    def _():
        @pl.loop(0, rows // 64)
        def _(at):
            span = pl.ds(pl.multiple_of(at * 64, 64), 64)
            normed = norm_rows(middle_ref[span, :], gains_ref[0:1, :], gains_ref[1:2, :])[2]
            normed_ref[span, :] = normed.astype(jnp.bfloat16)
            out_ref[span, :] = middle_ref[span, :]

    for sub in range(4):
        part = product(normed_ref[sub * tiles : (sub + 1) * tiles, :], up_ref[...])
        hidden_ref[sub * tiles : (sub + 1) * tiles, :] = part.astype(jnp.bfloat16)
    move_planes(hidden_ref, upper_ref, lower_ref, moved_ref)

    for lane in range(0, hidden_ref.shape[1], LANES):
        lanes = slice(lane, lane + LANES)
        kern = [kern_ref[tap : tap + 1, lanes] for tap in range(9)]

        @pl.loop(0, tiles // ROWS)
        def _(at):
            row = pl.multiple_of(at * ROWS, ROWS)
            found = chunk_sources(hidden_ref, moved_ref, row, lanes)
            real = real_ref[pl.ds(row, ROWS), :] > 0.0
            for sub in range(4):
                center = found[sub, 0, 0] * kern[4]
                total = center
                for tap in range(9):
                    if tap != 4:
                        total = total + found[TAPS_OF[sub][tap]] * kern[tap]
                mixed = jnp.where(real, total, center)
                half = 0.5 + 0.5 * lax.erf(mixed * SQRT_HALF)
                bell = jnp.exp(-0.5 * mixed * mixed) * INV_SQRT_TWO_PI
                span = pl.ds(pl.multiple_of(sub * tiles + row, ROWS), ROWS)
                active_ref[span, lanes] = (mixed * half).astype(jnp.bfloat16)
                slope_ref[span, lanes] = (half + mixed * bell).astype(jnp.bfloat16)

    for sub in range(4):
        span = slice(sub * tiles, (sub + 1) * tiles)
        out_ref[span, :] += product(active_ref[span, :], down_ref[...])


def untied(kernel, count, ties):
    def run(*refs):
        kernel(*refs[:count], *refs[count + ties :])

    return run


def whole(shape):
    return pl.BlockSpec(shape, lambda j: (0,) * len(shape))


def mlp_forward(middle, gains, w_up, w_down, kernel, stacks, real_rows):
    rows = middle.shape[0]
    block = 256
    by_lane = pl.BlockSpec((rows, block), lambda j: (0, j))
    low = jax.ShapeDtypeStruct((rows, FF), jnp.bfloat16)
    return pl.pallas_call(
        mlp_forward_kernel,
        grid=(FF // block,),
        out_shape=(jax.ShapeDtypeStruct((rows, C), jnp.float32), low, low, low),
        in_specs=[
            whole((rows, C)),
            whole((2, C)),
            pl.BlockSpec((C, block), lambda j: (0, j)),
            pl.BlockSpec((block, C), lambda j: (j, 0)),
            pl.BlockSpec((9, block), lambda j: (0, j)),
            whole(stacks[0].shape),
            whole(stacks[1].shape),
            whole(real_rows.shape),
        ],
        out_specs=(whole((rows, C)), by_lane, by_lane, by_lane),
        scratch_shapes=[
            pltpu.VMEM((rows, C), jnp.bfloat16),
            pltpu.VMEM((4, 3, rows // 4, block), jnp.float32),
        ],
        compiler_params=pltpu.CompilerParams(vmem_limit_bytes=VMEM_LIMIT),
        cost_estimate=pl.CostEstimate(flops=14 * 10**9, bytes_accessed=18 * 10**6, transcendentals=4 * 10**6),
        name="mlp_forward",
    )(middle, gains, w_up, w_down, kernel, stacks[0], stacks[1], real_rows)


def mlp_backward_kernel(
    grad_ref, middle_ref, gains_ref, up_ref, down_ref, kern_ref, upper_ref, lower_ref, real_ref,
    hidden_ref, active_ref, slope_ref,
    out_ref, dup_ref, ddown_ref, dkern_ref, dgain_ref,
    low_ref, low_t_ref, normed_t_ref, mixed_ref, dhid_ref, moved_ref, back_ref,
):
    rows = grad_ref.shape[0]
    tiles = rows // 4
    block = hidden_ref.shape[1]

    @pl.when(pl.program_id(0) == 0)
    def _():
        for sub in range(4):
            span = slice(sub * tiles, (sub + 1) * tiles)
            low_ref[span, :] = grad_ref[span, :].astype(jnp.bfloat16)
        normed = norm_rows(middle_ref[...], gains_ref[0:1, :], gains_ref[1:2, :])[2]
        normed_t_ref[...] = normed.T.astype(jnp.bfloat16)
        low_t_ref[...] = grad_ref[...].T.astype(jnp.bfloat16)
        back_ref[...] = jnp.zeros_like(back_ref)

    for sub in range(4):
        span = slice(sub * tiles, (sub + 1) * tiles)
        part = back_product(low_ref[span, :], down_ref[...]).astype(jnp.bfloat16).astype(jnp.float32)
        mixed_ref[span, :] = (part * slope_ref[span, :].astype(jnp.float32)).astype(jnp.bfloat16)
    ddown_ref[...] = product(low_t_ref[...], active_ref[...]).T.astype(jnp.bfloat16)
    move_planes(mixed_ref, upper_ref, lower_ref, moved_ref)

    for lane in range(0, block, LANES):
        lanes = slice(lane, lane + LANES)
        kern = [kern_ref[tap : tap + 1, lanes] for tap in range(9)]

        def step(at, sums):
            row = pl.multiple_of(at * ROWS, ROWS)
            found = chunk_sources(mixed_ref, moved_ref, row, lanes)
            real = real_ref[pl.ds(row, ROWS), :] > 0.0
            sums = list(sums)
            for sub in range(4):
                span = pl.ds(pl.multiple_of(sub * tiles + row, ROWS), ROWS)
                hidden = hidden_ref[span, lanes].astype(jnp.float32)
                center = found[sub, 0, 0] * kern[4]
                total = center
                for tap in range(9):
                    term = found[TAPS_OF[sub][tap]]
                    if tap != 4:
                        total = total + term * kern[8 - tap]
                    piece = hidden * term
                    sums[tap] = sums[tap] + piece[:8] + piece[8:]
                dhid_ref[span, lanes] = jnp.where(real, total, center).astype(jnp.bfloat16)
            return tuple(sums)

        sums = lax.fori_loop(0, tiles // ROWS, step, (jnp.zeros((8, LANES), jnp.float32),) * 9)
        for tap in range(9):
            dkern_ref[8 - tap : 9 - tap, lanes] = jnp.sum(sums[tap], 0, keepdims=True)

    dup_ref[...] = product(normed_t_ref[...], dhid_ref[...]).astype(jnp.bfloat16)
    for sub in range(4):
        span = slice(sub * tiles, (sub + 1) * tiles)
        back_ref[span, :] += back_product(dhid_ref[span, :], up_ref[...])

    @pl.when(pl.program_id(0) == pl.num_programs(0) - 1)
    def _():
        def step(at, sums):
            span = pl.ds(pl.multiple_of(at * 64, 64), 64)
            grad = back_ref[span, :]
            unit, inverse, _ = norm_rows(middle_ref[span, :], gains_ref[0:1, :], gains_ref[1:2, :])
            out_ref[span, :] = grad_ref[span, :] + norm_rows_back(unit, inverse, gains_ref[0:1, :], grad)
            return (
                sums[0] + jnp.sum(grad * unit, 0, keepdims=True),
                sums[1] + jnp.sum(grad, 0, keepdims=True),
            )

        zero = jnp.zeros((1, C), jnp.float32)
        sums = lax.fori_loop(0, rows // 64, step, (zero, zero))
        dgain_ref[0:1, :] = sums[0]
        dgain_ref[1:2, :] = sums[1]


def mlp_backward(grad, middle, gains, w_up, w_down, kernel, stacks, real_rows, kept, ties):
    rows = middle.shape[0]
    block = 256
    by_lane = pl.BlockSpec((rows, block), lambda j: (0, j))
    up_spec = pl.BlockSpec((C, block), lambda j: (0, j))
    down_spec = pl.BlockSpec((block, C), lambda j: (j, 0))
    tap_spec = pl.BlockSpec((9, block), lambda j: (0, j))
    return pl.pallas_call(
        untied(mlp_backward_kernel, 12, len(ties)),
        grid=(FF // block,),
        out_shape=(
            jax.ShapeDtypeStruct((rows, C), jnp.float32),
            jax.ShapeDtypeStruct((C, FF), jnp.bfloat16),
            jax.ShapeDtypeStruct((FF, C), jnp.bfloat16),
            jax.ShapeDtypeStruct((9, FF), jnp.float32),
            jax.ShapeDtypeStruct((2, C), jnp.float32),
        ),
        in_specs=[
            whole((rows, C)),
            whole((rows, C)),
            whole((2, C)),
            up_spec,
            down_spec,
            tap_spec,
            whole(stacks[0].shape),
            whole(stacks[1].shape),
            whole(real_rows.shape),
            by_lane,
            by_lane,
            by_lane,
        ]
        + [pl.BlockSpec(memory_space=pl.ANY)] * len(ties),
        out_specs=(whole((rows, C)), up_spec, down_spec, tap_spec, whole((2, C))),
        scratch_shapes=[
            pltpu.VMEM((rows, C), jnp.bfloat16),
            pltpu.VMEM((C, rows), jnp.bfloat16),
            pltpu.VMEM((C, rows), jnp.bfloat16),
            pltpu.VMEM((rows, block), jnp.bfloat16),
            pltpu.VMEM((rows, block), jnp.bfloat16),
            pltpu.VMEM((4, 3, rows // 4, block), jnp.float32),
            pltpu.VMEM((rows, C), jnp.float32),
        ],
        compiler_params=pltpu.CompilerParams(vmem_limit_bytes=VMEM_LIMIT),
        cost_estimate=pl.CostEstimate(flops=18 * 10**9, bytes_accessed=18 * 10**6, transcendentals=0),
        name="mlp_backward",
    )(grad, middle, gains, w_up, w_down, kernel, stacks[0], stacks[1], real_rows, *kept, *ties)


WIDE = 384
BLOCK_TILES = 32
KEY_SPAN = 128


def block_places(tiles):
    places = []
    for index in range(-(-tiles // BLOCK_TILES)):
        start = min(index * BLOCK_TILES, tiles - BLOCK_TILES)
        places.append((start, min(max(start - 48, 0), tiles - KEY_SPAN)))
    return places


def block_bias(image_of):
    parts = []
    for start, low in block_places(image_of.shape[0]):
        same = image_of[low : low + KEY_SPAN, None] == jnp.tile(image_of[start : start + BLOCK_TILES], 4)[None, :]
        parts.append(jnp.where(same, 0.0, NEG_FILL))
    return jnp.stack(parts)


def place_of(index, tiles):
    start = jnp.minimum(index * BLOCK_TILES, tiles - BLOCK_TILES)
    low = jnp.clip(start - 48, 0, tiles - KEY_SPAN)
    return (pl.multiple_of(start, ROWS), pl.multiple_of(low, ROWS))


def four_planes(ref, start, lanes):
    tiles = ref.shape[0] // 4
    return jnp.concatenate(
        [ref[pl.ds(pl.multiple_of(sub * tiles + start, ROWS), BLOCK_TILES), lanes] for sub in range(4)], 0
    )


def put_planes(ref, start, lanes, values):
    tiles = ref.shape[0] // 4
    for sub in range(4):
        ref[pl.ds(pl.multiple_of(sub * tiles + start, ROWS), BLOCK_TILES), lanes] = values[
            sub * BLOCK_TILES : (sub + 1) * BLOCK_TILES
        ]


def head_pair(values, group):
    if group == 2:
        return values
    first = lax.broadcasted_iota(jnp.int32, values.shape, 1) < HD
    zero = jnp.zeros_like(values)
    return jnp.concatenate([jnp.where(first, values, zero), jnp.where(first, zero, values)], 0)


def softmax_columns(raw, bias):
    parts = []
    for half in range(raw.shape[0] // KEY_SPAN):
        scores = raw[half * KEY_SPAN : (half + 1) * KEY_SPAN] * HD ** (-0.5) + bias
        weights = jnp.exp(scores - jnp.max(scores, 0, keepdims=True))
        parts.append(weights * (1.0 / jnp.sum(weights, 0, keepdims=True)))
    return parts


def norm_store(source_ref, gains_ref, at, target_ref):
    @pl.loop(0, source_ref.shape[0] // 64)
    def _(step):
        span = pl.ds(pl.multiple_of(step * 64, 64), 64)
        normed = norm_rows(source_ref[span, :], gains_ref[at : at + 1, :], gains_ref[at + 1 : at + 2, :])[2]
        target_ref[span, :] = normed.astype(jnp.bfloat16)


def attention_forward_kernel(
    resid_ref, gains_ref, wq_ref, wo_ref, wk_ref, wv_ref, wr_ref, bias_ref,
    middle_ref, normed_ref, query_ref, reduced_ref, key_ref, value_ref, attended_ref,
):
    rows = resid_ref.shape[0]
    tiles = rows // 4
    norm_store(resid_ref, gains_ref, 0, normed_ref)
    query_ref[:, C:] = jnp.zeros((rows, WIDE - C), jnp.bfloat16)
    reduced = jnp.zeros((tiles, C), jnp.float32)
    for sub in range(4):
        span = slice(sub * tiles, (sub + 1) * tiles)
        query_ref[span, :C] = product(normed_ref[span, :], wq_ref[...]).astype(jnp.bfloat16)
        reduced = reduced + product(normed_ref[span, :], wr_ref[sub * C : (sub + 1) * C, :])
    reduced_ref[...] = reduced
    normed_kv = norm_rows(reduced, gains_ref[2:3, :], gains_ref[3:4, :])[2].astype(jnp.bfloat16)
    for ref, weight in ((key_ref, wk_ref), (value_ref, wv_ref)):
        ref[:, C:] = jnp.zeros((tiles, WIDE - C), jnp.bfloat16)
        ref[:, :C] = product(normed_kv, weight[...]).astype(jnp.bfloat16)

    @pl.loop(0, bias_ref.shape[0])
    def _(index):
        start, low = place_of(index, tiles)
        bias = bias_ref[index]
        for group in range(3):
            lanes = slice(group * LANES, (group + 1) * LANES)
            query = four_planes(query_ref, start, lanes)
            keys = head_pair(key_ref[pl.ds(low, KEY_SPAN), lanes], group)
            values = head_pair(value_ref[pl.ds(low, KEY_SPAN), lanes], group)
            probs = softmax_columns(back_product(keys, query), bias)
            probs = jnp.concatenate(probs, 0).T.astype(jnp.bfloat16)
            put_planes(attended_ref, start, lanes, product(probs, values).astype(jnp.bfloat16))

    for sub in range(4):
        span = slice(sub * tiles, (sub + 1) * tiles)
        middle_ref[span, :] = resid_ref[span, :] + product(attended_ref[span, :C], wo_ref[...])


def in_vmem(count):
    return [pl.BlockSpec(memory_space=pltpu.VMEM)] * count


def attention_forward(resid, gains, wq, wo, wk, wv, wr, bias):
    rows = resid.shape[0]
    tiles = rows // 4
    low = jnp.bfloat16
    shapes = (
        jax.ShapeDtypeStruct((rows, C), jnp.float32),
        jax.ShapeDtypeStruct((rows, C), low),
        jax.ShapeDtypeStruct((rows, WIDE), low),
        jax.ShapeDtypeStruct((tiles, C), jnp.float32),
        jax.ShapeDtypeStruct((tiles, WIDE), low),
        jax.ShapeDtypeStruct((tiles, WIDE), low),
        jax.ShapeDtypeStruct((rows, WIDE), low),
    )
    return pl.pallas_call(
        attention_forward_kernel,
        out_shape=shapes,
        in_specs=in_vmem(8),
        out_specs=tuple(in_vmem(7)),
        compiler_params=pltpu.CompilerParams(vmem_limit_bytes=VMEM_LIMIT),
        cost_estimate=pl.CostEstimate(flops=6 * 10**9, bytes_accessed=14 * 10**6, transcendentals=10**6),
        name="attention_forward",
    )(resid, gains, wq, wo, wk, wv, wr, bias)


def attention_backward_kernel(
    grad_ref, resid_ref, gains_ref, wq_ref, wo_ref, wk_ref, wv_ref, wr_ref, bias_ref,
    normed_ref, query_ref, reduced_ref, key_ref, value_ref, attended_ref,
    out_ref, dqo_ref, dkv_ref, dwr_ref, dgain_ref,
    turned_ref, datt_ref, dquery_ref, dkey_ref, dvalue_ref, first_ref,
):
    rows = resid_ref.shape[0]
    tiles = rows // 4
    low_type = jnp.bfloat16
    datt_ref[:, C:] = jnp.zeros((rows, WIDE - C), low_type)
    turned_ref[...] = grad_ref[...].T.astype(low_type)
    dqo_ref[C:, :] = product(turned_ref[...], attended_ref[:, :C]).T.astype(low_type)
    for sub in range(4):
        span = slice(sub * tiles, (sub + 1) * tiles)
        datt_ref[span, :C] = back_product(grad_ref[span, :].astype(low_type), wo_ref[...]).astype(low_type)
    dkey_ref[...] = jnp.zeros_like(dkey_ref)
    dvalue_ref[...] = jnp.zeros_like(dvalue_ref)
    blocks = bias_ref.shape[0]

    @pl.loop(0, blocks)
    def _(step):
        index = blocks - 1 - step
        start, low = place_of(index, tiles)
        bias = bias_ref[index]
        tile_at = lax.rem(lax.broadcasted_iota(jnp.int32, (4 * BLOCK_TILES, LANES), 0), BLOCK_TILES)
        fresh = tile_at >= index * BLOCK_TILES - start
        span = pl.ds(low, KEY_SPAN)
        for group in range(3):
            lanes = slice(group * LANES, (group + 1) * LANES)
            query = four_planes(query_ref, start, lanes)
            datt = four_planes(datt_ref, start, lanes)
            datt = jnp.where(fresh, datt, jnp.zeros_like(datt))
            keys = head_pair(key_ref[span, lanes], group)
            values = head_pair(value_ref[span, lanes], group)
            probs = softmax_columns(back_product(keys, query), bias)
            dprobs = back_product(values, datt)
            dscores = []
            for half, prob in enumerate(probs):
                dprob = dprobs[half * KEY_SPAN : (half + 1) * KEY_SPAN]
                inner = jnp.sum(prob * dprob, 0, keepdims=True)
                dscores.append(prob * (dprob - inner) * HD ** (-0.5))
            dscores = jnp.concatenate(dscores, 0)
            probs = jnp.concatenate(probs, 0).astype(low_type)
            dquery = product(dscores.T.astype(low_type), keys)
            put_planes(dquery_ref, start, lanes, dquery.astype(low_type))
            dkeys = product(dscores.astype(low_type), query)
            dvalues = product(probs, datt)
            if group < 2:
                first = lax.broadcasted_iota(jnp.int32, (KEY_SPAN, LANES), 1) < HD
                dkeys = jnp.where(first, dkeys[:KEY_SPAN], dkeys[KEY_SPAN:])
                dvalues = jnp.where(first, dvalues[:KEY_SPAN], dvalues[KEY_SPAN:])
            dkey_ref[span, lanes] += dkeys
            dvalue_ref[span, lanes] += dvalues

    unit, inverse, normed = norm_rows(reduced_ref[...], gains_ref[2:3, :], gains_ref[3:4, :])
    normed_t = normed.T.astype(low_type)
    dkeys = dkey_ref[:, :C].astype(low_type)
    dvalues = dvalue_ref[:, :C].astype(low_type)
    dkv_ref[:C, :] = product(normed_t, dkeys).astype(low_type)
    dkv_ref[C:, :] = product(normed_t, dvalues).astype(low_type)
    dnormed = back_product(dkeys, wk_ref[...]) + back_product(dvalues, wv_ref[...])
    dgain_ref[2:3, :] = jnp.sum(dnormed * unit, 0, keepdims=True)
    dgain_ref[3:4, :] = jnp.sum(dnormed, 0, keepdims=True)
    dreduced = norm_rows_back(unit, inverse, gains_ref[2:3, :], dnormed).astype(low_type)
    turned_ref[...] = normed_ref[...].T
    dqo_ref[:C, :] = product(turned_ref[...], dquery_ref[:, :C]).astype(low_type)
    for sub in range(4):
        span = slice(sub * tiles, (sub + 1) * tiles)
        part = slice(sub * C, (sub + 1) * C)
        dwr_ref[part, :] = outer_sum(normed_ref[span, :], dreduced).astype(low_type)
        first_ref[span, :] = back_product(dquery_ref[span, :C], wq_ref[...]) + back_product(dreduced, wr_ref[part, :])

    def step(at, sums):
        span = pl.ds(pl.multiple_of(at * 64, 64), 64)
        grad = first_ref[span, :]
        unit, inverse, _ = norm_rows(resid_ref[span, :], gains_ref[0:1, :], gains_ref[1:2, :])
        out_ref[span, :] = grad_ref[span, :] + norm_rows_back(unit, inverse, gains_ref[0:1, :], grad)
        return (sums[0] + jnp.sum(grad * unit, 0, keepdims=True), sums[1] + jnp.sum(grad, 0, keepdims=True))

    zero = jnp.zeros((1, C), jnp.float32)
    sums = lax.fori_loop(0, rows // 64, step, (zero, zero))
    dgain_ref[0:1, :] = sums[0]
    dgain_ref[1:2, :] = sums[1]


def attention_backward(grad, resid, gains, wq, wo, wk, wv, wr, bias, kept, ties):
    rows = resid.shape[0]
    tiles = rows // 4
    low = jnp.bfloat16
    shapes = (
        jax.ShapeDtypeStruct((rows, C), jnp.float32),
        jax.ShapeDtypeStruct((2 * C, C), low),
        jax.ShapeDtypeStruct((2 * C, C), low),
        jax.ShapeDtypeStruct((4 * C, C), low),
        jax.ShapeDtypeStruct((4, C), jnp.float32),
    )
    return pl.pallas_call(
        untied(attention_backward_kernel, 15, len(ties)),
        out_shape=shapes,
        in_specs=in_vmem(15) + [pl.BlockSpec(memory_space=pl.ANY)] * len(ties),
        out_specs=tuple(in_vmem(5)),
        scratch_shapes=[
            pltpu.VMEM((C, rows), low),
            pltpu.VMEM((rows, WIDE), low),
            pltpu.VMEM((rows, WIDE), low),
            pltpu.VMEM((tiles, WIDE), jnp.float32),
            pltpu.VMEM((tiles, WIDE), jnp.float32),
            pltpu.VMEM((rows, C), jnp.float32),
        ],
        compiler_params=pltpu.CompilerParams(vmem_limit_bytes=VMEM_LIMIT),
        cost_estimate=pl.CostEstimate(flops=12 * 10**9, bytes_accessed=18 * 10**6, transcendentals=10**6),
        name="attention_backward",
    )(grad, resid, gains, wq, wo, wk, wv, wr, bias, *kept, *ties)


BOTH = ("grp", "tok")


def axis_bits(axis):
    count = lax.axis_size(axis)
    return [1 << place for place in reversed(range(count.bit_length() - 1))]


def swap(values, axis, bit):
    count = lax.axis_size(axis)
    return lax.ppermute(values, axis, [(i, i ^ bit) for i in range(count)])


def my_bit(axis, bit):
    return lax.axis_index(axis) // bit % 2


def bit_order():
    tok_bits = axis_bits("tok")
    return [("grp", bit) for bit in axis_bits("grp")] + [("tok", bit) for bit in tok_bits]


def sum_all(values):
    for axis, bit in reversed(bit_order()):
        values = values + swap(values, axis, bit)
    return values


def scatter_order():
    bits = bit_order()
    return [bits[-1]] + bits[:-1][::-1][len(axis_bits("tok")) - 1 :] + bits[:-1][::-1][: len(axis_bits("tok")) - 1]


class Chain:
    def __init__(self, units):
        bits = bit_order()
        self.left = list(bits)
        self.order = scatter_order()
        self.values = units.reshape((units.shape[0],) + (2,) * len(bits) + (units.shape[1] >> len(bits), C))
        self.back = None

    def begin(self):
        axis, bit = self.order.pop(0)
        dim = 1 + self.left.index((axis, bit))
        self.left.remove((axis, bit))
        mine = my_bit(axis, bit)
        self.away = lax.dynamic_index_in_dim(self.values, 1 - mine, dim, keepdims=False)
        self.stay = lax.dynamic_index_in_dim(self.values, mine, dim, keepdims=False)
        self.back = swap(self.away, axis, bit)

    def end(self):
        self.values = (self.stay.astype(jnp.float32) + self.back.astype(jnp.float32)).astype(jnp.bfloat16)
        self.back = None


class SumChain:
    def __init__(self, values):
        self.order = list(reversed(bit_order()))
        self.values = values
        self.back = None

    def begin(self):
        axis, bit = self.order.pop(0)
        self.away = self.values
        self.back = swap(self.away, axis, bit)

    def end(self):
        self.values = self.values + self.back
        self.back = None


class Beside:
    def __init__(self):
        self.chains = []

    def step(self):
        ties = []
        for chain in self.chains:
            if chain.back is not None:
                ties.append(chain.back)
                chain.end()
        for chain in self.chains:
            if chain.order:
                chain.begin()
                ties.append(chain.away)
        return ties

    def finish(self):
        while any(chain.order or chain.back is not None for chain in self.chains):
            self.step()


def gather_unit(piece):
    bits = bit_order()
    held = []
    values = piece[None]
    for axis, bit in reversed(scatter_order()):
        other = swap(values, axis, bit)
        mine = my_bit(axis, bit) == 0
        pair = jnp.stack([jnp.where(mine, values, other), jnp.where(mine, other, values)])
        held.insert(0, (axis, bit))
        values = pair
    values = values.reshape((2,) * len(bits) + piece.shape)
    order = [held.index(name) for name in bits] + [len(bits), len(bits) + 1]
    return values.transpose(order).reshape(-1, piece.shape[1])


def body(
    patches,
    labels,
    valid_mask,
    crop_counts,
    owners,
    slot_weight,
    slot_moment,
    slot_second,
    norm_params,
    norm_moment,
    norm_second,
    head_weight,
    head_moment,
    head_second,
):
    tok_dev = patches.shape[0]
    n_tok = lax.axis_size("tok")
    n_grp = lax.axis_size("grp")
    tok_index = lax.axis_index("tok")
    group_tok = tok_dev * n_tok
    counts = crop_counts[0]
    n_unit = owners.shape[0]
    slot_rows, columns = slot_weight.shape
    unit_order = jnp.arange(n_unit, dtype=jnp.int32)
    same_owner = owners[:, None] == owners[None, :]
    rank_of = jnp.sum(same_owner & (unit_order[None, :] < unit_order[:, None]), 1)
    slot_of = owners * slot_rows + rank_of
    chunk = columns // n_tok // C
    pieces = slot_weight.astype(jnp.bfloat16).reshape(slot_rows, n_tok, chunk, C)
    pieces = lax.all_to_all(pieces, "tok", split_axis=1, concat_axis=0, tiled=True)
    unit_part = jnp.take(pieces.reshape(slot_rows * n_tok, chunk, C), slot_of, axis=0)
    first_unit = gather_unit(unit_part[0])
    embedding = first_unit[:PIN]
    kernels = first_unit[PIN : PIN + BLOCKS * 9 * FF // C].reshape(BLOCKS, 9, FF).astype(jnp.float32)
    layers = []
    for layer_at in range(BLOCKS):
        own = lax.all_gather(unit_part[1 + 4 * layer_at : 5 + 4 * layer_at], BOTH, axis=1, tiled=True)
        keyval = own[0, 2 * C :].reshape(C, 2, C)
        layers.append(
            (
                (own[0, :C], own[0, C : 2 * C], keyval[:, 0], keyval[:, 1], own[1]),
                (own[2].reshape(C, FF), own[3], kernels[layer_at]),
            )
        )

    towards = [(i + 1, i) for i in range(n_tok - 1)]
    window = tok_dev + OVER
    tiles = window // 4
    patches = jnp.concatenate([patches, lax.ppermute(patches[:OVER], "tok", towards)], 0)
    marks = jnp.stack([labels, valid_mask])
    marks = jnp.concatenate([marks, lax.ppermute(marks[:, :OVER], "tok", towards)], 1)
    patches = patches.reshape(tiles, 4, PIN).transpose(1, 0, 2).reshape(window, PIN)
    marks = marks.reshape(2, tiles, 4).transpose(0, 2, 1).reshape(2, window)
    labels = marks[0]
    first_tok = tok_index * tok_dev
    positions = first_tok + 4 * jnp.arange(tiles, dtype=jnp.int32)
    begin_at, half_side, tile_y, tile_x, _ = image_layout(positions, counts)
    own_image = (begin_at >= first_tok) & (begin_at < first_tok + tok_dev) & (positions < group_tok)
    is_real = positions < counts[0] * BIG_SIDE**2 + counts[1] * SMALL_SIDE**2
    shifts = shift_matrices(begin_at, half_side, tile_y, tile_x, is_real)
    image_of = jnp.where(positions < group_tok, begin_at, -1)
    bias = block_bias(image_of)
    stacks = shift_stacks(shifts)
    real_rows = jnp.broadcast_to(is_real.astype(jnp.float32)[:, None], (tiles, LANES))
    keep_mask = marks[1].astype(jnp.float32) * jnp.tile((own_image & is_real).astype(jnp.float32), 4)
    pixel_total = sum_all(jnp.sum(keep_mask)[None])[0]
    tail = 6 * BLOCKS
    embed_pre = product(patches, embedding)
    resid = layer_norm(embed_pre, norm_params[tail], norm_params[tail + 1])
    kept_all = []
    for layer_at in range(BLOCKS):
        attn_part, mlp_part = layers[layer_at]
        at = 6 * layer_at
        middle, *attn_kept = attention_forward(resid, norm_params[at : at + 4], *attn_part, bias)
        output, *mlp_kept = mlp_forward(middle, norm_params[at + 4 : at + 6], *mlp_part, stacks, real_rows)
        kept_all.append((resid, attn_kept, middle, mlp_kept))
        resid = output
    final = layer_norm(resid, norm_params[tail + 2], norm_params[tail + 3]).astype(jnp.bfloat16)
    head_low = head_weight.astype(jnp.bfloat16)
    logits = product(final, head_low)
    row_peak = jnp.max(logits, -1, keepdims=True)
    log_norm = row_peak[:, 0] + jnp.log(jnp.sum(jnp.exp(logits - row_peak), -1))
    onehot = (labels[:, None] == jnp.arange(head_weight.shape[1], dtype=jnp.int32)[None, :]).astype(
        jnp.float32
    )
    picked = jnp.sum(logits * onehot, 1)
    loss_local = jnp.sum((log_norm - picked) * keep_mask)
    probs = jnp.exp(logits - log_norm[:, None])
    d_logits = ((probs - onehot) * (keep_mask / pixel_total)[:, None]).astype(jnp.bfloat16)
    d_head = outer_sum(final, d_logits)
    grad_res, gain_final, shift_final = norm_back(
        resid, norm_params[tail + 2], norm_params[tail + 3], back_product(d_logits, head_low)
    )
    beside = Beside()
    head_chain = SumChain(d_head)
    beside.chains.append(head_chain)
    unit_chains = [None] * BLOCKS
    kernel_grads = [None] * BLOCKS
    gain_grads = [None] * BLOCKS
    for layer_at in reversed(range(BLOCKS)):
        attn_part, mlp_part = layers[layer_at]
        at = 6 * layer_at
        entry, attn_kept, middle, mlp_kept = kept_all[layer_at]
        grad_res, d_up, d_down, kernel_grads[layer_at], mlp_gains = mlp_backward(
            grad_res, middle, norm_params[at + 4 : at + 6], *mlp_part, stacks, real_rows, mlp_kept, beside.step()
        )
        mlp_chain = Chain(jnp.stack([d_up.reshape(-1, C), d_down]))
        beside.chains.append(mlp_chain)
        grad_res, d_qo, d_kv, d_reduce, attn_gains = attention_backward(
            grad_res, entry, norm_params[at : at + 4], *attn_part, bias, attn_kept, beside.step()
        )
        d_kv = jnp.stack([d_kv[:C], d_kv[C:]], 1).reshape(2 * C, C)
        attn_units = jnp.stack([jnp.concatenate([d_qo, d_kv], 0), d_reduce])
        gain_grads[layer_at] = jnp.concatenate([attn_gains, mlp_gains], 0)
        if layer_at:
            attn_chain = Chain(attn_units)
            beside.chains.append(attn_chain)
            unit_chains[layer_at] = (attn_chain, mlp_chain)
    d_embed_pre, gain_embed, shift_embed = norm_back(
        embed_pre, norm_params[tail], norm_params[tail + 1], grad_res
    )
    d_embedding = outer_sum(patches, d_embed_pre.astype(jnp.bfloat16))
    first_grad = jnp.concatenate(
        [
            d_embedding.astype(jnp.bfloat16),
            jnp.stack(kernel_grads).reshape(-1, C).astype(jnp.bfloat16),
            jnp.zeros((C * FF // C - PIN - BLOCKS * 9 * FF // C, C), jnp.bfloat16),
        ]
    )
    last_chain = Chain(jnp.concatenate([first_grad[None], attn_units], 0))
    norm_grads = jnp.concatenate(
        gain_grads + [jnp.stack([gain_embed, shift_embed, gain_final, shift_final])], 0
    )
    small_chain = SumChain(jnp.concatenate([norm_grads, jnp.full((1, C), loss_local)], 0))
    beside.chains += [last_chain, small_chain]
    beside.finish()
    parts = [last_chain.values, mlp_chain.values]
    for attn_chain, mlp_chain in unit_chains[1:]:
        parts += [attn_chain.values, mlp_chain.values]
    stacked = jnp.concatenate(parts, 0)
    row_ids = jnp.arange(slot_rows * n_tok, dtype=jnp.int32)
    matches = slot_of[None, :] == row_ids[:, None]
    unit_at = jnp.where(jnp.any(matches, 1), jnp.argmax(matches, 1), n_unit)
    padded = jnp.concatenate([stacked, jnp.zeros_like(stacked[:1])], 0)
    placed = jnp.take(padded, unit_at, axis=0)[:, None]
    owned = lax.all_to_all(placed, "tok", split_axis=0, concat_axis=1, tiled=True)
    owned = owned.astype(jnp.float32).reshape(slot_rows, columns)
    head_total = head_chain.values
    norm_total, loss_sum = (small_chain.values[:-1], small_chain.values[-1, 0])
    slot_m, slot_v, slot_w = adamw_step(
        slot_weight, slot_moment, slot_second, owned, RATE_MATRIX, DECAY_RATE
    )
    norm_m, norm_v, norm_w = adamw_step(
        norm_params, norm_moment, norm_second, norm_total, RATE_VECTOR, 0.0
    )
    head_m, head_v, head_w = adamw_step(
        head_weight, head_moment, head_second, head_total, RATE_MATRIX, DECAY_RATE
    )
    return (
        loss_sum,
        pixel_total,
        slot_m,
        slot_v,
        slot_w,
        norm_m,
        norm_v,
        norm_w,
        head_m,
        head_v,
        head_w,
    )


def solution(mesh):
    in_specs = (
        P(("grp", "tok"), None),
        P(("grp", "tok")),
        P(("grp", "tok")),
        P("grp", None),
        P(),
        P("tok", "grp"),
        P("tok", "grp"),
        P("tok", "grp"),
        P(),
        P(),
        P(),
        P(),
        P(),
        P(),
    )
    out_specs = (
        P(),
        P(),
        P("tok", "grp"),
        P("tok", "grp"),
        P("tok", "grp"),
        P(),
        P(),
        P(),
        P(),
        P(),
        P(),
    )
    return jax.shard_map(body, mesh=mesh, in_specs=in_specs, out_specs=out_specs, check_vma=False)
```

time: 870 us -> 817 us (0.939)
  matrix products: 336 us -> 5.9 us
  Pallas kernels: 0 us -> 303 us
  other arithmetic: 166 us -> 67.5 us
  waiting for transfers between devices: 137 us -> 206 us
  starting transfers between devices: 65.6 us -> 84.5 us
  local copies, waits for them, and re-layouts: 126 us -> 117 us
    pallas_call x0 -> x12, Pallas kernels: none -> 303 us  [the longest x3 96.4 us: mlp_backward(): pl.pallas_call(untied(mlp_backward_kernel, 12, len(ties)), grid=(FF // bl...]
    dot_general x92 -> x2, matrix products: 122 us -> 1.86 us  [product(): return jnp.dot(left, right, preferred_element_type=jnp.float32)]
    dot_general x15 -> x0, matrix products: 107 us -> none  [the longest x3 39 us: attend_backward(): jnp.einsum('hqk,khd->qhd', grad_scores, split_heads(keyval[:, :C]), prefe...]
    all_gather x3, waiting for transfers between devices: 8.16 us -> 100 us  [body(): lax.all_gather(unit_part[1 + 4 * layer_at:5 + 4 * layer_at], BOTH, axis=1...]
    convert_element_type x29 -> x32, other arithmetic: 89.7 us -> 12.4 us  [the longest x24 11.3 us: end(): (self.stay.astype(jnp.float32) + self.back.astype(jnp.float32)).astype(jn...]
    dot_general x19 -> x1, matrix products: 50.8 us -> 0.58 us  [back_product(): lax.dot_general(gradient, weight, (((1,), (1,)), ((), ())), preferred_ele...]
    dot_general x20 -> x2, matrix products: 35.2 us -> 3.46 us  [outer_sum(): lax.dot_general(left, right, (((0,), (0,)), ((), ())), preferred_element_...]
    squeeze x18 -> x43, local copies, waits for them, and re-layouts: 2.38 us -> 32.6 us  [the longest x31 12.1 us: begin(): lax.dynamic_index_in_dim(self.values, 1 - mine, dim, keepdims=False)]
  transfers between devices with their start and end apart: 47 -> 57, of which waited for: 27 -> 28; matrix products, arithmetic and copies ran while one was open for 27% -> 18% of each run, Pallas kernels for 0% -> 22%
where the time goes in v3:
time: 817 us; the launch traced here: 806 us
  Pallas kernels  303 us (37%)
  waiting for transfers between devices  206 us (25%)
  local copies, waits for them, and re-layouts  117 us (14%)
  starting transfers between devices  84.5 us (10%)
  other arithmetic  67.5 us (8%)
  between operations  22.6 us (3%)
    all_gather x3, waiting for transfers between devices, body(): lax.all_gather(unit_part[1 + 4 * layer_at:5 + 4 * layer_at], BOTH, axis=1...  100 us
    pallas_call x3, Pallas kernels, mlp_backward(): pl.pallas_call(untied(mlp_backward_kernel, 12, len(ties)), grid=(FF // bl...  96.4 us
    ppermute x50, waiting for transfers between devices, swap(): return lax.ppermute(values, axis, [(i, i ^ bit) for i in range(count)])  96.3 us
    pallas_call x3, Pallas kernels, attention_backward(): pl.pallas_call(untied(attention_backward_kernel, 15, len(ties)), out_shap...  79.8 us
    pallas_call x3, Pallas kernels, mlp_forward(): pl.pallas_call(mlp_forward_kernel, grid=(FF // block,), out_shape=(jax.Sh...  73.6 us
    ppermute x50, starting transfers between devices, swap(): return lax.ppermute(values, axis, [(i, i ^ bit) for i in range(count)])  60.3 us
    pallas_call x3, Pallas kernels, attention_forward(): pl.pallas_call(attention_forward_kernel, out_shape=shapes, in_specs=in_vm...  53.4 us
    unnamed x198, local copies, waits for them, and re-layouts  19.8 us
  transfers between devices with their start and end apart: 57, of which 28 were waited for; matrix products, arithmetic and copies ran while one was open for 18% of the time, Pallas kernels for 22%

profile of v3, /device:TPU:1, one launch (start us, length us, event | category | flops | bytes accessed | tf_op | source)
XLA Modules:
  0.0 806.5 jit_solution(18008021916394765987)
XLA Ops:
  8.3 2.1 collective-permute-start
  13.2 7.3 all-to-all-start
  20.6 2.0 collective-permute-start.6
  24.8 9.5 %all-to-all-done = bf16[2,8,40,320]{3,2,0,1:T(8,128)(2,1)S(1)} async-done(((bf16[2,8,40,320]{3,2,0,1:T(8,128)(2,1)}), bf16[2,8,40,320]{3,2,0,1:T(8,128)(2,1)S(1)}, u32[]{:S(2)}, u32[]{:S(2)}) %all-to-all-start) | async-done | bytes 409632 | tf_op jit(solution)/shard_map/all_to_all | solution.py:782
  52.7 3.4 collective-permute-done.1
  56.9 2.4 collective-permute-done.2
  60.9 3.8 collective-permute-done.3
  67.8 2.6 collective-permute-start.7
  75.8 2.3 collective-permute-start.9
  83.2 2.0 collective-permute-start.11
  87.7 4.6 collective-permute-start.5
  92.3 2.1 pad_maximum_fusion.1
  94.4 2.9 reshape.945
  97.3 2.1 copy.313
  112.7 3.4 slice_bitcast_fusion.4
  117.8 44.0 %all-gather.6.cloned.1.call-done = bf16[4,1280,320]{2,1,0:T(8,128)(2,1)} async-done(((bf16[4,40,320]{2,1,0:T(8,128)(2,1)}), bf16[4,1280,320]{2,1,0:T(8,128)(2,1)}) %all-gather.6.cloned.1.call-update) | async-done | bytes 3276816 | tf_op jit(solution)/shard_map/all_gather | solution.py:789
  163.1 3.4 slice_bitcast_fusion.2
  169.7 56.0 %all-gather.8.cloned.1.call-done = bf16[4,1280,320]{2,1,0:T(8,128)(2,1)} async-done(((bf16[4,40,320]{2,1,0:T(8,128)(2,1)}), bf16[4,1280,320]{2,1,0:T(8,128)(2,1)}) %all-gather.8.cloned.1.call-update) | async-done | bytes 3276816 | tf_op jit(solution)/shard_map/all_gather | solution.py:789
  228.4 3.3 slice_bitcast_fusion
  236.2 1.9 slice_bitcast_fusion.10
  238.1 17.9 %attention_forward.3 = (f32[1216,320]{1,0:T(8,128)}, bf16[1216,320]{1,0:T(8,128)(2,1)}, bf16[1216,384]{1,0:T(8,128)(2,1)}, f32[304,320]{1,0:T(8,128)}, bf16[304,...) custom-call(f32[1216,320]{1,0:T(8,128)} %multiply_add_fusion.resid_ref.refs_1_, ...), custom_call_target="tpu_custom_call" | custom-call | flops 6000000000 | bytes 14000000 | tf_op jit(solution)/shard_map/attention_forward/pallas_call | solution.py:519
  256.7 24.4 %mlp_forward.3 = (f32[1216,320]{1,0:T(8,128)}, bf16[1216,1280]{1,0:T(8,128)(2,1)}, bf16[1216,1280]{1,0:T(8,128)(2,1)}, bf16[1216,1280]{1,0:T(8,128)(2,1)}) custom-call(f32[1216,320]{1,0:T(8,128)} %get-tuple-element.75.middle_ref.refs_1_, f32[2,320]{1,0:T(2,128)} %get-tuple-element.284.gains_ref.refs_2_, bf16[320,1280]{1,0:T(8,128)(2,1)} %reshape_squeeze.19.up_ref.refs_3_, ...), custom_call_target="tpu_custom_call" | custom-call | flops 14000000000 | bytes 18000000 | tf_op jit(solution)/shard_map/mlp_forward/pallas_call | solution.py:248
  283.0 17.8 %attention_forward.4 = (f32[1216,320]{1,0:T(8,128)}, bf16[1216,320]{1,0:T(8,128)(2,1)}, bf16[1216,384]{1,0:T(8,128)(2,1)}, f32[304,320]{1,0:T(8,128)}, bf16[304,...) custom-call(f32[1216,320]{1,0:T(8,128)} %get-tuple-element.76.resid_ref.refs_1_, ...), custom_call_target="tpu_custom_call" | custom-call | flops 6000000000 | bytes 14000000 | tf_op jit(solution)/shard_map/attention_forward/pallas_call | solution.py:519
  300.8 24.5 %mlp_forward.4 = (f32[1216,320]{1,0:T(8,128)}, bf16[1216,1280]{1,0:T(8,128)(2,1)}, bf16[1216,1280]{1,0:T(8,128)(2,1)}, bf16[1216,1280]{1,0:T(8,128)(2,1)}) custom-call(f32[1216,320]{1,0:T(8,128)} %get-tuple-element.77.middle_ref.refs_1_, f32[2,320]{1,0:T(2,128)} %get-tuple-element.283.gains_ref.refs_2_, bf16[320,1280]{1,0:T(8,128)(2,1)} %reshape_squeeze.21.up_ref.refs_3_, ...), custom_call_target="tpu_custom_call" | custom-call | flops 14000000000 | bytes 18000000 | tf_op jit(solution)/shard_map/mlp_forward/pallas_call | solution.py:248
  325.3 1.9 slice_bitcast_fusion.6
  327.2 17.8 %attention_forward.5 = (f32[1216,320]{1,0:T(8,128)}, bf16[1216,320]{1,0:T(8,128)(2,1)}, bf16[1216,384]{1,0:T(8,128)(2,1)}, f32[304,320]{1,0:T(8,128)}, bf16[304,...) custom-call(f32[1216,320]{1,0:T(8,128)} %get-tuple-element.78.resid_ref.refs_1_, ...), custom_call_target="tpu_custom_call" | custom-call | flops 6000000000 | bytes 14000000 | tf_op jit(solution)/shard_map/attention_forward/pallas_call | solution.py:519
  345.0 24.7 %mlp_forward.5 = (f32[1216,320]{1,0:T(8,128)}, bf16[1216,1280]{1,0:T(8,128)(2,1)}, bf16[1216,1280]{1,0:T(8,128)(2,1)}, bf16[1216,1280]{1,0:T(8,128)(2,1)}) custom-call(f32[1216,320]{1,0:T(8,128)} %get-tuple-element.79.middle_ref.refs_1_, f32[2,320]{1,0:T(2,128)} %get-tuple-element.282.gains_ref.refs_2_, bf16[320,1280]{1,0:T(8,128)(2,1)} %reshape_squeeze.23.up_ref.refs_3_, ...), custom_call_target="tpu_custom_call" | custom-call | flops 14000000000 | bytes 18000000 | tf_op jit(solution)/shard_map/mlp_forward/pallas_call | solution.py:248
  378.1 2.3 multiply_reduce_fusion.1
  383.2 32.1 %mlp_backward.3 = (f32[1216,320]{1,0:T(8,128)}, bf16[320,1280]{1,0:T(8,128)(2,1)}, bf16[1280,320]{1,0:T(8,128)(2,1)}, f32[9,1280]{1,0:T(8,128)}, f32[2,320]{1,0:T(2,128)}) custom-call(f32[1216,320]{1,0:T(8,128)} %broadcast_add_fusion.refs_0_, f32[1216,320]{1,0:T(8,128)} %get-tuple-element.79.middle_ref.refs_1_, ...), custom_call_target="tpu_custom_call" | custom-call | flops 17999998976 | bytes 18000000 | tf_op jit(solution)/shard_map/mlp_backward/pallas_call | solution.py:357
  415.3 2.3 stack.257
  421.5 26.8 %attention_backward.3 = (f32[1216,320]{1,0:T(8,128)}, bf16[640,320]{1,0:T(8,128)(2,1)}, bf16[640,320]{1,0:T(8,128)(2,1)}, bf16[1280,320]{1,0:T(8,128)(2,1)}, f32[4,320]{1,0:T(4,128)}) custom-call(f32[1216,320]{1,0:T(8,128)} %get-tuple-element.84.refs_0_, f32[1216,320]{1,0:T(8,128)} %get-tuple-element.78.resid_ref.refs_1_, ...), custom_call_target="tpu_custom_call" | custom-call | flops 12000000000 | bytes 18000000 | tf_op jit(solution)/shard_map/attention_backward/pallas_call | solution.py:626
  452.9 13.9 %collective-permute-done.15.refs_15_ = f32[320,150]{1,0:T(8,128)} collective-permute-done((f32[320,150]{1,0:T(8,128)S(1)}, f32[320,150]{1,0:T(8,128)}, u32[]{:S(2)}, u32[]{:S(2)}) %collective-permute-start.15) | collective-permute-done | bytes 192032 | tf_op jit(solution)/shard_map/ppermute | solution.py:655
  473.9 2.5 collective-permute-done.18.refs_12_
  482.8 32.1 %mlp_backward.4 = (f32[1216,320]{1,0:T(8,128)}, bf16[320,1280]{1,0:T(8,128)(2,1)}, bf16[1280,320]{1,0:T(8,128)(2,1)}, f32[9,1280]{1,0:T(8,128)}, f32[2,320]{1,0:T(2,128)}) custom-call(f32[1216,320]{1,0:T(8,128)} %get-tuple-element.93.refs_0_, f32[1216,320]{1,0:T(8,128)} %get-tuple-element.77.middle_ref.refs_1_, ...), custom_call_target="tpu_custom_call" | custom-call | flops 17999998976 | bytes 18000000 | tf_op jit(solution)/shard_map/mlp_backward/pallas_call | solution.py:357
  514.9 2.4 stack.266
  519.9 2.3 collective-permute-start.21
  531.5 26.4 %attention_backward.4 = (f32[1216,320]{1,0:T(8,128)}, bf16[640,320]{1,0:T(8,128)(2,1)}, bf16[640,320]{1,0:T(8,128)(2,1)}, bf16[1280,320]{1,0:T(8,128)(2,1)}, f32[4,320]{1,0:T(4,128)}) custom-call(f32[1216,320]{1,0:T(8,128)} %get-tuple-element.100.refs_0_, f32[1216,320]{1,0:T(8,128)} %get-tuple-element.76.resid_ref.refs_1_, ...), custom_call_target="tpu_custom_call" | custom-call | flops 12000000000 | bytes 18000000 | tf_op jit(solution)/shard_map/attention_backward/pallas_call | solution.py:626
  581.2 32.2 %mlp_backward.5 = (f32[1216,320]{1,0:T(8,128)}, bf16[320,1280]{1,0:T(8,128)(2,1)}, bf16[1280,320]{1,0:T(8,128)(2,1)}, f32[9,1280]{1,0:T(8,128)}, f32[2,320]{1,0:T(2,128)}) custom-call(f32[1216,320]{1,0:T(8,128)} %get-tuple-element.109.refs_0_, f32[1216,320]{1,0:T(8,128)} %get-tuple-element.75.middle_ref.refs_1_, ...), custom_call_target="tpu_custom_call" | custom-call | flops 17999998976 | bytes 18000000 | tf_op jit(solution)/shard_map/mlp_backward/pallas_call | solution.py:357
  614.3 2.2 stack.275
  619.0 2.2 fusion.10.refs_24_
  621.3 2.6 collective-permute-start.37
  629.9 2.0 copy.376.refs_18_
  634.1 26.5 %attention_backward.5 = (f32[1216,320]{1,0:T(8,128)}, bf16[640,320]{1,0:T(8,128)(2,1)}, bf16[640,320]{1,0:T(8,128)(2,1)}, bf16[1280,320]{1,0:T(8,128)(2,1)}, f32[4,320]{1,0:T(4,128)}) custom-call(f32[1216,320]{1,0:T(8,128)} %get-tuple-element.116.refs_0_, f32[1216,320]{1,0:T(8,128)} %multiply_add_fusion.resid_ref.refs_1_, ...), custom_call_target="tpu_custom_call" | custom-call | flops 12000000000 | bytes 18000000 | tf_op jit(solution)/shard_map/attention_backward/pallas_call | solution.py:626
  660.7 2.3 multiply_reduce_fusion
  664.9 2.4 fusion.111
  667.4 2.3 convolution_convert_fusion
  670.5 2.0 concatenate.44
  674.1 1.9 pad_maximum_fusion
  677.4 3.4 collective-permute-done.47
  680.8 2.0 collective-permute-start.32
  687.5 4.8 collective-permute-done.43
  695.0 2.4 collective-permute-done.44
  698.1 5.9 collective-permute-done.38
  705.7 14.1 %collective-permute-done.33 = bf16[3,2,2,2,40,320]{5,4,3,2,1,0:T(8,128)(2,1)S(1)} collective-permute-done((bf16[3,2,2,2,40,320]{5,4,3,2,1,0:T(8,128)(2,1)S(1)}, bf16[3,2,2,2,40,320]{5,4,3,2,1,0:T(8,128)(2,1)S(1)}, u32[]{:S(2)}, u32[]{:S(2)}) %collective-permute-start.33) | collective-permute-done | bytes 614432 | tf_op jit(solution)/shard_map/ppermute | solution.py:655
  720.9 4.3 collective-permute-done.39
  726.2 6.1 collective-permute-done.34
  733.3 2.7 collective-permute-done.40
  737.0 5.0 collective-permute-done.35
  743.7 3.6 collective-permute-done.36
  748.9 3.0 collective-permute-done.41
  755.8 12.7 %all-to-all-start.1 = ((bf16[16,1,40,320]{3,2,1,0:T(8,128)(2,1)}), bf16[16,1,40,320]{3,2,1,0:T(8,128)(2,1)S(1)}, u32[]{:S(2)}, u32[]{:S(2)}) async-start(bf16[16,1,40,320]{3,2,1,0:T(8,128)(2,1)} %fusion.35), calls=%async_computation.1 | async-start | bytes 983040 | tf_op jit(solution)/shard_map/all_to_all | solution.py:898
  772.1 5.5 collective-permute-done.28
  777.7 3.8 collective-permute-start.29
  793.5 4.8 multiply_subtract_fusion
  (542 shorter events, 187.7 us)
Async XLA Ops:
  8.3 84.0 %collective-permute-start = (bf16[192,1152]{1,0:T(8,128)(2,1)S(1)}, bf16[192,1152]{1,0:T(8,128)(2,1)}, u32[]{:S(2)}, u32[]{:S(2)}) collective-permute-start(bf16[192,1152]{1,0:T(8,128)(2,1)S(1)} %slice.298), channel_id=1, source_target_pairs={{1,0},{2,1},{3,2},{4,3},{5,4},{6,5},{7,6},{9,8},{10,9},{11,10},{12... | collective-permute-start | bytes 1327112 | tf_op jit(solution)/shard_map/ppermute | solution.py:801
  13.2 21.1 %all-to-all-start = ((bf16[2,8,40,320]{3,2,0,1:T(8,128)(2,1)}), bf16[2,8,40,320]{3,2,0,1:T(8,128)(2,1)S(1)}, u32[]{:S(2)}, u32[]{:S(2)}) async-start(bf16[2,8,40,320]{3,2,0,1:T(8,128)(2,1)} %copy.314), calls=%async_computation | async-start | bytes 983040 | tf_op jit(solution)/shard_map/all_to_all | solution.py:782
  20.5 90.8 %all-gather.4.cloned.1.call-start = ((), (), s32[]{:S(2)}) async-start(), calls=%async_computation.2 | async-start | bytes 4055040 | tf_op jit(solution)/shard_map/all_gather | solution.py:789
  20.6 40.1 %collective-permute-start.6 = (s32[2,192]{1,0:T(2,128)S(1)}, s32[2,192]{1,0:T(2,128)S(1)}, u32[]{:S(2)}, u32[]{:S(2)}) collective-permute-start(s32[2,192]{1,0:T(2,128)S(1)} %pad_add_fusion.1), channel_id=1, source_target_pairs={{1,0},{2,1},{3,2},{4,3},{5,4},{6,5},{7,6},{9,8},{10,9},{11,10},{12... | collective-permute-start | bytes 4616 | tf_op jit(solution)/shard_map/ppermute | solution.py:803
  35.9 126.0 %all-gather.6.cloned.1.call-start = ((), (), s32[]{:S(2)}) async-start(), calls=%async_computation.3 | async-start | bytes 4055040 | tf_op jit(solution)/shard_map/all_gather | solution.py:789
  46.3 179.3 %all-gather.8.cloned.1.call-start = ((), (), s32[]{:S(2)}) async-start(), calls=%async_computation.4 | async-start | bytes 4055040 | tf_op jit(solution)/shard_map/all_gather | solution.py:789
  51.9 4.2 collective-permute-start.1
  52.7 56.4 %copy-start.65 = (f32[320]{0:T(512)}, f32[320]{0:T(512)S(1)}, u32[]{:S(2)}) copy-start(f32[320]{0:T(512)S(1)} %get-tuple-element.203) | copy-start | bytes 3844
  56.2 3.1 collective-permute-start.2
  59.4 5.3 collective-permute-start.3
  64.8 21.9 %collective-permute-start.4 = (bf16[2,2,2,1,40,320]{5,4,2,1,0,3:T(8,128)(2,1)S(1)}, bf16[2,2,2,1,40,320]{5,4,2,1,0,3:T(8,128)(2,1)S(1)}, u32[]{:S(2)}, u32[]{:S(2)}) collective-permute-start(bf16[2,2,2,1,40,320]{5,4,2,1,0,3:T(8,128)(2,1)S(1)} %fusion.70), channel_id=1, source_target_pairs={{0,8},{8,0},{16,24},{24,16},{1,9},{9,1},{17,25},{25,17},{2,10},{10... | collective-permute-start | bytes 614408 | tf_op jit(solution)/shard_map/ppermute | solution.py:655
  67.8 3.7 collective-permute-start.7
  72.8 2.4 collective-permute-start.8
  75.8 3.3 collective-permute-start.9
  79.7 2.9 collective-permute-start.10
  83.2 2.9 collective-permute-start.11
  87.7 11.7 %collective-permute-start.5 = (bf16[2,2,2,2,1,40,320]{6,5,3,2,1,0,4:T(8,128)(2,1)}, bf16[2,2,2,2,1,40,320]{6,5,3,2,1,0,4:T(8,128)(2,1)}, u32[]{:S(2)}, u32[]{:S(2)}) collective-permute-start(bf16[2,2,2,2,1,40,320]{6,5,3,2,1,0,4:T(8,128)(2,1)} %fusion.62), channel_id=1, source_target_pairs={{0,1},{1,0},{2,3},{3,2},{4,5},{5,4},{6,7},{7,6},{8,9},{9,8},{10,11... | collective-permute-start | bytes 1228808 | tf_op jit(solution)/shard_map/ppermute | solution.py:655
  381.5 37.9 %collective-permute-start.12 = (f32[320,150]{1,0:T(8,128)S(1)}, f32[320,150]{1,0:T(8,128)}, u32[]{:S(2)}, u32[]{:S(2)}) collective-permute-start(f32[320,150]{1,0:T(8,128)S(1)} %copy-done.48), channel_id=1, source_target_pairs={{0,1},{1,0},{2,3},{3,2},{4,5},{5,4},{6,7},{7,6},{8,9},{9,8},{10,11... | collective-permute-start | bytes 576008 | tf_op jit(solution)/shard_map/ppermute | solution.py:655
  419.1 59.3 %collective-permute-start.14 = (bf16[2,2,2,2,2,40,320]{6,5,0,3,4,1,2:T(8,128)(2,1)}, bf16[2,2,2,2,2,40,320]{6,5,0,3,4,1,2:T(8,128)(2,1)S(1)}, u32[]{:S(2)}, u32[]{:S(2)}) collective-permute-start(bf16[2,2,2,2,2,40,320]{6,5,0,3,4,1,2:T(8,128)(2,1)} %bitcast.423), channel_id=1, source_target_pairs={{0,1},{1,0},{2,3},{3,2},{4,5},{5,4},{6,7},{7,6},{8,9},{9,8},{10,11... | collective-permute-start | bytes 2457608 | tf_op jit(solution)/shard_map/ppermute | solution.py:655
  420.4 27.9 %collective-permute-start.13 = (f32[320,150]{1,0:T(8,128)S(1)}, f32[320,150]{1,0:T(8,128)S(1)}, u32[]{:S(2)}, u32[]{:S(2)}) collective-permute-start(f32[320,150]{1,0:T(8,128)S(1)} %add.687.refs_16_), channel_id=1, source_target_pairs={{0,2},{1,3},{2,0},{3,1},{4,6},{5,7},{6,4},{7,5},{8,10},{9,11},{10,... | collective-permute-start | bytes 576008 | tf_op jit(solution)/shard_map/ppermute | solution.py:655
  449.5 17.4 %collective-permute-start.15 = (f32[320,150]{1,0:T(8,128)S(1)}, f32[320,150]{1,0:T(8,128)}, u32[]{:S(2)}, u32[]{:S(2)}) collective-permute-start(f32[320,150]{1,0:T(8,128)S(1)} %add.689.refs_14_), channel_id=1, source_target_pairs={{0,4},{1,5},{2,6},{3,7},{4,0},{5,1},{6,2},{7,3},{8,12},{9,13},{10,... | collective-permute-start | bytes 576008 | tf_op jit(solution)/shard_map/ppermute | solution.py:655
  467.9 8.4 %collective-permute-start.18 = (f32[320,150]{1,0:T(8,128)S(1)}, f32[320,150]{1,0:T(8,128)S(1)}, u32[]{:S(2)}, u32[]{:S(2)}) collective-permute-start(f32[320,150]{1,0:T(8,128)S(1)} %add.693.refs_18_), channel_id=1, source_target_pairs={{0,8},{8,0},{16,24},{24,16},{1,9},{9,1},{17,25},{25,17},{2,10},{10... | collective-permute-start | bytes 576008 | tf_op jit(solution)/shard_map/ppermute | solution.py:655
  472.7 49.5 %collective-permute-start.17 = (bf16[2,2,2,2,2,40,320]{6,5,3,0,4,1,2:T(8,128)(2,1)}, bf16[2,2,2,2,2,40,320]{6,5,3,0,4,1,2:T(8,128)(2,1)S(1)}, u32[]{:S(2)}, u32[]{:S(2)}) collective-permute-start(bf16[2,2,2,2,2,40,320]{6,5,3,0,4,1,2:T(8,128)(2,1)} %bitcast.422), channel_id=1, source_target_pairs={{0,1},{1,0},{2,3},{3,2},{4,5},{5,4},{6,7},{7,6},{8,9},{9,8},{10,11... | collective-permute-start | bytes 2457608 | tf_op jit(solution)/shard_map/ppermute | solution.py:655
  477.2 156.6 %collective-permute-start.22 = (f32[320,150]{1,0:T(8,128)}, f32[320,150]{1,0:T(8,128)}, u32[]{:S(2)}, u32[]{:S(2)}) collective-permute-start(f32[320,150]{1,0:T(8,128)} %add.698.refs_16_), channel_id=1, source_target_pairs={{0,16},{8,24},{16,0},{24,8},{1,17},{9,25},{17,1},{25,9},{2,18},{10... | collective-permute-start | bytes 576008 | tf_op jit(solution)/shard_map/ppermute | solution.py:655
  481.4 44.3 %collective-permute-start.16 = (bf16[2,2,2,2,40,320]{5,4,0,2,3,1:T(8,128)(2,1)}, bf16[2,2,2,2,40,320]{5,4,0,2,3,1:T(8,128)(2,1)}, u32[]{:S(2)}, u32[]{:S(2)}) collective-permute-start(bf16[2,2,2,2,40,320]{5,4,0,2,3,1:T(8,128)(2,1)} %dynamic-slice_bitcast_fusion.6), channel_id=1, source_target_pairs={{0,8},{8,0},{16,24},{24,16},{1,9},{9,1},{17,25},{25,17},{2,10},{10... | collective-permute-start | bytes 1228808 | tf_op jit(solution)/shard_map/ppermute | solution.py:655
  519.9 58.4 %collective-permute-start.21 = (bf16[2,2,2,2,2,40,320]{6,5,4,3,0,1,2:T(8,128)(2,1)}, bf16[2,2,2,2,2,40,320]{6,5,4,3,0,1,2:T(8,128)(2,1)S(1)}, u32[]{:S(2)}, u32[]{:S(2)}) collective-permute-start(bf16[2,2,2,2,2,40,320]{6,5,4,3,0,1,2:T(8,128)(2,1)} %bitcast.421), channel_id=1, source_target_pairs={{0,1},{1,0},{2,3},{3,2},{4,5},{5,4},{6,7},{7,6},{8,9},{9,8},{10,11... | collective-permute-start | bytes 2457608 | tf_op jit(solution)/shard_map/ppermute | solution.py:655
  523.5 41.8 %collective-permute-start.20 = (bf16[2,2,2,2,40,320]{5,4,2,0,3,1:T(8,128)(2,1)S(1)}, bf16[2,2,2,2,40,320]{5,4,2,0,3,1:T(8,128)(2,1)}, u32[]{:S(2)}, u32[]{:S(2)}) collective-permute-start(bf16[2,2,2,2,40,320]{5,4,2,0,3,1:T(8,128)(2,1)S(1)} %dynamic-slice_bitcast_fusion.5), channel_id=1, source_target_pairs={{0,8},{8,0},{16,24},{24,16},{1,9},{9,1},{17,25},{25,17},{2,10},{10... | collective-permute-start | bytes 1228808 | tf_op jit(solution)/shard_map/ppermute | solution.py:655
  526.9 31.0 %copy-start.26 = (bf16[2,2,2,2,40,320]{5,4,0,2,3,1:T(8,128)(2,1)}, bf16[2,2,2,2,40,320]{5,4,0,2,3,1:T(8,128)(2,1)S(1)}, u32[]{:S(2)}) copy-start(bf16[2,2,2,2,40,320]{5,4,0,2,3,1:T(8,128)(2,1)S(1)} %fusion.23) | copy-start | bytes 1228804
  529.4 37.1 %collective-permute-start.19 = (bf16[2,2,2,40,320]{4,3,0,1,2:T(8,128)(2,1)}, bf16[2,2,2,40,320]{4,3,0,1,2:T(8,128)(2,1)}, u32[]{:S(2)}, u32[]{:S(2)}) collective-permute-start(bf16[2,2,2,40,320]{4,3,0,1,2:T(8,128)(2,1)} %dynamic-slice_bitcast_fusion.12), channel_id=1, source_target_pairs={{0,16},{8,24},{16,0},{24,8},{1,17},{9,25},{17,1},{25,9},{2,18},{10... | collective-permute-start | bytes 614408 | tf_op jit(solution)/shard_map/ppermute | solution.py:655
  563.9 61.0 %collective-permute-start.26 = (bf16[2,2,2,2,2,40,320]{6,5,4,3,1,0,2:T(8,128)(2,1)}, bf16[2,2,2,2,2,40,320]{6,5,4,3,1,0,2:T(8,128)(2,1)S(1)}, u32[]{:S(2)}, u32[]{:S(2)}) collective-permute-start(bf16[2,2,2,2,2,40,320]{6,5,4,3,1,0,2:T(8,128)(2,1)} %bitcast.420), channel_id=1, source_target_pairs={{0,1},{1,0},{2,3},{3,2},{4,5},{5,4},{6,7},{7,6},{8,9},{9,8},{10,11... | collective-permute-start | bytes 2457608 | tf_op jit(solution)/shard_map/ppermute | solution.py:655
  567.5 6.2 collective-permute-start.23
  568.3 8.4 %collective-permute-start.24 = (bf16[2,2,2,40,320]{4,3,1,0,2:T(8,128)(2,1)S(1)}, bf16[2,2,2,40,320]{4,3,1,0,2:T(8,128)(2,1)S(1)}, u32[]{:S(2)}, u32[]{:S(2)}) collective-permute-start(bf16[2,2,2,40,320]{4,3,1,0,2:T(8,128)(2,1)S(1)} %dynamic-slice_bitcast_fusion.11), channel_id=1, source_target_pairs={{0,16},{8,24},{16,0},{24,8},{1,17},{9,25},{17,1},{25,9},{2,18},{10... | collective-permute-start | bytes 614408 | tf_op jit(solution)/shard_map/ppermute | solution.py:655
  574.4 178.6 %collective-permute-start.51 = (bf16[2,40,320]{2,1,0:T(8,128)(2,1)}, bf16[2,40,320]{2,1,0:T(8,128)(2,1)}, u32[]{:S(2)}, u32[]{:S(2)}) collective-permute-start(bf16[2,40,320]{2,1,0:T(8,128)(2,1)} %dynamic-slice_bitcast_fusion.24.refs_20_), channel_id=1, source_target_pairs={{0,4},{1,5},{2,6},{3,7},{4,0},{5,1},{6,2},{7,3},{8,12},{9,13},{10,... | collective-permute-start | bytes 153608 | tf_op jit(solution)/shard_map/ppermute | solution.py:655
  577.6 43.7 %collective-permute-start.49 = (bf16[2,2,40,320]{3,2,1,0:T(8,128)(2,1)}, bf16[2,2,40,320]{3,2,1,0:T(8,128)(2,1)}, u32[]{:S(2)}, u32[]{:S(2)}) collective-permute-start(bf16[2,2,40,320]{3,2,1,0:T(8,128)(2,1)} %dynamic-slice_bitcast_fusion.17.refs_21_), channel_id=1, source_target_pairs={{0,2},{1,3},{2,0},{3,1},{4,6},{5,7},{6,4},{7,5},{8,10},{9,11},{10,... | collective-permute-start | bytes 307208 | tf_op jit(solution)/shard_map/ppermute | solution.py:655
  579.6 47.9 %collective-permute-start.25 = (bf16[2,2,2,2,40,320]{5,4,3,2,0,1:T(8,128)(2,1)S(1)}, bf16[2,2,2,2,40,320]{5,4,3,2,0,1:T(8,128)(2,1)}, u32[]{:S(2)}, u32[]{:S(2)}) collective-permute-start(bf16[2,2,2,2,40,320]{5,4,3,2,0,1:T(8,128)(2,1)S(1)} %dynamic-slice_bitcast_fusion.4), channel_id=1, source_target_pairs={{0,8},{8,0},{16,24},{24,16},{1,9},{9,1},{17,25},{25,17},{2,10},{10... | collective-permute-start | bytes 1228808 | tf_op jit(solution)/shard_map/ppermute | solution.py:655
  621.3 63.8 %collective-permute-start.37 = (bf16[2,2,2,2,2,40,320]{6,5,4,3,2,1,0:T(8,128)(2,1)}, bf16[2,2,2,2,2,40,320]{6,5,4,3,2,1,0:T(8,128)(2,1)}, u32[]{:S(2)}, u32[]{:S(2)}) collective-permute-start(bf16[2,2,2,2,2,40,320]{6,5,4,3,2,1,0:T(8,128)(2,1)} %fusion.10.refs_24_), channel_id=1, source_target_pairs={{0,1},{1,0},{2,3},{3,2},{4,5},{5,4},{6,7},{7,6},{8,9},{9,8},{10,11... | collective-permute-start | bytes 2457608 | tf_op jit(solution)/shard_map/ppermute | solution.py:655
  624.9 127.2 %collective-permute-start.50 = (bf16[2,40,320]{2,1,0:T(8,128)(2,1)S(1)}, bf16[2,40,320]{2,1,0:T(8,128)(2,1)}, u32[]{:S(2)}, u32[]{:S(2)}) collective-permute-start(bf16[2,40,320]{2,1,0:T(8,128)(2,1)S(1)} %dynamic-slice_bitcast_fusion.20), channel_id=1, source_target_pairs={{0,4},{1,5},{2,6},{3,7},{4,0},{5,1},{6,2},{7,3},{8,12},{9,13},{10,... | collective-permute-start | bytes 153608 | tf_op jit(solution)/shard_map/ppermute | solution.py:655
  627.6 55.3 %collective-permute-start.42 = (bf16[2,2,2,2,40,320]{5,4,3,2,1,0:T(8,128)(2,1)}, bf16[2,2,2,2,40,320]{5,4,3,2,1,0:T(8,128)(2,1)}, u32[]{:S(2)}, u32[]{:S(2)}) collective-permute-start(bf16[2,2,2,2,40,320]{5,4,3,2,1,0:T(8,128)(2,1)} %dynamic-slice_bitcast_fusion.3.refs_23_), channel_id=1, source_target_pairs={{0,8},{8,0},{16,24},{24,16},{1,9},{9,1},{17,25},{25,17},{2,10},{10... | collective-permute-start | bytes 1228808 | tf_op jit(solution)/shard_map/ppermute | solution.py:655
  633.8 42.2 %collective-permute-start.46 = (bf16[2,2,2,40,320]{4,3,2,1,0:T(8,128)(2,1)}, bf16[2,2,2,40,320]{4,3,2,1,0:T(8,128)(2,1)}, u32[]{:S(2)}, u32[]{:S(2)}) collective-permute-start(bf16[2,2,2,40,320]{4,3,2,1,0:T(8,128)(2,1)} %dynamic-slice_bitcast_fusion.10.refs_22_), channel_id=1, source_target_pairs={{0,16},{8,24},{16,0},{24,8},{1,17},{9,25},{17,1},{25,9},{2,18},{10... | collective-permute-start | bytes 614408 | tf_op jit(solution)/shard_map/ppermute | solution.py:655
  634.1 26.6 %copy-start.66 = (f32[320]{0:T(512)S(1)}, f32[320]{0:T(512)}, u32[]{:S(2)}) copy-start(f32[320]{0:T(512)} %copy-done.65) | copy-start | bytes 3844
  677.0 3.8 collective-permute-start.47
  680.8 12.5 %collective-permute-start.32 = (bf16[3,2,2,2,2,40,320]{6,5,4,3,2,1,0:T(8,128)(2,1)S(1)}, bf16[3,2,2,2,2,40,320]{6,5,4,3,2,1,0:T(8,128)(2,1)S(1)}, u32[]{:S(2)}, u32[]{:S(2)}) collective-permute-start(bf16[3,2,2,2,2,40,320]{6,5,4,3,2,1,0:T(8,128)(2,1)S(1)} %dynamic-slice_bitcast_fusion), channel_id=1, source_target_pairs={{0,1},{1,0},{2,3},{3,2},{4,5},{5,4},{6,7},{7,6},{8,9},{9,8},{10,11... | collective-permute-start | bytes 3686408 | tf_op jit(solution)/shard_map/ppermute | solution.py:655
  682.9 69.1 %collective-permute-start.48 = (bf16[2,40,320]{2,1,0:T(8,128)(2,1)S(1)}, bf16[2,40,320]{2,1,0:T(8,128)(2,1)S(1)}, u32[]{:S(2)}, u32[]{:S(2)}) collective-permute-start(bf16[2,40,320]{2,1,0:T(8,128)(2,1)S(1)} %dynamic-slice_bitcast_fusion.21), channel_id=1, source_target_pairs={{0,4},{1,5},{2,6},{3,7},{4,0},{5,1},{6,2},{7,3},{8,12},{9,13},{10,... | collective-permute-start | bytes 153608 | tf_op jit(solution)/shard_map/ppermute | solution.py:655
  685.1 7.3 collective-permute-start.43
  692.4 11.6 %collective-permute-start.38 = (bf16[2,2,2,2,40,320]{5,4,3,2,1,0:T(8,128)(2,1)S(1)}, bf16[2,2,2,2,40,320]{5,4,3,2,1,0:T(8,128)(2,1)S(1)}, u32[]{:S(2)}, u32[]{:S(2)}) collective-permute-start(bf16[2,2,2,2,40,320]{5,4,3,2,1,0:T(8,128)(2,1)S(1)} %dynamic-slice_bitcast_fusion.2), channel_id=1, source_target_pairs={{0,8},{8,0},{16,24},{24,16},{1,9},{9,1},{17,25},{25,17},{2,10},{10... | collective-permute-start | bytes 1228808 | tf_op jit(solution)/shard_map/ppermute | solution.py:655
  693.3 4.1 collective-permute-start.44
  697.4 22.4 %collective-permute-start.33 = (bf16[3,2,2,2,40,320]{5,4,3,2,1,0:T(8,128)(2,1)S(1)}, bf16[3,2,2,2,40,320]{5,4,3,2,1,0:T(8,128)(2,1)S(1)}, u32[]{:S(2)}, u32[]{:S(2)}) collective-permute-start(bf16[3,2,2,2,40,320]{5,4,3,2,1,0:T(8,128)(2,1)S(1)} %dynamic-slice_bitcast_fusion.1), channel_id=1, source_target_pairs={{0,8},{8,0},{16,24},{24,16},{1,9},{9,1},{17,25},{25,17},{2,10},{10... | collective-permute-start | bytes 1843208 | tf_op jit(solution)/shard_map/ppermute | solution.py:655
  704.0 48.0 %collective-permute-start.45 = (bf16[2,40,320]{2,1,0:T(8,128)(2,1)S(1)}, bf16[2,40,320]{2,1,0:T(8,128)(2,1)S(1)}, u32[]{:S(2)}, u32[]{:S(2)}) collective-permute-start(bf16[2,40,320]{2,1,0:T(8,128)(2,1)S(1)} %dynamic-slice_bitcast_fusion.22), channel_id=1, source_target_pairs={{0,4},{1,5},{2,6},{3,7},{4,0},{5,1},{6,2},{7,3},{8,12},{9,13},{10,... | collective-permute-start | bytes 153608 | tf_op jit(solution)/shard_map/ppermute | solution.py:655
  719.8 5.4 collective-permute-start.39
  725.2 7.1 collective-permute-start.34
  726.2 26.8 %copy-start.42 = (bf16[2,2,40,320]{3,2,0,1:T(8,128)(2,1)S(1)}, bf16[2,2,40,320]{3,2,0,1:T(8,128)(2,1)}, u32[]{:S(2)}) copy-start(bf16[2,2,40,320]{3,2,0,1:T(8,128)(2,1)} %copy-done.41) | copy-start | bytes 307204
  732.4 3.7 collective-permute-start.40
  736.1 5.9 collective-permute-start.35
  742.1 5.2 collective-permute-start.36
  747.3 4.6 collective-permute-start.41
  752.1 31.9 %copy-start.23 = (f32[320,150]{0,1:T(8,128)S(1)}, f32[320,150]{0,1:T(8,128)}, u32[]{:S(2)}) copy-start(f32[320,150]{0,1:T(8,128)} %param.25) | copy-start | bytes 576004
  753.9 30.2 %copy-start.51 = (f32[320,150]{0,1:T(8,128)S(1)}, f32[320,150]{0,1:T(8,128)}, u32[]{:S(2)}) copy-start(f32[320,150]{0,1:T(8,128)} %param.27) | copy-start | bytes 576004
  754.9 29.5 %copy-start.52 = (f32[320,150]{0,1:T(8,128)S(1)}, f32[320,150]{0,1:T(8,128)}, u32[]{:S(2)}) copy-start(f32[320,150]{0,1:T(8,128)} %param.26) | copy-start | bytes 576004
  755.8 36.2 %all-to-all-start.1 = ((bf16[16,1,40,320]{3,2,1,0:T(8,128)(2,1)}), bf16[16,1,40,320]{3,2,1,0:T(8,128)(2,1)S(1)}, u32[]{:S(2)}, u32[]{:S(2)}) async-start(bf16[16,1,40,320]{3,2,1,0:T(8,128)(2,1)} %fusion.35), calls=%async_computation.1 | async-start | bytes 983040 | tf_op jit(solution)/shard_map/all_to_all | solution.py:898
  769.5 1.3 collective-permute-start.27
  770.7 6.9 collective-permute-start.28
  777.7 5.2 collective-permute-start.29
  782.9 2.8 collective-permute-start.30
  785.7 5.1 collective-permute-start.31
  (76 other events, 551.6 us)
Sparse Core Ops, SparseCore 0:
  36.0 61.9 all-gather.3
  101.5 60.2 all-gather.5
  165.4 60.2 all-gather.7

commit v4 on v3

v4 whole, which is shorter than its diff:
```python
import functools

import jax
import jax.numpy as jnp
import numpy as np
from jax import lax
from jax.experimental import pallas as pl
from jax.experimental.pallas import tpu as pltpu
from jax.sharding import PartitionSpec as P

C = 320
HEADS = 5
HD = 64
FF = 1280
PIN = 1152
BLOCKS = 3
BIG_SIDE = 14
SMALL_SIDE = 6
STEP = 10
KVH = 49


EPS_NORM = 1e-06
BETA_ONE = 0.9
BETA_TWO = 0.999
ADAM_EPS = 1e-08
RATE_MATRIX = 0.05
RATE_VECTOR = 0.3
DECAY_RATE = 0.05
NEG_FILL = -1e30
PREC_HIGH = lax.Precision.HIGHEST


def layer_norm(values, gain_vec, shift_vec):
    center = values - jnp.mean(values, -1, keepdims=True)
    inverse = lax.rsqrt(jnp.mean(center * center, -1, keepdims=True) + EPS_NORM)
    return center * inverse * gain_vec + shift_vec


def adamw_step(weight, moment, second, gradient, rate_now, decay_now):
    moment = BETA_ONE * moment + (1.0 - BETA_ONE) * gradient
    second = BETA_TWO * second + (1.0 - BETA_TWO) * gradient * gradient
    m_hat = moment / (1.0 - BETA_ONE**STEP)
    v_hat = second / (1.0 - BETA_TWO**STEP)
    weight = weight - rate_now * (m_hat / (jnp.sqrt(v_hat) + ADAM_EPS) + decay_now * weight)
    return (moment, second, weight)


def product(left, right):
    return jnp.dot(left, right, preferred_element_type=jnp.float32)


def outer_sum(left, right):
    return lax.dot_general(
        left, right, (((0,), (0,)), ((), ())), preferred_element_type=jnp.float32
    )


def back_product(gradient, weight):
    return lax.dot_general(
        gradient, weight, (((1,), (1,)), ((), ())), preferred_element_type=jnp.float32
    )


def norm_back(values, gain_vec, shift_vec, gradient):
    _, pull_back = jax.vjp(layer_norm, values, gain_vec, shift_vec)
    return pull_back(gradient)


OVER = 4 * KVH - 4


def image_layout(positions, counts):
    big_tok = BIG_SIDE * BIG_SIDE
    small_tok = SMALL_SIDE * SMALL_SIDE
    big_end = counts[0] * big_tok
    small_end = big_end + counts[1] * small_tok
    is_big = positions < big_end
    is_small = jnp.logical_and(positions >= big_end, positions < small_end)
    half_side = jnp.where(is_big, BIG_SIDE // 2, SMALL_SIDE // 2)
    begin_at = jnp.where(
        is_big,
        positions // big_tok * big_tok,
        jnp.where(is_small, big_end + (positions - big_end) // small_tok * small_tok, small_end),
    )
    tile_idx = (positions - begin_at) // 4
    return (begin_at, half_side, tile_idx // half_side, tile_idx % half_side, positions < small_end)


def shift_stacks(half_side, tile_y, tile_x, is_real):
    tiles = half_side.shape[0]
    step_y = np.array([[0, 1 - 2 * (sub // 2), 1 - 2 * (sub // 2)] for sub in range(4)], np.int32)[:, :, None]
    step_x = np.array([[1 - 2 * (sub % 2), 0, 1 - 2 * (sub % 2)] for sub in range(4)], np.int32)[:, :, None]
    at_y = tile_y + step_y
    at_x = tile_x + step_x
    inside = is_real & (at_y >= 0) & (at_y < half_side) & (at_x >= 0) & (at_x < half_side)
    source = jnp.arange(tiles, dtype=jnp.int32) + step_y * half_side + step_x
    source = jnp.where(inside, source, -1)
    cut = row_cut(tiles)
    columns = jnp.arange(SPAN, dtype=jnp.int32)
    upper = (source[:, :, :cut, None] == columns).astype(jnp.bfloat16)
    lower = (source[:, :, cut:, None] == columns + (tiles - SPAN)).astype(jnp.bfloat16)
    return (upper.reshape(4, 3 * cut, SPAN), lower.reshape(4, 3 * (tiles - cut), SPAN))


def tap_source(sub, tap):
    y_at = sub // 2 + tap // 3 - 1
    x_at = sub % 2 + tap % 3 - 1
    return (y_at % 2 * 2 + x_at % 2, y_at // 2, x_at // 2)


SQRT_HALF = 0.7071067811865476
INV_SQRT_TWO_PI = 0.3989422804014327
TAPS_OF = [[tap_source(sub, tap) for tap in range(9)] for sub in range(4)]
VMEM_LIMIT = 56 * 1024 * 1024
SPAN = 256
ROWS = 16
LANES = 128


def row_cut(tiles):
    return (tiles // 2 + 15) // 16 * 16


def move_planes(planes_ref, upper_ref, lower_ref, moved_ref):
    tiles = planes_ref.shape[0] // 4
    cut = row_cut(tiles)
    for sub in range(4):
        base = sub * tiles
        part = product(upper_ref[sub], planes_ref[base : base + SPAN, :])
        for key in range(3):
            moved_ref[sub, key, :cut, :] = part[key * cut : (key + 1) * cut]
        part = product(lower_ref[sub], planes_ref[base + tiles - SPAN : base + tiles, :])
        for key in range(3):
            moved_ref[sub, key, cut:, :] = part[key * (tiles - cut) : (key + 1) * (tiles - cut)]


def chunk_sources(planes_ref, moved_ref, row, lanes):
    tiles = planes_ref.shape[0] // 4
    found = {}
    for sub in range(4):
        found[sub, 0, 0] = planes_ref[pl.ds(pl.multiple_of(sub * tiles + row, ROWS), ROWS), lanes].astype(jnp.float32)
        step_y = 1 - 2 * (sub // 2)
        step_x = 1 - 2 * (sub % 2)
        for key, step in enumerate(((0, step_x), (step_y, 0), (step_y, step_x))):
            found[(sub,) + step] = moved_ref[sub, key, pl.ds(row, ROWS), lanes]
    return found


def norm_rows(values, gain, shift):
    center = values - jnp.mean(values, -1, keepdims=True)
    inverse = lax.rsqrt(jnp.mean(center * center, -1, keepdims=True) + EPS_NORM)
    unit = center * inverse
    return (unit, inverse, unit * gain + shift)


def norm_rows_back(unit, inverse, gain, grad):
    scaled = grad * gain
    return inverse * (
        scaled - jnp.mean(scaled, -1, keepdims=True) - unit * jnp.mean(scaled * unit, -1, keepdims=True)
    )


def mlp_forward_kernel(
    advance,
    middle_ref, gains_ref, up_ref, down_ref, kern_ref, upper_ref, lower_ref, real_ref,
    out_ref, hidden_ref, active_ref, slope_ref, turned_ref,
    normed_ref, moved_ref, planes_ref,
):
    rows = middle_ref.shape[0]
    block = hidden_ref.shape[1]
    tiles = rows // 4

    @pl.when(pl.program_id(0) == 0)
    def _():
        normed = norm_rows(middle_ref[...], gains_ref[0:1, :], gains_ref[1:2, :])[2]
        normed_ref[...] = normed.astype(jnp.bfloat16)
        out_ref[...] = middle_ref[...]
        spread_rows(up_ref[0], planes_ref)
        for quarter in range(FF // C):
            for at, lane, width in lane_parts(C):
                part = planes_ref[at, pl.ds(quarter, C, stride=FF // C), :][:, :width]
                begin = quarter * C + lane
                turned_ref[:, begin : begin + width] = part.astype(jnp.bfloat16)

    advance()
    for sub in range(4):
        columns = pl.ds(pl.multiple_of(pl.program_id(0) * block, block), block)
        part = product(normed_ref[sub * tiles : (sub + 1) * tiles, :], turned_ref[:, columns])
        hidden_ref[sub * tiles : (sub + 1) * tiles, :] = part.astype(jnp.bfloat16)
    move_planes(hidden_ref, upper_ref, lower_ref, moved_ref)

    for lane in range(0, hidden_ref.shape[1], LANES):
        lanes = slice(lane, lane + LANES)
        kern = [kern_ref[0, tap : tap + 1, lanes] for tap in range(9)]

        @pl.loop(0, tiles // ROWS, unroll=tiles // ROWS)
        def _(at):
            row = pl.multiple_of(at * ROWS, ROWS)
            found = chunk_sources(hidden_ref, moved_ref, row, lanes)
            real = real_ref[pl.ds(row, ROWS), :] > 0.0
            for sub in range(4):
                center = found[sub, 0, 0] * kern[4]
                total = center
                for tap in range(9):
                    if tap != 4:
                        total = total + found[TAPS_OF[sub][tap]] * kern[tap]
                mixed = jnp.where(real, total, center)
                half = 0.5 + 0.5 * lax.erf(mixed * SQRT_HALF)
                bell = jnp.exp(-0.5 * mixed * mixed) * INV_SQRT_TWO_PI
                span = pl.ds(pl.multiple_of(sub * tiles + row, ROWS), ROWS)
                active_ref[span, lanes] = (mixed * half).astype(jnp.bfloat16)
                slope_ref[span, lanes] = (half + mixed * bell).astype(jnp.bfloat16)

    for sub in range(4):
        span = slice(sub * tiles, (sub + 1) * tiles)
        out_ref[span, :] += product(active_ref[span, :], down_ref[0])


def lane_parts(width):
    return [(at, lane, min(LANES, width - lane)) for at, lane in enumerate(range(0, width, LANES))]


def spread_rows(source, planes_ref):
    for at, lane, width in lane_parts(source.shape[1]):
        planes_ref[at, :, :width] = source[:, lane : lane + width].astype(jnp.float32)


class Plan:
    def __init__(self, value, out, scratch, make, space=None):
        self.value, self.out, self.scratch, self.make = value, out, scratch, make
        self.in_spec = whole(value.shape)
        self.out_spec = pl.BlockSpec(memory_space=space) if space is not None else whole(out.shape)


def plan_sum(value):
    return Plan(value, jax.ShapeDtypeStruct(value.shape, value.dtype), sum_scratch(value.shape), SumRide)


def plan_units(value, begin, end):
    if begin == 0:
        value = unit_blocks(value)
    total, (chunk, width) = value.shape[0], value.shape[-2:]
    inside = unit_layout(unit_order(0))[end] if end < len(bit_order()) else ()
    out = jax.ShapeDtypeStruct((total,) + inside + (chunk, width), value.dtype)

    def make(ride_in, ride_out, scratch):
        sources = [(ride_in, at) for at in range(total)]
        return UnitRide(sources, ride_out, scratch, begin, end)

    return Plan(value, out, unit_scratch(total, chunk, width, begin, end), make)


def plan_gather(piece):
    total, chunk, width = piece.shape
    out = jax.ShapeDtypeStruct((total,) + (2,) * len(bit_order()) + (chunk, width), piece.dtype)
    scratch = gather_scratch(total) + [pltpu.VMEM(out.shape, piece.dtype), pltpu.SemaphoreType.DMA((1,))]
    return Plan(piece, out, scratch, PieceRide, pl.ANY)


class Rides:
    def __init__(self, rides):
        self.rides = rides
        self.phases = max(ride.phases for ride in rides)
        names = [name for name in bit_order() if any(name in ride.names for ride in rides)]
        self.peers = [UnitRide.partner(rides[0], name) for name in names]

    def signal(self):
        signal_all(self.peers)

    def advance(self, phase):
        if phase == 0:
            pl.semaphore_wait(pltpu.get_barrier_semaphore(), len(self.peers))
        for ride in self.rides:
            if phase <= ride.phases:
                ride.advance(phase)


def rides_of(plans, ins, outs, scratch):
    rides = []
    for plan, ride_in, ride_out in zip(plans, ins, outs):
        count = len(plan.scratch)
        rides.append(plan.make(ride_in, ride_out, scratch[:count]))
        scratch = scratch[count:]
    return Rides(rides)


def ridden(kernel, inputs, outputs, scratch, steps, plans):
    def run(*refs):
        own_in, refs = refs[:inputs], refs[inputs:]
        ride_in, refs = refs[: len(plans)], refs[len(plans) :]
        own_out, refs = refs[:outputs], refs[outputs:]
        ride_out, rest = refs[: len(plans)], refs[len(plans) :]
        rides = rides_of(plans, ride_in, ride_out, rest[scratch:])
        first = min(steps, rides.phases + 1)

        def advance():
            for phase in range(first):
                pl.when(pl.program_id(0) == phase)(functools.partial(rides.advance, phase))

        pl.when(pl.program_id(0) == 0)(rides.signal)
        kernel(advance, *own_in, *own_out, *rest[:scratch])
        if rides.phases >= first:

            @pl.when(pl.program_id(0) == steps - 1)
            def _():
                for phase in range(first, rides.phases + 1):
                    rides.advance(phase)

    return run


def whole(shape):
    return pl.BlockSpec(shape, lambda j: (0,) * len(shape))


def unit_spec(at):
    return pl.BlockSpec((1, FF, C), lambda j: (at, 0, 0))


def mlp_forward(middle, gains, units, at, kernel, layer_at, stacks, real_rows, plans, meeting):
    rows = middle.shape[0]
    block = 256
    by_lane = pl.BlockSpec((rows, block), lambda j: (0, j))
    low = jax.ShapeDtypeStruct((rows, FF), jnp.bfloat16)
    body_of = functools.partial(mlp_forward_kernel, lambda: None)
    limits = dict(vmem_limit_bytes=VMEM_LIMIT)
    if plans:
        body_of = ridden(mlp_forward_kernel, 8, 5, 3, FF // block, plans)
        limits.update(collective_id=meeting, has_side_effects=True)
    return pl.pallas_call(
        body_of,
        grid=(FF // block,),
        out_shape=(
            jax.ShapeDtypeStruct((rows, C), jnp.float32),
            low,
            low,
            low,
            jax.ShapeDtypeStruct((C, FF), jnp.bfloat16),
            *[plan.out for plan in plans],
        ),
        in_specs=[
            whole((rows, C)),
            whole((2, C)),
            unit_spec(at),
            pl.BlockSpec((1, block, C), lambda j: (at + 1, j, 0)),
            pl.BlockSpec((1, 9, block), lambda j: (layer_at, 0, j)),
            whole(stacks[0].shape),
            whole(stacks[1].shape),
            whole(real_rows.shape),
        ]
        + [plan.in_spec for plan in plans],
        out_specs=(whole((rows, C)), by_lane, by_lane, by_lane, whole((C, FF)))
        + tuple(plan.out_spec for plan in plans),
        scratch_shapes=[
            pltpu.VMEM((rows, C), jnp.bfloat16),
            pltpu.VMEM((4, 3, rows // 4, block), jnp.float32),
            pltpu.VMEM((3, FF, LANES), jnp.float32),
        ]
        + sum([plan.scratch for plan in plans], []),
        compiler_params=pltpu.CompilerParams(**limits),
        cost_estimate=pl.CostEstimate(flops=14 * 10**9, bytes_accessed=18 * 10**6, transcendentals=4 * 10**6),
        name="mlp_forward",
    )(middle, gains, units, units, kernel, stacks[0], stacks[1], real_rows, *[plan.value for plan in plans])


def mlp_backward_kernel(
    advance,
    grad_ref, middle_ref, gains_ref, up_ref, down_ref, kern_ref, upper_ref, lower_ref, real_ref,
    hidden_ref, active_ref, slope_ref,
    out_ref, dunits_ref, dkern_ref, dgain_ref,
    low_ref, low_t_ref, normed_t_ref, mixed_ref, dhid_ref, moved_ref, back_ref, wide_ref, planes_ref,
):
    rows = grad_ref.shape[0]
    tiles = rows // 4
    block = hidden_ref.shape[1]

    @pl.when(pl.program_id(0) == 0)
    def _():
        for sub in range(4):
            span = slice(sub * tiles, (sub + 1) * tiles)
            low_ref[span, :] = grad_ref[span, :].astype(jnp.bfloat16)
        normed = norm_rows(middle_ref[...], gains_ref[0:1, :], gains_ref[1:2, :])[2]
        normed_t_ref[...] = normed.T.astype(jnp.bfloat16)
        low_t_ref[...] = grad_ref[...].T.astype(jnp.bfloat16)
        back_ref[...] = jnp.zeros_like(back_ref)

    advance()
    for sub in range(4):
        span = slice(sub * tiles, (sub + 1) * tiles)
        part = back_product(low_ref[span, :], down_ref[0]).astype(jnp.bfloat16).astype(jnp.float32)
        mixed_ref[span, :] = (part * slope_ref[span, :].astype(jnp.float32)).astype(jnp.bfloat16)
    down_rows = pl.ds(pl.multiple_of(pl.program_id(0) * block, block), block)
    dunits_ref[1, down_rows, :] = product(low_t_ref[...], active_ref[...]).T.astype(jnp.bfloat16)
    move_planes(mixed_ref, upper_ref, lower_ref, moved_ref)

    for lane in range(0, block, LANES):
        lanes = slice(lane, lane + LANES)
        kern = [kern_ref[0, tap : tap + 1, lanes] for tap in range(9)]

        def step(at, sums):
            row = pl.multiple_of(at * ROWS, ROWS)
            found = chunk_sources(mixed_ref, moved_ref, row, lanes)
            real = real_ref[pl.ds(row, ROWS), :] > 0.0
            sums = list(sums)
            for sub in range(4):
                span = pl.ds(pl.multiple_of(sub * tiles + row, ROWS), ROWS)
                hidden = hidden_ref[span, lanes].astype(jnp.float32)
                center = found[sub, 0, 0] * kern[4]
                total = center
                for tap in range(9):
                    term = found[TAPS_OF[sub][tap]]
                    if tap != 4:
                        total = total + term * kern[8 - tap]
                    piece = hidden * term
                    sums[tap] = sums[tap] + piece[:8] + piece[8:]
                dhid_ref[span, lanes] = jnp.where(real, total, center).astype(jnp.bfloat16)
            return tuple(sums)

        sums = lax.fori_loop(0, tiles // ROWS, step, (jnp.zeros((8, LANES), jnp.float32),) * 9, unroll=True)
        for tap in range(9):
            dkern_ref[8 - tap : 9 - tap, lanes] = jnp.sum(sums[tap], 0, keepdims=True)

    columns = pl.ds(pl.multiple_of(pl.program_id(0) * block, block), block)
    wide_ref[:, columns] = product(normed_t_ref[...], dhid_ref[...])
    for sub in range(4):
        span = slice(sub * tiles, (sub + 1) * tiles)
        back_ref[span, :] += back_product(dhid_ref[span, :], up_ref[...])

    @pl.when(pl.program_id(0) == pl.num_programs(0) - 1)
    def _():
        grad = back_ref[...]
        unit, inverse, _ = norm_rows(middle_ref[...], gains_ref[0:1, :], gains_ref[1:2, :])
        out_ref[...] = grad_ref[...] + norm_rows_back(unit, inverse, gains_ref[0:1, :], grad)
        dgain_ref[0:1, :] = jnp.sum(grad * unit, 0, keepdims=True)
        dgain_ref[1:2, :] = jnp.sum(grad, 0, keepdims=True)
        for quarter in range(FF // C):
            for at, lane, width in lane_parts(C):
                begin = quarter * C + lane
                part = wide_ref[:, begin : begin + width]
                if width < LANES:
                    part = jnp.concatenate([part, jnp.zeros((C, LANES - width), jnp.float32)], 1)
                planes_ref[at, pl.ds(quarter, C, stride=FF // C), :] = part
        for at, lane, width in lane_parts(C):
            dunits_ref[0, :, lane : lane + width] = planes_ref[at, :, :width].astype(jnp.bfloat16)


def mlp_backward(grad, middle, gains, w_up, units, at, kernel, layer_at, stacks, real_rows, kept, plans, meeting):
    rows = middle.shape[0]
    block = 256
    by_lane = pl.BlockSpec((rows, block), lambda j: (0, j))
    up_spec = pl.BlockSpec((C, block), lambda j: (0, j))
    tap_spec = pl.BlockSpec((9, block), lambda j: (0, j))
    return pl.pallas_call(
        ridden(mlp_backward_kernel, 12, 4, 9, FF // block, plans),
        grid=(FF // block,),
        out_shape=(
            jax.ShapeDtypeStruct((rows, C), jnp.float32),
            jax.ShapeDtypeStruct((2, FF, C), jnp.bfloat16),
            jax.ShapeDtypeStruct((9, FF), jnp.float32),
            jax.ShapeDtypeStruct((2, C), jnp.float32),
            *[plan.out for plan in plans],
        ),
        in_specs=[
            whole((rows, C)),
            whole((rows, C)),
            whole((2, C)),
            up_spec,
            pl.BlockSpec((1, block, C), lambda j: (at + 1, j, 0)),
            pl.BlockSpec((1, 9, block), lambda j: (layer_at, 0, j)),
            whole(stacks[0].shape),
            whole(stacks[1].shape),
            whole(real_rows.shape),
            by_lane,
            by_lane,
            by_lane,
        ]
        + [plan.in_spec for plan in plans],
        out_specs=(whole((rows, C)), whole((2, FF, C)), tap_spec, whole((2, C)))
        + tuple(plan.out_spec for plan in plans),
        scratch_shapes=[
            pltpu.VMEM((rows, C), jnp.bfloat16),
            pltpu.VMEM((C, rows), jnp.bfloat16),
            pltpu.VMEM((C, rows), jnp.bfloat16),
            pltpu.VMEM((rows, block), jnp.bfloat16),
            pltpu.VMEM((rows, block), jnp.bfloat16),
            pltpu.VMEM((4, 3, rows // 4, block), jnp.float32),
            pltpu.VMEM((rows, C), jnp.float32),
            pltpu.VMEM((C, FF), jnp.float32),
            pltpu.VMEM((3, FF, LANES), jnp.float32),
        ]
        + sum([plan.scratch for plan in plans], []),
        compiler_params=pltpu.CompilerParams(
            collective_id=meeting, has_side_effects=True, vmem_limit_bytes=VMEM_LIMIT
        ),
        cost_estimate=pl.CostEstimate(flops=18 * 10**9, bytes_accessed=18 * 10**6, transcendentals=0),
        name="mlp_backward",
    )(grad, middle, gains, w_up, units, kernel, stacks[0], stacks[1], real_rows, *kept, *[plan.value for plan in plans])


WIDE = 384
BLOCK_TILES = 32
KEY_SPAN = 128


def block_places(tiles):
    places = []
    for index in range(-(-tiles // BLOCK_TILES)):
        start = min(index * BLOCK_TILES, tiles - BLOCK_TILES)
        places.append((start, min(max(start - 48, 0), tiles - KEY_SPAN)))
    return places


def block_bias(tiles, image_at):
    starts, lows = np.array(block_places(tiles), np.int32).T[:, :, None]
    columns = starts + np.tile(np.arange(BLOCK_TILES, dtype=np.int32), 4)
    rows = lows + np.arange(KEY_SPAN, dtype=np.int32)
    same = image_at(jnp.asarray(rows))[:, :, None] == image_at(jnp.asarray(columns))[:, None, :]
    return jnp.where(same, 0.0, NEG_FILL)


def place_of(index, tiles):
    start = jnp.minimum(index * BLOCK_TILES, tiles - BLOCK_TILES)
    low = jnp.clip(start - 48, 0, tiles - KEY_SPAN)
    return (pl.multiple_of(start, ROWS), pl.multiple_of(low, ROWS))


def four_planes(ref, start, lanes):
    tiles = ref.shape[0] // 4
    return jnp.concatenate(
        [ref[pl.ds(pl.multiple_of(sub * tiles + start, ROWS), BLOCK_TILES), lanes] for sub in range(4)], 0
    )


def put_planes(ref, start, lanes, values):
    tiles = ref.shape[0] // 4
    for sub in range(4):
        ref[pl.ds(pl.multiple_of(sub * tiles + start, ROWS), BLOCK_TILES), lanes] = values[
            sub * BLOCK_TILES : (sub + 1) * BLOCK_TILES
        ]


def head_pair(values, group):
    if group == 2:
        return values
    first = lax.broadcasted_iota(jnp.int32, values.shape, 1) < HD
    zero = jnp.zeros_like(values)
    return jnp.concatenate([jnp.where(first, values, zero), jnp.where(first, zero, values)], 0)


def softmax_columns(raw, bias):
    parts = []
    for half in range(raw.shape[0] // KEY_SPAN):
        scores = raw[half * KEY_SPAN : (half + 1) * KEY_SPAN] * HD ** (-0.5) + bias
        weights = jnp.exp(scores - jnp.max(scores, 0, keepdims=True))
        parts.append(weights * (1.0 / jnp.sum(weights, 0, keepdims=True)))
    return parts


def norm_store(source_ref, gains_ref, at, target_ref):
    normed = norm_rows(source_ref[...], gains_ref[at : at + 1, :], gains_ref[at + 1 : at + 2, :])[2]
    target_ref[...] = normed.astype(jnp.bfloat16)


def part_keyval(unit_ref, planes_ref, kv_ref):
    spread_rows(unit_ref[0, 2 * C :, :], planes_ref)
    for which in range(2):
        for at, lane, width in lane_parts(C):
            part = planes_ref[at, pl.ds(which, C, stride=2), :][:, :width]
            kv_ref[which, :, lane : lane + width] = part.astype(jnp.bfloat16)


def attention_forward_kernel(
    resid_ref, gains_ref, unit_ref, reduce_ref, bias_ref,
    middle_ref, normed_ref, query_ref, reduced_ref, key_ref, value_ref, attended_ref, kv_ref,
    planes_ref,
):
    part_keyval(unit_ref, planes_ref, kv_ref)
    rows = resid_ref.shape[0]
    tiles = rows // 4
    norm_store(resid_ref, gains_ref, 0, normed_ref)
    query_ref[:, C:] = jnp.zeros((rows, WIDE - C), jnp.bfloat16)
    reduced = jnp.zeros((tiles, C), jnp.float32)
    for sub in range(4):
        span = slice(sub * tiles, (sub + 1) * tiles)
        query_ref[span, :C] = product(normed_ref[span, :], unit_ref[0, :C, :]).astype(jnp.bfloat16)
        reduced = reduced + product(normed_ref[span, :], reduce_ref[0, sub * C : (sub + 1) * C, :])
    reduced_ref[...] = reduced
    normed_kv = norm_rows(reduced, gains_ref[2:3, :], gains_ref[3:4, :])[2].astype(jnp.bfloat16)
    for which, ref in enumerate((key_ref, value_ref)):
        ref[:, C:] = jnp.zeros((tiles, WIDE - C), jnp.bfloat16)
        ref[:, :C] = product(normed_kv, kv_ref[which]).astype(jnp.bfloat16)

    @pl.loop(0, bias_ref.shape[0], unroll=bias_ref.shape[0])
    def _(index):
        start, low = place_of(index, tiles)
        bias = bias_ref[index]
        for group in range(3):
            lanes = slice(group * LANES, (group + 1) * LANES)
            query = four_planes(query_ref, start, lanes)
            keys = head_pair(key_ref[pl.ds(low, KEY_SPAN), lanes], group)
            values = head_pair(value_ref[pl.ds(low, KEY_SPAN), lanes], group)
            probs = softmax_columns(back_product(keys, query), bias)
            probs = jnp.concatenate(probs, 0).T.astype(jnp.bfloat16)
            put_planes(attended_ref, start, lanes, product(probs, values).astype(jnp.bfloat16))

    for sub in range(4):
        span = slice(sub * tiles, (sub + 1) * tiles)
        middle_ref[span, :] = resid_ref[span, :] + product(attended_ref[span, :C], unit_ref[0, C : 2 * C, :])


def attention_forward(resid, gains, units, at, reduces, reduce_at, bias):
    rows = resid.shape[0]
    tiles = rows // 4
    low = jnp.bfloat16
    shapes = (
        jax.ShapeDtypeStruct((rows, C), jnp.float32),
        jax.ShapeDtypeStruct((rows, C), low),
        jax.ShapeDtypeStruct((rows, WIDE), low),
        jax.ShapeDtypeStruct((tiles, C), jnp.float32),
        jax.ShapeDtypeStruct((tiles, WIDE), low),
        jax.ShapeDtypeStruct((tiles, WIDE), low),
        jax.ShapeDtypeStruct((rows, WIDE), low),
        jax.ShapeDtypeStruct((2, C, C), low),
    )
    return pl.pallas_call(
        attention_forward_kernel,
        grid=(1,),
        out_shape=shapes,
        in_specs=[whole((rows, C)), whole((4, C)), unit_spec(at), unit_spec(reduce_at), whole(bias.shape)],
        out_specs=tuple(whole(shape.shape) for shape in shapes),
        scratch_shapes=[pltpu.VMEM((3, 2 * C, LANES), jnp.float32)],
        compiler_params=pltpu.CompilerParams(vmem_limit_bytes=VMEM_LIMIT),
        cost_estimate=pl.CostEstimate(flops=6 * 10**9, bytes_accessed=14 * 10**6, transcendentals=10**6),
        name="attention_forward",
    )(resid, gains, units, reduces, bias)


def embed_forward_kernel(
    patches_ref, halo_ref, unit_ref, gains_ref, pre_ref, resid_ref, kern_ref, planes_ref, taps_ref
):
    rows = pre_ref.shape[0]
    tiles = rows // 4
    used = FF * 9 * BLOCKS // C
    for ref, base in ((patches_ref, 0), (halo_ref, patches_ref.shape[0])):
        step = 64

        @pl.loop(0, ref.shape[0] // step, unroll=4)
        def _(at):
            span = pl.ds(pl.multiple_of(at * step, step), step)
            into = pl.ds(pl.multiple_of(base + at * step, step), step)
            part = product(ref[span, :], unit_ref[0, :PIN, :])
            for place, lane, width in lane_parts(C):
                planes_ref[place, into, :width] = part[:, lane : lane + width]

    for sub in range(4):
        for place, lane, width in lane_parts(C):
            pre_ref[sub * tiles : (sub + 1) * tiles, lane : lane + width] = planes_ref[
                place, pl.ds(sub, tiles, stride=4), :
            ][:, :width]
    taps = unit_ref[0, PIN : PIN + taps_ref.shape[1], :]
    spread_rows(taps, taps_ref)
    for layer_at in range(BLOCKS):
        for quarter in range(FF // C):
            for place, lane, width in lane_parts(C):
                begin = quarter * C + lane
                kern_ref[layer_at, :, begin : begin + width] = taps_ref[
                    place, pl.ds(layer_at * (used // BLOCKS) + quarter, 9, stride=FF // C), :
                ][:, :width]

    resid_ref[...] = norm_rows(pre_ref[...], gains_ref[0:1, :], gains_ref[1:2, :])[2]


def embed_forward(patches, halo, units, gains):
    rows = patches.shape[0] + halo.shape[0]
    wide = jax.ShapeDtypeStruct((rows, C), jnp.float32)
    taps = jax.ShapeDtypeStruct((BLOCKS, 9, FF), jnp.float32)
    return pl.pallas_call(
        embed_forward_kernel,
        grid=(1,),
        out_shape=(wide, wide, taps),
        in_specs=[whole(patches.shape), whole(halo.shape), unit_spec(0), whole((2, C))],
        out_specs=(whole(wide.shape), whole(wide.shape), whole(taps.shape)),
        scratch_shapes=[
            pltpu.VMEM((3, rows, LANES), jnp.float32),
            pltpu.VMEM((3, FF - PIN, LANES), jnp.float32),
        ],
        compiler_params=pltpu.CompilerParams(vmem_limit_bytes=VMEM_LIMIT),
        cost_estimate=pl.CostEstimate(flops=10**9, bytes_accessed=8 * 10**6, transcendentals=0),
        name="embed_forward",
    )(patches, halo, units, gains)


def embed_backward_kernel(
    grad_ref, pre_ref, gains_ref, patches_ref, halo_ref, *refs
):
    taps_refs = refs[:BLOCKS]
    unit_ref, dgain_ref, planes_ref, turned_ref, taps_ref = refs[BLOCKS:]
    rows = pre_ref.shape[0]
    tiles = rows // 4
    half = tiles // 2
    used = FF * 9 * BLOCKS // C
    sums = [jnp.zeros((1, C), jnp.float32)] * 2
    for sub in range(4):
        for part_at in range(2):
            span = slice(sub * tiles + part_at * half, sub * tiles + (part_at + 1) * half)
            unit, inverse, _ = norm_rows(pre_ref[span, :], gains_ref[0:1, :], gains_ref[1:2, :])
            grad = grad_ref[span, :]
            back = norm_rows_back(unit, inverse, gains_ref[0:1, :], grad)
            sums[0] = sums[0] + jnp.sum(grad * unit, 0, keepdims=True)
            sums[1] = sums[1] + jnp.sum(grad, 0, keepdims=True)
            for place, lane, width in lane_parts(C):
                value = back[:, lane : lane + width]
                if width < LANES:
                    value = jnp.concatenate([value, jnp.zeros((half, LANES - width), jnp.float32)], 1)
                planes_ref[place, pl.ds(4 * part_at * half + sub, half, stride=4), :] = value
    dgain_ref[0:1, :] = sums[0]
    dgain_ref[1:2, :] = sums[1]
    for place, lane, width in lane_parts(C):
        turned_ref[lane : lane + width, :] = planes_ref[place].T[:width, :].astype(jnp.bfloat16)
    split = patches_ref.shape[0]
    grads = product(turned_ref[:, :split], patches_ref[...]) + product(turned_ref[:, split:], halo_ref[...])
    unit_ref[0, :PIN, :] = grads.T.astype(jnp.bfloat16)
    taps_ref[...] = jnp.zeros_like(taps_ref)
    for layer_at, ref in enumerate(taps_refs):
        for quarter in range(FF // C):
            for place, lane, width in lane_parts(C):
                begin = quarter * C + lane
                value = ref[:, begin : begin + width]
                if width < LANES:
                    value = jnp.concatenate([value, jnp.zeros((9, LANES - width), jnp.float32)], 1)
                taps_ref[place, pl.ds(layer_at * (used // BLOCKS) + quarter, 9, stride=FF // C), :] = value
    for place, lane, width in lane_parts(C):
        unit_ref[0, PIN:, lane : lane + width] = taps_ref[place, :, :width].astype(jnp.bfloat16)


def embed_backward(grad, pre, gains, patches, halo, taps):
    rows = pre.shape[0]
    shapes = (jax.ShapeDtypeStruct((1, FF, C), jnp.bfloat16), jax.ShapeDtypeStruct((2, C), jnp.float32))
    operands = (grad, pre, gains, patches, halo, *taps)
    return pl.pallas_call(
        embed_backward_kernel,
        grid=(1,),
        out_shape=shapes,
        in_specs=[whole(part.shape) for part in operands],
        out_specs=tuple(whole(shape.shape) for shape in shapes),
        scratch_shapes=[
            pltpu.VMEM((3, rows, LANES), jnp.float32),
            pltpu.VMEM((C, rows), jnp.bfloat16),
            pltpu.VMEM((3, FF - PIN, LANES), jnp.float32),
        ],
        compiler_params=pltpu.CompilerParams(vmem_limit_bytes=VMEM_LIMIT),
        cost_estimate=pl.CostEstimate(flops=10**9, bytes_accessed=8 * 10**6, transcendentals=0),
        name="embed_backward",
    )(*operands)


def attention_backward_kernel(
    advance,
    grad_ref, resid_ref, gains_ref, unit_ref, reduce_ref, bias_ref,
    normed_ref, query_ref, reduced_ref, key_ref, value_ref, attended_ref, kv_ref,
    out_ref, dunits_ref, dgain_ref,
    turned_ref, datt_ref, dquery_ref, dkey_ref, dvalue_ref, first_ref, planes_ref,
):
    rows = resid_ref.shape[0]
    tiles = rows // 4
    low_type = jnp.bfloat16
    datt_ref[:, C:] = jnp.zeros((rows, WIDE - C), low_type)
    turned_ref[...] = grad_ref[...].T.astype(low_type)
    dunits_ref[0, C : 2 * C, :] = product(turned_ref[...], attended_ref[:, :C]).T.astype(low_type)
    for sub in range(4):
        span = slice(sub * tiles, (sub + 1) * tiles)
        datt_ref[span, :C] = back_product(grad_ref[span, :].astype(low_type), unit_ref[0, C : 2 * C, :]).astype(low_type)
    dkey_ref[...] = jnp.zeros_like(dkey_ref)
    dvalue_ref[...] = jnp.zeros_like(dvalue_ref)
    blocks = bias_ref.shape[0]

    def one_block(step):
        index = blocks - 1 - step
        start, low = place_of(index, tiles)
        bias = bias_ref[index]
        tile_at = lax.rem(lax.broadcasted_iota(jnp.int32, (4 * BLOCK_TILES, LANES), 0), BLOCK_TILES)
        fresh = tile_at >= index * BLOCK_TILES - start
        span = pl.ds(low, KEY_SPAN)
        for group in range(3):
            lanes = slice(group * LANES, (group + 1) * LANES)
            query = four_planes(query_ref, start, lanes)
            datt = four_planes(datt_ref, start, lanes)
            datt = jnp.where(fresh, datt, jnp.zeros_like(datt))
            keys = head_pair(key_ref[span, lanes], group)
            values = head_pair(value_ref[span, lanes], group)
            probs = softmax_columns(back_product(keys, query), bias)
            dprobs = back_product(values, datt)
            dscores = []
            for half, prob in enumerate(probs):
                dprob = dprobs[half * KEY_SPAN : (half + 1) * KEY_SPAN]
                inner = jnp.sum(prob * dprob, 0, keepdims=True)
                dscores.append(prob * (dprob - inner) * HD ** (-0.5))
            dscores = jnp.concatenate(dscores, 0)
            probs = jnp.concatenate(probs, 0).astype(low_type)
            dquery = product(dscores.T.astype(low_type), keys)
            put_planes(dquery_ref, start, lanes, dquery.astype(low_type))
            dkeys = product(dscores.astype(low_type), query)
            dvalues = product(probs, datt)
            if group < 2:
                first = lax.broadcasted_iota(jnp.int32, (KEY_SPAN, LANES), 1) < HD
                dkeys = jnp.where(first, dkeys[:KEY_SPAN], dkeys[KEY_SPAN:])
                dvalues = jnp.where(first, dvalues[:KEY_SPAN], dvalues[KEY_SPAN:])
            dkey_ref[span, lanes] += dkeys
            dvalue_ref[span, lanes] += dvalues

    advance(0)
    pl.loop(0, blocks // 2, unroll=blocks // 2)(one_block)
    advance(1)
    pl.loop(blocks // 2, blocks, unroll=blocks - blocks // 2)(one_block)
    advance(2)
    unit, inverse, normed = norm_rows(reduced_ref[...], gains_ref[2:3, :], gains_ref[3:4, :])
    normed_t = normed.T.astype(low_type)
    dkeys = dkey_ref[:, :C].astype(low_type)
    dvalues = dvalue_ref[:, :C].astype(low_type)
    for which, grads in enumerate((dkeys, dvalues)):
        dweight = product(normed_t, grads)
        for at, lane, width in lane_parts(C):
            part = dweight[:, lane : lane + width]
            if width < LANES:
                part = jnp.concatenate([part, jnp.zeros((C, LANES - width), jnp.float32)], 1)
            planes_ref[at, pl.ds(which, C, stride=2), :] = part
    for at, lane, width in lane_parts(C):
        dunits_ref[0, 2 * C :, lane : lane + width] = planes_ref[at, :, :width].astype(low_type)
    dnormed = back_product(dkeys, kv_ref[0]) + back_product(dvalues, kv_ref[1])
    dgain_ref[2:3, :] = jnp.sum(dnormed * unit, 0, keepdims=True)
    dgain_ref[3:4, :] = jnp.sum(dnormed, 0, keepdims=True)
    dreduced = norm_rows_back(unit, inverse, gains_ref[2:3, :], dnormed).astype(low_type)
    turned_ref[...] = normed_ref[...].T
    dunits_ref[0, :C, :] = product(turned_ref[...], dquery_ref[:, :C]).astype(low_type)
    for sub in range(4):
        span = slice(sub * tiles, (sub + 1) * tiles)
        part = slice(sub * C, (sub + 1) * C)
        dunits_ref[1, part, :] = outer_sum(normed_ref[span, :], dreduced).astype(low_type)
        first_ref[span, :] = back_product(
            dquery_ref[span, :C], unit_ref[0, :C, :]
        ) + back_product(dreduced, reduce_ref[0, part, :])

    grad = first_ref[...]
    unit, inverse, _ = norm_rows(resid_ref[...], gains_ref[0:1, :], gains_ref[1:2, :])
    out_ref[...] = grad_ref[...] + norm_rows_back(unit, inverse, gains_ref[0:1, :], grad)
    dgain_ref[0:1, :] = jnp.sum(grad * unit, 0, keepdims=True)
    dgain_ref[1:2, :] = jnp.sum(grad, 0, keepdims=True)


def attention_backward(grad, resid, gains, units, at, reduces, reduce_at, bias, kept, plans, meeting):
    rows = resid.shape[0]
    tiles = rows // 4
    low = jnp.bfloat16
    shapes = (
        jax.ShapeDtypeStruct((rows, C), jnp.float32),
        jax.ShapeDtypeStruct((2, FF, C), low),
        jax.ShapeDtypeStruct((4, C), jnp.float32),
    )
    count = len(plans)

    def run(*refs):
        own_in, ride_in = refs[:13], refs[13 : 13 + count]
        own_out, ride_out = refs[13 + count : 16 + count], refs[16 + count : 16 + 2 * count]
        rest = refs[16 + 2 * count :]
        rides = rides_of(plans, ride_in, ride_out, rest[7:])
        rides.signal()
        attention_backward_kernel(rides.advance, *own_in, *own_out, *rest[:7])
        for phase in range(3, rides.phases + 1):
            rides.advance(phase)

    return pl.pallas_call(
        run,
        grid=(1,),
        out_shape=shapes + tuple(plan.out for plan in plans),
        in_specs=[
            whole((rows, C)),
            whole((rows, C)),
            whole((4, C)),
            unit_spec(at),
            unit_spec(reduce_at),
            whole(bias.shape),
        ]
        + [whole(part.shape) for part in kept]
        + [plan.in_spec for plan in plans],
        out_specs=tuple(whole(shape.shape) for shape in shapes) + tuple(plan.out_spec for plan in plans),
        scratch_shapes=[
            pltpu.VMEM((C, rows), low),
            pltpu.VMEM((rows, WIDE), low),
            pltpu.VMEM((rows, WIDE), low),
            pltpu.VMEM((tiles, WIDE), jnp.float32),
            pltpu.VMEM((tiles, WIDE), jnp.float32),
            pltpu.VMEM((rows, C), jnp.float32),
            pltpu.VMEM((3, 2 * C, LANES), jnp.float32),
        ]
        + sum([plan.scratch for plan in plans], []),
        compiler_params=pltpu.CompilerParams(collective_id=meeting, has_side_effects=True, vmem_limit_bytes=VMEM_LIMIT),
        cost_estimate=pl.CostEstimate(flops=12 * 10**9, bytes_accessed=18 * 10**6, transcendentals=10**6),
        name="attention_backward",
    )(grad, resid, gains, units, reduces, bias, *kept, *[plan.value for plan in plans])


BOTH = ("grp", "tok")


def axis_bits(axis):
    count = lax.axis_size(axis)
    return [1 << place for place in reversed(range(count.bit_length() - 1))]


def bit_order():
    tok_bits = axis_bits("tok")
    return [("grp", bit) for bit in axis_bits("grp")] + [("tok", bit) for bit in tok_bits]


MESH = pl.DeviceIdType.MESH


def exchange_setup():
    grp, tok = lax.axis_index("grp"), lax.axis_index("tok")
    n_tok = lax.axis_size("tok")
    peers = [(lax.bitwise_xor(grp, bit), tok) for bit in axis_bits("grp")]
    peers += [(grp, lax.bitwise_xor(tok, step)) for step in range(1, n_tok)]
    return (grp, tok, n_tok, peers)


def signal_all(peers):
    barrier = pltpu.get_barrier_semaphore()
    for peer in peers:
        pl.semaphore_signal(barrier, inc=1, device_id=peer, device_id_type=MESH)


def greet(peers):
    signal_all(peers)
    pl.semaphore_wait(pltpu.get_barrier_semaphore(), len(peers))


def send(source, target, sems, at, peer):
    copy = pltpu.make_async_remote_copy(
        src_ref=source,
        dst_ref=target,
        send_sem=sems[0].at[at],
        recv_sem=sems[1].at[at],
        device_id=peer,
        device_id_type=MESH,
    )
    copy.start()
    return copy


def gather_view(ref, unit, place, done):
    index = [slice(None) if name in done else place(name) for name in bit_order()]
    return ref.at[tuple([unit] + index)]


class GatherRide:
    def __init__(self, full_ref, scratch):
        self.grp, self.tok = lax.axis_index("grp"), lax.axis_index("tok")
        self.phases = len(bit_order())
        self.names = bit_order()
        self.full_ref = full_ref
        self.sems = scratch[:2]

    def order(self, unit):
        grp_bits = [("grp", bit) for bit in axis_bits("grp")]
        flip = grp_bits[::-1] if unit % 2 else grp_bits
        return [("tok", bit) for bit in axis_bits("tok")[:-1]] + flip + [("tok", 1)]

    def place(self, name):
        return (self.grp if name[0] == "grp" else self.tok) // name[1] % 2

    def partner(self, name):
        axis, bit = name
        if axis == "grp":
            return (lax.bitwise_xor(self.grp, bit), self.tok)
        return (self.grp, lax.bitwise_xor(self.tok, bit))

    def copy(self, unit, phase):
        order = self.order(unit)
        held = gather_view(self.full_ref, unit, self.place, order[:phase])
        at = phase * self.full_ref.shape[0] + unit
        return pltpu.make_async_remote_copy(
            src_ref=held,
            dst_ref=held,
            send_sem=self.sems[0].at[at],
            recv_sem=self.sems[1].at[at],
            device_id=self.partner(order[phase]),
            device_id_type=MESH,
        )

    def put(self, unit, value):
        self.full_ref[(unit,) + tuple(self.place(name) for name in bit_order())] = value

    def advance(self, phase):
        for unit in range(self.full_ref.shape[0]):
            if phase:
                self.copy(unit, phase - 1).wait()
            if phase < self.phases:
                self.copy(unit, phase).start()


def gather_scratch(total):
    phases = len(bit_order())
    return [pltpu.SemaphoreType.DMA((phases * total,))] * 2


class PieceRide(GatherRide):
    def __init__(self, piece_ref, out_ref, scratch):
        super().__init__(scratch[2], scratch)
        self.piece_ref, self.out_ref = piece_ref, out_ref
        self.out_sem = scratch[3]

    def advance(self, phase):
        if phase == 0:
            for unit in range(self.full_ref.shape[0]):
                self.put(unit, self.piece_ref[unit])
        super().advance(phase)
        if phase == self.phases:
            copy = pltpu.make_async_copy(self.full_ref, self.out_ref, self.out_sem.at[0])
            copy.start()
            copy.wait()


def start_kernel(
    slot_ref, piece_ref, count_ref, patch_ref, mark_ref,
    full_ref, later_ref, total_ref, patch_halo_ref, mark_halo_ref,
    recv_ref, near_s, near_r, halo_s, halo_r, *scratch,
):
    grp, tok, n_tok, peers = exchange_setup()
    slot_rows = piece_ref.shape[1]
    units, first = slot_ref.shape[0], full_ref.shape[0]
    gather = GatherRide(full_ref, scratch[:2])
    count = SumRide(count_ref, total_ref, scratch[2:])
    greet(peers)
    copies = []
    for step in range(1, n_tok):
        peer = lax.bitwise_xor(tok, step)
        landing = recv_ref.at[pl.ds(tok * slot_rows, slot_rows)]
        copies.append(send(piece_ref.at[peer], landing, (near_s, near_r), step, (grp, peer)))
    recv_ref[pl.ds(tok * slot_rows, slot_rows)] = piece_ref[tok]
    count.advance(0)
    for copy in copies:
        copy.wait()
    for unit in range(first):
        gather.put(unit, recv_ref[slot_ref[unit]])
    gather.advance(0)
    before = (grp, lax.rem(tok + n_tok - 1, n_tok))
    mark_copy = send(mark_ref, mark_halo_ref, (halo_s, halo_r), 0, before)
    patch_copy = send(patch_ref.at[pl.ds(0, patch_halo_ref.shape[0])], patch_halo_ref, (halo_s, halo_r), 1, before)
    for unit in range(first, units):
        later_ref[unit - first] = recv_ref[slot_ref[unit]]
    for phase in range(1, gather.phases + 1):
        count.advance(phase)
        gather.advance(phase)
    mark_copy.wait()
    patch_copy.wait()


def start_exchange(slot_of, pieces, count, patches, marks, first):
    n_tok, slot_rows, chunk, width = pieces.shape
    phases = len(bit_order())
    units = slot_of.shape[0]
    vmem = pl.BlockSpec(memory_space=pltpu.VMEM)
    full_shape = (first,) + (2,) * phases + (chunk, width)
    return pl.pallas_call(
        start_kernel,
        out_shape=(
            jax.ShapeDtypeStruct(full_shape, pieces.dtype),
            jax.ShapeDtypeStruct((units - first, chunk, width), pieces.dtype),
            jax.ShapeDtypeStruct(count.shape, count.dtype),
            jax.ShapeDtypeStruct((OVER, patches.shape[1]), patches.dtype),
            jax.ShapeDtypeStruct(marks.shape, marks.dtype),
        ),
        in_specs=[pl.BlockSpec(memory_space=pltpu.SMEM), vmem, vmem, pl.BlockSpec(memory_space=pl.ANY), vmem],
        out_specs=(vmem, vmem, vmem, pl.BlockSpec(memory_space=pl.ANY), vmem),
        scratch_shapes=[
            pltpu.VMEM((n_tok * slot_rows, chunk, width), pieces.dtype),
            pltpu.SemaphoreType.DMA((n_tok,)),
            pltpu.SemaphoreType.DMA((n_tok,)),
            pltpu.SemaphoreType.DMA((2,)),
            pltpu.SemaphoreType.DMA((2,)),
        ]
        + gather_scratch(first)
        + sum_scratch(count.shape),
        compiler_params=pltpu.CompilerParams(collective_id=0, has_side_effects=True, vmem_limit_bytes=VMEM_LIMIT),
        name="start_exchange",
    )(slot_of, pieces, count, patches, marks)


def unit_order(unit):
    grp_bits = [("grp", bit) for bit in axis_bits("grp")]
    if unit % 2:
        grp_bits = grp_bits[::-1]
    return [("tok", 1)] + grp_bits + [("tok", bit) for bit in axis_bits("tok")[:-1][::-1]]


def unit_layout(order):
    left = bit_order()
    shapes = []
    for name in order:
        at = left.index(name)
        shapes.append((1 << at, 2, 1 << (len(left) - 1 - at)))
        left.remove(name)
    return shapes


SPLIT = 3


class UnitRide:
    def __init__(self, sources, out_ref, scratch, begin=0, end=None, base=0):
        self.grp, self.tok = lax.axis_index("grp"), lax.axis_index("tok")
        self.begin = begin
        self.end = len(bit_order()) if end is None else end
        self.phases = self.end - begin
        self.names = unit_order(0)[self.begin : self.end]
        self.sources = sources
        self.out_ref, self.base = out_ref, base
        self.sems = scratch[:2]
        self.buffers = scratch[2:]

    def partner(self, name):
        axis, bit = name
        if axis == "grp":
            return (lax.bitwise_xor(self.grp, bit), self.tok)
        return (self.grp, lax.bitwise_xor(self.tok, bit))

    def half_of(self, name):
        return (self.grp if name[0] == "grp" else self.tok) // name[1] % 2

    def before(self, unit, phase):
        if phase == 0:
            ref, at = self.sources[unit]
            return ref.at[at]
        return self.buffers[unit * 2 * self.phases + 2 * (phase - 1) + 1]

    def landing(self, unit, phase):
        return self.buffers[unit * 2 * self.phases + 2 * phase]

    def copy(self, unit, phase):
        name = unit_order(unit)[self.begin + phase]
        at = phase * len(self.sources) + unit
        return pltpu.make_async_remote_copy(
            src_ref=self.before(unit, phase).at[:, 1 - self.half_of(name)],
            dst_ref=self.landing(unit, phase),
            send_sem=self.sems[0].at[at],
            recv_sem=self.sems[1].at[at],
            device_id=self.partner(name),
            device_id_type=MESH,
        )

    def finish(self, unit, phase):
        order = unit_order(unit)
        shapes = unit_layout(order)
        self.copy(unit, phase).wait()
        outer, _, inner = shapes[self.begin + phase]
        source, landed = self.before(unit, phase), self.landing(unit, phase)
        mine = self.half_of(order[self.begin + phase])
        target = self.out_ref.at[self.base + unit]
        if phase + 1 < self.phases:
            target = self.before(unit, phase + 1)
        whole_done = self.begin + phase + 1 == len(order)
        if not whole_done:
            low = shapes[self.begin + phase + 1][2]

        @pl.loop(0, outer * inner, unroll=min(4, outer * inner))
        def _(at):
            value = source[at // inner, mine, at % inner] + landed[at // inner, at % inner]
            if whole_done:
                target[...] = value
            else:
                target[at // (2 * low), at // low % 2, at % low] = value

    def advance(self, phase):
        for unit in range(len(self.sources)):
            if phase:
                self.finish(unit, phase - 1)
            if phase < self.phases:
                self.copy(unit, phase).start()


def unit_scratch(total, chunk, width, begin=0, end=None):
    end = len(bit_order()) if end is None else end
    dma = pltpu.SemaphoreType.DMA
    buffers = [dma(((end - begin) * total,)), dma(((end - begin) * total,))]
    for unit in range(total):
        shapes = unit_layout(unit_order(unit))
        for phase in range(begin, end):
            outer, _, inner = shapes[phase]
            buffers.append(pltpu.VMEM((outer, inner, chunk, width), jnp.bfloat16))
            following = shapes[phase + 1] if phase + 1 < end else (1, 1, 1)
            buffers.append(pltpu.VMEM(following + (chunk, width), jnp.bfloat16))
    return buffers


def unit_blocks(units):
    chunk = units.shape[1] >> len(bit_order())
    return units.reshape((units.shape[0],) + unit_layout(unit_order(0))[0] + (chunk, units.shape[2]))


class SumRide:
    def __init__(self, source_ref, total_ref, scratch):
        self.grp, self.tok = lax.axis_index("grp"), lax.axis_index("tok")
        self.order = unit_order(0)
        self.names = self.order
        self.phases = len(self.order)
        self.source_ref, self.total_ref = source_ref, total_ref
        self.sums = scratch[2]
        self.sems = scratch[:2]

    partner = UnitRide.partner

    def copy(self, phase):
        return pltpu.make_async_remote_copy(
            src_ref=self.sums.at[2 * phase],
            dst_ref=self.sums.at[2 * phase + 1],
            send_sem=self.sems[0].at[phase],
            recv_sem=self.sems[1].at[phase],
            device_id=self.partner(self.order[phase]),
            device_id_type=MESH,
        )

    def advance(self, phase):
        if phase == 0:
            self.sums[0] = self.source_ref[...]
        else:
            self.copy(phase - 1).wait()
            self.sums[2 * phase] = self.sums[2 * phase - 2] + self.sums[2 * phase - 1]
        if phase < self.phases:
            self.copy(phase).start()
        else:
            self.total_ref[...] = self.sums[2 * phase]


def sum_scratch(shape):
    phases = len(bit_order())
    dma = pltpu.SemaphoreType.DMA
    return [dma((phases,)), dma((phases,)), pltpu.VMEM((2 * phases + 1,) + shape, jnp.float32)]


def tail_kernel(counts, rows, *refs):
    unit_at_ref, early_ref, part_ref = refs[:3]
    blocks, refs = refs[3 : 3 + len(counts)], refs[3 + len(counts) :]
    small_refs, refs = refs[: len(rows)], refs[len(rows) :]
    owned_ref, small_out_ref, chunk_ref, place_ref, near_s, near_r, small_ref = refs[:7]
    scratch = refs[7:]
    sources = [(ref, at) for ref, count in zip(blocks, counts) for at in range(count)]
    total = len(sources)
    parts = part_ref.shape[0]
    grp, tok, n_tok, peers = exchange_setup()
    signal_all(peers)
    begin = 0
    for ref, count in zip(small_refs, rows):
        small_ref[begin : begin + count, :] = ref[...]
        begin += count
    small_ref[begin:, :] = jnp.zeros((small_ref.shape[0] - begin, C), jnp.float32)
    cut = 3 + 2 + 2 * total * len(bit_order())
    rides = Rides(
        [
            UnitRide(sources, chunk_ref, scratch[3:cut]),
            SumRide(small_ref, small_out_ref, scratch[:3]),
            UnitRide([(part_ref, at) for at in range(parts)], chunk_ref, scratch[cut:], SPLIT, None, total),
        ]
    )
    rides.peers = peers
    for phase in range(rides.phases + 1):
        rides.advance(phase)
    total += parts
    for at in range(early_ref.shape[0]):
        chunk_ref[total + at] = early_ref[at]
    last = total + early_ref.shape[0]
    chunk_ref[last] = jnp.zeros(chunk_ref.shape[1:], chunk_ref.dtype)
    slot_rows = owned_ref.shape[1]

    @pl.loop(0, n_tok * slot_rows)
    def _(at):
        place_ref[at // slot_rows, at % slot_rows] = chunk_ref[unit_at_ref[at]]

    copies = []
    for step in range(1, n_tok):
        peer = lax.bitwise_xor(tok, step)
        copies.append(send(place_ref.at[peer], owned_ref.at[tok], (near_s, near_r), step, (grp, peer)))
    owned_ref[tok] = place_ref[tok]
    for copy in copies:
        copy.wait()


def tail_exchange(unit_at, early, part, sources, smalls, n_tok):
    chunk, width = early.shape[1:]
    counts = tuple(source.shape[0] for source in sources)
    rows = tuple(small.shape[0] for small in smalls)
    total = sum(counts)
    low = early.dtype
    vmem = pl.BlockSpec(memory_space=pltpu.VMEM)
    slot_rows = unit_at.shape[0] // n_tok
    dma = pltpu.SemaphoreType.DMA
    small = (-(-sum(rows) // 8) * 8, C)
    return pl.pallas_call(
        lambda *refs: tail_kernel(counts, rows, *refs),
        out_shape=(
            jax.ShapeDtypeStruct((n_tok, slot_rows, chunk, width), low),
            jax.ShapeDtypeStruct(small, jnp.float32),
        ),
        in_specs=[pl.BlockSpec(memory_space=pltpu.SMEM)] + [vmem] * (2 + len(sources) + len(smalls)),
        out_specs=(vmem, vmem),
        scratch_shapes=[
            pltpu.VMEM((total + part.shape[0] + early.shape[0] + 1, chunk, width), low),
            pltpu.VMEM((n_tok, slot_rows, chunk, width), low),
            dma((n_tok,)),
            dma((n_tok,)),
            pltpu.VMEM(small, jnp.float32),
        ]
        + sum_scratch(small)
        + unit_scratch(total, chunk, width)
        + unit_scratch(part.shape[0], chunk, width, SPLIT),
        compiler_params=pltpu.CompilerParams(collective_id=1, has_side_effects=True, vmem_limit_bytes=VMEM_LIMIT),
        name="tail_exchange",
    )(unit_at, early, part, *[unit_blocks(source) for source in sources], *smalls)


def body(
    patches,
    labels,
    valid_mask,
    crop_counts,
    owners,
    slot_weight,
    slot_moment,
    slot_second,
    norm_params,
    norm_moment,
    norm_second,
    head_weight,
    head_moment,
    head_second,
):
    tok_dev = patches.shape[0]
    n_tok = lax.axis_size("tok")
    n_grp = lax.axis_size("grp")
    tok_index = lax.axis_index("tok")
    group_tok = tok_dev * n_tok
    counts = crop_counts[0]
    n_unit = owners.shape[0]
    slot_rows, columns = slot_weight.shape
    unit_order = jnp.arange(n_unit, dtype=jnp.int32)
    same_owner = owners[:, None] == owners[None, :]
    rank_of = jnp.sum(same_owner & (unit_order[None, :] < unit_order[:, None]), 1)
    slot_of = owners * slot_rows + rank_of
    chunk = columns // n_tok // C
    first_tok = tok_index * tok_dev
    small_end = counts[0] * BIG_SIDE**2 + counts[1] * SMALL_SIDE**2
    counted = valid_mask * (first_tok + jnp.arange(tok_dev, dtype=jnp.int32) < small_end)
    counted = jnp.full((8, LANES), jnp.sum(counted.astype(jnp.float32)))
    pieces = slot_weight.astype(jnp.bfloat16).reshape(slot_rows, n_tok, chunk, C).transpose(1, 0, 2, 3)
    first_units = 1 + n_unit // BLOCKS
    marks = jnp.stack([labels, valid_mask])
    own, later, counted, patch_halo, mark_halo = start_exchange(
        slot_of, pieces, counted, patches, marks[:, :OVER], first_units
    )
    pixel_total = counted[0, 0]
    own = own.reshape(first_units, FF, C)
    layers = [((own, 1, own, 2), (own, 3))]
    units = lax.all_gather(later[:4], BOTH, axis=1, tiled=True)
    layers.append(((units, 0, units, 1), (units, 2)))
    last_mlp = lax.all_gather(later[6:], BOTH, axis=1, tiled=True)

    window = tok_dev + OVER
    tiles = window // 4
    marks = jnp.concatenate([marks, mark_halo], 1)
    marks = marks.reshape(2, tiles, 4).transpose(0, 2, 1).reshape(2, window)
    labels = marks[0]
    positions = first_tok + 4 * jnp.arange(tiles, dtype=jnp.int32)
    begin_at, half_side, tile_y, tile_x, is_real = image_layout(positions, counts)
    own_image = (begin_at >= first_tok) & (begin_at < first_tok + tok_dev) & (positions < group_tok)
    stacks = shift_stacks(half_side, tile_y, tile_x, is_real)

    def image_at(tile):
        at = first_tok + 4 * tile
        return jnp.where(at < group_tok, image_layout(at, counts)[0], -1)

    bias = block_bias(tiles, image_at)
    real_rows = jnp.broadcast_to(is_real.astype(jnp.float32)[:, None], (tiles, LANES))
    keep_mask = marks[1].astype(jnp.float32) * jnp.tile((own_image & is_real).astype(jnp.float32), 4)
    tail = 6 * BLOCKS
    embed_pre, resid, kernels = embed_forward(patches, patch_halo, own, norm_params[tail : tail + 2])
    kept_all = []
    single = []
    for layer_at in range(BLOCKS):
        if layer_at == len(layers):
            layers.append(((single[0], 0, single[1], 0), (last_mlp, 0)))
        attn_units, mlp_units = layers[layer_at]
        at = 6 * layer_at
        middle, *attn_kept = attention_forward(resid, norm_params[at : at + 4], *attn_units, bias)
        plans = []
        if layer_at + 1 < BLOCKS:
            plans = [plan_gather(later[4 + layer_at : 5 + layer_at])]
        output, *mlp_kept = mlp_forward(
            middle, norm_params[at + 4 : at + 6], *mlp_units, kernels, layer_at, stacks, real_rows,
            plans, 2 + 2 * BLOCKS + layer_at,
        )
        if plans:
            single.append(mlp_kept.pop().reshape(1, FF, C))
        w_up = mlp_kept.pop()
        kept_all.append((resid, attn_kept, middle, mlp_kept, w_up))
        resid = output
    final = layer_norm(resid, norm_params[tail + 2], norm_params[tail + 3]).astype(jnp.bfloat16)
    head_low = head_weight.astype(jnp.bfloat16)
    logits = product(final, head_low)
    row_peak = jnp.max(logits, -1, keepdims=True)
    log_norm = row_peak[:, 0] + jnp.log(jnp.sum(jnp.exp(logits - row_peak), -1))
    onehot = (labels[:, None] == jnp.arange(head_weight.shape[1], dtype=jnp.int32)[None, :]).astype(
        jnp.float32
    )
    picked = jnp.sum(logits * onehot, 1)
    loss_local = jnp.sum((log_norm - picked) * keep_mask)
    probs = jnp.exp(logits - log_norm[:, None])
    d_logits = ((probs - onehot) * (keep_mask / pixel_total)[:, None]).astype(jnp.bfloat16)
    d_head = outer_sum(final, d_logits)
    grad_res, gain_final, shift_final = norm_back(
        resid, norm_params[tail + 2], norm_params[tail + 3], back_product(d_logits, head_low)
    )
    pad = -d_head.size % (8 * LANES)
    plans = [plan_sum(jnp.pad(d_head.reshape(-1), (0, pad)).reshape(-1, LANES))]
    early = []
    kernel_grads = [None] * BLOCKS
    gain_grads = []
    phases = len(bit_order())
    for layer_at in reversed(range(BLOCKS)):
        attn_units, mlp_units = layers[layer_at]
        at = 6 * layer_at
        entry, attn_kept, middle, mlp_kept, w_up = kept_all[layer_at]
        grad_res, mlp_grads, kernel_grads[layer_at], mlp_gains, *ridden_out = mlp_backward(
            grad_res, middle, norm_params[at + 4 : at + 6], w_up, *mlp_units, kernels, layer_at,
            stacks, real_rows, mlp_kept, plans, 2 + layer_at,
        )
        plans = [plan_units(mlp_grads, 0, SPLIT)]
        if layer_at + 1 == BLOCKS:
            head_total = ridden_out[0].reshape(-1)[: d_head.size].reshape(d_head.shape)
        else:
            early.insert(0, ridden_out[1])
            plans.append(plan_units(ridden_out[0], SPLIT, phases))
        grad_res, attn_grads, attn_gains, *ridden_out = attention_backward(
            grad_res, entry, norm_params[at : at + 4], *attn_units, bias, attn_kept, plans, 2 + BLOCKS + layer_at
        )
        if layer_at + 1 < BLOCKS:
            early.insert(0, ridden_out[1])
        plans = [plan_units(attn_grads, 0, SPLIT), plan_units(ridden_out[0], SPLIT, phases)]
        gain_grads = [attn_gains, mlp_gains] + gain_grads
    part = ridden_out[0]
    first_grad, embed_gains = embed_backward(
        grad_res, embed_pre, norm_params[tail : tail + 2], patches, patch_halo, kernel_grads
    )
    early = jnp.concatenate(early, 0)
    final_gains = jnp.stack([gain_final, shift_final])
    smalls = gain_grads + [embed_gains, final_gains, jnp.full((1, C), loss_local)]
    row_ids = jnp.arange(slot_rows * n_tok, dtype=jnp.int32)
    matches = slot_of[None, :] == row_ids[:, None]
    unit_at = jnp.where(jnp.any(matches, 1), jnp.argmax(matches, 1), n_unit)
    owned, small = tail_exchange(unit_at, early, part, [first_grad, attn_grads], smalls, n_tok)
    owned = owned.transpose(1, 0, 2, 3).astype(jnp.float32).reshape(slot_rows, columns)
    norm_rows_all = norm_params.shape[0]
    norm_total, loss_sum = (small[:norm_rows_all], small[norm_rows_all, 0])
    slot_m, slot_v, slot_w = adamw_step(
        slot_weight, slot_moment, slot_second, owned, RATE_MATRIX, DECAY_RATE
    )
    norm_m, norm_v, norm_w = adamw_step(
        norm_params, norm_moment, norm_second, norm_total, RATE_VECTOR, 0.0
    )
    head_m, head_v, head_w = adamw_step(
        head_weight, head_moment, head_second, head_total, RATE_MATRIX, DECAY_RATE
    )
    return (
        loss_sum,
        pixel_total,
        slot_m,
        slot_v,
        slot_w,
        norm_m,
        norm_v,
        norm_w,
        head_m,
        head_v,
        head_w,
    )


def solution(mesh):
    in_specs = (
        P(("grp", "tok"), None),
        P(("grp", "tok")),
        P(("grp", "tok")),
        P("grp", None),
        P(),
        P("tok", "grp"),
        P("tok", "grp"),
        P("tok", "grp"),
        P(),
        P(),
        P(),
        P(),
        P(),
        P(),
    )
    out_specs = (
        P(),
        P(),
        P("tok", "grp"),
        P("tok", "grp"),
        P("tok", "grp"),
        P(),
        P(),
        P(),
        P(),
        P(),
        P(),
    )
    return jax.shard_map(body, mesh=mesh, in_specs=in_specs, out_specs=out_specs, check_vma=False)
```

time: 817 us -> 494 us (0.60)
  waiting for transfers between devices: 206 us -> 8.82 us
  Pallas kernels: 303 us -> 403 us
  local copies, waits for them, and re-layouts: 117 us -> 26.8 us
  starting transfers between devices: 84.5 us -> 0.08 us
  other arithmetic: 67.5 us -> 31.2 us
    pallas_call x12 -> x16, Pallas kernels: 303 us -> 403 us  [the longest x3 98 us: mlp_backward(): pl.pallas_call(ridden(mlp_backward_kernel, 12, 4, 9, FF // block, plans),...]
    ppermute x52 -> x0, waiting for transfers between devices: 96.3 us -> none  [the longest x50 96.3 us: swap(): return lax.ppermute(values, axis, [(i, i ^ bit) for i in range(count)])]
    all_gather x3 -> x2, waiting for transfers between devices: 100 us -> 8.79 us  [the longest x1 8.79 us: body(): last_mlp = lax.all_gather(later[6:], BOTH, axis=1, tiled=True)]
    ppermute x52 -> x0, starting transfers between devices: 64.4 us -> none  [the longest x50 60.3 us: swap(): return lax.ppermute(values, axis, [(i, i ^ bit) for i in range(count)])]
    squeeze x43 -> x0, local copies, waits for them, and re-layouts: 32.6 us -> none  [the longest x31 12.1 us: begin(): lax.dynamic_index_in_dim(self.values, 1 - mine, dim, keepdims=False)]
    all_to_all x2 -> x0, starting transfers between devices: 20 us -> none  [the longest x1 12.7 us: body(): lax.all_to_all(placed, 'tok', split_axis=0, concat_axis=1, tiled=True)]
    another operation x27 -> x0, local copies, waits for them, and re-layouts: 17.5 us -> none  [the longest x3 6.88 us: body(): mlp_chain = Chain(jnp.stack([d_up.reshape(-1, C), d_down]))]
    ppermute x10 -> x0, local copies, waits for them, and re-layouts: 13.1 us -> none  [swap(): return lax.ppermute(values, axis, [(i, i ^ bit) for i in range(count)])]
  transfers between devices with their start and end apart: 57 -> 2, of which waited for: 28 -> 1; matrix products, arithmetic and copies ran while one was open for 18% -> 3% of each run, Pallas kernels for 22% -> 21%
where the time goes in v4:
time: 494 us; the launch traced here: 489 us
  Pallas kernels  403 us (82%)
  other arithmetic  31.2 us (6%)
  local copies, waits for them, and re-layouts  26.8 us (5%)
  between operations  16.4 us (3%)
  waiting for transfers between devices  8.82 us (2%)
    pallas_call x3, Pallas kernels, mlp_backward(): pl.pallas_call(ridden(mlp_backward_kernel, 12, 4, 9, FF // block, plans),...  98 us
    pallas_call x3, Pallas kernels, mlp_forward(): pl.pallas_call(body_of, grid=(FF // block,), out_shape=(jax.ShapeDtypeStr...  80 us
    pallas_call x3, Pallas kernels, attention_backward(): pl.pallas_call(run, grid=(1,), out_shape=shapes + tuple((plan.out for pla...  74.2 us
    pallas_call x1, Pallas kernels, start_exchange(): pl.pallas_call(start_kernel, out_shape=(jax.ShapeDtypeStruct(full_shape,...  58.8 us
    pallas_call x1, Pallas kernels, tail_exchange(): pl.pallas_call(lambda *refs: tail_kernel(counts, rows, *refs), out_shape=...  44.8 us
    pallas_call x3, Pallas kernels, attention_forward(): pl.pallas_call(attention_forward_kernel, grid=(1,), out_shape=shapes, in_...  32.1 us
  transfers between devices with their start and end apart: 2, of which 1 were waited for; matrix products, arithmetic and copies ran while one was open for 3% of the time, Pallas kernels for 21%

profile of v4, /device:TPU:1, one launch (start us, length us, event | category | flops | bytes accessed | tf_op | source)
XLA Modules:
  0.0 489.5 jit_solution(13383044411057852284)
XLA Ops:
  7.2 1.3 fusion.75
  8.6 0.9 convert_reduce_fusion
  9.5 1.2 multiply_add_fusion.5.slot_ref
  10.6 1.4 convert_element_type.65
  12.1 0.5 reshape.288
  12.6 0.8 copy.77
  14.8 0.6 convert_reduce_fusion.1
  15.4 0.6 pad_add_fusion.1.mark_ref
  16.0 1.2 broadcast_in_dim.42.count_ref
  17.2 58.8 %start_exchange.1 = (bf16[5,2,2,2,2,2,40,320]{7,6,5,4,3,2,1,0:T(8,128)(2,1)}, bf16[8,40,320]{2,1,0:T(8,128)(2,1)}, f32[8,128]{1,0:T(8,128)}, bf16[192,1152]{1,0:T(8,128)(2,1)}, s32[2,192]{1,0:T(2,128)}) custom-call(s32[13]{0:T(128)} %multiply_add_fusion.5.slot_ref, bf16[8,2,40,320]{3,2,1,0:T(8,128)(2,1)} %bitcast.38, f32[8,128]{1,0:T(8,128)} %broadcast_in_dim.42.count_ref, ...), custom_call_target="tpu_custom_call" | custom-call | tf_op jit(solution)/shard_map/start_exchange/pallas_call | solution.py:1065
  76.1 1.6 slice.101
  77.7 1.5 slice.106
  79.2 0.6 fusion.72
  79.9 0.6 fusion.73
  80.9 1.4 fusion.71
  82.4 1.3 fusion.refs_5_.upper_ref.refs_6_
  84.2 1.1 compare_select_fusion.bias_ref.refs_5_
  85.3 1.2 compare_convert_fusion.refs_6_.lower_ref.refs_7_
  86.5 7.9 %embed_forward.1 = (f32[1216,320]{1,0:T(8,128)}, f32[1216,320]{1,0:T(8,128)}, f32[3,9,1280]{2,1,0:T(8,128)}) custom-call(bf16[1024,1152]{1,0:T(8,128)(2,1)} %patches_ref.3, bf16[192,1152]{1,0:T(8,128)(2,1)} %get-tuple-element.97.halo_ref, bf16[5,1280,320]{2,1,0:T(8,128)(2,1)} %bitcast.29, f32[2,320]{1,0:T(2,128)} %get-tuple-element.238.gains_ref), custom_call_target="tpu_custom_call" | custom-call | flops 1000000000 | bytes 8000000 | tf_op jit(solution)/shard_map/embed_forward/pallas_call | solution.py:678
  94.4 10.7 %attention_forward.3 = (f32[1216,320]{1,0:T(8,128)}, bf16[1216,320]{1,0:T(8,128)(2,1)}, bf16[1216,384]{1,0:T(8,128)(2,1)}, f32[304,320]{1,0:T(8,128)}, bf16[304,...) custom-call(f32[1216,320]{1,0:T(8,128)} %get-tuple-element.99.resid_ref.re, ...), custom_call_target="tpu_custom_call" | custom-call | flops 6000000000 | bytes 14000000 | tf_op jit(solution)/shard_map/attention_forward/pallas_call | solution.py:626
  105.1 0.8 broadcast_in_dim.47.refs_7_.real_ref.refs_8_
  105.9 33.1 %mlp_forward.3 = (f32[1216,320]{1,0:T(8,128)}, bf16[1216,1280]{1,0:T(8,128)(2,1)}, bf16[1216,1280]{1,0:T(8,128)(2,1)}, bf16[1216,1280]{1,0:T(8,128)(2,1)}, bf16[...) custom-call(f32[1216,320]{1,0:T(8,128)} %get-tuple-element.100.refs_0_.refs_1_, ...), custom_call_target="tpu_custom_call" | custom-call | flops 14000000000 | bytes 18000000 | tf_op jit(solution)/shard_map/mlp_forward/pallas_call | solution.py:331
  139.3 1.2 slice.111
  140.5 0.9 copy.68
  141.4 0.9 copy.69
  142.3 0.9 copy.71
  143.3 0.8 iota_reduce_fusion
  144.6 10.7 %attention_forward.4 = (f32[1216,320]{1,0:T(8,128)}, bf16[1216,320]{1,0:T(8,128)(2,1)}, bf16[1216,384]{1,0:T(8,128)(2,1)}, f32[304,320]{1,0:T(8,128)}, bf16[304,...) custom-call(f32[1216,320]{1,0:T(8,128)} %get-tuple-element.103.resid_ref.r, ...), custom_call_target="tpu_custom_call" | custom-call | flops 6000000000 | bytes 14000000 | tf_op jit(solution)/shard_map/attention_forward/pallas_call | solution.py:626
  155.3 28.7 %mlp_forward.4 = (f32[1216,320]{1,0:T(8,128)}, bf16[1216,1280]{1,0:T(8,128)(2,1)}, bf16[1216,1280]{1,0:T(8,128)(2,1)}, bf16[1216,1280]{1,0:T(8,128)(2,1)}, bf16[...) custom-call(f32[1216,320]{1,0:T(8,128)} %get-tuple-element.104.refs_0_.refs_1_, ...), custom_call_target="tpu_custom_call" | custom-call | flops 14000000000 | bytes 18000000 | tf_op jit(solution)/shard_map/mlp_forward/pallas_call | solution.py:331
  184.1 10.7 %attention_forward.5 = (f32[1216,320]{1,0:T(8,128)}, bf16[1216,320]{1,0:T(8,128)(2,1)}, bf16[1216,384]{1,0:T(8,128)(2,1)}, f32[304,320]{1,0:T(8,128)}, bf16[304,...) custom-call(f32[1216,320]{1,0:T(8,128)} %get-tuple-element.105.resid_ref.r, ...), custom_call_target="tpu_custom_call" | custom-call | flops 6000000000 | bytes 14000000 | tf_op jit(solution)/shard_map/attention_forward/pallas_call | solution.py:626
  194.8 8.8 %all-gather.5.cloned.1.call-done.up_ref.down_ref.refs_4_ = bf16[2,1280,320]{2,1,0:T(8,128)(2,1)} async-done(((bf16[2,40,320]{2,1,0:T(8,128)(2,1)}), bf16[2,1280,320]{2,1,0:T(8,128)(2,1)}) %all-gather.5.cloned.1.call-update) | async-done | bytes 1638416 | tf_op jit(solution)/shard_map/all_gather | solution.py:1365
  203.6 18.2 %mlp_forward.5 = (f32[1216,320]{1,0:T(8,128)}, bf16[1216,1280]{1,0:T(8,128)(2,1)}, bf16[1216,1280]{1,0:T(8,128)(2,1)}, bf16[1216,1280]{1,0:T(8,128)(2,1)}, bf16[320,1280]{1,0:T(8,128)(2,1)}) custom-call(f32[1216,320]{1,0:T(8,128)} %get-tuple-element.108.middle_ref.refs_1_, f32[2,320]{1,0:T(2,128)} %get-tuple-element.235.gains_ref.refs_2_, ...), custom_call_target="tpu_custom_call" | custom-call | flops 14000000000 | bytes 18000000 | tf_op jit(solution)/shard_map/mlp_forward/pallas_call | solution.py:331
  221.8 1.9 reduce_sum.99
  224.4 0.6 copy-done.17
  225.4 0.6 fusion.76
  226.2 1.3 multiply_reduce_fusion.3
  227.4 1.8 fusion.77
  229.3 1.2 fusion.66
  230.5 1.9 copy.64
  232.4 2.3 multiply_reduce_fusion
  235.1 0.7 pad_bitcast_fusion.refs_12_
  235.8 2.3 fusion.70
  238.1 0.6 pad_maximum_fusion.1.refs_12_
  238.6 1.5 broadcast_add_fusion.refs_0_
  240.1 35.5 %mlp_backward.3 = (f32[1216,320]{1,0:T(8,128)}, bf16[2,1280,320]{2,1,0:T(8,128)(2,1)}, f32[9,1280]{1,0:T(8,128)}, f32[2,320]{1,0:T(2,128)}, f32[376,128]{1,0:T(8,128)}) custom-call(f32[1216,320]{1,0:T(8,128)} %broadcast_add_fusion.refs_0_, f32[1216,320]{1,0:T(8,128)} %get-tuple-element.108.middle_ref.refs_1_, f32[2,320]{1,0:T(2,128)} %get-tuple-element.235.gains_ref.refs_2_, ...), custom_call_target="tpu_custom_call" | custom-call | flops 17999998976 | bytes 18000000 | tf_op jit(solution)/shard_map/mlp_backward/pallas_call | solution.py:454
  275.6 24.7 %attention_backward.3 = (f32[1216,320]{1,0:T(8,128)}, bf16[2,1280,320]{2,1,0:T(8,128)(2,1)}, f32[4,320]{1,0:T(4,128)}, bf16[2,2,2,1,40,320]{5,4,3,2,1,0:T(8,128)(2,1)}) custom-call(f32[1216,320]{1,0:T(8,128)} %get-tuple-element.116.refs_0_, f32[1216,320]{1,0:T(8,128)} %get-tuple-element.105.resid_ref.refs_1_, f32[4,320]{1,0:T(4,128)} %get-tuple-element.239.gains_ref.refs_2_, ...), custom_call_target="tpu_custom_call" | custom-call | flops 12000000000 | bytes 18000000 | tf_op jit(solution)/shard_map/attention_backward/pallas_call | solution.py:872
  300.3 30.5 %mlp_backward.4 = (f32[1216,320]{1,0:T(8,128)}, bf16[2,1280,320]{2,1,0:T(8,128)(2,1)}, f32[9,1280]{1,0:T(8,128)}, f32[2,320]{1,0:T(2,128)}, bf16[2,2,2,1,40,320]...) custom-call(f32[1216,320]{1,0:T(8,128)} %get-tuple-element.125.refs_0_, f32[1216,320]{1,0:T(8,128)} %get-tuple-element.104.refs_0_.refs_1_, ...), custom_call_target="tpu_custom_call" | custom-call | flops 17999998976 | bytes 18000000 | tf_op jit(solution)/shard_map/mlp_backward/pallas_call | solution.py:454
  330.9 23.7 %attention_backward.4 = (f32[1216,320]{1,0:T(8,128)}, bf16[2,1280,320]{2,1,0:T(8,128)(2,1)}, f32[4,320]{1,0:T(4,128)}, bf16[2,2,2,1,40,320]{5,4,3,2,1,0:T(8,128)(2,1)}, bf16[2,40,320]{2,1,0:T(8,128)(2,1)}) custom-call(f32[1216,320]{1,0:T(8,128)} %get-tuple-element.132.refs_0_, f32[1216,320]{1,0:T(8,128)} %get-tuple-element.103.resid_ref.refs_1_, ...), custom_call_target="tpu_custom_call" | custom-call | flops 12000000000 | bytes 18000000 | tf_op jit(solution)/shard_map/attention_backward/pallas_call | solution.py:872
  354.6 32.0 %mlp_backward.5 = (f32[1216,320]{1,0:T(8,128)}, bf16[2,1280,320]{2,1,0:T(8,128)(2,1)}, f32[9,1280]{1,0:T(8,128)}, f32[2,320]{1,0:T(2,128)}, bf16[2,2,2,1,40,320]...) custom-call(f32[1216,320]{1,0:T(8,128)} %get-tuple-element.142.refs_0_, f32[1216,320]{1,0:T(8,128)} %get-tuple-element.100.refs_0_.refs_1_, ...), custom_call_target="tpu_custom_call" | custom-call | flops 17999998976 | bytes 18000000 | tf_op jit(solution)/shard_map/mlp_backward/pallas_call | solution.py:454
  386.6 25.7 %attention_backward.5 = (f32[1216,320]{1,0:T(8,128)}, bf16[2,1280,320]{2,1,0:T(8,128)(2,1)}, f32[4,320]{1,0:T(4,128)}, bf16[2,2,2,1,40,320]{5,4,3,2,1,0:T(8,128)(2,1)}, bf16[2,40,320]{2,1,0:T(8,128)(2,1)}) custom-call(f32[1216,320]{1,0:T(8,128)} %get-tuple-element.149.refs_0_, f32[1216,320]{1,0:T(8,128)} %get-tuple-element.99.resid_ref.refs_1_, ...), custom_call_target="tpu_custom_call" | custom-call | flops 12000000000 | bytes 18000000 | tf_op jit(solution)/shard_map/attention_backward/pallas_call | solution.py:872
  412.4 1.6 pad_maximum_fusion.refs_1_
  414.0 6.7 %embed_backward.1 = (bf16[1,1280,320]{2,1,0:T(8,128)(2,1)}, f32[2,320]{1,0:T(2,128)}) custom-call(f32[1216,320]{1,0:T(8,128)} %get-tuple-element.164.grad_ref, f32[1216,320]{1,0:T(8,128)} %get-tuple-element.165.pre_ref, f32[2,320]{1,0:T(2,128)} %get-tuple-element.238.gains_ref, bf16[1024,1152]{1,0:T(8,128)(2,1)} %patches_ref.3, ...), custom_call_target="tpu_custom_call" | custom-call | flops 1000000000 | bytes 8000000 | tf_op jit(solution)/shard_map/embed_backward/pallas_call | solution.py:741
  420.7 1.2 broadcast_in_dim.50.refs_13_
  421.8 44.8 %tail_exchange.1 = (bf16[8,2,40,320]{3,2,1,0:T(8,128)(2,1)}, f32[24,320]{1,0:T(8,128)}) custom-call(s32[16]{0:T(128)} %broadcast_select_fusion.1.refs_0_, bf16[8,40,320]{2,1,0:T(8,128)(2,1)} %pad_maximum_fusion.refs_1_, bf16[2,2,2,1,40,320]{5,4,3,2,1,0:T(8,128)(2,1)} %get-tuple-element.163.refs_2_, bf16[1,16,2,1,40,320]{5,4,3,2,1,0:T(8,128)(2,1)} %bitcast.39, ...), custom_call_target="tpu_custom_call" | custom-call | tf_op jit(solution)/shard_map/tail_exchange/pallas_call | solution.py:1298
  466.7 1.1 convert_bitcast_fusion
  467.9 0.8 reshape.308
  468.7 1.2 slice.112
  469.9 1.1 reshape.306
  471.1 2.0 multiply_subtract_fusion.1
  473.1 1.9 copy.72
  475.0 0.8 copy.73
  475.8 0.8 copy.74
  476.6 0.7 multiply_subtract_fusion.2
  477.3 4.8 multiply_subtract_fusion
  (105 shorter events, 3.8 us)
Async XLA Ops:
  7.2 7.6 %copy-start.22 = (s32[1024]{0:T(1024)S(1)}, s32[1024]{0:T(1024)}, u32[]{:S(2)}) copy-start(s32[1024]{0:T(1024)} %param.20) | copy-start | bytes 12292
  7.2 8.2 %copy-start.26 = (s32[1024]{0:T(1024)S(1)}, s32[1024]{0:T(1024)}, u32[]{:S(2)}) copy-start(s32[1024]{0:T(1024)} %param.19) | copy-start | bytes 12292
  7.2 137.4 %all-gather.3.cloned.1.call-start = ((), (), s32[]{:S(2)}) async-start(), calls=%async_computation | async-start | bytes 4055040 | tf_op jit(solution)/shard_map/all_gather | solution.py:1363
  13.5 65.8 %copy-start.12 = (f32[22,320]{1,0:T(8,128)S(1)}, f32[22,320]{1,0:T(8,128)}, u32[]{:S(2)}) copy-start(f32[22,320]{1,0:T(8,128)} %param.26) | copy-start | bytes 84484
  13.5 67.2 %copy-start.30 = (s32[4,3]{1,0:T(4,128)S(1)}, s32[4,3]{1,0:T(4,128)}, u32[]{:S(2)}) copy-start(s32[4,3]{1,0:T(4,128)} %constant.168) | copy-start | bytes 148
  13.5 67.2 %copy-start.31 = (s32[4,3]{1,0:T(4,128)S(1)}, s32[4,3]{1,0:T(4,128)}, u32[]{:S(2)}) copy-start(s32[4,3]{1,0:T(4,128)} %constant.169) | copy-start | bytes 148
  76.1 7.7 %copy-start.32 = (s32[2,192]{1,0:T(2,128)S(1)}, s32[2,192]{1,0:T(2,128)}, u32[]{:S(2)}) copy-start(s32[2,192]{1,0:T(2,128)} %get-tuple-element.110) | copy-start | bytes 4612
  76.1 8.1 %copy-start.28 = (s32[10,128]{1,0:T(8,128)S(1)}, s32[10,128]{1,0:T(8,128)}, u32[]{:S(2)}) copy-start(s32[10,128]{1,0:T(8,128)} %constant.166) | copy-start | bytes 15364
  76.1 8.1 %copy-start.29 = (s32[10,128]{1,0:T(8,128)S(1)}, s32[10,128]{1,0:T(8,128)}, u32[]{:S(2)}) copy-start(s32[10,128]{1,0:T(8,128)} %constant.167) | copy-start | bytes 15364
  77.7 125.9 %all-gather.5.cloned.1.call-start = ((), (), s32[]{:S(2)}) async-start(), calls=%async_computation.1 | async-start | bytes 2027520 | tf_op jit(solution)/shard_map/all_gather | solution.py:1365
  105.9 34.6 %copy-start.9 = (f32[320,150]{0,1:T(8,128)S(1)}, f32[320,150]{0,1:T(8,128)}, u32[]{:S(2)}) copy-start(f32[320,150]{0,1:T(8,128)} %param.30) | copy-start | bytes 576004
  105.9 35.5 %copy-start.10 = (f32[320,150]{0,1:T(8,128)S(1)}, f32[320,150]{0,1:T(8,128)}, u32[]{:S(2)}) copy-start(f32[320,150]{0,1:T(8,128)} %param.31) | copy-start | bytes 576004
  105.9 36.4 %copy-start.2 = (f32[320,150]{0,1:T(8,128)S(1)}, f32[320,150]{0,1:T(8,128)}, u32[]{:S(2)}) copy-start(f32[320,150]{0,1:T(8,128)} %param.29) | copy-start | bytes 576004
  105.9 37.2 %copy-start.33 = (s32[13]{0:T(128)S(1)}, s32[13]{0:T(128)}, u32[]{:S(2)}) copy-start(s32[13]{0:T(128)} %multiply_add_fusion.5.slot_ref) | copy-start | bytes 160
  139.1 86.8 %copy-start.15 = (s32[1216]{0:T(1024)}, s32[1216]{0:T(1024)S(1)}, u32[]{:S(2)}) copy-start(s32[1216]{0:T(1024)S(1)} %eq.114) | copy-start | bytes 14596
  221.8 2.1 copy-start
  224.3 0.6 copy-start.17
  224.4 1.6 copy-start.13
  225.3 2.1 copy-start.3
  226.2 3.1 copy-start.16
  232.4 2.3 copy-start.27
  232.4 2.3 copy-start.8
  232.4 3.3 copy-start.18
  232.4 3.4 copy-start.14
  386.6 25.8 %copy-start.19 = (bf16[2,40,320]{2,1,0:T(8,128)(2,1)S(1)}, bf16[2,40,320]{2,1,0:T(8,128)(2,1)}, u32[]{:S(2)}) copy-start(bf16[2,40,320]{2,1,0:T(8,128)(2,1)} %get-tuple-element.162) | copy-start | bytes 153604
  386.6 25.8 %copy-start.20 = (bf16[2,40,320]{2,1,0:T(8,128)(2,1)S(1)}, bf16[2,40,320]{2,1,0:T(8,128)(2,1)}, u32[]{:S(2)}) copy-start(bf16[2,40,320]{2,1,0:T(8,128)(2,1)} %get-tuple-element.161) | copy-start | bytes 153604
  386.6 25.8 %copy-start.21 = (bf16[2,40,320]{2,1,0:T(8,128)(2,1)S(1)}, bf16[2,40,320]{2,1,0:T(8,128)(2,1)}, u32[]{:S(2)}) copy-start(bf16[2,40,320]{2,1,0:T(8,128)(2,1)} %get-tuple-element.160) | copy-start | bytes 153604
  467.8 2.1 copy-start.11
  467.8 3.2 copy-start.4
  467.8 3.2 copy-start.5
  467.8 3.2 copy-start.6
  471.0 5.6 %copy-start.23 = (f32[22,320]{1,0:T(8,128)S(1)}, f32[22,320]{1,0:T(8,128)}, u32[]{:S(2)}) copy-start(f32[22,320]{1,0:T(8,128)} %param.28) | copy-start | bytes 84484
  471.0 5.6 %copy-start.24 = (f32[22,320]{1,0:T(8,128)S(1)}, f32[22,320]{1,0:T(8,128)}, u32[]{:S(2)}) copy-start(f32[22,320]{1,0:T(8,128)} %param.27) | copy-start | bytes 84484
  471.0 5.6 %copy-start.25 = (f32[24,320]{1,0:T(8,128)S(1)}, f32[24,320]{1,0:T(8,128)}, u32[]{:S(2)}) copy-start(f32[24,320]{1,0:T(8,128)} %get-tuple-element.178) | copy-start | bytes 92164
  471.0 6.2 %copy-start.1 = (f32[2,102400]{1,0:T(2,128)S(1)}, f32[2,102400]{1,0:T(2,128)}, u32[]{:S(2)}) copy-start(f32[2,102400]{1,0:T(2,128)} %param.23) | copy-start | bytes 2457604
  473.1 4.2 copy-start.7
Sparse Core Ops, SparseCore 0:
  77.8 66.4 all-gather.2
  147.8 55.7 all-gather.4

commit v5 on v4

--- a/solution.py
+++ b/solution.py
@@ -162,7 +162,6 @@
 
 
 def mlp_forward_kernel(
-    advance,
     middle_ref, gains_ref, up_ref, down_ref, kern_ref, upper_ref, lower_ref, real_ref,
     out_ref, hidden_ref, active_ref, slope_ref, turned_ref,
     normed_ref, moved_ref, planes_ref,
@@ -183,7 +182,6 @@
                 begin = quarter * C + lane
                 turned_ref[:, begin : begin + width] = part.astype(jnp.bfloat16)
 
-    advance()
     for sub in range(4):
         columns = pl.ds(pl.multiple_of(pl.program_id(0) * block, block), block)
         part = product(normed_ref[sub * tiles : (sub + 1) * tiles, :], turned_ref[:, columns])
@@ -233,8 +231,9 @@
         self.out_spec = pl.BlockSpec(memory_space=space) if space is not None else whole(out.shape)
 
 
-def plan_sum(value):
-    return Plan(value, jax.ShapeDtypeStruct(value.shape, value.dtype), sum_scratch(value.shape), SumRide)
+def plan_sum(value, begin, end):
+    make = functools.partial(SumRide, begin=begin, end=end)
+    return Plan(value, jax.ShapeDtypeStruct(value.shape, value.dtype), sum_scratch(value.shape), make)
 
 
 def plan_units(value, begin, end):
@@ -249,13 +248,6 @@
         return UnitRide(sources, ride_out, scratch, begin, end)
 
     return Plan(value, out, unit_scratch(total, chunk, width, begin, end), make)
-
-
-def plan_gather(piece):
-    total, chunk, width = piece.shape
-    out = jax.ShapeDtypeStruct((total,) + (2,) * len(bit_order()) + (chunk, width), piece.dtype)
-    scratch = gather_scratch(total) + [pltpu.VMEM(out.shape, piece.dtype), pltpu.SemaphoreType.DMA((1,))]
-    return Plan(piece, out, scratch, PieceRide, pl.ANY)
 
 
 class Rides:
@@ -318,18 +310,13 @@
     return pl.BlockSpec((1, FF, C), lambda j: (at, 0, 0))
 
 
-def mlp_forward(middle, gains, units, at, kernel, layer_at, stacks, real_rows, plans, meeting):
+def mlp_forward(middle, gains, units, at, kernel, layer_at, stacks, real_rows):
     rows = middle.shape[0]
     block = 256
     by_lane = pl.BlockSpec((rows, block), lambda j: (0, j))
     low = jax.ShapeDtypeStruct((rows, FF), jnp.bfloat16)
-    body_of = functools.partial(mlp_forward_kernel, lambda: None)
-    limits = dict(vmem_limit_bytes=VMEM_LIMIT)
-    if plans:
-        body_of = ridden(mlp_forward_kernel, 8, 5, 3, FF // block, plans)
-        limits.update(collective_id=meeting, has_side_effects=True)
     return pl.pallas_call(
-        body_of,
+        mlp_forward_kernel,
         grid=(FF // block,),
         out_shape=(
             jax.ShapeDtypeStruct((rows, C), jnp.float32),
@@ -337,7 +324,6 @@
             low,
             low,
             jax.ShapeDtypeStruct((C, FF), jnp.bfloat16),
-            *[plan.out for plan in plans],
         ),
         in_specs=[
             whole((rows, C)),
@@ -348,20 +334,17 @@
             whole(stacks[0].shape),
             whole(stacks[1].shape),
             whole(real_rows.shape),
-        ]
-        + [plan.in_spec for plan in plans],
-        out_specs=(whole((rows, C)), by_lane, by_lane, by_lane, whole((C, FF)))
-        + tuple(plan.out_spec for plan in plans),
+        ],
+        out_specs=(whole((rows, C)), by_lane, by_lane, by_lane, whole((C, FF))),
         scratch_shapes=[
             pltpu.VMEM((rows, C), jnp.bfloat16),
             pltpu.VMEM((4, 3, rows // 4, block), jnp.float32),
             pltpu.VMEM((3, FF, LANES), jnp.float32),
-        ]
-        + sum([plan.scratch for plan in plans], []),
-        compiler_params=pltpu.CompilerParams(**limits),
+        ],
+        compiler_params=pltpu.CompilerParams(vmem_limit_bytes=VMEM_LIMIT),
         cost_estimate=pl.CostEstimate(flops=14 * 10**9, bytes_accessed=18 * 10**6, transcendentals=4 * 10**6),
         name="mlp_forward",
-    )(middle, gains, units, units, kernel, stacks[0], stacks[1], real_rows, *[plan.value for plan in plans])
+    )(middle, gains, units, units, kernel, stacks[0], stacks[1], real_rows)
 
 
 def mlp_backward_kernel(
@@ -755,6 +738,70 @@
     )(*operands)
 
 
+def head_kernel(
+    resid_ref, gains_ref, weight_ref, label_ref, keep_ref, total_ref,
+    grad_ref, dhead_ref, dgain_ref, loss_ref,
+    final_ref, turned_ref,
+):
+    rows = resid_ref.shape[0]
+    tiles = rows // 4
+    classes = weight_ref.shape[1]
+    low = weight_ref[...].astype(jnp.bfloat16)
+    share = 1.0 / total_ref[0:1, 0:1]
+    sums = [jnp.zeros((1, C), jnp.float32)] * 2
+    loss = jnp.zeros((1, 1), jnp.float32)
+    for sub in range(4):
+        span = slice(sub * tiles, (sub + 1) * tiles)
+        unit, inverse, final = norm_rows(resid_ref[span, :], gains_ref[0:1, :], gains_ref[1:2, :])
+        final = final.astype(jnp.bfloat16)
+        final_ref[span, :] = final
+        logits = product(final, low)
+        peak = jnp.max(logits, -1, keepdims=True)
+        log_norm = peak + jnp.log(jnp.sum(jnp.exp(logits - peak), -1, keepdims=True))
+        keep = keep_ref[span, :]
+        hit = lax.broadcasted_iota(jnp.int32, (tiles, classes), 1) == label_ref[span, :]
+        picked = jnp.sum(jnp.where(hit, logits, 0.0), -1, keepdims=True)
+        loss = loss + jnp.sum((log_norm - picked) * keep, 0, keepdims=True)
+        dlogits = (jnp.exp(logits - log_norm) - jnp.where(hit, 1.0, 0.0)) * (keep * share)
+        turned_ref[:, span] = dlogits.T.astype(jnp.bfloat16)
+        grad = back_product(dlogits.astype(jnp.bfloat16), low)
+        grad_ref[span, :] = norm_rows_back(unit, inverse, gains_ref[0:1, :], grad)
+        sums[0] = sums[0] + jnp.sum(grad * unit, 0, keepdims=True)
+        sums[1] = sums[1] + jnp.sum(grad, 0, keepdims=True)
+    dhead_ref[:classes, :] = product(turned_ref[...], final_ref[...])
+    dhead_ref[classes:, :] = jnp.zeros((dhead_ref.shape[0] - classes, C), jnp.float32)
+    dgain_ref[0:1, :] = sums[0]
+    dgain_ref[1:2, :] = sums[1]
+    loss_ref[...] = jnp.broadcast_to(loss, (1, C))
+
+
+def head_step(resid, gains, weight, labels, keep, total):
+    rows = resid.shape[0]
+    classes = weight.shape[1]
+    wide = jnp.float32
+    shapes = (
+        jax.ShapeDtypeStruct((rows, C), wide),
+        jax.ShapeDtypeStruct((-(-classes // 8) * 8, C), wide),
+        jax.ShapeDtypeStruct((2, C), wide),
+        jax.ShapeDtypeStruct((1, C), wide),
+    )
+    operands = (resid, gains, weight, labels, keep, total)
+    return pl.pallas_call(
+        head_kernel,
+        grid=(1,),
+        out_shape=shapes,
+        in_specs=[whole(part.shape) for part in operands],
+        out_specs=tuple(whole(shape.shape) for shape in shapes),
+        scratch_shapes=[
+            pltpu.VMEM((rows, C), jnp.bfloat16),
+            pltpu.VMEM((classes, rows), jnp.bfloat16),
+        ],
+        compiler_params=pltpu.CompilerParams(vmem_limit_bytes=VMEM_LIMIT),
+        cost_estimate=pl.CostEstimate(flops=10**9, bytes_accessed=5 * 10**6, transcendentals=10**6),
+        name="head_step",
+    )(*operands)
+
+
 def attention_backward_kernel(
     advance,
     grad_ref, resid_ref, gains_ref, unit_ref, reduce_ref, bias_ref,
@@ -1004,23 +1051,6 @@
     return [pltpu.SemaphoreType.DMA((phases * total,))] * 2
 
 
-class PieceRide(GatherRide):
-    def __init__(self, piece_ref, out_ref, scratch):
-        super().__init__(scratch[2], scratch)
-        self.piece_ref, self.out_ref = piece_ref, out_ref
-        self.out_sem = scratch[3]
-
-    def advance(self, phase):
-        if phase == 0:
-            for unit in range(self.full_ref.shape[0]):
-                self.put(unit, self.piece_ref[unit])
-        super().advance(phase)
-        if phase == self.phases:
-            copy = pltpu.make_async_copy(self.full_ref, self.out_ref, self.out_sem.at[0])
-            copy.start()
-            copy.wait()
-
-
 def start_kernel(
     slot_ref, piece_ref, count_ref, patch_ref, mark_ref,
     full_ref, later_ref, total_ref, patch_halo_ref, mark_halo_ref,
@@ -1199,9 +1229,9 @@
 
 
 class SumRide:
-    def __init__(self, source_ref, total_ref, scratch):
+    def __init__(self, source_ref, total_ref, scratch, begin=0, end=None):
         self.grp, self.tok = lax.axis_index("grp"), lax.axis_index("tok")
-        self.order = unit_order(0)
+        self.order = unit_order(0)[begin:end]
         self.names = self.order
         self.phases = len(self.order)
         self.source_ref, self.total_ref = source_ref, total_ref
@@ -1352,17 +1382,19 @@
     counted = valid_mask * (first_tok + jnp.arange(tok_dev, dtype=jnp.int32) < small_end)
     counted = jnp.full((8, LANES), jnp.sum(counted.astype(jnp.float32)))
     pieces = slot_weight.astype(jnp.bfloat16).reshape(slot_rows, n_tok, chunk, C).transpose(1, 0, 2, 3)
-    first_units = 1 + n_unit // BLOCKS
+    first_units = 1 + 2 * (n_unit // BLOCKS)
     marks = jnp.stack([labels, valid_mask])
     own, later, counted, patch_halo, mark_halo = start_exchange(
         slot_of, pieces, counted, patches, marks[:, :OVER], first_units
     )
     pixel_total = counted[0, 0]
     own = own.reshape(first_units, FF, C)
-    layers = [((own, 1, own, 2), (own, 3))]
-    units = lax.all_gather(later[:4], BOTH, axis=1, tiled=True)
-    layers.append(((units, 0, units, 1), (units, 2)))
-    last_mlp = lax.all_gather(later[6:], BOTH, axis=1, tiled=True)
+    units = lax.all_gather(later, BOTH, axis=1, tiled=True)
+    layers = [
+        ((own, 1, own, 2), (own, 3)),
+        ((own, 5, own, 6), (own, 7)),
+        ((units, 0, units, 1), (units, 2)),
+    ]
 
     window = tok_dev + OVER
     tiles = window // 4
@@ -1384,43 +1416,20 @@
     tail = 6 * BLOCKS
     embed_pre, resid, kernels = embed_forward(patches, patch_halo, own, norm_params[tail : tail + 2])
     kept_all = []
-    single = []
     for layer_at in range(BLOCKS):
-        if layer_at == len(layers):
-            layers.append(((single[0], 0, single[1], 0), (last_mlp, 0)))
         attn_units, mlp_units = layers[layer_at]
         at = 6 * layer_at
         middle, *attn_kept = attention_forward(resid, norm_params[at : at + 4], *attn_units, bias)
-        plans = []
-        if layer_at + 1 < BLOCKS:
-            plans = [plan_gather(later[4 + layer_at : 5 + layer_at])]
         output, *mlp_kept = mlp_forward(
             middle, norm_params[at + 4 : at + 6], *mlp_units, kernels, layer_at, stacks, real_rows,
-            plans, 2 + 2 * BLOCKS + layer_at,
         )
-        if plans:
-            single.append(mlp_kept.pop().reshape(1, FF, C))
         w_up = mlp_kept.pop()
         kept_all.append((resid, attn_kept, middle, mlp_kept, w_up))
         resid = output
-    final = layer_norm(resid, norm_params[tail + 2], norm_params[tail + 3]).astype(jnp.bfloat16)
-    head_low = head_weight.astype(jnp.bfloat16)
-    logits = product(final, head_low)
-    row_peak = jnp.max(logits, -1, keepdims=True)
-    log_norm = row_peak[:, 0] + jnp.log(jnp.sum(jnp.exp(logits - row_peak), -1))
-    onehot = (labels[:, None] == jnp.arange(head_weight.shape[1], dtype=jnp.int32)[None, :]).astype(
-        jnp.float32
-    )
-    picked = jnp.sum(logits * onehot, 1)
-    loss_local = jnp.sum((log_norm - picked) * keep_mask)
-    probs = jnp.exp(logits - log_norm[:, None])
-    d_logits = ((probs - onehot) * (keep_mask / pixel_total)[:, None]).astype(jnp.bfloat16)
-    d_head = outer_sum(final, d_logits)
-    grad_res, gain_final, shift_final = norm_back(
-        resid, norm_params[tail + 2], norm_params[tail + 3], back_product(d_logits, head_low)
-    )
-    pad = -d_head.size % (8 * LANES)
-    plans = [plan_sum(jnp.pad(d_head.reshape(-1), (0, pad)).reshape(-1, LANES))]
+    grad_res, d_head, final_gains, loss_row = head_step(
+        resid, norm_params[tail + 2 : tail + 4], head_weight, labels[:, None], keep_mask[:, None], counted
+    )
+    plans = [plan_sum(d_head, 0, SPLIT)]
     early = []
     kernel_grads = [None] * BLOCKS
     gain_grads = []
@@ -1435,7 +1444,7 @@
         )
         plans = [plan_units(mlp_grads, 0, SPLIT)]
         if layer_at + 1 == BLOCKS:
-            head_total = ridden_out[0].reshape(-1)[: d_head.size].reshape(d_head.shape)
+            plans.append(plan_sum(ridden_out[0], SPLIT, phases))
         else:
             early.insert(0, ridden_out[1])
             plans.append(plan_units(ridden_out[0], SPLIT, phases))
@@ -1444,6 +1453,8 @@
         )
         if layer_at + 1 < BLOCKS:
             early.insert(0, ridden_out[1])
+        else:
+            head_total = ridden_out[1][: head_weight.shape[1]].T
         plans = [plan_units(attn_grads, 0, SPLIT), plan_units(ridden_out[0], SPLIT, phases)]
         gain_grads = [attn_gains, mlp_gains] + gain_grads
     part = ridden_out[0]
@@ -1451,8 +1462,7 @@
         grad_res, embed_pre, norm_params[tail : tail + 2], patches, patch_halo, kernel_grads
     )
     early = jnp.concatenate(early, 0)
-    final_gains = jnp.stack([gain_final, shift_final])
-    smalls = gain_grads + [embed_gains, final_gains, jnp.full((1, C), loss_local)]
+    smalls = gain_grads + [embed_gains, final_gains, loss_row]
     row_ids = jnp.arange(slot_rows * n_tok, dtype=jnp.int32)
     matches = slot_of[None, :] == row_ids[:, None]
     unit_at = jnp.where(jnp.any(matches, 1), jnp.argmax(matches, 1), n_unit)

time: 494 us -> 463 us (0.937)
  local copies, waits for them, and re-layouts: 26.8 us -> 13.1 us
  other arithmetic: 31.2 us -> 19.8 us
  waiting for transfers between devices: 8.82 us -> 0.04 us
  Pallas kernels: 403 us -> 410 us
    pallas_call x1, Pallas kernels: 58.8 us -> 79.4 us  [start_exchange(): pl.pallas_call(start_kernel, out_shape=(jax.ShapeDtypeStruct(full_shape,...]
    pallas_call x3 -> x4, Pallas kernels: 80 us -> 62.9 us  [the longest x3 55.8 us: mlp_forward(): pl.pallas_call(mlp_forward_kernel, grid=(FF // block,), out_shape=(jax.Sh...]
    all_gather x2 -> x1, waiting for transfers between devices: 8.79 us -> 0.02 us  [body(): units = lax.all_gather(later, BOTH, axis=1, tiled=True)]
    reduce_sum x6 -> x0, other arithmetic: 8.36 us -> none  [the longest x2 4.15 us: layer_norm(): center = values - jnp.mean(values, -1, keepdims=True)]
    unnamed x74 -> x39, local copies, waits for them, and re-layouts: 7.07 us -> 0.98 us
  transfers between devices with their start and end apart: 2 -> 1, of which waited for: 1 -> 0; matrix products, arithmetic and copies ran while one was open for 3% -> 3% of each run, Pallas kernels for 21% -> 15%
where the time goes in v5:
time: 463 us; the launch traced here: 459 us
  Pallas kernels  410 us (89%)
  other arithmetic  19.8 us (4%)
  between operations  16.1 us (3%)
  local copies, waits for them, and re-layouts  13.1 us (3%)
    pallas_call x3, Pallas kernels, mlp_backward(): pl.pallas_call(ridden(mlp_backward_kernel, 12, 4, 9, FF // block, plans),...  97.5 us
    pallas_call x1, Pallas kernels, start_exchange(): pl.pallas_call(start_kernel, out_shape=(jax.ShapeDtypeStruct(full_shape,...  79.4 us
    pallas_call x3, Pallas kernels, attention_backward(): pl.pallas_call(run, grid=(1,), out_shape=shapes + tuple((plan.out for pla...  78.9 us
    pallas_call x3, Pallas kernels, mlp_forward(): pl.pallas_call(mlp_forward_kernel, grid=(FF // block,), out_shape=(jax.Sh...  55.8 us
    pallas_call x1, Pallas kernels, tail_exchange(): pl.pallas_call(lambda *refs: tail_kernel(counts, rows, *refs), out_shape=...  44.8 us
    pallas_call x3, Pallas kernels, attention_forward(): pl.pallas_call(attention_forward_kernel, grid=(1,), out_shape=shapes, in_...  32.2 us
  transfers between devices with their start and end apart: 1, of which 0 were waited for; matrix products, arithmetic and copies ran while one was open for 3% of the time, Pallas kernels for 15%

profile of v5, /device:TPU:1, one launch (start us, length us, event | category | flops | bytes accessed | tf_op | source)
XLA Modules:
  0.0 459.1 jit_solution(7584254050780303524)
XLA Ops:
  7.2 0.0 all-gather.2.cloned.1.call-start
  7.2 0.9 convert_reduce_fusion
  8.2 1.2 multiply_add_fusion.3.slot_ref
  9.3 1.3 fusion.68
  10.6 1.4 convert_element_type.50
  12.1 0.6 reshape.225
  12.6 0.0 copy-start.16
  12.6 0.0 copy-start.17
  12.7 0.8 copy.54
  14.8 0.6 convert_reduce_fusion.1
  15.4 0.6 pad_add_fusion.1.mark_ref
  16.0 1.2 broadcast_in_dim.36.count_ref
  17.2 79.4 %start_exchange.1 = (bf16[9,2,2,2,2,2,40,320]{7,6,5,4,3,2,1,0:T(8,128)(2,1)}, bf16[4,40,320]{2,1,0:T(8,128)(2,1)}, f32[8,128]{1,0:T(8,128)}, bf16[192,1152]{1,0:T(8,128)(2,1)}, s32[2,192]{1,0:T(2,128)}) custom-call(s32[13]{0:T(128)} %multiply_add_fusion.3.slot_ref, bf16[8,2,40,320]{3,2,1,0:T(8,128)(2,1)} %bitcast.45, f32[8,128]{1,0:T(8,128)} %broadcast_in_dim.36.count_ref, ...), custom_call_target="tpu_custom_call" | custom-call | tf_op jit(solution)/shard_map/start_exchange/pallas_call | solution.py:1095
  96.7 0.0 all-gather.2.cloned.1.call-update
  96.7 0.2 add_select_fusion.5
  96.9 0.1 add_select_fusion
  97.0 0.7 pad_add_fusion
  97.7 0.1 slice.94
  97.8 0.1 tile.10
  97.9 0.1 eq.91
  98.0 0.1 eq.95
  98.1 0.9 copy.49.weight_ref
  98.9 1.2 slice.90
  100.1 0.2 reshape.227
  100.3 0.1 copy.48
  100.5 0.1 convert_element_type.56
  100.6 1.1 copy.51.keep_ref
  101.7 1.1 broadcast_in_dim_squeeze.4.label_ref
  102.8 0.6 fusion.66
  103.4 7.9 %embed_forward.1 = (f32[1216,320]{1,0:T(8,128)}, f32[1216,320]{1,0:T(8,128)}, f32[3,9,1280]{2,1,0:T(8,128)}) custom-call(bf16[1024,1152]{1,0:T(8,128)(2,1)} %patches_ref.3, bf16[192,1152]{1,0:T(8,128)(2,1)} %get-tuple-element.100.halo_ref, bf16[9,1280,320]{2,1,0:T(8,128)(2,1)} %bitcast.29, f32[2,320]{1,0:T(2,128)} %get-tuple-element.200.gains_ref), custom_call_target="tpu_custom_call" | custom-call | flops 1000000000 | bytes 8000000 | tf_op jit(solution)/shard_map/embed_forward/pallas_call | solution.py:661
  111.4 0.1 fusion.35
  111.5 0.6 iota_reduce_fusion
  112.1 0.5 broadcast_select_fusion.1.refs_0_
  112.6 0.6 fusion.67
  113.3 1.1 compare_select_fusion.bias_ref.refs_5_
  114.3 1.2 compare_convert_fusion.lower_ref.refs_7_
  115.6 1.3 fusion.upper_ref.refs_6_
  116.9 10.7 %attention_forward.3 = (f32[1216,320]{1,0:T(8,128)}, bf16[1216,320]{1,0:T(8,128)(2,1)}, bf16[1216,384]{1,0:T(8,128)(2,1)}, f32[304,320]{1,0:T(8,128)}, bf16[304,...) custom-call(f32[1216,320]{1,0:T(8,128)} %get-tuple-element.102.resid_ref.r, ...), custom_call_target="tpu_custom_call" | custom-call | flops 6000000000 | bytes 14000000 | tf_op jit(solution)/shard_map/attention_forward/pallas_call | solution.py:609
  127.6 0.8 broadcast_in_dim.41.real_ref.refs_8_
  128.4 18.4 %mlp_forward.3 = (f32[1216,320]{1,0:T(8,128)}, bf16[1216,1280]{1,0:T(8,128)(2,1)}, bf16[1216,1280]{1,0:T(8,128)(2,1)}, bf16[1216,1280]{1,0:T(8,128)(2,1)}, bf16[320,1280]{1,0:T(8,128)(2,1)}) custom-call(f32[1216,320]{1,0:T(8,128)} %get-tuple-element.103.middle_ref.refs_1_, f32[2,320]{1,0:T(2,128)} %get-tuple-element.199.gains_ref.refs_2_, ...), custom_call_target="tpu_custom_call" | custom-call | flops 14000000000 | bytes 18000000 | tf_op jit(solution)/shard_map/mlp_forward/pallas_call | solution.py:318
  146.8 10.8 %attention_forward.4 = (f32[1216,320]{1,0:T(8,128)}, bf16[1216,320]{1,0:T(8,128)(2,1)}, bf16[1216,384]{1,0:T(8,128)(2,1)}, f32[304,320]{1,0:T(8,128)}, bf16[304,...) custom-call(f32[1216,320]{1,0:T(8,128)} %get-tuple-element.105.resid_ref.r, ...), custom_call_target="tpu_custom_call" | custom-call | flops 6000000000 | bytes 14000000 | tf_op jit(solution)/shard_map/attention_forward/pallas_call | solution.py:609
  157.6 18.9 %mlp_forward.4 = (f32[1216,320]{1,0:T(8,128)}, bf16[1216,1280]{1,0:T(8,128)(2,1)}, bf16[1216,1280]{1,0:T(8,128)(2,1)}, bf16[1216,1280]{1,0:T(8,128)(2,1)}, bf16[320,1280]{1,0:T(8,128)(2,1)}) custom-call(f32[1216,320]{1,0:T(8,128)} %get-tuple-element.106.middle_ref.refs_1_, f32[2,320]{1,0:T(2,128)} %get-tuple-element.198.gains_ref.refs_2_, ...), custom_call_target="tpu_custom_call" | custom-call | flops 14000000000 | bytes 18000000 | tf_op jit(solution)/shard_map/mlp_forward/pallas_call | solution.py:318
  176.5 0.0 all-gather.2.cloned.1.call-done.unit_ref.reduce_ref.up_ref.down_ref.refs_4_.refs_3_
  176.5 10.7 %attention_forward.5 = (f32[1216,320]{1,0:T(8,128)}, bf16[1216,320]{1,0:T(8,128)(2,1)}, bf16[1216,384]{1,0:T(8,128)(2,1)}, f32[304,320]{1,0:T(8,128)}, bf16[304,...) custom-call(f32[1216,320]{1,0:T(8,128)} %get-tuple-element.107.resid_ref.r, ...), custom_call_target="tpu_custom_call" | custom-call | flops 6000000000 | bytes 14000000 | tf_op jit(solution)/shard_map/attention_forward/pallas_call | solution.py:609
  187.2 18.5 %mlp_forward.5 = (f32[1216,320]{1,0:T(8,128)}, bf16[1216,1280]{1,0:T(8,128)(2,1)}, bf16[1216,1280]{1,0:T(8,128)(2,1)}, bf16[1216,1280]{1,0:T(8,128)(2,1)}, bf16[320,1280]{1,0:T(8,128)(2,1)}) custom-call(f32[1216,320]{1,0:T(8,128)} %get-tuple-element.109.middle_ref.refs_1_, f32[2,320]{1,0:T(2,128)} %get-tuple-element.197.gains_ref.refs_2_, ...), custom_call_target="tpu_custom_call" | custom-call | flops 14000000000 | bytes 18000000 | tf_op jit(solution)/shard_map/mlp_forward/pallas_call | solution.py:318
  205.7 7.0 %head_step.1 = (f32[1216,320]{1,0:T(8,128)}, f32[152,320]{1,0:T(8,128)}, f32[2,320]{1,0:T(2,128)}, f32[1,320]{1,0:T(1,128)}) custom-call(f32[1216,320]{1,0:T(8,128)} %get-tuple-element.110.resid_ref, f32[2,320]{1,0:T(2,128)} %get-tuple-element.196.gains_ref, f32[320,150]{1,0:T(8,128)} %copy.49.weight_ref, s32[1216,1]{1,0:T(8,128)} %broadcast_in_dim_squeeze.4.label_ref, ...), custom_call_target="tpu_custom_call" | custom-call | flops 1000000000 | bytes 5000000 | tf_op jit(solution)/shard_map/head_step/pallas_call | solution.py:789
  212.8 33.5 %mlp_backward.3 = (f32[1216,320]{1,0:T(8,128)}, bf16[2,1280,320]{2,1,0:T(8,128)(2,1)}, f32[9,1280]{1,0:T(8,128)}, f32[2,320]{1,0:T(2,128)}, f32[152,320]{1,0:T(8,128)}) custom-call(f32[1216,320]{1,0:T(8,128)} %get-tuple-element.113.refs_0_, f32[1216,320]{1,0:T(8,128)} %get-tuple-element.109.middle_ref.refs_1_, ...), custom_call_target="tpu_custom_call" | custom-call | flops 17999998976 | bytes 18000000 | tf_op jit(solution)/shard_map/mlp_backward/pallas_call | solution.py:437
  246.3 31.5 %attention_backward.3 = (f32[1216,320]{1,0:T(8,128)}, bf16[2,1280,320]{2,1,0:T(8,128)(2,1)}, f32[4,320]{1,0:T(4,128)}, bf16[2,2,2,1,40,320]{5,4,3,2,1,0:T(8,128)(2,1)}, f32[152,320]{1,0:T(8,128)}) custom-call(f32[1216,320]{1,0:T(8,128)} %get-tuple-element.119.refs_0_, f32[1216,320]{1,0:T(8,128)} %get-tuple-element.107.resid_ref.refs_1_, ...), custom_call_target="tpu_custom_call" | custom-call | flops 12000000000 | bytes 18000000 | tf_op jit(solution)/shard_map/attention_backward/pallas_call | solution.py:919
  277.8 32.2 %mlp_backward.4 = (f32[1216,320]{1,0:T(8,128)}, bf16[2,1280,320]{2,1,0:T(8,128)(2,1)}, f32[9,1280]{1,0:T(8,128)}, f32[2,320]{1,0:T(2,128)}, bf16[2,2,2,1,40,320]...) custom-call(f32[1216,320]{1,0:T(8,128)} %get-tuple-element.129.refs_0_, ...), custom_call_target="tpu_custom_call" | custom-call | flops 17999998976 | bytes 18000000 | tf_op jit(solution)/shard_map/mlp_backward/pallas_call | solution.py:437
  310.0 23.0 %attention_backward.4 = (f32[1216,320]{1,0:T(8,128)}, bf16[2,1280,320]{2,1,0:T(8,128)(2,1)}, f32[4,320]{1,0:T(4,128)}, bf16[2,2,2,1,40,320]{5,4,3,2,1,0:T(8,128)(2,1)}, bf16[2,40,320]{2,1,0:T(8,128)(2,1)}) custom-call(f32[1216,320]{1,0:T(8,128)} %get-tuple-element.136.refs_0_, f32[1216,320]{1,0:T(8,128)} %get-tuple-element.105.resid_ref.refs_1_, ...), custom_call_target="tpu_custom_call" | custom-call | flops 12000000000 | bytes 18000000 | tf_op jit(solution)/shard_map/attention_backward/pallas_call | solution.py:919
  333.1 31.7 %mlp_backward.5 = (f32[1216,320]{1,0:T(8,128)}, bf16[2,1280,320]{2,1,0:T(8,128)(2,1)}, f32[9,1280]{1,0:T(8,128)}, f32[2,320]{1,0:T(2,128)}, bf16[2,2,2,1,40,320]...) custom-call(f32[1216,320]{1,0:T(8,128)} %get-tuple-element.146.refs_0_, ...), custom_call_target="tpu_custom_call" | custom-call | flops 17999998976 | bytes 18000000 | tf_op jit(solution)/shard_map/mlp_backward/pallas_call | solution.py:437
  364.8 24.4 %attention_backward.5 = (f32[1216,320]{1,0:T(8,128)}, bf16[2,1280,320]{2,1,0:T(8,128)(2,1)}, f32[4,320]{1,0:T(4,128)}, bf16[2,2,2,1,40,320]{5,4,3,2,1,0:T(8,128)(2,1)}, bf16[2,40,320]{2,1,0:T(8,128)(2,1)}) custom-call(f32[1216,320]{1,0:T(8,128)} %get-tuple-element.153.refs_0_, f32[1216,320]{1,0:T(8,128)} %get-tuple-element.102.resid_ref.refs_1_, ...), custom_call_target="tpu_custom_call" | custom-call | flops 12000000000 | bytes 18000000 | tf_op jit(solution)/shard_map/attention_backward/pallas_call | solution.py:919
  389.2 1.6 pad_maximum_fusion.refs_1_
  390.8 6.7 %embed_backward.1 = (bf16[1,1280,320]{2,1,0:T(8,128)(2,1)}, f32[2,320]{1,0:T(2,128)}) custom-call(f32[1216,320]{1,0:T(8,128)} %get-tuple-element.168.grad_ref, f32[1216,320]{1,0:T(8,128)} %get-tuple-element.169.pre_ref, f32[2,320]{1,0:T(2,128)} %get-tuple-element.200.gains_ref, bf16[1024,1152]{1,0:T(8,128)(2,1)} %patches_ref.3, ...), custom_call_target="tpu_custom_call" | custom-call | flops 1000000000 | bytes 8000000 | tf_op jit(solution)/shard_map/embed_backward/pallas_call | solution.py:724
  397.5 44.8 %tail_exchange.1 = (bf16[8,2,40,320]{3,2,1,0:T(8,128)(2,1)}, f32[24,320]{1,0:T(8,128)}) custom-call(s32[16]{0:T(128)} %broadcast_select_fusion.1.refs_0_, bf16[8,40,320]{2,1,0:T(8,128)(2,1)} %pad_maximum_fusion.refs_1_, bf16[2,2,2,1,40,320]{5,4,3,2,1,0:T(8,128)(2,1)} %get-tuple-element.167.refs_2_, bf16[1,16,2,1,40,320]{5,4,3,2,1,0:T(8,128)(2,1)} %bitcast.46, ...), custom_call_target="tpu_custom_call" | custom-call | tf_op jit(solution)/shard_map/tail_exchange/pallas_call | solution.py:1328
  442.3 1.2 slice.89
  443.4 1.1 convert_bitcast_fusion
  444.5 0.0 copy-start.2
  444.6 0.1 copy.52
  444.7 0.0 copy-start
  444.7 0.8 reshape.238
  445.5 1.6 multiply_subtract_fusion.2
  447.1 1.0 multiply_subtract_fusion.1
  448.1 3.9 multiply_subtract_fusion
  (43 shorter events, 0.2 us)
Async XLA Ops:
  7.2 7.6 %copy-start.12 = (s32[1024]{0:T(1024)S(1)}, s32[1024]{0:T(1024)}, u32[]{:S(2)}) copy-start(s32[1024]{0:T(1024)} %param.20) | copy-start | bytes 12292
  7.2 8.2 %copy-start.13 = (s32[1024]{0:T(1024)S(1)}, s32[1024]{0:T(1024)}, u32[]{:S(2)}) copy-start(s32[1024]{0:T(1024)} %param.19) | copy-start | bytes 12292
  7.2 169.3 %all-gather.2.cloned.1.call-start = ((), (), s32[]{:S(2)}) async-start(), calls=%async_computation | async-start | bytes 4055040 | tf_op jit(solution)/shard_map/all_gather | solution.py:1392
  12.6 84.2 %copy-start.16 = (s32[4,3]{1,0:T(4,128)S(1)}, s32[4,3]{1,0:T(4,128)}, u32[]{:S(2)}) copy-start(s32[4,3]{1,0:T(4,128)} %constant.153) | copy-start | bytes 148
  12.6 84.2 %copy-start.17 = (s32[4,3]{1,0:T(4,128)S(1)}, s32[4,3]{1,0:T(4,128)}, u32[]{:S(2)}) copy-start(s32[4,3]{1,0:T(4,128)} %constant.152) | copy-start | bytes 148
  12.7 85.4 %copy-start.1 = (f32[320,150]{0,1:T(8,128)S(1)}, f32[320,150]{0,1:T(8,128)}, u32[]{:S(2)}) copy-start(f32[320,150]{0,1:T(8,128)} %param.29) | copy-start | bytes 576004
  96.6 6.2 %copy-start.8 = (f32[22,320]{1,0:T(8,128)S(1)}, f32[22,320]{1,0:T(8,128)}, u32[]{:S(2)}) copy-start(f32[22,320]{1,0:T(8,128)} %param.26) | copy-start | bytes 84484
  103.4 7.9 %copy-start.18 = (s32[13]{0:T(128)S(1)}, s32[13]{0:T(128)}, u32[]{:S(2)}) copy-start(s32[13]{0:T(128)} %multiply_add_fusion.3.slot_ref) | copy-start | bytes 160
  103.4 9.8 %copy-start.14 = (s32[10,128]{1,0:T(8,128)S(1)}, s32[10,128]{1,0:T(8,128)}, u32[]{:S(2)}) copy-start(s32[10,128]{1,0:T(8,128)} %constant.151) | copy-start | bytes 15364
  103.4 9.8 %copy-start.15 = (s32[10,128]{1,0:T(8,128)S(1)}, s32[10,128]{1,0:T(8,128)}, u32[]{:S(2)}) copy-start(s32[10,128]{1,0:T(8,128)} %constant.150) | copy-start | bytes 15364
  364.8 24.4 %copy-start.9 = (bf16[2,40,320]{2,1,0:T(8,128)(2,1)S(1)}, bf16[2,40,320]{2,1,0:T(8,128)(2,1)}, u32[]{:S(2)}) copy-start(bf16[2,40,320]{2,1,0:T(8,128)(2,1)} %get-tuple-element.166) | copy-start | bytes 153604
  364.8 24.4 %copy-start.10 = (bf16[2,40,320]{2,1,0:T(8,128)(2,1)S(1)}, bf16[2,40,320]{2,1,0:T(8,128)(2,1)}, u32[]{:S(2)}) copy-start(bf16[2,40,320]{2,1,0:T(8,128)(2,1)} %get-tuple-element.165) | copy-start | bytes 153604
  364.8 24.4 %copy-start.11 = (bf16[2,40,320]{2,1,0:T(8,128)(2,1)S(1)}, bf16[2,40,320]{2,1,0:T(8,128)(2,1)}, u32[]{:S(2)}) copy-start(bf16[2,40,320]{2,1,0:T(8,128)(2,1)} %get-tuple-element.164) | copy-start | bytes 153604
  444.5 2.6 copy-start.2
  444.5 2.5 copy-start.5
  444.6 2.5 copy-start.6
  444.6 2.5 copy-start.7
  444.7 3.4 copy-start
  445.5 2.6 copy-start.3
  445.5 2.6 copy-start.4
Sparse Core Ops, SparseCore 0:
  96.8 63.8 all-gather.1

commit v6 on v5

--- a/solution.py
+++ b/solution.py
@@ -284,20 +284,22 @@
         own_out, refs = refs[:outputs], refs[outputs:]
         ride_out, rest = refs[: len(plans)], refs[len(plans) :]
         rides = rides_of(plans, ride_in, ride_out, rest[scratch:])
-        first = min(steps, rides.phases + 1)
-
-        def advance():
-            for phase in range(first):
-                pl.when(pl.program_id(0) == phase)(functools.partial(rides.advance, phase))
-
-        pl.when(pl.program_id(0) == 0)(rides.signal)
-        kernel(advance, *own_in, *own_out, *rest[:scratch])
-        if rides.phases >= first:
-
-            @pl.when(pl.program_id(0) == steps - 1)
-            def _():
-                for phase in range(first, rides.phases + 1):
-                    rides.advance(phase)
+        places = [0] + list(range(1, steps - 1, 2))
+        for phase, step in enumerate(places):
+            if phase == 0:
+
+                @pl.when(pl.program_id(0) == step)
+                def _():
+                    rides.signal()
+                    rides.advance(0)
+            elif phase <= rides.phases:
+                pl.when(pl.program_id(0) == step)(functools.partial(rides.advance, phase))
+        kernel(*own_in, *own_out, *rest[:scratch])
+
+        @pl.when(pl.program_id(0) == steps - 1)
+        def _():
+            for phase in range(len(places), rides.phases + 1):
+                rides.advance(phase)
 
     return run
 
@@ -348,7 +350,6 @@
 
 
 def mlp_backward_kernel(
-    advance,
     grad_ref, middle_ref, gains_ref, up_ref, down_ref, kern_ref, upper_ref, lower_ref, real_ref,
     hidden_ref, active_ref, slope_ref,
     out_ref, dunits_ref, dkern_ref, dgain_ref,
@@ -368,7 +369,6 @@
         low_t_ref[...] = grad_ref[...].T.astype(jnp.bfloat16)
         back_ref[...] = jnp.zeros_like(back_ref)
 
-    advance()
     for sub in range(4):
         span = slice(sub * tiles, (sub + 1) * tiles)
         part = back_product(low_ref[span, :], down_ref[0]).astype(jnp.bfloat16).astype(jnp.float32)
@@ -812,6 +812,7 @@
     rows = resid_ref.shape[0]
     tiles = rows // 4
     low_type = jnp.bfloat16
+    advance(0)
     datt_ref[:, C:] = jnp.zeros((rows, WIDE - C), low_type)
     turned_ref[...] = grad_ref[...].T.astype(low_type)
     dunits_ref[0, C : 2 * C, :] = product(turned_ref[...], attended_ref[:, :C]).T.astype(low_type)
@@ -856,11 +857,9 @@
             dkey_ref[span, lanes] += dkeys
             dvalue_ref[span, lanes] += dvalues
 
-    advance(0)
     pl.loop(0, blocks // 2, unroll=blocks // 2)(one_block)
     advance(1)
     pl.loop(blocks // 2, blocks, unroll=blocks - blocks // 2)(one_block)
-    advance(2)
     unit, inverse, normed = norm_rows(reduced_ref[...], gains_ref[2:3, :], gains_ref[3:4, :])
     normed_t = normed.T.astype(low_type)
     dkeys = dkey_ref[:, :C].astype(low_type)
@@ -878,6 +877,7 @@
     dgain_ref[2:3, :] = jnp.sum(dnormed * unit, 0, keepdims=True)
     dgain_ref[3:4, :] = jnp.sum(dnormed, 0, keepdims=True)
     dreduced = norm_rows_back(unit, inverse, gains_ref[2:3, :], dnormed).astype(low_type)
+    advance(2)
     turned_ref[...] = normed_ref[...].T
     dunits_ref[0, :C, :] = product(turned_ref[...], dquery_ref[:, :C]).astype(low_type)
     for sub in range(4):
@@ -1051,14 +1051,26 @@
     return [pltpu.SemaphoreType.DMA((phases * total,))] * 2
 
 
+def slot_numbers(owner_ref, slot_rows):
+    owners = [owner_ref[unit] for unit in range(owner_ref.shape[0])]
+    slots = []
+    for unit, owner in enumerate(owners):
+        rank = jnp.int32(0)
+        for earlier in owners[:unit]:
+            rank = rank + (earlier == owner).astype(jnp.int32)
+        slots.append(owner * slot_rows + rank)
+    return slots
+
+
 def start_kernel(
-    slot_ref, piece_ref, count_ref, patch_ref, mark_ref,
+    owner_ref, piece_ref, count_ref, patch_ref, mark_ref,
     full_ref, later_ref, total_ref, patch_halo_ref, mark_halo_ref,
     recv_ref, near_s, near_r, halo_s, halo_r, *scratch,
 ):
     grp, tok, n_tok, peers = exchange_setup()
     slot_rows = piece_ref.shape[1]
-    units, first = slot_ref.shape[0], full_ref.shape[0]
+    units, first = owner_ref.shape[0], full_ref.shape[0]
+    slots = slot_numbers(owner_ref, slot_rows)
     gather = GatherRide(full_ref, scratch[:2])
     count = SumRide(count_ref, total_ref, scratch[2:])
     greet(peers)
@@ -1072,24 +1084,27 @@
     for copy in copies:
         copy.wait()
     for unit in range(first):
-        gather.put(unit, recv_ref[slot_ref[unit]])
+        gather.put(unit, recv_ref[slots[unit]])
     gather.advance(0)
     before = (grp, lax.rem(tok + n_tok - 1, n_tok))
     mark_copy = send(mark_ref, mark_halo_ref, (halo_s, halo_r), 0, before)
     patch_copy = send(patch_ref.at[pl.ds(0, patch_halo_ref.shape[0])], patch_halo_ref, (halo_s, halo_r), 1, before)
     for unit in range(first, units):
-        later_ref[unit - first] = recv_ref[slot_ref[unit]]
+        later_ref[unit - first] = recv_ref[slots[unit]]
     for phase in range(1, gather.phases + 1):
         count.advance(phase)
         gather.advance(phase)
+    total_ref[...] = jnp.broadcast_to(
+        jnp.sum(jnp.sum(total_ref[...], 0, keepdims=True), 1, keepdims=True), total_ref.shape
+    )
     mark_copy.wait()
     patch_copy.wait()
 
 
-def start_exchange(slot_of, pieces, count, patches, marks, first):
+def start_exchange(owners, pieces, count, patches, marks, first):
     n_tok, slot_rows, chunk, width = pieces.shape
     phases = len(bit_order())
-    units = slot_of.shape[0]
+    units = owners.shape[0]
     vmem = pl.BlockSpec(memory_space=pltpu.VMEM)
     full_shape = (first,) + (2,) * phases + (chunk, width)
     return pl.pallas_call(
@@ -1114,7 +1129,7 @@
         + sum_scratch(count.shape),
         compiler_params=pltpu.CompilerParams(collective_id=0, has_side_effects=True, vmem_limit_bytes=VMEM_LIMIT),
         name="start_exchange",
-    )(slot_of, pieces, count, patches, marks)
+    )(owners, pieces, count, patches, marks)
 
 
 def unit_order(unit):
@@ -1269,7 +1284,7 @@
 
 
 def tail_kernel(counts, rows, *refs):
-    unit_at_ref, early_ref, part_ref = refs[:3]
+    owner_ref, early_ref, part_ref = refs[:3]
     blocks, refs = refs[3 : 3 + len(counts)], refs[3 + len(counts) :]
     small_refs, refs = refs[: len(rows)], refs[len(rows) :]
     owned_ref, small_out_ref, chunk_ref, place_ref, near_s, near_r, small_ref = refs[:7]
@@ -1301,10 +1316,14 @@
     last = total + early_ref.shape[0]
     chunk_ref[last] = jnp.zeros(chunk_ref.shape[1:], chunk_ref.dtype)
     slot_rows = owned_ref.shape[1]
+    slots = slot_numbers(owner_ref, slot_rows)
 
     @pl.loop(0, n_tok * slot_rows)
     def _(at):
-        place_ref[at // slot_rows, at % slot_rows] = chunk_ref[unit_at_ref[at]]
+        unit_at = jnp.int32(last)
+        for unit, slot in enumerate(slots):
+            unit_at = jnp.where(slot == at, unit, unit_at)
+        place_ref[at // slot_rows, at % slot_rows] = chunk_ref[unit_at]
 
     copies = []
     for step in range(1, n_tok):
@@ -1315,14 +1334,13 @@
         copy.wait()
 
 
-def tail_exchange(unit_at, early, part, sources, smalls, n_tok):
+def tail_exchange(owners, slot_rows, early, part, sources, smalls, n_tok):
     chunk, width = early.shape[1:]
     counts = tuple(source.shape[0] for source in sources)
     rows = tuple(small.shape[0] for small in smalls)
     total = sum(counts)
     low = early.dtype
     vmem = pl.BlockSpec(memory_space=pltpu.VMEM)
-    slot_rows = unit_at.shape[0] // n_tok
     dma = pltpu.SemaphoreType.DMA
     small = (-(-sum(rows) // 8) * 8, C)
     return pl.pallas_call(
@@ -1345,7 +1363,7 @@
         + unit_scratch(part.shape[0], chunk, width, SPLIT),
         compiler_params=pltpu.CompilerParams(collective_id=1, has_side_effects=True, vmem_limit_bytes=VMEM_LIMIT),
         name="tail_exchange",
-    )(unit_at, early, part, *[unit_blocks(source) for source in sources], *smalls)
+    )(owners, early, part, *[unit_blocks(source) for source in sources], *smalls)
 
 
 def body(
@@ -1372,20 +1390,16 @@
     counts = crop_counts[0]
     n_unit = owners.shape[0]
     slot_rows, columns = slot_weight.shape
-    unit_order = jnp.arange(n_unit, dtype=jnp.int32)
-    same_owner = owners[:, None] == owners[None, :]
-    rank_of = jnp.sum(same_owner & (unit_order[None, :] < unit_order[:, None]), 1)
-    slot_of = owners * slot_rows + rank_of
     chunk = columns // n_tok // C
     first_tok = tok_index * tok_dev
     small_end = counts[0] * BIG_SIDE**2 + counts[1] * SMALL_SIDE**2
     counted = valid_mask * (first_tok + jnp.arange(tok_dev, dtype=jnp.int32) < small_end)
-    counted = jnp.full((8, LANES), jnp.sum(counted.astype(jnp.float32)))
+    counted = counted.astype(jnp.float32).reshape(-1, LANES)
     pieces = slot_weight.astype(jnp.bfloat16).reshape(slot_rows, n_tok, chunk, C).transpose(1, 0, 2, 3)
     first_units = 1 + 2 * (n_unit // BLOCKS)
     marks = jnp.stack([labels, valid_mask])
     own, later, counted, patch_halo, mark_halo = start_exchange(
-        slot_of, pieces, counted, patches, marks[:, :OVER], first_units
+        owners, pieces, counted, patches, marks[:, :OVER], first_units
     )
     pixel_total = counted[0, 0]
     own = own.reshape(first_units, FF, C)
@@ -1429,44 +1443,50 @@
     grad_res, d_head, final_gains, loss_row = head_step(
         resid, norm_params[tail + 2 : tail + 4], head_weight, labels[:, None], keep_mask[:, None], counted
     )
-    plans = [plan_sum(d_head, 0, SPLIT)]
+    unit_plans = []
+    head_cuts = [0, 1, 2, 3, 4, len(bit_order())]
     early = []
     kernel_grads = [None] * BLOCKS
     gain_grads = []
     phases = len(bit_order())
+
+    def head_plans(value):
+        if len(head_cuts) < 2:
+            return []
+        begin = head_cuts.pop(0)
+        return [plan_sum(value, begin, head_cuts[0])]
+
     for layer_at in reversed(range(BLOCKS)):
         attn_units, mlp_units = layers[layer_at]
         at = 6 * layer_at
         entry, attn_kept, middle, mlp_kept, w_up = kept_all[layer_at]
         grad_res, mlp_grads, kernel_grads[layer_at], mlp_gains, *ridden_out = mlp_backward(
             grad_res, middle, norm_params[at + 4 : at + 6], w_up, *mlp_units, kernels, layer_at,
-            stacks, real_rows, mlp_kept, plans, 2 + layer_at,
+            stacks, real_rows, mlp_kept, unit_plans + head_plans(d_head), 2 + layer_at,
         )
-        plans = [plan_units(mlp_grads, 0, SPLIT)]
-        if layer_at + 1 == BLOCKS:
-            plans.append(plan_sum(ridden_out[0], SPLIT, phases))
-        else:
+        d_head = ridden_out.pop()
+        unit_plans = [plan_units(mlp_grads, 0, SPLIT)]
+        if ridden_out:
             early.insert(0, ridden_out[1])
-            plans.append(plan_units(ridden_out[0], SPLIT, phases))
+            unit_plans.append(plan_units(ridden_out[0], SPLIT, phases))
+        plans = unit_plans + head_plans(d_head)
         grad_res, attn_grads, attn_gains, *ridden_out = attention_backward(
             grad_res, entry, norm_params[at : at + 4], *attn_units, bias, attn_kept, plans, 2 + BLOCKS + layer_at
         )
+        if len(plans) > len(unit_plans):
+            d_head = ridden_out.pop()
         if layer_at + 1 < BLOCKS:
             early.insert(0, ridden_out[1])
-        else:
-            head_total = ridden_out[1][: head_weight.shape[1]].T
-        plans = [plan_units(attn_grads, 0, SPLIT), plan_units(ridden_out[0], SPLIT, phases)]
+        unit_plans = [plan_units(attn_grads, 0, SPLIT), plan_units(ridden_out[0], SPLIT, phases)]
         gain_grads = [attn_gains, mlp_gains] + gain_grads
+    head_total = d_head[: head_weight.shape[1]].T
     part = ridden_out[0]
     first_grad, embed_gains = embed_backward(
         grad_res, embed_pre, norm_params[tail : tail + 2], patches, patch_halo, kernel_grads
     )
     early = jnp.concatenate(early, 0)
     smalls = gain_grads + [embed_gains, final_gains, loss_row]
-    row_ids = jnp.arange(slot_rows * n_tok, dtype=jnp.int32)
-    matches = slot_of[None, :] == row_ids[:, None]
-    unit_at = jnp.where(jnp.any(matches, 1), jnp.argmax(matches, 1), n_unit)
-    owned, small = tail_exchange(unit_at, early, part, [first_grad, attn_grads], smalls, n_tok)
+    owned, small = tail_exchange(owners, slot_rows, early, part, [first_grad, attn_grads], smalls, n_tok)
     owned = owned.transpose(1, 0, 2, 3).astype(jnp.float32).reshape(slot_rows, columns)
     norm_rows_all = norm_params.shape[0]
     norm_total, loss_sum = (small[:norm_rows_all], small[norm_rows_all, 0])

time: 463 us -> 456 us (0.985)
  no operation moved by 1% of the time
where the time goes in v6:
time: 456 us; the launch traced here: 453 us
  Pallas kernels  408 us (89%)
  other arithmetic  16.4 us (4%)
  between operations  16.3 us (4%)
  local copies, waits for them, and re-layouts  11.9 us (3%)
    pallas_call x3, Pallas kernels, mlp_backward(): pl.pallas_call(ridden(mlp_backward_kernel, 12, 4, 9, FF // block, plans),...  96.6 us
    pallas_call x1, Pallas kernels, start_exchange(): pl.pallas_call(start_kernel, out_shape=(jax.ShapeDtypeStruct(full_shape,...  79.6 us
    pallas_call x3, Pallas kernels, attention_backward(): pl.pallas_call(run, grid=(1,), out_shape=shapes + tuple((plan.out for pla...  77.9 us
    pallas_call x3, Pallas kernels, mlp_forward(): pl.pallas_call(mlp_forward_kernel, grid=(FF // block,), out_shape=(jax.Sh...  56 us
    pallas_call x1, Pallas kernels, tail_exchange(): pl.pallas_call(lambda *refs: tail_kernel(counts, rows, *refs), out_shape=...  44.5 us
    pallas_call x3, Pallas kernels, attention_forward(): pl.pallas_call(attention_forward_kernel, grid=(1,), out_shape=shapes, in_...  32.1 us
  transfers between devices with their start and end apart: 1, of which 0 were waited for; matrix products, arithmetic and copies ran while one was open for 3% of the time, Pallas kernels for 15%

profile of v6, /device:TPU:1, one launch (start us, length us, event | category | flops | bytes accessed | tf_op | source)
XLA Modules:
  0.0 452.8 jit_solution(701537634372438264)
XLA Ops:
  7.2 0.0 all-gather.2.cloned.1.call-start
  7.2 1.3 fusion.66
  8.6 1.4 convert_element_type.46
  10.0 0.6 reshape.225
  10.6 0.0 copy-start.16
  10.6 0.0 copy-start.17
  10.6 0.0 copy-start.1
  10.6 0.8 copy.46
  12.7 0.6 pad_add_fusion.1.mark_ref
  13.3 0.6 convert_bitcast_fusion.1.count_ref
  13.9 79.6 %start_exchange.1 = (bf16[9,2,2,2,2,2,40,320]{7,6,5,4,3,2,1,0:T(8,128)(2,1)}, bf16[4,40,320]{2,1,0:T(8,128)(2,1)}, f32[8,128]{1,0:T(8,128)}, bf16[192,1152]{1,0:T(8,128)(2,1)}, s32[2,192]{1,0:T(2,128)}) custom-call(s32[13]{0:T(128)} %refs_0_.1, bf16[8,2,40,320]{3,2,1,0:T(8,128)(2,1)} %bitcast.47, f32[8,128]{1,0:T(8,128)} %convert_bitcast_fusion.1.count_ref, ...), custom_call_target="tpu_custom_call" | custom-call | tf_op jit(solution)/shard_map/start_exchange/pallas_call | solution.py:1110
  93.5 0.0 copy-start.8
  93.5 0.0 all-gather.2.cloned.1.call-update
  93.6 0.2 add_select_fusion.5
  93.8 0.1 add_select_fusion
  93.9 0.1 slice.94
  94.0 0.1 tile.10
  94.1 0.1 eq.57
  94.2 0.1 eq.61
  94.3 0.9 copy.41.weight_ref
  95.1 1.2 slice.90
  96.3 0.7 pad_add_fusion
  97.0 0.2 reshape.228
  97.2 0.1 copy.40
  97.4 0.1 convert_element_type.52
  97.5 1.1 copy.43.keep_ref
  98.6 1.1 broadcast_in_dim_squeeze.4.label_ref
  99.7 0.6 fusion.64
  100.3 8.0 %embed_forward.1 = (f32[1216,320]{1,0:T(8,128)}, f32[1216,320]{1,0:T(8,128)}, f32[3,9,1280]{2,1,0:T(8,128)}) custom-call(bf16[1024,1152]{1,0:T(8,128)(2,1)} %patches_ref.3, bf16[192,1152]{1,0:T(8,128)(2,1)} %get-tuple-element.101.halo_ref, bf16[9,1280,320]{2,1,0:T(8,128)(2,1)} %bitcast.31, f32[2,320]{1,0:T(2,128)} %get-tuple-element.204.gains_ref), custom_call_target="tpu_custom_call" | custom-call | flops 1000000000 | bytes 8000000 | tf_op jit(solution)/shard_map/embed_forward/pallas_call | solution.py:661
  108.3 0.6 fusion.65
  108.9 1.1 compare_select_fusion.bias_ref.refs_5_
  110.0 1.2 compare_convert_fusion.lower_ref.refs_7_
  111.2 1.3 fusion.upper_ref.refs_6_
  112.5 10.7 %attention_forward.3 = (f32[1216,320]{1,0:T(8,128)}, bf16[1216,320]{1,0:T(8,128)(2,1)}, bf16[1216,384]{1,0:T(8,128)(2,1)}, f32[304,320]{1,0:T(8,128)}, bf16[304,...) custom-call(f32[1216,320]{1,0:T(8,128)} %get-tuple-element.103.resid_ref.r, ...), custom_call_target="tpu_custom_call" | custom-call | flops 6000000000 | bytes 14000000 | tf_op jit(solution)/shard_map/attention_forward/pallas_call | solution.py:609
  123.2 0.8 broadcast_in_dim.34.real_ref.refs_8_
  124.0 18.5 %mlp_forward.3 = (f32[1216,320]{1,0:T(8,128)}, bf16[1216,1280]{1,0:T(8,128)(2,1)}, bf16[1216,1280]{1,0:T(8,128)(2,1)}, bf16[1216,1280]{1,0:T(8,128)(2,1)}, bf16[320,1280]{1,0:T(8,128)(2,1)}) custom-call(f32[1216,320]{1,0:T(8,128)} %get-tuple-element.104.middle_ref.refs_1_, f32[2,320]{1,0:T(2,128)} %get-tuple-element.203.gains_ref.refs_2_, ...), custom_call_target="tpu_custom_call" | custom-call | flops 14000000000 | bytes 18000000 | tf_op jit(solution)/shard_map/mlp_forward/pallas_call | solution.py:320
  142.5 10.7 %attention_forward.4 = (f32[1216,320]{1,0:T(8,128)}, bf16[1216,320]{1,0:T(8,128)(2,1)}, bf16[1216,384]{1,0:T(8,128)(2,1)}, f32[304,320]{1,0:T(8,128)}, bf16[304,...) custom-call(f32[1216,320]{1,0:T(8,128)} %get-tuple-element.106.resid_ref.r, ...), custom_call_target="tpu_custom_call" | custom-call | flops 6000000000 | bytes 14000000 | tf_op jit(solution)/shard_map/attention_forward/pallas_call | solution.py:609
  153.2 19.0 %mlp_forward.4 = (f32[1216,320]{1,0:T(8,128)}, bf16[1216,1280]{1,0:T(8,128)(2,1)}, bf16[1216,1280]{1,0:T(8,128)(2,1)}, bf16[1216,1280]{1,0:T(8,128)(2,1)}, bf16[320,1280]{1,0:T(8,128)(2,1)}) custom-call(f32[1216,320]{1,0:T(8,128)} %get-tuple-element.107.middle_ref.refs_1_, f32[2,320]{1,0:T(2,128)} %get-tuple-element.202.gains_ref.refs_2_, ...), custom_call_target="tpu_custom_call" | custom-call | flops 14000000000 | bytes 18000000 | tf_op jit(solution)/shard_map/mlp_forward/pallas_call | solution.py:320
  172.2 0.0 all-gather.2.cloned.1.call-done.unit_ref.reduce_ref.up_ref.down_ref.refs_4_.refs_3_
  172.2 10.7 %attention_forward.5 = (f32[1216,320]{1,0:T(8,128)}, bf16[1216,320]{1,0:T(8,128)(2,1)}, bf16[1216,384]{1,0:T(8,128)(2,1)}, f32[304,320]{1,0:T(8,128)}, bf16[304,...) custom-call(f32[1216,320]{1,0:T(8,128)} %get-tuple-element.108.resid_ref.r, ...), custom_call_target="tpu_custom_call" | custom-call | flops 6000000000 | bytes 14000000 | tf_op jit(solution)/shard_map/attention_forward/pallas_call | solution.py:609
  182.9 18.5 %mlp_forward.5 = (f32[1216,320]{1,0:T(8,128)}, bf16[1216,1280]{1,0:T(8,128)(2,1)}, bf16[1216,1280]{1,0:T(8,128)(2,1)}, bf16[1216,1280]{1,0:T(8,128)(2,1)}, bf16[320,1280]{1,0:T(8,128)(2,1)}) custom-call(f32[1216,320]{1,0:T(8,128)} %get-tuple-element.110.middle_ref.refs_1_, f32[2,320]{1,0:T(2,128)} %get-tuple-element.201.gains_ref.refs_2_, ...), custom_call_target="tpu_custom_call" | custom-call | flops 14000000000 | bytes 18000000 | tf_op jit(solution)/shard_map/mlp_forward/pallas_call | solution.py:320
  201.4 7.1 %head_step.1 = (f32[1216,320]{1,0:T(8,128)}, f32[152,320]{1,0:T(8,128)}, f32[2,320]{1,0:T(2,128)}, f32[1,320]{1,0:T(1,128)}) custom-call(f32[1216,320]{1,0:T(8,128)} %get-tuple-element.111.resid_ref, f32[2,320]{1,0:T(2,128)} %get-tuple-element.200.gains_ref, f32[320,150]{1,0:T(8,128)} %copy.41.weight_ref, s32[1216,1]{1,0:T(8,128)} %broadcast_in_dim_squeeze.4.label_ref, ...), custom_call_target="tpu_custom_call" | custom-call | flops 1000000000 | bytes 5000000 | tf_op jit(solution)/shard_map/head_step/pallas_call | solution.py:789
  208.5 25.6 %mlp_backward.3 = (f32[1216,320]{1,0:T(8,128)}, bf16[2,1280,320]{2,1,0:T(8,128)(2,1)}, f32[9,1280]{1,0:T(8,128)}, f32[2,320]{1,0:T(2,128)}, f32[152,320]{1,0:T(8,128)}) custom-call(f32[1216,320]{1,0:T(8,128)} %get-tuple-element.114.refs_0_, f32[1216,320]{1,0:T(8,128)} %get-tuple-element.110.middle_ref.refs_1_, ...), custom_call_target="tpu_custom_call" | custom-call | flops 17999998976 | bytes 18000000 | tf_op jit(solution)/shard_map/mlp_backward/pallas_call | solution.py:437
  234.1 26.6 %attention_backward.3 = (f32[1216,320]{1,0:T(8,128)}, bf16[2,1280,320]{2,1,0:T(8,128)(2,1)}, f32[4,320]{1,0:T(4,128)}, bf16[2,2,2,1,40,320]{5,4,3,2,1,0:T(8,128)(2,1)}, f32[152,320]{1,0:T(8,128)}) custom-call(f32[1216,320]{1,0:T(8,128)} %get-tuple-element.120.refs_0_, f32[1216,320]{1,0:T(8,128)} %get-tuple-element.108.resid_ref.refs_1_, ...), custom_call_target="tpu_custom_call" | custom-call | flops 12000000000 | bytes 18000000 | tf_op jit(solution)/shard_map/attention_backward/pallas_call | solution.py:919
  260.7 30.3 %mlp_backward.4 = (f32[1216,320]{1,0:T(8,128)}, bf16[2,1280,320]{2,1,0:T(8,128)(2,1)}, f32[9,1280]{1,0:T(8,128)}, f32[2,320]{1,0:T(2,128)}, bf16[2,2,2,1,40,320]...) custom-call(f32[1216,320]{1,0:T(8,128)} %get-tuple-element.130.refs_0_, ...), custom_call_target="tpu_custom_call" | custom-call | flops 17999998976 | bytes 18000000 | tf_op jit(solution)/shard_map/mlp_backward/pallas_call | solution.py:437
  291.1 27.2 %attention_backward.4 = (f32[1216,320]{1,0:T(8,128)}, bf16[2,1280,320]{2,1,0:T(8,128)(2,1)}, f32[4,320]{1,0:T(4,128)}, bf16[2,2,2,1,40,320]{5,4,3,2,1,0:T(8,128)...) custom-call(f32[1216,320]{1,0:T(8,128)} %get-tuple-element.138.refs_0_, ...), custom_call_target="tpu_custom_call" | custom-call | flops 12000000000 | bytes 18000000 | tf_op jit(solution)/shard_map/attention_backward/pallas_call | solution.py:919
  318.3 40.6 %mlp_backward.5 = (f32[1216,320]{1,0:T(8,128)}, bf16[2,1280,320]{2,1,0:T(8,128)(2,1)}, f32[9,1280]{1,0:T(8,128)}, f32[2,320]{1,0:T(2,128)}, bf16[2,2,2,1,40,320]...) custom-call(f32[1216,320]{1,0:T(8,128)} %get-tuple-element.149.refs_0_, ...), custom_call_target="tpu_custom_call" | custom-call | flops 17999998976 | bytes 18000000 | tf_op jit(solution)/shard_map/mlp_backward/pallas_call | solution.py:437
  358.9 24.0 %attention_backward.5 = (f32[1216,320]{1,0:T(8,128)}, bf16[2,1280,320]{2,1,0:T(8,128)(2,1)}, f32[4,320]{1,0:T(4,128)}, bf16[2,2,2,1,40,320]{5,4,3,2,1,0:T(8,128)(2,1)}, bf16[2,40,320]{2,1,0:T(8,128)(2,1)}) custom-call(f32[1216,320]{1,0:T(8,128)} %get-tuple-element.157.refs_0_, f32[1216,320]{1,0:T(8,128)} %get-tuple-element.103.resid_ref.refs_1_, ...), custom_call_target="tpu_custom_call" | custom-call | flops 12000000000 | bytes 18000000 | tf_op jit(solution)/shard_map/attention_backward/pallas_call | solution.py:919
  383.0 1.6 pad_maximum_fusion.refs_1_
  384.6 6.7 %embed_backward.1 = (bf16[1,1280,320]{2,1,0:T(8,128)(2,1)}, f32[2,320]{1,0:T(2,128)}) custom-call(f32[1216,320]{1,0:T(8,128)} %get-tuple-element.172.grad_ref, f32[1216,320]{1,0:T(8,128)} %get-tuple-element.173.pre_ref, f32[2,320]{1,0:T(2,128)} %get-tuple-element.204.gains_ref, bf16[1024,1152]{1,0:T(8,128)(2,1)} %patches_ref.3, ...), custom_call_target="tpu_custom_call" | custom-call | flops 1000000000 | bytes 8000000 | tf_op jit(solution)/shard_map/embed_backward/pallas_call | solution.py:724
  391.3 44.5 %tail_exchange.1 = (bf16[8,2,40,320]{3,2,1,0:T(8,128)(2,1)}, f32[24,320]{1,0:T(8,128)}) custom-call(s32[13]{0:T(128)} %refs_0_.1, bf16[8,40,320]{2,1,0:T(8,128)(2,1)} %pad_maximum_fusion.refs_1_, bf16[2,2,2,1,40,320]{5,4,3,2,1,0:T(8,128)(2,1)} %get-tuple-element.171.refs_2_, bf16[1,16,2,1,40,320]{5,4,3,2,1,0:T(8,128)(2,1)} %bitcast.48, ...), custom_call_target="tpu_custom_call" | custom-call | tf_op jit(solution)/shard_map/tail_exchange/pallas_call | solution.py:1346
  435.8 1.2 slice.89
  437.0 1.1 convert_bitcast_fusion
  438.1 0.0 copy-start.2
  438.1 0.0 copy-start.5
  438.1 0.0 copy-start.6
  438.1 0.1 copy.44
  438.2 0.0 copy-start
  438.2 0.8 reshape.239
  439.0 0.0 copy-start.3
  439.0 0.0 copy-start.4
  439.0 1.6 multiply_subtract_fusion.2
  440.6 1.0 multiply_subtract_fusion.1
  441.6 3.9 multiply_subtract_fusion
  (35 shorter events, 0.2 us)
Async XLA Ops:
  7.2 5.5 %copy-start.12 = (s32[1024]{0:T(1024)S(1)}, s32[1024]{0:T(1024)}, u32[]{:S(2)}) copy-start(s32[1024]{0:T(1024)} %param.20) | copy-start | bytes 12292
  7.2 5.5 %copy-start.13 = (s32[1024]{0:T(1024)S(1)}, s32[1024]{0:T(1024)}, u32[]{:S(2)}) copy-start(s32[1024]{0:T(1024)} %param.19) | copy-start | bytes 12292
  7.2 165.0 %all-gather.2.cloned.1.call-start = ((), (), s32[]{:S(2)}) async-start(), calls=%async_computation | async-start | bytes 4055040 | tf_op jit(solution)/shard_map/all_gather | solution.py:1406
  10.6 83.2 %copy-start.16 = (s32[4,3]{1,0:T(4,128)S(1)}, s32[4,3]{1,0:T(4,128)}, u32[]{:S(2)}) copy-start(s32[4,3]{1,0:T(4,128)} %constant.143) | copy-start | bytes 148
  10.6 83.2 %copy-start.17 = (s32[4,3]{1,0:T(4,128)S(1)}, s32[4,3]{1,0:T(4,128)}, u32[]{:S(2)}) copy-start(s32[4,3]{1,0:T(4,128)} %constant.142) | copy-start | bytes 148
  10.6 83.7 %copy-start.1 = (f32[320,150]{0,1:T(8,128)S(1)}, f32[320,150]{0,1:T(8,128)}, u32[]{:S(2)}) copy-start(f32[320,150]{0,1:T(8,128)} %param.29) | copy-start | bytes 576004
  93.5 6.2 %copy-start.8 = (f32[22,320]{1,0:T(8,128)S(1)}, f32[22,320]{1,0:T(8,128)}, u32[]{:S(2)}) copy-start(f32[22,320]{1,0:T(8,128)} %param.26) | copy-start | bytes 84484
  100.3 8.6 %copy-start.14 = (s32[10,128]{1,0:T(8,128)S(1)}, s32[10,128]{1,0:T(8,128)}, u32[]{:S(2)}) copy-start(s32[10,128]{1,0:T(8,128)} %constant.141) | copy-start | bytes 15364
  100.3 8.6 %copy-start.15 = (s32[10,128]{1,0:T(8,128)S(1)}, s32[10,128]{1,0:T(8,128)}, u32[]{:S(2)}) copy-start(s32[10,128]{1,0:T(8,128)} %constant.140) | copy-start | bytes 15364
  358.9 24.1 %copy-start.9 = (bf16[2,40,320]{2,1,0:T(8,128)(2,1)S(1)}, bf16[2,40,320]{2,1,0:T(8,128)(2,1)}, u32[]{:S(2)}) copy-start(bf16[2,40,320]{2,1,0:T(8,128)(2,1)} %get-tuple-element.170) | copy-start | bytes 153604
  358.9 24.1 %copy-start.10 = (bf16[2,40,320]{2,1,0:T(8,128)(2,1)S(1)}, bf16[2,40,320]{2,1,0:T(8,128)(2,1)}, u32[]{:S(2)}) copy-start(bf16[2,40,320]{2,1,0:T(8,128)(2,1)} %get-tuple-element.169) | copy-start | bytes 153604
  358.9 24.1 %copy-start.11 = (bf16[2,40,320]{2,1,0:T(8,128)(2,1)S(1)}, bf16[2,40,320]{2,1,0:T(8,128)(2,1)}, u32[]{:S(2)}) copy-start(bf16[2,40,320]{2,1,0:T(8,128)(2,1)} %get-tuple-element.168) | copy-start | bytes 153604
  438.1 2.6 copy-start.2
  438.1 2.5 copy-start.5
  438.1 2.5 copy-start.6
  438.1 2.5 copy-start.7
  438.2 3.4 copy-start
  439.0 2.6 copy-start.3
  439.0 2.6 copy-start.4
Sparse Core Ops, SparseCore 0:
  93.7 63.8 all-gather.1

commit v7 on v6

--- a/solution.py
+++ b/solution.py
@@ -233,7 +233,7 @@
 
 def plan_sum(value, begin, end):
     make = functools.partial(SumRide, begin=begin, end=end)
-    return Plan(value, jax.ShapeDtypeStruct(value.shape, value.dtype), sum_scratch(value.shape), make)
+    return Plan(value, jax.ShapeDtypeStruct(value.shape, value.dtype), sum_scratch(value.shape, jnp.bfloat16), make)
 
 
 def plan_units(value, begin, end):
@@ -365,8 +365,8 @@
             span = slice(sub * tiles, (sub + 1) * tiles)
             low_ref[span, :] = grad_ref[span, :].astype(jnp.bfloat16)
         normed = norm_rows(middle_ref[...], gains_ref[0:1, :], gains_ref[1:2, :])[2]
-        normed_t_ref[...] = normed.T.astype(jnp.bfloat16)
-        low_t_ref[...] = grad_ref[...].T.astype(jnp.bfloat16)
+        normed_t_ref[...] = normed.astype(jnp.bfloat16).T
+        low_t_ref[...] = low_ref[...].T
         back_ref[...] = jnp.zeros_like(back_ref)
 
     for sub in range(4):
@@ -584,7 +584,7 @@
             keys = head_pair(key_ref[pl.ds(low, KEY_SPAN), lanes], group)
             values = head_pair(value_ref[pl.ds(low, KEY_SPAN), lanes], group)
             probs = softmax_columns(back_product(keys, query), bias)
-            probs = jnp.concatenate(probs, 0).T.astype(jnp.bfloat16)
+            probs = jnp.concatenate(probs, 0).astype(jnp.bfloat16).T
             put_planes(attended_ref, start, lanes, product(probs, values).astype(jnp.bfloat16))
 
     for sub in range(4):
@@ -814,7 +814,7 @@
     low_type = jnp.bfloat16
     advance(0)
     datt_ref[:, C:] = jnp.zeros((rows, WIDE - C), low_type)
-    turned_ref[...] = grad_ref[...].T.astype(low_type)
+    turned_ref[...] = grad_ref[...].astype(low_type).T
     dunits_ref[0, C : 2 * C, :] = product(turned_ref[...], attended_ref[:, :C]).T.astype(low_type)
     for sub in range(4):
         span = slice(sub * tiles, (sub + 1) * tiles)
@@ -846,9 +846,10 @@
                 dscores.append(prob * (dprob - inner) * HD ** (-0.5))
             dscores = jnp.concatenate(dscores, 0)
             probs = jnp.concatenate(probs, 0).astype(low_type)
-            dquery = product(dscores.T.astype(low_type), keys)
+            dscores = dscores.astype(low_type)
+            dquery = product(dscores.T, keys)
             put_planes(dquery_ref, start, lanes, dquery.astype(low_type))
-            dkeys = product(dscores.astype(low_type), query)
+            dkeys = product(dscores, query)
             dvalues = product(probs, datt)
             if group < 2:
                 first = lax.broadcasted_iota(jnp.int32, (KEY_SPAN, LANES), 1) < HD
@@ -1267,20 +1268,20 @@
 
     def advance(self, phase):
         if phase == 0:
-            self.sums[0] = self.source_ref[...]
+            self.sums[0] = self.source_ref[...].astype(self.sums.dtype)
         else:
             self.copy(phase - 1).wait()
             self.sums[2 * phase] = self.sums[2 * phase - 2] + self.sums[2 * phase - 1]
         if phase < self.phases:
             self.copy(phase).start()
         else:
-            self.total_ref[...] = self.sums[2 * phase]
-
-
-def sum_scratch(shape):
+            self.total_ref[...] = self.sums[2 * phase].astype(self.total_ref.dtype)
+
+
+def sum_scratch(shape, dtype=jnp.float32):
     phases = len(bit_order())
     dma = pltpu.SemaphoreType.DMA
-    return [dma((phases,)), dma((phases,)), pltpu.VMEM((2 * phases + 1,) + shape, jnp.float32)]
+    return [dma((phases,)), dma((phases,)), pltpu.VMEM((2 * phases + 1,) + shape, dtype)]
 
 
 def tail_kernel(counts, rows, *refs):
@@ -1444,7 +1445,7 @@
         resid, norm_params[tail + 2 : tail + 4], head_weight, labels[:, None], keep_mask[:, None], counted
     )
     unit_plans = []
-    head_cuts = [0, 1, 2, 3, 4, len(bit_order())]
+    head_cuts = [0, SPLIT, len(bit_order())]
     early = []
     kernel_grads = [None] * BLOCKS
     gain_grads = []
@@ -1464,7 +1465,8 @@
             grad_res, middle, norm_params[at + 4 : at + 6], w_up, *mlp_units, kernels, layer_at,
             stacks, real_rows, mlp_kept, unit_plans + head_plans(d_head), 2 + layer_at,
         )
-        d_head = ridden_out.pop()
+        if layer_at + 1 == BLOCKS:
+            d_head = ridden_out.pop()
         unit_plans = [plan_units(mlp_grads, 0, SPLIT)]
         if ridden_out:
             early.insert(0, ridden_out[1])

time: 456 us -> 443 us (0.971)
  Pallas kernels: 408 us -> 395 us
    pallas_call x3, Pallas kernels: 96.6 us -> 88 us  [mlp_backward(): pl.pallas_call(ridden(mlp_backward_kernel, 12, 4, 9, FF // block, plans),...]
    pallas_call x3, Pallas kernels: 77.9 us -> 73.1 us  [attention_backward(): pl.pallas_call(run, grid=(1,), out_shape=shapes + tuple((plan.out for pla...]
where the time goes in v7:
time: 443 us; the launch traced here: 439 us
  Pallas kernels  395 us (89%)
  other arithmetic  16.4 us (4%)
  between operations  16.1 us (4%)
  local copies, waits for them, and re-layouts  11.9 us (3%)
    pallas_call x3, Pallas kernels, mlp_backward(): pl.pallas_call(ridden(mlp_backward_kernel, 12, 4, 9, FF // block, plans),...  88 us
    pallas_call x1, Pallas kernels, start_exchange(): pl.pallas_call(start_kernel, out_shape=(jax.ShapeDtypeStruct(full_shape,...  79.6 us
    pallas_call x3, Pallas kernels, attention_backward(): pl.pallas_call(run, grid=(1,), out_shape=shapes + tuple((plan.out for pla...  73.1 us
    pallas_call x3, Pallas kernels, mlp_forward(): pl.pallas_call(mlp_forward_kernel, grid=(FF // block,), out_shape=(jax.Sh...  55.9 us
    pallas_call x1, Pallas kernels, tail_exchange(): pl.pallas_call(lambda *refs: tail_kernel(counts, rows, *refs), out_shape=...  45.8 us
    pallas_call x3, Pallas kernels, attention_forward(): pl.pallas_call(attention_forward_kernel, grid=(1,), out_shape=shapes, in_...  30.6 us
  transfers between devices with their start and end apart: 1, of which 0 were waited for; matrix products, arithmetic and copies ran while one was open for 3% of the time, Pallas kernels for 15%

profile of v7, /device:TPU:1, one launch (start us, length us, event | category | flops | bytes accessed | tf_op | source)
XLA Modules:
  0.0 439.2 jit_solution(7568380370420880817)
XLA Ops:
  7.2 0.0 all-gather.2.cloned.1.call-start
  7.2 1.3 fusion.66
  8.6 1.4 convert_element_type.46
  10.0 0.6 reshape.225
  10.6 0.0 copy-start.16
  10.6 0.0 copy-start.17
  10.6 0.0 copy-start.1
  10.6 0.8 copy.46
  12.7 0.6 pad_add_fusion.1.mark_ref
  13.3 0.6 convert_bitcast_fusion.1.count_ref
  13.9 79.6 %start_exchange.1 = (bf16[9,2,2,2,2,2,40,320]{7,6,5,4,3,2,1,0:T(8,128)(2,1)}, bf16[4,40,320]{2,1,0:T(8,128)(2,1)}, f32[8,128]{1,0:T(8,128)}, bf16[192,1152]{1,0:T(8,128)(2,1)}, s32[2,192]{1,0:T(2,128)}) custom-call(s32[13]{0:T(128)} %refs_0_.1, bf16[8,2,40,320]{3,2,1,0:T(8,128)(2,1)} %bitcast.47, f32[8,128]{1,0:T(8,128)} %convert_bitcast_fusion.1.count_ref, ...), custom_call_target="tpu_custom_call" | custom-call | tf_op jit(solution)/shard_map/start_exchange/pallas_call | solution.py:1111
  93.5 0.0 copy-start.8
  93.5 0.0 all-gather.2.cloned.1.call-update
  93.6 0.2 add_select_fusion.5
  93.8 0.1 add_select_fusion
  93.9 0.1 slice.94
  94.0 0.1 tile.10
  94.1 0.1 eq.57
  94.2 0.1 eq.61
  94.2 0.9 copy.41.weight_ref
  95.1 1.2 slice.90
  96.3 0.7 pad_add_fusion
  97.0 0.2 reshape.228
  97.2 0.1 copy.40
  97.4 0.1 convert_element_type.52
  97.5 1.1 copy.43.keep_ref
  98.6 1.1 broadcast_in_dim_squeeze.4.label_ref
  99.7 0.6 fusion.64
  100.3 7.9 %embed_forward.1 = (f32[1216,320]{1,0:T(8,128)}, f32[1216,320]{1,0:T(8,128)}, f32[3,9,1280]{2,1,0:T(8,128)}) custom-call(bf16[1024,1152]{1,0:T(8,128)(2,1)} %patches_ref.3, bf16[192,1152]{1,0:T(8,128)(2,1)} %get-tuple-element.98.halo_ref, bf16[9,1280,320]{2,1,0:T(8,128)(2,1)} %bitcast.31, f32[2,320]{1,0:T(2,128)} %get-tuple-element.198.gains_ref), custom_call_target="tpu_custom_call" | custom-call | flops 1000000000 | bytes 8000000 | tf_op jit(solution)/shard_map/embed_forward/pallas_call | solution.py:661
  108.2 0.6 fusion.65
  108.9 1.1 compare_select_fusion.bias_ref.refs_5_
  110.0 1.2 compare_convert_fusion.lower_ref.refs_7_
  111.2 1.3 fusion.upper_ref.refs_6_
  112.5 10.2 %attention_forward.3 = (f32[1216,320]{1,0:T(8,128)}, bf16[1216,320]{1,0:T(8,128)(2,1)}, bf16[1216,384]{1,0:T(8,128)(2,1)}, f32[304,320]{1,0:T(8,128)}, bf16[304,...) custom-call(f32[1216,320]{1,0:T(8,128)} %get-tuple-element.100.resid_ref.r, ...), custom_call_target="tpu_custom_call" | custom-call | flops 6000000000 | bytes 14000000 | tf_op jit(solution)/shard_map/attention_forward/pallas_call | solution.py:609
  122.7 0.8 broadcast_in_dim.34.real_ref.refs_8_
  123.5 18.4 %mlp_forward.3 = (f32[1216,320]{1,0:T(8,128)}, bf16[1216,1280]{1,0:T(8,128)(2,1)}, bf16[1216,1280]{1,0:T(8,128)(2,1)}, bf16[1216,1280]{1,0:T(8,128)(2,1)}, bf16[320,1280]{1,0:T(8,128)(2,1)}) custom-call(f32[1216,320]{1,0:T(8,128)} %get-tuple-element.101.middle_ref.refs_1_, f32[2,320]{1,0:T(2,128)} %get-tuple-element.197.gains_ref.refs_2_, ...), custom_call_target="tpu_custom_call" | custom-call | flops 14000000000 | bytes 18000000 | tf_op jit(solution)/shard_map/mlp_forward/pallas_call | solution.py:320
  141.9 10.2 %attention_forward.4 = (f32[1216,320]{1,0:T(8,128)}, bf16[1216,320]{1,0:T(8,128)(2,1)}, bf16[1216,384]{1,0:T(8,128)(2,1)}, f32[304,320]{1,0:T(8,128)}, bf16[304,...) custom-call(f32[1216,320]{1,0:T(8,128)} %get-tuple-element.103.resid_ref.r, ...), custom_call_target="tpu_custom_call" | custom-call | flops 6000000000 | bytes 14000000 | tf_op jit(solution)/shard_map/attention_forward/pallas_call | solution.py:609
  152.1 19.0 %mlp_forward.4 = (f32[1216,320]{1,0:T(8,128)}, bf16[1216,1280]{1,0:T(8,128)(2,1)}, bf16[1216,1280]{1,0:T(8,128)(2,1)}, bf16[1216,1280]{1,0:T(8,128)(2,1)}, bf16[320,1280]{1,0:T(8,128)(2,1)}) custom-call(f32[1216,320]{1,0:T(8,128)} %get-tuple-element.104.middle_ref.refs_1_, f32[2,320]{1,0:T(2,128)} %get-tuple-element.196.gains_ref.refs_2_, ...), custom_call_target="tpu_custom_call" | custom-call | flops 14000000000 | bytes 18000000 | tf_op jit(solution)/shard_map/mlp_forward/pallas_call | solution.py:320
  171.1 0.0 all-gather.2.cloned.1.call-done.unit_ref.reduce_ref.up_ref.down_ref.refs_4_.refs_3_
  171.2 10.2 %attention_forward.5 = (f32[1216,320]{1,0:T(8,128)}, bf16[1216,320]{1,0:T(8,128)(2,1)}, bf16[1216,384]{1,0:T(8,128)(2,1)}, f32[304,320]{1,0:T(8,128)}, bf16[304,...) custom-call(f32[1216,320]{1,0:T(8,128)} %get-tuple-element.105.resid_ref.r, ...), custom_call_target="tpu_custom_call" | custom-call | flops 6000000000 | bytes 14000000 | tf_op jit(solution)/shard_map/attention_forward/pallas_call | solution.py:609
  181.4 18.5 %mlp_forward.5 = (f32[1216,320]{1,0:T(8,128)}, bf16[1216,1280]{1,0:T(8,128)(2,1)}, bf16[1216,1280]{1,0:T(8,128)(2,1)}, bf16[1216,1280]{1,0:T(8,128)(2,1)}, bf16[320,1280]{1,0:T(8,128)(2,1)}) custom-call(f32[1216,320]{1,0:T(8,128)} %get-tuple-element.107.middle_ref.refs_1_, f32[2,320]{1,0:T(2,128)} %get-tuple-element.195.gains_ref.refs_2_, ...), custom_call_target="tpu_custom_call" | custom-call | flops 14000000000 | bytes 18000000 | tf_op jit(solution)/shard_map/mlp_forward/pallas_call | solution.py:320
  199.9 7.1 %head_step.1 = (f32[1216,320]{1,0:T(8,128)}, f32[152,320]{1,0:T(8,128)}, f32[2,320]{1,0:T(2,128)}, f32[1,320]{1,0:T(1,128)}) custom-call(f32[1216,320]{1,0:T(8,128)} %get-tuple-element.108.resid_ref, f32[2,320]{1,0:T(2,128)} %get-tuple-element.194.gains_ref, f32[320,150]{1,0:T(8,128)} %copy.41.weight_ref, s32[1216,1]{1,0:T(8,128)} %broadcast_in_dim_squeeze.4.label_ref, ...), custom_call_target="tpu_custom_call" | custom-call | flops 1000000000 | bytes 5000000 | tf_op jit(solution)/shard_map/head_step/pallas_call | solution.py:789
  206.9 28.7 %mlp_backward.3 = (f32[1216,320]{1,0:T(8,128)}, bf16[2,1280,320]{2,1,0:T(8,128)(2,1)}, f32[9,1280]{1,0:T(8,128)}, f32[2,320]{1,0:T(2,128)}, f32[152,320]{1,0:T(8,128)}) custom-call(f32[1216,320]{1,0:T(8,128)} %get-tuple-element.111.refs_0_, f32[1216,320]{1,0:T(8,128)} %get-tuple-element.107.middle_ref.refs_1_, ...), custom_call_target="tpu_custom_call" | custom-call | flops 17999998976 | bytes 18000000 | tf_op jit(solution)/shard_map/mlp_backward/pallas_call | solution.py:437
  235.6 25.7 %attention_backward.3 = (f32[1216,320]{1,0:T(8,128)}, bf16[2,1280,320]{2,1,0:T(8,128)(2,1)}, f32[4,320]{1,0:T(4,128)}, bf16[2,2,2,1,40,320]{5,4,3,2,1,0:T(8,128)(2,1)}, f32[152,320]{1,0:T(8,128)}) custom-call(f32[1216,320]{1,0:T(8,128)} %get-tuple-element.117.refs_0_, f32[1216,320]{1,0:T(8,128)} %get-tuple-element.105.resid_ref.refs_1_, ...), custom_call_target="tpu_custom_call" | custom-call | flops 12000000000 | bytes 18000000 | tf_op jit(solution)/shard_map/attention_backward/pallas_call | solution.py:920
  261.3 28.8 %mlp_backward.4 = (f32[1216,320]{1,0:T(8,128)}, bf16[2,1280,320]{2,1,0:T(8,128)(2,1)}, f32[9,1280]{1,0:T(8,128)}, f32[2,320]{1,0:T(2,128)}, bf16[2,2,2,1,40,320]...) custom-call(f32[1216,320]{1,0:T(8,128)} %get-tuple-element.127.refs_0_, ...), custom_call_target="tpu_custom_call" | custom-call | flops 17999998976 | bytes 18000000 | tf_op jit(solution)/shard_map/mlp_backward/pallas_call | solution.py:437
  290.1 24.4 %attention_backward.4 = (f32[1216,320]{1,0:T(8,128)}, bf16[2,1280,320]{2,1,0:T(8,128)(2,1)}, f32[4,320]{1,0:T(4,128)}, bf16[2,2,2,1,40,320]{5,4,3,2,1,0:T(8,128)(2,1)}, bf16[2,40,320]{2,1,0:T(8,128)(2,1)}) custom-call(f32[1216,320]{1,0:T(8,128)} %get-tuple-element.134.refs_0_, f32[1216,320]{1,0:T(8,128)} %get-tuple-element.103.resid_ref.refs_1_, ...), custom_call_target="tpu_custom_call" | custom-call | flops 12000000000 | bytes 18000000 | tf_op jit(solution)/shard_map/attention_backward/pallas_call | solution.py:920
  314.5 30.5 %mlp_backward.5 = (f32[1216,320]{1,0:T(8,128)}, bf16[2,1280,320]{2,1,0:T(8,128)(2,1)}, f32[9,1280]{1,0:T(8,128)}, f32[2,320]{1,0:T(2,128)}, bf16[2,2,2,1,40,320]...) custom-call(f32[1216,320]{1,0:T(8,128)} %get-tuple-element.144.refs_0_, ...), custom_call_target="tpu_custom_call" | custom-call | flops 17999998976 | bytes 18000000 | tf_op jit(solution)/shard_map/mlp_backward/pallas_call | solution.py:437
  345.1 23.1 %attention_backward.5 = (f32[1216,320]{1,0:T(8,128)}, bf16[2,1280,320]{2,1,0:T(8,128)(2,1)}, f32[4,320]{1,0:T(4,128)}, bf16[2,2,2,1,40,320]{5,4,3,2,1,0:T(8,128)(2,1)}, bf16[2,40,320]{2,1,0:T(8,128)(2,1)}) custom-call(f32[1216,320]{1,0:T(8,128)} %get-tuple-element.151.refs_0_, f32[1216,320]{1,0:T(8,128)} %get-tuple-element.100.resid_ref.refs_1_, ...), custom_call_target="tpu_custom_call" | custom-call | flops 12000000000 | bytes 18000000 | tf_op jit(solution)/shard_map/attention_backward/pallas_call | solution.py:920
  368.2 1.6 pad_maximum_fusion.refs_1_
  369.8 6.7 %embed_backward.1 = (bf16[1,1280,320]{2,1,0:T(8,128)(2,1)}, f32[2,320]{1,0:T(2,128)}) custom-call(f32[1216,320]{1,0:T(8,128)} %get-tuple-element.166.grad_ref, f32[1216,320]{1,0:T(8,128)} %get-tuple-element.167.pre_ref, f32[2,320]{1,0:T(2,128)} %get-tuple-element.198.gains_ref, bf16[1024,1152]{1,0:T(8,128)(2,1)} %patches_ref.3, ...), custom_call_target="tpu_custom_call" | custom-call | flops 1000000000 | bytes 8000000 | tf_op jit(solution)/shard_map/embed_backward/pallas_call | solution.py:724
  376.5 45.8 %tail_exchange.1 = (bf16[8,2,40,320]{3,2,1,0:T(8,128)(2,1)}, f32[24,320]{1,0:T(8,128)}) custom-call(s32[13]{0:T(128)} %refs_0_.1, bf16[8,40,320]{2,1,0:T(8,128)(2,1)} %pad_maximum_fusion.refs_1_, bf16[2,2,2,1,40,320]{5,4,3,2,1,0:T(8,128)(2,1)} %get-tuple-element.165.refs_2_, bf16[1,16,2,1,40,320]{5,4,3,2,1,0:T(8,128)(2,1)} %bitcast.48, ...), custom_call_target="tpu_custom_call" | custom-call | tf_op jit(solution)/shard_map/tail_exchange/pallas_call | solution.py:1347
  422.3 1.2 slice.89
  423.5 1.1 convert_bitcast_fusion
  424.6 0.0 copy-start.2
  424.6 0.0 copy-start.5
  424.6 0.0 copy-start.6
  424.6 0.1 copy.44
  424.7 0.0 copy-start
  424.7 0.8 reshape.239
  425.5 0.0 copy-start.3
  425.5 0.0 copy-start.4
  425.5 1.6 multiply_subtract_fusion.2
  427.1 1.0 multiply_subtract_fusion.1
  428.1 3.9 multiply_subtract_fusion
  (35 shorter events, 0.2 us)
Async XLA Ops:
  7.2 5.5 %copy-start.12 = (s32[1024]{0:T(1024)S(1)}, s32[1024]{0:T(1024)}, u32[]{:S(2)}) copy-start(s32[1024]{0:T(1024)} %param.20) | copy-start | bytes 12292
  7.2 5.5 %copy-start.13 = (s32[1024]{0:T(1024)S(1)}, s32[1024]{0:T(1024)}, u32[]{:S(2)}) copy-start(s32[1024]{0:T(1024)} %param.19) | copy-start | bytes 12292
  7.2 163.9 %all-gather.2.cloned.1.call-start = ((), (), s32[]{:S(2)}) async-start(), calls=%async_computation | async-start | bytes 4055040 | tf_op jit(solution)/shard_map/all_gather | solution.py:1407
  10.6 83.2 %copy-start.16 = (s32[4,3]{1,0:T(4,128)S(1)}, s32[4,3]{1,0:T(4,128)}, u32[]{:S(2)}) copy-start(s32[4,3]{1,0:T(4,128)} %constant.143) | copy-start | bytes 148
  10.6 83.2 %copy-start.17 = (s32[4,3]{1,0:T(4,128)S(1)}, s32[4,3]{1,0:T(4,128)}, u32[]{:S(2)}) copy-start(s32[4,3]{1,0:T(4,128)} %constant.142) | copy-start | bytes 148
  10.6 83.7 %copy-start.1 = (f32[320,150]{0,1:T(8,128)S(1)}, f32[320,150]{0,1:T(8,128)}, u32[]{:S(2)}) copy-start(f32[320,150]{0,1:T(8,128)} %param.29) | copy-start | bytes 576004
  93.5 6.2 %copy-start.8 = (f32[22,320]{1,0:T(8,128)S(1)}, f32[22,320]{1,0:T(8,128)}, u32[]{:S(2)}) copy-start(f32[22,320]{1,0:T(8,128)} %param.26) | copy-start | bytes 84484
  100.3 8.5 %copy-start.14 = (s32[10,128]{1,0:T(8,128)S(1)}, s32[10,128]{1,0:T(8,128)}, u32[]{:S(2)}) copy-start(s32[10,128]{1,0:T(8,128)} %constant.141) | copy-start | bytes 15364
  100.3 8.5 %copy-start.15 = (s32[10,128]{1,0:T(8,128)S(1)}, s32[10,128]{1,0:T(8,128)}, u32[]{:S(2)}) copy-start(s32[10,128]{1,0:T(8,128)} %constant.140) | copy-start | bytes 15364
  345.0 23.2 %copy-start.9 = (bf16[2,40,320]{2,1,0:T(8,128)(2,1)S(1)}, bf16[2,40,320]{2,1,0:T(8,128)(2,1)}, u32[]{:S(2)}) copy-start(bf16[2,40,320]{2,1,0:T(8,128)(2,1)} %get-tuple-element.164) | copy-start | bytes 153604
  345.0 23.2 %copy-start.10 = (bf16[2,40,320]{2,1,0:T(8,128)(2,1)S(1)}, bf16[2,40,320]{2,1,0:T(8,128)(2,1)}, u32[]{:S(2)}) copy-start(bf16[2,40,320]{2,1,0:T(8,128)(2,1)} %get-tuple-element.163) | copy-start | bytes 153604
  345.1 23.2 %copy-start.11 = (bf16[2,40,320]{2,1,0:T(8,128)(2,1)S(1)}, bf16[2,40,320]{2,1,0:T(8,128)(2,1)}, u32[]{:S(2)}) copy-start(bf16[2,40,320]{2,1,0:T(8,128)(2,1)} %get-tuple-element.162) | copy-start | bytes 153604
  424.6 2.6 copy-start.2
  424.6 2.5 copy-start.5
  424.6 2.5 copy-start.6
  424.6 2.5 copy-start.7
  424.7 3.4 copy-start
  425.5 2.6 copy-start.3
  425.5 2.6 copy-start.4
Sparse Core Ops, SparseCore 0:
  93.7 63.8 all-gather.1

commit v8 on v7

--- a/solution.py
+++ b/solution.py
@@ -227,8 +227,8 @@
 class Plan:
     def __init__(self, value, out, scratch, make, space=None):
         self.value, self.out, self.scratch, self.make = value, out, scratch, make
-        self.in_spec = whole(value.shape)
-        self.out_spec = pl.BlockSpec(memory_space=space) if space is not None else whole(out.shape)
+        self.in_spec = pl.BlockSpec(memory_space=space) if space is not None else whole(value.shape)
+        self.out_spec = whole(out.shape)
 
 
 def plan_sum(value, begin, end):
@@ -247,7 +247,8 @@
         sources = [(ride_in, at) for at in range(total)]
         return UnitRide(sources, ride_out, scratch, begin, end)
 
-    return Plan(value, out, unit_scratch(total, chunk, width, begin, end), make)
+    space = pl.ANY if begin == 0 else None
+    return Plan(value, out, unit_scratch(total, chunk, width, begin, end), make, space)
 
 
 class Rides:
@@ -1065,7 +1066,7 @@
 
 def start_kernel(
     owner_ref, piece_ref, count_ref, patch_ref, mark_ref,
-    full_ref, later_ref, total_ref, patch_halo_ref, mark_halo_ref,
+    full_ref, later_ref, total_ref, patch_halo_ref, mark_halo_ref, scalar_ref,
     recv_ref, near_s, near_r, halo_s, halo_r, *scratch,
 ):
     grp, tok, n_tok, peers = exchange_setup()
@@ -1098,6 +1099,7 @@
     total_ref[...] = jnp.broadcast_to(
         jnp.sum(jnp.sum(total_ref[...], 0, keepdims=True), 1, keepdims=True), total_ref.shape
     )
+    scalar_ref[...] = total_ref[0:1, 0:1]
     mark_copy.wait()
     patch_copy.wait()
 
@@ -1116,9 +1118,10 @@
             jax.ShapeDtypeStruct(count.shape, count.dtype),
             jax.ShapeDtypeStruct((OVER, patches.shape[1]), patches.dtype),
             jax.ShapeDtypeStruct(marks.shape, marks.dtype),
+            jax.ShapeDtypeStruct((1, 1), jnp.float32),
         ),
         in_specs=[pl.BlockSpec(memory_space=pltpu.SMEM), vmem, vmem, pl.BlockSpec(memory_space=pl.ANY), vmem],
-        out_specs=(vmem, vmem, vmem, pl.BlockSpec(memory_space=pl.ANY), vmem),
+        out_specs=(vmem, vmem, vmem, pl.BlockSpec(memory_space=pl.ANY), vmem, vmem),
         scratch_shapes=[
             pltpu.VMEM((n_tok * slot_rows, chunk, width), pieces.dtype),
             pltpu.SemaphoreType.DMA((n_tok,)),
@@ -1163,6 +1166,10 @@
         self.sources = sources
         self.out_ref, self.base = out_ref, base
         self.sems = scratch[:2]
+        self.stays = []
+        if begin == 0:
+            self.stay_sem, self.stays = scratch[2], scratch[3 : 3 + len(sources)]
+            scratch = scratch[1 + len(sources) :]
         self.buffers = scratch[2:]
 
     def partner(self, name):
@@ -1195,12 +1202,21 @@
             device_id_type=MESH,
         )
 
+    def stay(self, unit):
+        mine = self.half_of(unit_order(unit)[0])
+        source = self.before(unit, 0).at[:, mine]
+        return pltpu.make_async_copy(source, self.stays[unit], self.stay_sem.at[unit])
+
     def finish(self, unit, phase):
         order = unit_order(unit)
         shapes = unit_layout(order)
         self.copy(unit, phase).wait()
         outer, _, inner = shapes[self.begin + phase]
-        source, landed = self.before(unit, phase), self.landing(unit, phase)
+        landed = self.landing(unit, phase)
+        kept = self.stays and phase == 0
+        if kept:
+            self.stay(unit).wait()
+        source = self.stays[unit] if kept else self.before(unit, phase)
         mine = self.half_of(order[self.begin + phase])
         target = self.out_ref.at[self.base + unit]
         if phase + 1 < self.phases:
@@ -1211,7 +1227,8 @@
 
         @pl.loop(0, outer * inner, unroll=min(4, outer * inner))
         def _(at):
-            value = source[at // inner, mine, at % inner] + landed[at // inner, at % inner]
+            own = source[at // inner, at % inner] if kept else source[at // inner, mine, at % inner]
+            value = own + landed[at // inner, at % inner]
             if whole_done:
                 target[...] = value
             else:
@@ -1223,12 +1240,17 @@
                 self.finish(unit, phase - 1)
             if phase < self.phases:
                 self.copy(unit, phase).start()
+            if self.stays and phase == 0:
+                self.stay(unit).start()
 
 
 def unit_scratch(total, chunk, width, begin=0, end=None):
     end = len(bit_order()) if end is None else end
     dma = pltpu.SemaphoreType.DMA
     buffers = [dma(((end - begin) * total,)), dma(((end - begin) * total,))]
+    if begin == 0:
+        outer, _, inner = unit_layout(unit_order(0))[0]
+        buffers += [dma((total,))] + [pltpu.VMEM((outer, inner, chunk, width), jnp.bfloat16)] * total
     for unit in range(total):
         shapes = unit_layout(unit_order(unit))
         for phase in range(begin, end):
@@ -1284,12 +1306,13 @@
     return [dma((phases,)), dma((phases,)), pltpu.VMEM((2 * phases + 1,) + shape, dtype)]
 
 
-def tail_kernel(counts, rows, *refs):
-    owner_ref, early_ref, part_ref = refs[:3]
-    blocks, refs = refs[3 : 3 + len(counts)], refs[3 + len(counts) :]
+def tail_kernel(counts, rows, pieces, cut, *refs):
+    owner_ref, part_ref, refs = refs[0], refs[1], refs[2:]
+    early_refs, refs = refs[: len(pieces)], refs[len(pieces) :]
+    blocks, refs = refs[: len(counts)], refs[len(counts) :]
     small_refs, refs = refs[: len(rows)], refs[len(rows) :]
-    owned_ref, small_out_ref, chunk_ref, place_ref, near_s, near_r, small_ref = refs[:7]
-    scratch = refs[7:]
+    owned_ref, small_out_ref, loss_ref, chunk_ref, place_ref, near_s, near_r, small_ref = refs[:8]
+    scratch = refs[8:]
     sources = [(ref, at) for ref, count in zip(blocks, counts) for at in range(count)]
     total = len(sources)
     parts = part_ref.shape[0]
@@ -1300,7 +1323,6 @@
         small_ref[begin : begin + count, :] = ref[...]
         begin += count
     small_ref[begin:, :] = jnp.zeros((small_ref.shape[0] - begin, C), jnp.float32)
-    cut = 3 + 2 + 2 * total * len(bit_order())
     rides = Rides(
         [
             UnitRide(sources, chunk_ref, scratch[3:cut]),
@@ -1312,9 +1334,12 @@
     for phase in range(rides.phases + 1):
         rides.advance(phase)
     total += parts
-    for at in range(early_ref.shape[0]):
-        chunk_ref[total + at] = early_ref[at]
-    last = total + early_ref.shape[0]
+    loss_ref[...] = small_out_ref[begin - 1 : begin, 0:1]
+    last = total
+    for ref, count in zip(early_refs, pieces):
+        for at in range(count):
+            chunk_ref[last + at] = ref[at]
+        last += count
     chunk_ref[last] = jnp.zeros(chunk_ref.shape[1:], chunk_ref.dtype)
     slot_rows = owned_ref.shape[1]
     slots = slot_numbers(owner_ref, slot_rows)
@@ -1336,35 +1361,41 @@
 
 
 def tail_exchange(owners, slot_rows, early, part, sources, smalls, n_tok):
-    chunk, width = early.shape[1:]
+    chunk, width = early[0].shape[1:]
+    pieces = tuple(value.shape[0] for value in early)
     counts = tuple(source.shape[0] for source in sources)
     rows = tuple(small.shape[0] for small in smalls)
     total = sum(counts)
-    low = early.dtype
+    low = part.dtype
     vmem = pl.BlockSpec(memory_space=pltpu.VMEM)
+    units = unit_scratch(total, chunk, width)
     dma = pltpu.SemaphoreType.DMA
     small = (-(-sum(rows) // 8) * 8, C)
     return pl.pallas_call(
-        lambda *refs: tail_kernel(counts, rows, *refs),
+        lambda *refs: tail_kernel(counts, rows, pieces, 3 + len(units), *refs),
         out_shape=(
             jax.ShapeDtypeStruct((n_tok, slot_rows, chunk, width), low),
             jax.ShapeDtypeStruct(small, jnp.float32),
+            jax.ShapeDtypeStruct((1, 1), jnp.float32),
         ),
-        in_specs=[pl.BlockSpec(memory_space=pltpu.SMEM)] + [vmem] * (2 + len(sources) + len(smalls)),
-        out_specs=(vmem, vmem),
+        in_specs=[pl.BlockSpec(memory_space=pltpu.SMEM)]
+        + [vmem] * (1 + len(early))
+        + [pl.BlockSpec(memory_space=pl.ANY)] * len(sources)
+        + [vmem] * len(smalls),
+        out_specs=(vmem, vmem, vmem),
         scratch_shapes=[
-            pltpu.VMEM((total + part.shape[0] + early.shape[0] + 1, chunk, width), low),
+            pltpu.VMEM((total + part.shape[0] + sum(pieces) + 1, chunk, width), low),
             pltpu.VMEM((n_tok, slot_rows, chunk, width), low),
             dma((n_tok,)),
             dma((n_tok,)),
             pltpu.VMEM(small, jnp.float32),
         ]
         + sum_scratch(small)
-        + unit_scratch(total, chunk, width)
+        + units
         + unit_scratch(part.shape[0], chunk, width, SPLIT),
         compiler_params=pltpu.CompilerParams(collective_id=1, has_side_effects=True, vmem_limit_bytes=VMEM_LIMIT),
         name="tail_exchange",
-    )(owners, early, part, *[unit_blocks(source) for source in sources], *smalls)
+    )(owners, part, *early, *[unit_blocks(source) for source in sources], *smalls)
 
 
 def body(
@@ -1399,10 +1430,10 @@
     pieces = slot_weight.astype(jnp.bfloat16).reshape(slot_rows, n_tok, chunk, C).transpose(1, 0, 2, 3)
     first_units = 1 + 2 * (n_unit // BLOCKS)
     marks = jnp.stack([labels, valid_mask])
-    own, later, counted, patch_halo, mark_halo = start_exchange(
+    own, later, counted, patch_halo, mark_halo, pixel_total = start_exchange(
         owners, pieces, counted, patches, marks[:, :OVER], first_units
     )
-    pixel_total = counted[0, 0]
+    pixel_total = pixel_total.reshape(())
     own = own.reshape(first_units, FF, C)
     units = lax.all_gather(later, BOTH, axis=1, tiled=True)
     layers = [
@@ -1486,12 +1517,12 @@
     first_grad, embed_gains = embed_backward(
         grad_res, embed_pre, norm_params[tail : tail + 2], patches, patch_halo, kernel_grads
     )
-    early = jnp.concatenate(early, 0)
     smalls = gain_grads + [embed_gains, final_gains, loss_row]
-    owned, small = tail_exchange(owners, slot_rows, early, part, [first_grad, attn_grads], smalls, n_tok)
+    owned, small, loss_sum = tail_exchange(owners, slot_rows, early, part, [first_grad, attn_grads], smalls, n_tok)
     owned = owned.transpose(1, 0, 2, 3).astype(jnp.float32).reshape(slot_rows, columns)
     norm_rows_all = norm_params.shape[0]
-    norm_total, loss_sum = (small[:norm_rows_all], small[norm_rows_all, 0])
+    norm_total = small[:norm_rows_all]
+    loss_sum = loss_sum.reshape(())
     slot_m, slot_v, slot_w = adamw_step(
         slot_weight, slot_moment, slot_second, owned, RATE_MATRIX, DECAY_RATE
     )

time: 443 us -> 439 us (level)
  transfers between devices with their start and end apart: 1 -> 1, of which waited for: 0 -> 0; matrix products, arithmetic and copies ran while one was open for 3% -> 2% of each run, Pallas kernels for 15% -> 15%
where the time goes in v8:
time: 439 us; the launch traced here: 435 us
  Pallas kernels  391 us (89%)
  between operations  19.6 us (4%)
  other arithmetic  14.8 us (3%)
  local copies, waits for them, and re-layouts  9.49 us (2%)
    pallas_call x3, Pallas kernels, mlp_backward(): pl.pallas_call(ridden(mlp_backward_kernel, 12, 4, 9, FF // block, plans),...  86.9 us
    pallas_call x1, Pallas kernels, start_exchange(): pl.pallas_call(start_kernel, out_shape=(jax.ShapeDtypeStruct(full_shape,...  79.6 us
    pallas_call x3, Pallas kernels, attention_backward(): pl.pallas_call(run, grid=(1,), out_shape=shapes + tuple((plan.out for pla...  71.5 us
    pallas_call x3, Pallas kernels, mlp_forward(): pl.pallas_call(mlp_forward_kernel, grid=(FF // block,), out_shape=(jax.Sh...  55.8 us
    pallas_call x1, Pallas kernels, tail_exchange(): pl.pallas_call(lambda *refs: tail_kernel(counts, rows, pieces, 3 + len(un...  45.4 us
    pallas_call x3, Pallas kernels, attention_forward(): pl.pallas_call(attention_forward_kernel, grid=(1,), out_shape=shapes, in_...  30.7 us
  transfers between devices with their start and end apart: 1, of which 0 were waited for; matrix products, arithmetic and copies ran while one was open for 2% of the time, Pallas kernels for 15%

profile of v8, /device:TPU:1, one launch (start us, length us, event | category | flops | bytes accessed | tf_op | source)
XLA Modules:
  0.0 435.3 jit_solution(822203618457674929)
XLA Ops:
  7.2 0.0 copy-start.9
  7.2 0.0 copy-start.10
  7.2 0.0 all-gather.2.cloned.1.call-start
  7.2 1.3 fusion.66
  8.6 1.4 convert_element_type.46
  10.0 0.6 reshape.231
  10.6 0.0 copy-start.13
  10.6 0.0 copy-start.14
  10.6 0.0 copy-start.1
  10.6 0.8 copy.46
  12.7 0.6 pad_add_fusion.1.mark_ref
  13.3 0.6 convert_bitcast_fusion.1.count_ref
  13.9 79.6 %start_exchange.1 = (bf16[9,2,2,2,2,2,40,320]{7,6,5,4,3,2,1,0:T(8,128)(2,1)}, bf16[4,40,320]{2,1,0:T(8,128)(2,1)}, f32[8,128]{1,0:T(8,128)}, bf16[192,1152]{1,0:...) custom-call(s32[13]{0:T(128)} %refs_0_.1, bf16[8,2,40,320]{3,2,1,0:T(8,128)(2,1)} %bitcast.47, ...), custom_call_target="tpu_custom_call" | custom-call | tf_op jit(solution)/shard_map/start_exchange/pallas_call | solution.py:1113
  93.5 0.0 copy-start.8
  93.5 0.0 all-gather.2.cloned.1.call-update
  93.6 0.2 add_select_fusion.5
  93.7 0.0 copy-done.13
  93.8 0.1 add_select_fusion
  93.9 0.1 slice.86
  94.0 0.1 tile.10
  94.1 0.1 eq.57
  94.2 0.1 eq.61
  94.3 0.9 copy.41.weight_ref
  95.2 0.7 pad_add_fusion
  95.8 0.2 reshape.234
  96.0 0.1 copy.40
  96.2 0.1 convert_element_type.52
  96.3 1.1 copy.43.keep_ref
  97.4 1.1 broadcast_in_dim_squeeze.4.label_ref
  98.5 0.6 fusion.64
  99.1 7.9 %embed_forward.1 = (f32[1216,320]{1,0:T(8,128)}, f32[1216,320]{1,0:T(8,128)}, f32[3,9,1280]{2,1,0:T(8,128)}) custom-call(bf16[1024,1152]{1,0:T(8,128)(2,1)} %patches_ref.3, bf16[192,1152]{1,0:T(8,128)(2,1)} %get-tuple-element.100.halo_ref, bf16[9,1280,320]{2,1,0:T(8,128)(2,1)} %bitcast.31, f32[2,320]{1,0:T(2,128)} %get-tuple-element.202.gains_ref), custom_call_target="tpu_custom_call" | custom-call | flops 1000000000 | bytes 8000000 | tf_op jit(solution)/shard_map/embed_forward/pallas_call | solution.py:662
  107.0 0.6 fusion.65
  107.7 1.1 compare_select_fusion.bias_ref.refs_5_
  108.8 1.2 compare_convert_fusion.lower_ref.refs_7_
  110.0 1.3 fusion.upper_ref.refs_6_
  111.3 10.2 %attention_forward.3 = (f32[1216,320]{1,0:T(8,128)}, bf16[1216,320]{1,0:T(8,128)(2,1)}, bf16[1216,384]{1,0:T(8,128)(2,1)}, f32[304,320]{1,0:T(8,128)}, bf16[304,...) custom-call(f32[1216,320]{1,0:T(8,128)} %get-tuple-element.102.resid_ref.r, ...), custom_call_target="tpu_custom_call" | custom-call | flops 6000000000 | bytes 14000000 | tf_op jit(solution)/shard_map/attention_forward/pallas_call | solution.py:610
  121.5 0.8 broadcast_in_dim.34.real_ref.refs_8_
  122.3 18.4 %mlp_forward.3 = (f32[1216,320]{1,0:T(8,128)}, bf16[1216,1280]{1,0:T(8,128)(2,1)}, bf16[1216,1280]{1,0:T(8,128)(2,1)}, bf16[1216,1280]{1,0:T(8,128)(2,1)}, bf16[320,1280]{1,0:T(8,128)(2,1)}) custom-call(f32[1216,320]{1,0:T(8,128)} %get-tuple-element.103.middle_ref.refs_1_, f32[2,320]{1,0:T(2,128)} %get-tuple-element.201.gains_ref.refs_2_, ...), custom_call_target="tpu_custom_call" | custom-call | flops 14000000000 | bytes 18000000 | tf_op jit(solution)/shard_map/mlp_forward/pallas_call | solution.py:321
  140.7 10.2 %attention_forward.4 = (f32[1216,320]{1,0:T(8,128)}, bf16[1216,320]{1,0:T(8,128)(2,1)}, bf16[1216,384]{1,0:T(8,128)(2,1)}, f32[304,320]{1,0:T(8,128)}, bf16[304,...) custom-call(f32[1216,320]{1,0:T(8,128)} %get-tuple-element.105.resid_ref.r, ...), custom_call_target="tpu_custom_call" | custom-call | flops 6000000000 | bytes 14000000 | tf_op jit(solution)/shard_map/attention_forward/pallas_call | solution.py:610
  151.0 18.9 %mlp_forward.4 = (f32[1216,320]{1,0:T(8,128)}, bf16[1216,1280]{1,0:T(8,128)(2,1)}, bf16[1216,1280]{1,0:T(8,128)(2,1)}, bf16[1216,1280]{1,0:T(8,128)(2,1)}, bf16[320,1280]{1,0:T(8,128)(2,1)}) custom-call(f32[1216,320]{1,0:T(8,128)} %get-tuple-element.106.middle_ref.refs_1_, f32[2,320]{1,0:T(2,128)} %get-tuple-element.200.gains_ref.refs_2_, ...), custom_call_target="tpu_custom_call" | custom-call | flops 14000000000 | bytes 18000000 | tf_op jit(solution)/shard_map/mlp_forward/pallas_call | solution.py:321
  169.8 0.0 all-gather.2.cloned.1.call-done.unit_ref.reduce_ref.up_ref.down_ref.refs_4_.refs_3_
  169.9 10.2 %attention_forward.5 = (f32[1216,320]{1,0:T(8,128)}, bf16[1216,320]{1,0:T(8,128)(2,1)}, bf16[1216,384]{1,0:T(8,128)(2,1)}, f32[304,320]{1,0:T(8,128)}, bf16[304,...) custom-call(f32[1216,320]{1,0:T(8,128)} %get-tuple-element.107.resid_ref.r, ...), custom_call_target="tpu_custom_call" | custom-call | flops 6000000000 | bytes 14000000 | tf_op jit(solution)/shard_map/attention_forward/pallas_call | solution.py:610
  180.1 18.5 %mlp_forward.5 = (f32[1216,320]{1,0:T(8,128)}, bf16[1216,1280]{1,0:T(8,128)(2,1)}, bf16[1216,1280]{1,0:T(8,128)(2,1)}, bf16[1216,1280]{1,0:T(8,128)(2,1)}, bf16[320,1280]{1,0:T(8,128)(2,1)}) custom-call(f32[1216,320]{1,0:T(8,128)} %get-tuple-element.109.middle_ref.refs_1_, f32[2,320]{1,0:T(2,128)} %get-tuple-element.199.gains_ref.refs_2_, ...), custom_call_target="tpu_custom_call" | custom-call | flops 14000000000 | bytes 18000000 | tf_op jit(solution)/shard_map/mlp_forward/pallas_call | solution.py:321
  198.6 7.0 %head_step.1 = (f32[1216,320]{1,0:T(8,128)}, f32[152,320]{1,0:T(8,128)}, f32[2,320]{1,0:T(2,128)}, f32[1,320]{1,0:T(1,128)}) custom-call(f32[1216,320]{1,0:T(8,128)} %get-tuple-element.110.resid_ref, f32[2,320]{1,0:T(2,128)} %get-tuple-element.198.gains_ref, f32[320,150]{1,0:T(8,128)} %copy.41.weight_ref, s32[1216,1]{1,0:T(8,128)} %broadcast_in_dim_squeeze.4.label_ref, ...), custom_call_target="tpu_custom_call" | custom-call | flops 1000000000 | bytes 5000000 | tf_op jit(solution)/shard_map/head_step/pallas_call | solution.py:790
  205.6 28.9 %mlp_backward.3 = (f32[1216,320]{1,0:T(8,128)}, bf16[2,1280,320]{2,1,0:T(8,128)(2,1)}, f32[9,1280]{1,0:T(8,128)}, f32[2,320]{1,0:T(2,128)}, f32[152,320]{1,0:T(8,128)}) custom-call(f32[1216,320]{1,0:T(8,128)} %get-tuple-element.113.refs_0_, f32[1216,320]{1,0:T(8,128)} %get-tuple-element.109.middle_ref.refs_1_, ...), custom_call_target="tpu_custom_call" | custom-call | flops 17999998976 | bytes 18000000 | tf_op jit(solution)/shard_map/mlp_backward/pallas_call | solution.py:438
  234.5 25.2 %attention_backward.3 = (f32[1216,320]{1,0:T(8,128)}, bf16[2,1280,320]{2,1,0:T(8,128)(2,1)}, f32[4,320]{1,0:T(4,128)}, bf16[2,2,2,1,40,320]{5,4,3,2,1,0:T(8,128)(2,1)}, f32[152,320]{1,0:T(8,128)}) custom-call(f32[1216,320]{1,0:T(8,128)} %get-tuple-element.119.refs_0_, f32[1216,320]{1,0:T(8,128)} %get-tuple-element.107.resid_ref.refs_1_, ...), custom_call_target="tpu_custom_call" | custom-call | flops 12000000000 | bytes 18000000 | tf_op jit(solution)/shard_map/attention_backward/pallas_call | solution.py:921
  259.6 28.2 %mlp_backward.4 = (f32[1216,320]{1,0:T(8,128)}, bf16[2,1280,320]{2,1,0:T(8,128)(2,1)}, f32[9,1280]{1,0:T(8,128)}, f32[2,320]{1,0:T(2,128)}, bf16[2,2,2,1,40,320]...) custom-call(f32[1216,320]{1,0:T(8,128)} %get-tuple-element.129.refs_0_, ...), custom_call_target="tpu_custom_call" | custom-call | flops 17999998976 | bytes 18000000 | tf_op jit(solution)/shard_map/mlp_backward/pallas_call | solution.py:438
  287.9 23.9 %attention_backward.4 = (f32[1216,320]{1,0:T(8,128)}, bf16[2,1280,320]{2,1,0:T(8,128)(2,1)}, f32[4,320]{1,0:T(4,128)}, bf16[2,2,2,1,40,320]{5,4,3,2,1,0:T(8,128)(2,1)}, bf16[2,40,320]{2,1,0:T(8,128)(2,1)}) custom-call(f32[1216,320]{1,0:T(8,128)} %get-tuple-element.136.refs_0_, f32[1216,320]{1,0:T(8,128)} %get-tuple-element.105.resid_ref.refs_1_, ...), custom_call_target="tpu_custom_call" | custom-call | flops 12000000000 | bytes 18000000 | tf_op jit(solution)/shard_map/attention_backward/pallas_call | solution.py:921
  311.7 29.8 %mlp_backward.5 = (f32[1216,320]{1,0:T(8,128)}, bf16[2,1280,320]{2,1,0:T(8,128)(2,1)}, f32[9,1280]{1,0:T(8,128)}, f32[2,320]{1,0:T(2,128)}, bf16[2,2,2,1,40,320]...) custom-call(f32[1216,320]{1,0:T(8,128)} %get-tuple-element.146.refs_0_, ...), custom_call_target="tpu_custom_call" | custom-call | flops 17999998976 | bytes 18000000 | tf_op jit(solution)/shard_map/mlp_backward/pallas_call | solution.py:438
  341.5 22.4 %attention_backward.5 = (f32[1216,320]{1,0:T(8,128)}, bf16[2,1280,320]{2,1,0:T(8,128)(2,1)}, f32[4,320]{1,0:T(4,128)}, bf16[2,2,2,1,40,320]{5,4,3,2,1,0:T(8,128)(2,1)}, bf16[2,40,320]{2,1,0:T(8,128)(2,1)}) custom-call(f32[1216,320]{1,0:T(8,128)} %get-tuple-element.153.refs_0_, f32[1216,320]{1,0:T(8,128)} %get-tuple-element.102.resid_ref.refs_1_, ...), custom_call_target="tpu_custom_call" | custom-call | flops 12000000000 | bytes 18000000 | tf_op jit(solution)/shard_map/attention_backward/pallas_call | solution.py:921
  364.0 6.7 %embed_backward.1 = (bf16[1,1280,320]{2,1,0:T(8,128)(2,1)}, f32[2,320]{1,0:T(2,128)}) custom-call(f32[1216,320]{1,0:T(8,128)} %get-tuple-element.168.grad_ref, f32[1216,320]{1,0:T(8,128)} %get-tuple-element.169.pre_ref, f32[2,320]{1,0:T(2,128)} %get-tuple-element.202.gains_ref, bf16[1024,1152]{1,0:T(8,128)(2,1)} %patches_ref.3, ...), custom_call_target="tpu_custom_call" | custom-call | flops 1000000000 | bytes 8000000 | tf_op jit(solution)/shard_map/embed_backward/pallas_call | solution.py:725
  370.7 45.4 %tail_exchange.1 = (bf16[8,2,40,320]{3,2,1,0:T(8,128)(2,1)}, f32[24,320]{1,0:T(8,128)}, f32[1,1]{1,0:T(1,128)}) custom-call(s32[13]{0:T(128)} %refs_0_.1, bf16[2,2,2,1,40,320]{5,4,3,2,1,0:T(8,128)(2,1)} %get-tuple-element.163.refs_1_, bf16[2,40,320]{2,1,0:T(8,128)(2,1)} %get-tuple-element.164.refs_2_, bf16[2,40,320]{2,1,0:T(8,128)(2,1)} %get-tuple-element.165.refs_3_, ...), custom_call_target="tpu_custom_call" | custom-call | tf_op jit(solution)/shard_map/tail_exchange/pallas_call | solution.py:1374
  416.0 1.1 convert_bitcast_fusion
  417.1 0.0 copy-start.2
  417.2 0.0 copy-start.5
  417.2 0.0 copy-start.6
  417.2 0.1 copy.44
  417.3 0.0 copy-start
  417.3 0.8 reshape.247
  418.1 0.0 copy-start.3
  418.1 0.0 copy-start.4
  418.1 1.6 multiply_subtract_fusion.2
  419.7 1.0 multiply_subtract_fusion.1
  420.7 3.9 multiply_subtract_fusion
  (26 shorter events, 0.1 us)
Async XLA Ops:
  7.2 5.5 %copy-start.9 = (s32[1024]{0:T(1024)S(1)}, s32[1024]{0:T(1024)}, u32[]{:S(2)}) copy-start(s32[1024]{0:T(1024)} %param.20) | copy-start | bytes 12292
  7.2 5.5 %copy-start.10 = (s32[1024]{0:T(1024)S(1)}, s32[1024]{0:T(1024)}, u32[]{:S(2)}) copy-start(s32[1024]{0:T(1024)} %param.19) | copy-start | bytes 12292
  7.2 162.7 %all-gather.2.cloned.1.call-start = ((), (), s32[]{:S(2)}) async-start(), calls=%async_computation | async-start | bytes 4055040 | tf_op jit(solution)/shard_map/all_gather | solution.py:1438
  10.6 83.2 %copy-start.13 = (s32[4,3]{1,0:T(4,128)S(1)}, s32[4,3]{1,0:T(4,128)}, u32[]{:S(2)}) copy-start(s32[4,3]{1,0:T(4,128)} %constant.143) | copy-start | bytes 148
  10.6 83.2 %copy-start.14 = (s32[4,3]{1,0:T(4,128)S(1)}, s32[4,3]{1,0:T(4,128)}, u32[]{:S(2)}) copy-start(s32[4,3]{1,0:T(4,128)} %constant.142) | copy-start | bytes 148
  10.6 83.7 %copy-start.1 = (f32[320,150]{0,1:T(8,128)S(1)}, f32[320,150]{0,1:T(8,128)}, u32[]{:S(2)}) copy-start(f32[320,150]{0,1:T(8,128)} %param.29) | copy-start | bytes 576004
  93.5 5.0 %copy-start.8 = (f32[22,320]{1,0:T(8,128)S(1)}, f32[22,320]{1,0:T(8,128)}, u32[]{:S(2)}) copy-start(f32[22,320]{1,0:T(8,128)} %param.26) | copy-start | bytes 84484
  99.1 8.5 %copy-start.11 = (s32[10,128]{1,0:T(8,128)S(1)}, s32[10,128]{1,0:T(8,128)}, u32[]{:S(2)}) copy-start(s32[10,128]{1,0:T(8,128)} %constant.141) | copy-start | bytes 15364
  99.1 8.5 %copy-start.12 = (s32[10,128]{1,0:T(8,128)S(1)}, s32[10,128]{1,0:T(8,128)}, u32[]{:S(2)}) copy-start(s32[10,128]{1,0:T(8,128)} %constant.140) | copy-start | bytes 15364
  417.1 2.6 copy-start.2
  417.2 2.5 copy-start.5
  417.2 2.5 copy-start.6
  417.2 2.5 copy-start.7
  417.3 3.4 copy-start
  418.1 2.6 copy-start.3
  418.1 2.6 copy-start.4
Sparse Core Ops, SparseCore 0:
  93.7 63.8 all-gather.1

commit v9 on v8

--- a/solution.py
+++ b/solution.py
@@ -627,12 +627,10 @@
     tiles = rows // 4
     used = FF * 9 * BLOCKS // C
     for ref, base in ((patches_ref, 0), (halo_ref, patches_ref.shape[0])):
-        step = 64
-
-        @pl.loop(0, ref.shape[0] // step, unroll=4)
-        def _(at):
-            span = pl.ds(pl.multiple_of(at * step, step), step)
-            into = pl.ds(pl.multiple_of(base + at * step, step), step)
+        step = 256 if ref.shape[0] % 256 == 0 else ref.shape[0]
+        for at in range(ref.shape[0] // step):
+            span = slice(at * step, (at + 1) * step)
+            into = slice(base + at * step, base + (at + 1) * step)
             part = product(ref[span, :], unit_ref[0, :PIN, :])
             for place, lane, width in lane_parts(C):
                 planes_ref[place, into, :width] = part[:, lane : lane + width]
@@ -740,7 +738,7 @@
 
 
 def head_kernel(
-    resid_ref, gains_ref, weight_ref, label_ref, keep_ref, total_ref,
+    resid_ref, gains_ref, weight_ref, mark_ref, total_ref,
     grad_ref, dhead_ref, dgain_ref, loss_ref,
     final_ref, turned_ref,
 ):
@@ -759,8 +757,8 @@
         logits = product(final, low)
         peak = jnp.max(logits, -1, keepdims=True)
         log_norm = peak + jnp.log(jnp.sum(jnp.exp(logits - peak), -1, keepdims=True))
-        keep = keep_ref[span, :]
-        hit = lax.broadcasted_iota(jnp.int32, (tiles, classes), 1) == label_ref[span, :]
+        keep = mark_ref[span, 1:2]
+        hit = lax.broadcasted_iota(jnp.int32, (tiles, classes), 1).astype(jnp.float32) == mark_ref[span, 0:1]
         picked = jnp.sum(jnp.where(hit, logits, 0.0), -1, keepdims=True)
         loss = loss + jnp.sum((log_norm - picked) * keep, 0, keepdims=True)
         dlogits = (jnp.exp(logits - log_norm) - jnp.where(hit, 1.0, 0.0)) * (keep * share)
@@ -776,7 +774,7 @@
     loss_ref[...] = jnp.broadcast_to(loss, (1, C))
 
 
-def head_step(resid, gains, weight, labels, keep, total):
+def head_step(resid, gains, weight, marks, total):
     rows = resid.shape[0]
     classes = weight.shape[1]
     wide = jnp.float32
@@ -786,7 +784,7 @@
         jax.ShapeDtypeStruct((2, C), wide),
         jax.ShapeDtypeStruct((1, C), wide),
     )
-    operands = (resid, gains, weight, labels, keep, total)
+    operands = (resid, gains, weight, marks, total)
     return pl.pallas_call(
         head_kernel,
         grid=(1,),
@@ -1473,7 +1471,7 @@
         kept_all.append((resid, attn_kept, middle, mlp_kept, w_up))
         resid = output
     grad_res, d_head, final_gains, loss_row = head_step(
-        resid, norm_params[tail + 2 : tail + 4], head_weight, labels[:, None], keep_mask[:, None], counted
+        resid, norm_params[tail + 2 : tail + 4], head_weight, jnp.stack([labels.astype(jnp.float32), keep_mask], 1), counted
     )
     unit_plans = []
     head_cuts = [0, SPLIT, len(bit_order())]

time: 439 us -> 441 us (level); the launches traced: 435 us -> 433 us
  no operation moved by 1% of the time
where the time goes in v9:
time: 441 us; the launch traced here: 433 us
  Pallas kernels  390 us (88%)
  between operations  19.8 us (4%)
  other arithmetic  14.8 us (3%)
  local copies, waits for them, and re-layouts  8.48 us (2%)
    pallas_call x3, Pallas kernels, mlp_backward(): pl.pallas_call(ridden(mlp_backward_kernel, 12, 4, 9, FF // block, plans),...  85.6 us
    pallas_call x1, Pallas kernels, start_exchange(): pl.pallas_call(start_kernel, out_shape=(jax.ShapeDtypeStruct(full_shape,...  79.6 us
    pallas_call x3, Pallas kernels, attention_backward(): pl.pallas_call(run, grid=(1,), out_shape=shapes + tuple((plan.out for pla...  72 us
    pallas_call x3, Pallas kernels, mlp_forward(): pl.pallas_call(mlp_forward_kernel, grid=(FF // block,), out_shape=(jax.Sh...  56 us
    pallas_call x1, Pallas kernels, tail_exchange(): pl.pallas_call(lambda *refs: tail_kernel(counts, rows, pieces, 3 + len(un...  45.6 us
    pallas_call x3, Pallas kernels, attention_forward(): pl.pallas_call(attention_forward_kernel, grid=(1,), out_shape=shapes, in_...  31.1 us
  transfers between devices with their start and end apart: 1, of which 0 were waited for; matrix products, arithmetic and copies ran while one was open for 2% of the time, Pallas kernels for 15%

profile of v9, /device:TPU:1, one launch (start us, length us, event | category | flops | bytes accessed | tf_op | source)
XLA Modules:
  0.0 432.8 jit_solution(18413243466743046070)
XLA Ops:
  7.2 0.0 copy-start.9
  7.2 0.0 copy-start.10
  7.2 0.0 all-gather.2.cloned.1.call-start
  7.2 1.3 fusion.66
  8.6 1.4 convert_element_type.59
  10.0 0.6 reshape.242
  10.6 0.0 copy-start.13
  10.6 0.0 copy-start.14
  10.6 0.0 copy-start.1
  10.6 0.8 copy.51
  12.7 0.6 pad_add_fusion.1.mark_ref
  13.3 0.6 convert_bitcast_fusion.1.count_ref
  13.9 79.6 %start_exchange.1 = (bf16[9,2,2,2,2,2,40,320]{7,6,5,4,3,2,1,0:T(8,128)(2,1)}, bf16[4,40,320]{2,1,0:T(8,128)(2,1)}, f32[8,128]{1,0:T(8,128)}, bf16[192,1152]{1,0:...) custom-call(s32[13]{0:T(128)} %refs_0_.1, bf16[8,2,40,320]{3,2,1,0:T(8,128)(2,1)} %bitcast.47, ...), custom_call_target="tpu_custom_call" | custom-call | tf_op jit(solution)/shard_map/start_exchange/pallas_call | solution.py:1111
  93.5 0.0 all-gather.2.cloned.1.call-update
  93.6 0.2 add_select_fusion.5
  93.8 0.1 add_select_fusion
  93.9 0.1 slice.86
  94.0 0.1 tile.10
  94.1 0.1 eq.57
  94.2 0.1 eq.61
  94.3 0.9 copy.47.weight_ref
  95.1 0.7 pad_add_fusion
  95.8 0.2 reshape.245
  96.0 0.1 copy.46
  96.2 0.1 convert_element_type.65
  96.3 0.1 convert_element_type.67
  96.4 1.1 copy.48.mark_ref
  97.5 0.0 copy-done.8
  97.5 0.6 fusion.64
  98.2 5.9 %embed_forward.1 = (f32[1216,320]{1,0:T(8,128)}, f32[1216,320]{1,0:T(8,128)}, f32[3,9,1280]{2,1,0:T(8,128)}) custom-call(bf16[1024,1152]{1,0:T(8,128)(2,1)} %patches_ref.3, bf16[192,1152]{1,0:T(8,128)(2,1)} %get-tuple-element.100.halo_ref, bf16[9,1280,320]{2,1,0:T(8,128)(2,1)} %bitcast.31, f32[2,320]{1,0:T(2,128)} %get-tuple-element.202.gains_ref), custom_call_target="tpu_custom_call" | custom-call | flops 1000000000 | bytes 8000000 | tf_op jit(solution)/shard_map/embed_forward/pallas_call | solution.py:660
  104.0 0.6 fusion.65
  104.7 1.1 compare_select_fusion.bias_ref.refs_5_
  105.7 1.2 compare_convert_fusion.lower_ref.refs_7_
  107.0 1.3 fusion.upper_ref.refs_6_
  108.3 10.2 %attention_forward.3 = (f32[1216,320]{1,0:T(8,128)}, bf16[1216,320]{1,0:T(8,128)(2,1)}, bf16[1216,384]{1,0:T(8,128)(2,1)}, f32[304,320]{1,0:T(8,128)}, bf16[304,...) custom-call(f32[1216,320]{1,0:T(8,128)} %get-tuple-element.102.resid_ref.r, ...), custom_call_target="tpu_custom_call" | custom-call | flops 6000000000 | bytes 14000000 | tf_op jit(solution)/shard_map/attention_forward/pallas_call | solution.py:610
  118.5 0.8 broadcast_in_dim.34.real_ref.refs_8_
  119.2 18.6 %mlp_forward.3 = (f32[1216,320]{1,0:T(8,128)}, bf16[1216,1280]{1,0:T(8,128)(2,1)}, bf16[1216,1280]{1,0:T(8,128)(2,1)}, bf16[1216,1280]{1,0:T(8,128)(2,1)}, bf16[320,1280]{1,0:T(8,128)(2,1)}) custom-call(f32[1216,320]{1,0:T(8,128)} %get-tuple-element.103.middle_ref.refs_1_, f32[2,320]{1,0:T(2,128)} %get-tuple-element.201.gains_ref.refs_2_, ...), custom_call_target="tpu_custom_call" | custom-call | flops 14000000000 | bytes 18000000 | tf_op jit(solution)/shard_map/mlp_forward/pallas_call | solution.py:321
  137.8 10.7 %attention_forward.4 = (f32[1216,320]{1,0:T(8,128)}, bf16[1216,320]{1,0:T(8,128)(2,1)}, bf16[1216,384]{1,0:T(8,128)(2,1)}, f32[304,320]{1,0:T(8,128)}, bf16[304,...) custom-call(f32[1216,320]{1,0:T(8,128)} %get-tuple-element.105.resid_ref.r, ...), custom_call_target="tpu_custom_call" | custom-call | flops 6000000000 | bytes 14000000 | tf_op jit(solution)/shard_map/attention_forward/pallas_call | solution.py:610
  148.5 18.9 %mlp_forward.4 = (f32[1216,320]{1,0:T(8,128)}, bf16[1216,1280]{1,0:T(8,128)(2,1)}, bf16[1216,1280]{1,0:T(8,128)(2,1)}, bf16[1216,1280]{1,0:T(8,128)(2,1)}, bf16[320,1280]{1,0:T(8,128)(2,1)}) custom-call(f32[1216,320]{1,0:T(8,128)} %get-tuple-element.106.middle_ref.refs_1_, f32[2,320]{1,0:T(2,128)} %get-tuple-element.200.gains_ref.refs_2_, ...), custom_call_target="tpu_custom_call" | custom-call | flops 14000000000 | bytes 18000000 | tf_op jit(solution)/shard_map/mlp_forward/pallas_call | solution.py:321
  167.4 0.0 all-gather.2.cloned.1.call-done.unit_ref.reduce_ref.up_ref.down_ref.refs_4_.refs_3_
  167.5 10.2 %attention_forward.5 = (f32[1216,320]{1,0:T(8,128)}, bf16[1216,320]{1,0:T(8,128)(2,1)}, bf16[1216,384]{1,0:T(8,128)(2,1)}, f32[304,320]{1,0:T(8,128)}, bf16[304,...) custom-call(f32[1216,320]{1,0:T(8,128)} %get-tuple-element.107.resid_ref.r, ...), custom_call_target="tpu_custom_call" | custom-call | flops 6000000000 | bytes 14000000 | tf_op jit(solution)/shard_map/attention_forward/pallas_call | solution.py:610
  177.7 18.5 %mlp_forward.5 = (f32[1216,320]{1,0:T(8,128)}, bf16[1216,1280]{1,0:T(8,128)(2,1)}, bf16[1216,1280]{1,0:T(8,128)(2,1)}, bf16[1216,1280]{1,0:T(8,128)(2,1)}, bf16[320,1280]{1,0:T(8,128)(2,1)}) custom-call(f32[1216,320]{1,0:T(8,128)} %get-tuple-element.109.middle_ref.refs_1_, f32[2,320]{1,0:T(2,128)} %get-tuple-element.199.gains_ref.refs_2_, ...), custom_call_target="tpu_custom_call" | custom-call | flops 14000000000 | bytes 18000000 | tf_op jit(solution)/shard_map/mlp_forward/pallas_call | solution.py:321
  196.2 7.0 %head_step.1 = (f32[1216,320]{1,0:T(8,128)}, f32[152,320]{1,0:T(8,128)}, f32[2,320]{1,0:T(2,128)}, f32[1,320]{1,0:T(1,128)}) custom-call(f32[1216,320]{1,0:T(8,128)} %get-tuple-element.110.resid_ref, f32[2,320]{1,0:T(2,128)} %get-tuple-element.198.gains_ref, f32[320,150]{1,0:T(8,128)} %copy.47.weight_ref, f32[1216,2]{1,0:T(8,128)} %copy.48.mark_ref, ...), custom_call_target="tpu_custom_call" | custom-call | flops 1000000000 | bytes 5000000 | tf_op jit(solution)/shard_map/head_step/pallas_call | solution.py:788
  203.3 28.1 %mlp_backward.3 = (f32[1216,320]{1,0:T(8,128)}, bf16[2,1280,320]{2,1,0:T(8,128)(2,1)}, f32[9,1280]{1,0:T(8,128)}, f32[2,320]{1,0:T(2,128)}, f32[152,320]{1,0:T(8,128)}) custom-call(f32[1216,320]{1,0:T(8,128)} %get-tuple-element.113.refs_0_, f32[1216,320]{1,0:T(8,128)} %get-tuple-element.109.middle_ref.refs_1_, ...), custom_call_target="tpu_custom_call" | custom-call | flops 17999998976 | bytes 18000000 | tf_op jit(solution)/shard_map/mlp_backward/pallas_call | solution.py:438
  231.4 25.6 %attention_backward.3 = (f32[1216,320]{1,0:T(8,128)}, bf16[2,1280,320]{2,1,0:T(8,128)(2,1)}, f32[4,320]{1,0:T(4,128)}, bf16[2,2,2,1,40,320]{5,4,3,2,1,0:T(8,128)(2,1)}, f32[152,320]{1,0:T(8,128)}) custom-call(f32[1216,320]{1,0:T(8,128)} %get-tuple-element.119.refs_0_, f32[1216,320]{1,0:T(8,128)} %get-tuple-element.107.resid_ref.refs_1_, ...), custom_call_target="tpu_custom_call" | custom-call | flops 12000000000 | bytes 18000000 | tf_op jit(solution)/shard_map/attention_backward/pallas_call | solution.py:919
  257.1 28.3 %mlp_backward.4 = (f32[1216,320]{1,0:T(8,128)}, bf16[2,1280,320]{2,1,0:T(8,128)(2,1)}, f32[9,1280]{1,0:T(8,128)}, f32[2,320]{1,0:T(2,128)}, bf16[2,2,2,1,40,320]...) custom-call(f32[1216,320]{1,0:T(8,128)} %get-tuple-element.129.refs_0_, ...), custom_call_target="tpu_custom_call" | custom-call | flops 17999998976 | bytes 18000000 | tf_op jit(solution)/shard_map/mlp_backward/pallas_call | solution.py:438
  285.3 24.3 %attention_backward.4 = (f32[1216,320]{1,0:T(8,128)}, bf16[2,1280,320]{2,1,0:T(8,128)(2,1)}, f32[4,320]{1,0:T(4,128)}, bf16[2,2,2,1,40,320]{5,4,3,2,1,0:T(8,128)(2,1)}, bf16[2,40,320]{2,1,0:T(8,128)(2,1)}) custom-call(f32[1216,320]{1,0:T(8,128)} %get-tuple-element.136.refs_0_, f32[1216,320]{1,0:T(8,128)} %get-tuple-element.105.resid_ref.refs_1_, ...), custom_call_target="tpu_custom_call" | custom-call | flops 12000000000 | bytes 18000000 | tf_op jit(solution)/shard_map/attention_backward/pallas_call | solution.py:919
  309.6 29.2 %mlp_backward.5 = (f32[1216,320]{1,0:T(8,128)}, bf16[2,1280,320]{2,1,0:T(8,128)(2,1)}, f32[9,1280]{1,0:T(8,128)}, f32[2,320]{1,0:T(2,128)}, bf16[2,2,2,1,40,320]...) custom-call(f32[1216,320]{1,0:T(8,128)} %get-tuple-element.146.refs_0_, ...), custom_call_target="tpu_custom_call" | custom-call | flops 17999998976 | bytes 18000000 | tf_op jit(solution)/shard_map/mlp_backward/pallas_call | solution.py:438
  338.9 22.1 %attention_backward.5 = (f32[1216,320]{1,0:T(8,128)}, bf16[2,1280,320]{2,1,0:T(8,128)(2,1)}, f32[4,320]{1,0:T(4,128)}, bf16[2,2,2,1,40,320]{5,4,3,2,1,0:T(8,128)(2,1)}, bf16[2,40,320]{2,1,0:T(8,128)(2,1)}) custom-call(f32[1216,320]{1,0:T(8,128)} %get-tuple-element.153.refs_0_, f32[1216,320]{1,0:T(8,128)} %get-tuple-element.102.resid_ref.refs_1_, ...), custom_call_target="tpu_custom_call" | custom-call | flops 12000000000 | bytes 18000000 | tf_op jit(solution)/shard_map/attention_backward/pallas_call | solution.py:919
  361.0 6.7 %embed_backward.1 = (bf16[1,1280,320]{2,1,0:T(8,128)(2,1)}, f32[2,320]{1,0:T(2,128)}) custom-call(f32[1216,320]{1,0:T(8,128)} %get-tuple-element.168.grad_ref, f32[1216,320]{1,0:T(8,128)} %get-tuple-element.169.pre_ref, f32[2,320]{1,0:T(2,128)} %get-tuple-element.202.gains_ref, bf16[1024,1152]{1,0:T(8,128)(2,1)} %patches_ref.3, ...), custom_call_target="tpu_custom_call" | custom-call | flops 1000000000 | bytes 8000000 | tf_op jit(solution)/shard_map/embed_backward/pallas_call | solution.py:723
  367.7 45.6 %tail_exchange.1 = (bf16[8,2,40,320]{3,2,1,0:T(8,128)(2,1)}, f32[24,320]{1,0:T(8,128)}, f32[1,1]{1,0:T(1,128)}) custom-call(s32[13]{0:T(128)} %refs_0_.1, bf16[2,2,2,1,40,320]{5,4,3,2,1,0:T(8,128)(2,1)} %get-tuple-element.163.refs_1_, bf16[2,40,320]{2,1,0:T(8,128)(2,1)} %get-tuple-element.164.refs_2_, bf16[2,40,320]{2,1,0:T(8,128)(2,1)} %get-tuple-element.165.refs_3_, ...), custom_call_target="tpu_custom_call" | custom-call | tf_op jit(solution)/shard_map/tail_exchange/pallas_call | solution.py:1372
  413.3 1.1 convert_bitcast_fusion
  414.4 0.0 copy-start.2
  414.4 0.0 copy-start.5
  414.4 0.0 copy-start.6
  414.5 0.1 copy.49
  414.5 0.0 copy-start
  414.6 0.8 reshape.258
  415.4 0.0 copy-start.3
  415.4 0.0 copy-start.4
  415.4 1.6 multiply_subtract_fusion.2
  417.0 0.0 copy-done.2
  417.0 1.0 multiply_subtract_fusion.1
  418.0 3.9 multiply_subtract_fusion
  (27 shorter events, 0.1 us)
Async XLA Ops:
  7.2 5.5 %copy-start.9 = (s32[1024]{0:T(1024)S(1)}, s32[1024]{0:T(1024)}, u32[]{:S(2)}) copy-start(s32[1024]{0:T(1024)} %param.20) | copy-start | bytes 12292
  7.2 5.5 %copy-start.10 = (s32[1024]{0:T(1024)S(1)}, s32[1024]{0:T(1024)}, u32[]{:S(2)}) copy-start(s32[1024]{0:T(1024)} %param.19) | copy-start | bytes 12292
  7.2 160.3 %all-gather.2.cloned.1.call-start = ((), (), s32[]{:S(2)}) async-start(), calls=%async_computation | async-start | bytes 4055040 | tf_op jit(solution)/shard_map/all_gather | solution.py:1436
  10.6 83.2 %copy-start.13 = (s32[4,3]{1,0:T(4,128)S(1)}, s32[4,3]{1,0:T(4,128)}, u32[]{:S(2)}) copy-start(s32[4,3]{1,0:T(4,128)} %constant.143) | copy-start | bytes 148
  10.6 83.2 %copy-start.14 = (s32[4,3]{1,0:T(4,128)S(1)}, s32[4,3]{1,0:T(4,128)}, u32[]{:S(2)}) copy-start(s32[4,3]{1,0:T(4,128)} %constant.142) | copy-start | bytes 148
  10.6 83.7 %copy-start.1 = (f32[320,150]{0,1:T(8,128)S(1)}, f32[320,150]{0,1:T(8,128)}, u32[]{:S(2)}) copy-start(f32[320,150]{0,1:T(8,128)} %param.29) | copy-start | bytes 576004
  13.9 83.6 %copy-start.8 = (f32[22,320]{1,0:T(8,128)S(1)}, f32[22,320]{1,0:T(8,128)}, u32[]{:S(2)}) copy-start(f32[22,320]{1,0:T(8,128)} %param.26) | copy-start | bytes 84484
  98.2 6.5 %copy-start.11 = (s32[10,128]{1,0:T(8,128)S(1)}, s32[10,128]{1,0:T(8,128)}, u32[]{:S(2)}) copy-start(s32[10,128]{1,0:T(8,128)} %constant.141) | copy-start | bytes 15364
  98.2 6.5 %copy-start.12 = (s32[10,128]{1,0:T(8,128)S(1)}, s32[10,128]{1,0:T(8,128)}, u32[]{:S(2)}) copy-start(s32[10,128]{1,0:T(8,128)} %constant.140) | copy-start | bytes 15364
  414.4 2.6 copy-start.2
  414.4 2.5 copy-start.5
  414.4 2.5 copy-start.6
  414.5 2.5 copy-start.7
  414.5 3.4 copy-start
  415.4 2.6 copy-start.3
  415.4 2.6 copy-start.4
Sparse Core Ops, SparseCore 0:
  93.7 63.8 all-gather.1
